TPU v7x, 32 devices: a whole 2x2x4 slice. The times are simulated.
32 devices in a mesh: gx: 4 (over y, core), gy: 8 (over z, x).
Axes of the slice: x: 2, y: 2, z: 4, core: 2. Of those that a mesh axis runs over, the one named last changes fastest.
Arguments:
- load: float32 [2, 128, 128, 128], P(None, 'gx', 'gy'), may hold values from -8 to 8
- zones: int32 [128, 128, 128], P('gx', 'gy'), may hold values from 0 to 7
- conductance: float32 [2, 8], replicated, may hold values from 0.2 to 1
- capacity: float32 [2, 8], replicated, may hold values from 0.5 to 2
- coupling: float32 [8], replicated, may hold values from 0.2 to 0.8
Outputs:
- solution: float32 [2, 128, 128, 128], P(None, 'gx', 'gy')
- residual: float32 [2, 128, 128, 128], P(None, 'gx', 'gy')
All inputs are finite; a program needn't handle non-finite values.
Results may differ from a plain program's by a relative error of at most 0.006.
Values sent between devices are 32-bit elements; how exact they have to be, the bound alone decides.
No kernel may reach another device: no remote copies, remote signals or barrier semaphores. Data moves between devices by JAX's collectives and lax.ppermute only.
A program may use at most 64 MiB of HBM per device.

v0:
```python
import jax
import jax.numpy as jnp
from jax import lax
from jax.sharding import PartitionSpec as P

BOX = 16
ITERS = 2


NEIGHBOURS = ((1, 0, 0), (-1, 0, 0), (0, 1, 0), (0, -1, 0), (0, 0, 1), (0, 0, -1))


def with_halo(block, sides, width):
    for axis, dim in sides:
        count = lax.axis_size(axis)
        forward = [(i, i + 1) for i in range(count - 1)]
        backward = [(target, source) for source, target in forward]
        low = lax.ppermute(
            lax.slice_in_dim(block, block.shape[dim] - width, None, axis=dim), axis, forward
        )
        high = lax.ppermute(lax.slice_in_dim(block, 0, width, axis=dim), axis, backward)
        block = jnp.concatenate([low, block, high], axis=dim)
    return block


def neighbour(array, offset_x, offset_y, offset_z):
    size_x, size_y, size_z = array.shape[-3:]
    return array[
        ...,
        1 + offset_x : size_x - 1 + offset_x,
        1 + offset_y : size_y - 1 + offset_y,
        1 + offset_z : size_z - 1 + offset_z,
    ]


def apply_operator(field, padded, kpadded, inside, mass):
    center = kpadded[:, 1:-1, 1:-1, 1:-1]
    flux = jnp.zeros_like(field)
    for offset_x, offset_y, offset_z in NEIGHBOURS:
        other_k = neighbour(kpadded, offset_x, offset_y, offset_z)
        other_in = neighbour(inside, offset_x, offset_y, offset_z)
        face = 0.5 * (center + jnp.where(other_in[None], other_k, center))
        flux = flux + face * (field - neighbour(padded, offset_x, offset_y, offset_z))
    first = mass[0] * field[0] + mass[2] * field[1] + flux[0]
    second = mass[2] * field[0] + mass[1] * field[1] + flux[1]
    return jnp.stack([first, second])


def box_matrix(cells):
    span = BOX + 2
    count = cells // BOX
    rows = jnp.arange(count * span)
    block_of = rows // span
    mode_of = rows % span
    columns = jnp.arange(cells + 2)
    offset = columns[None, :] - BOX * block_of[:, None]
    valid = (offset >= 0) & (offset < span)
    angle_arg = (
        jnp.pi
        * (offset + 1).astype(jnp.float32)
        * (mode_of[:, None] + 1).astype(jnp.float32)
        / (span + 1)
    )
    basis = jnp.sqrt(2.0 / (span + 1)) * jnp.sin(angle_arg)
    return jnp.where(valid, basis, 0.0)


def box_eigen():
    span = BOX + 2
    modes = jnp.arange(span).astype(jnp.float32)
    return 4.0 * jnp.sin(jnp.pi * (modes + 1.0) / (2.0 * (span + 1))) ** 2


def box_means(values):
    fields, size_x, size_y, size_z = values.shape
    shaped = values.reshape(fields, size_x // BOX, BOX, size_y // BOX, BOX, size_z // BOX, BOX)
    return jnp.mean(shaped, axis=(2, 4, 6))


def solve_boxes(padded, cbar, kbar):
    highest = lax.Precision.HIGHEST
    fields, length_x, length_y, length_z = padded.shape
    matrix_x = box_matrix(length_x - 2)
    matrix_y = box_matrix(length_y - 2)
    matrix_z = box_matrix(length_z - 2)
    spectral = jnp.einsum("am,fmyz->fayz", matrix_x, padded, precision=highest)
    spectral = jnp.einsum("bn,fanz->fabz", matrix_y, spectral, precision=highest)
    spectral = jnp.einsum("co,fabo->fabc", matrix_z, spectral, precision=highest)
    boxes_x, boxes_y, boxes_z = cbar.shape[1:]
    span = BOX + 2
    eigen = box_eigen()
    summed = eigen[:, None, None] + eigen[None, :, None] + eigen[None, None, :]
    divisor = (
        cbar[:, :, None, :, None, :, None]
        + kbar[:, :, None, :, None, :, None] * summed[None, None, :, None, :, None, :]
    )
    spectral = spectral.reshape(fields, boxes_x, span, boxes_y, span, boxes_z, span) / divisor
    spectral = spectral.reshape(fields, boxes_x * span, boxes_y * span, boxes_z * span)
    spectral = jnp.einsum("co,fabc->fabo", matrix_z, spectral, precision=highest)
    spectral = jnp.einsum("bn,fabo->fano", matrix_y, spectral, precision=highest)
    return jnp.einsum("am,fano->fmno", matrix_x, spectral, precision=highest)


def gather_rims(extended):
    size_x = extended.shape[1] - 2
    size_y = extended.shape[2] - 2
    edges = jnp.concatenate([extended[:, 0:1], extended[:, -1:]], axis=1)
    arrived = with_halo(edges, (("gx", 1),), 1)
    middle = extended[:, 1:-1]
    middle = middle.at[:, 0].add(arrived[:, 0]).at[:, size_x - 1].add(arrived[:, 3])
    edges = jnp.concatenate([middle[:, :, 0:1], middle[:, :, -1:]], axis=2)
    arrived = with_halo(edges, (("gy", 2),), 1)
    result = middle[:, :, 1:-1]
    return result.at[:, :, 0].add(arrived[:, :, 0]).at[:, :, size_y - 1].add(arrived[:, :, 3])


def shards(load, zones, conductance, capacity, coupling):
    cross = coupling * jnp.sqrt(capacity[0] * capacity[1])
    tables = jnp.concatenate([conductance, capacity, cross[None]], axis=0)
    marks = with_halo(zones + 1, (("gx", 0), ("gy", 1)), 1)
    marks = jnp.pad(marks, ((0, 0), (0, 0), (1, 1)))
    inside = marks > 0
    labels = jnp.arange(1, tables.shape[1] + 1, dtype=jnp.int32)
    indicator = (marks[None] == labels[:, None, None, None]).astype(jnp.float32)
    coeffs = jnp.einsum("tq,qxyz->txyz", tables, indicator, precision=lax.Precision.HIGHEST)
    kpadded = coeffs[0:2]
    mass = coeffs[2:5, 1:-1, 1:-1, 1:-1]
    cbar = box_means(mass[0:2])
    kbar = box_means(kpadded[:, 1:-1, 1:-1, 1:-1])
    solution = jnp.zeros_like(load)
    residual = load
    direction = load
    previous = jnp.float32(1.0)
    for iteration in range(ITERS):
        padded = with_halo(residual, (("gx", 1), ("gy", 2)), 1)
        padded = jnp.pad(padded, ((0, 0), (0, 0), (0, 0), (1, 1)))
        extended = solve_boxes(padded, cbar, kbar)[..., 1:-1]
        precond = gather_rims(extended)
        product = lax.psum(jnp.sum(residual * precond), ("gx", "gy"))
        if iteration == 0:
            direction = precond
        else:
            direction = precond + product / previous * direction
        operate_padded = with_halo(direction, (("gx", 1), ("gy", 2)), 1)
        operate_padded = jnp.pad(operate_padded, ((0, 0), (0, 0), (0, 0), (1, 1)))
        image = apply_operator(direction, operate_padded, kpadded, inside, mass)
        curvature = lax.psum(jnp.sum(direction * image), ("gx", "gy"))
        alpha = product / curvature
        solution = solution + alpha * direction
        residual = residual - alpha * image
        previous = product
    return (solution, residual)


def solution(mesh):
    in_specs = (P(None, "gx", "gy", None), P("gx", "gy", None), P(), P(), P())
    out_specs = (P(None, "gx", "gy", None), P(None, "gx", "gy", None))
    return jax.shard_map(shards, mesh=mesh, in_specs=in_specs, out_specs=out_specs, check_vma=False)
```

profile of v0, /device:TPU:0, one launch (start us, length us, event | category | flops | bytes accessed | tf_op | source)
XLA Modules:
  0.0 320.7 jit_solution(9534765781686281665)
XLA Ops:
  2.7 3.0 collective-permute-start
  7.4 4.5 %collective-permute-start.4 = (s32[1,16,128]{2,1,0:T(8,128)S(1)}, s32[1,16,128]{2,1,0:T(8,128)S(1)}, u32[]{:S(2)}, u32[]{:S(2)}) collective-permute-start(s32[1,16,128]{2,1,0:T(8,128)S(1)} %get-tuple-element.140), channel_id=1, source_target_pairs={{0,8},{8,16},{16,24},{1,9},{9,17},{17,25},{2,10},{10,18},{18,26},{... | collective-permute-start | bytes 24584 | tf_op jit(solution)/shard_map/ppermute | solution.py:18
  18.2 3.4 %collective-permute-start.6 = (s32[34,1,128]{2,1,0:T(1,128)S(1)}, s32[34,1,128]{2,1,0:T(1,128)S(1)}, u32[]{:S(2)}, u32[]{:S(2)}) collective-permute-start(s32[34,1,128]{2,1,0:T(1,128)S(1)} %get-tuple-element.138), channel_id=1, source_target_pairs={{0,1},{1,2},{2,3},{3,4},{4,5},{5,6},{6,7},{8,9},{9,10},{10,11},{11... | collective-permute-start | bytes 52232 | tf_op jit(solution)/shard_map/ppermute | solution.py:18
  23.0 4.5 %collective-permute-start.2 = (f32[2,34,1,128]{3,1,2,0:T(8,128)S(1)}, f32[2,34,1,128]{3,1,2,0:T(8,128)S(1)}, u32[]{:S(2)}, u32[]{:S(2)}) collective-permute-start(f32[2,34,1,128]{3,1,2,0:T(8,128)S(1)} %get-tuple-element.128), channel_id=1, source_target_pairs={{0,1},{1,2},{2,3},{3,4},{4,5},{5,6},{6,7},{8,9},{9,10},{10,11},{11... | collective-permute-start | bytes 104456 | tf_op jit(solution)/shard_map/ppermute | solution.py:18
  29.4 2.4 fusion
  31.8 2.2 copy-done
  42.5 2.5 fusion.14
  49.6 2.2 collective-permute-start.8
  53.9 3.8 %collective-permute-done.9 = f32[2,1,18,128]{3,0,2,1:T(2,128)S(1)} collective-permute-done((f32[2,1,18,128]{3,0,2,1:T(2,128)S(1)}, f32[2,1,18,128]{3,0,2,1:T(2,128)S(1)}, u32[]{:S(2)}, u32[]{:S(2)}) %collective-permute-start.9) | collective-permute-done | bytes 18464 | tf_op jit(solution)/shard_map/ppermute | solution.py:21
  57.7 5.0 %collective-permute-start.10 = (f32[2,32,1,128]{3,0,2,1:T(2,128)S(1)}, f32[2,32,1,128]{3,0,2,1:T(2,128)S(1)}, u32[]{:S(2)}, u32[]{:S(2)}) collective-permute-start(f32[2,32,1,128]{3,0,2,1:T(2,128)S(1)} %get-tuple-element.121), channel_id=1, source_target_pairs={{0,1},{1,2},{2,3},{3,4},{4,5},{5,6},{6,7},{8,9},{9,10},{10,11},{11... | collective-permute-start | bytes 98312 | tf_op jit(solution)/shard_map/ppermute | solution.py:18
  64.3 5.2 %collective-permute-done.11 = f32[2,32,1,128]{3,0,2,1:T(2,128)S(1)} collective-permute-done((f32[2,32,1,128]{3,0,2,1:T(2,128)S(1)}, f32[2,32,1,128]{3,0,2,1:T(2,128)S(1)}, u32[]{:S(2)}, u32[]{:S(2)}) %collective-permute-start.11) | collective-permute-done | bytes 32800 | tf_op jit(solution)/shard_map/ppermute | solution.py:21
  69.5 3.3 %collective-permute-start.13 = (f32[2,1,16,128]{3,0,2,1:T(2,128)S(1)}, f32[2,1,16,128]{3,0,2,1:T(2,128)S(1)}, u32[]{:S(2)}, u32[]{:S(2)}) collective-permute-start(f32[2,1,16,128]{3,0,2,1:T(2,128)S(1)} %get-tuple-element.134), channel_id=1, source_target_pairs={{0,8},{8,16},{16,24},{1,9},{9,17},{17,25},{2,10},{10,18},{18,26},{... | collective-permute-start | bytes 49160 | tf_op jit(solution)/shard_map/ppermute | solution.py:18
  76.6 4.8 %collective-permute-start.15 = (f32[2,34,1,128]{3,0,2,1:T(2,128)S(1)}, f32[2,34,1,128]{3,0,2,1:T(2,128)S(1)}, u32[]{:S(2)}, u32[]{:S(2)}) collective-permute-start(f32[2,34,1,128]{3,0,2,1:T(2,128)S(1)} %get-tuple-element.126), channel_id=1, source_target_pairs={{0,1},{1,2},{2,3},{3,4},{4,5},{5,6},{6,7},{8,9},{9,10},{10,11},{11... | collective-permute-start | bytes 104456 | tf_op jit(solution)/shard_map/ppermute | solution.py:18
  83.6 3.7 %collective-permute-done.14 = f32[2,34,1,128]{3,0,2,1:T(2,128)S(1)} collective-permute-done((f32[2,34,1,128]{3,0,2,1:T(2,128)S(1)}, f32[2,34,1,128]{3,0,2,1:T(2,128)S(1)}, u32[]{:S(2)}, u32[]{:S(2)}) %collective-permute-start.14) | collective-permute-done | bytes 34848 | tf_op jit(solution)/shard_map/ppermute | solution.py:21
  87.3 3.3 %select_maximum_fusion.14 = f32[2,34,18,130]{3,0,2,1:T(2,128)S(1)} fusion(f32[2,34,1,128]{3,0,2,1:T(2,128)S(1)} %collective-permute-done.14, f32[2,34,1,128]{3,0,2,1:T(2,128)S(1)} %collective-permute-done.15, f32[2,1,16,128]{3,0,2,1:T(2,128)S(1)} %collective-permute-done.12, f32[2,32,16,128]{3,0,2,1:T(2,128)S(1)} %fusion.89, ...), kind=kLoop, calls=%fused_computation.46 | loop fusion | flops 1909440 | bytes 1263168 | tf_op jit(solution)/shard_map/concatenate | solution.py:22
  90.6 7.2 %fusion.66 = f32[2,32,16,128]{3,0,2,1:T(2,128)S(1)} fusion(f32[2,32,16,128]{3,0,2,1:T(2,128)S(1)} %fusion.89, f32[2,34,18,130]{3,0,2,1:T(2,128)S(1)} %select_maximum_fusion.14, f32[2,34,1,128]{3,0,2,1:T(2,128)S(1)} %collective-permute-done.15, f32[2,1,16,128]{3,0,2,1:T(2,128)S(1)} %collective-permute-done.12, ...), kind=kLoop, calls=%fused_computation.101 | loop fusion | flops 5636096 | bytes 6262784 | tf_op jit(solution)/shard_map/add | solution.py:43
  101.4 41.0 %all-reduce.5 = (f32[]{:T(128)}, f32[]{:T(128)}) all-reduce(f32[]{:T(128)} %get-tuple-element.107, f32[]{:T(128)} %get-tuple-element.106), channel_id=1, replica_groups=mesh['gx'=4,'gy'=8] {'gx','gy'}, use_global_device_ids=true, to_apply=%region_5.6 | all-reduce | flops 2 | bytes 16 | tf_op jit(solution)/shard_map/psum | solution.py:139
  147.2 4.5 %collective-permute-done.17 = f32[2,1,16,128]{3,0,2,1:T(2,128)S(1)} collective-permute-done((f32[2,1,16,128]{3,0,2,1:T(2,128)S(1)}, f32[2,1,16,128]{3,0,2,1:T(2,128)S(1)}, u32[]{:S(2)}, u32[]{:S(2)}) %collective-permute-start.17) | collective-permute-done | bytes 16416 | tf_op jit(solution)/shard_map/ppermute | solution.py:21
  151.7 3.0 collective-permute-start.18
  156.3 4.2 %collective-permute-done.19 = f32[2,34,1,128]{3,0,2,1:T(2,128)S(1)} collective-permute-done((f32[2,34,1,128]{3,0,2,1:T(2,128)S(1)}, f32[2,34,1,128]{3,0,2,1:T(2,128)S(1)}, u32[]{:S(2)}, u32[]{:S(2)}) %collective-permute-start.19) | collective-permute-done | bytes 34848 | tf_op jit(solution)/shard_map/ppermute | solution.py:21
  173.7 3.0 collective-permute-start.20
  178.7 2.6 collective-permute-done.21
  181.4 3.5 %collective-permute-start.22 = (f32[2,32,1,128]{3,0,2,1:T(2,128)S(1)}, f32[2,32,1,128]{3,0,2,1:T(2,128)S(1)}, u32[]{:S(2)}, u32[]{:S(2)}) collective-permute-start(f32[2,32,1,128]{3,0,2,1:T(2,128)S(1)} %get-tuple-element.119), channel_id=1, source_target_pairs={{0,1},{1,2},{2,3},{3,4},{4,5},{5,6},{6,7},{8,9},{9,10},{10,11},{11... | collective-permute-start | bytes 98312 | tf_op jit(solution)/shard_map/ppermute | solution.py:18
  186.5 4.3 %collective-permute-done.23 = f32[2,32,1,128]{3,0,2,1:T(2,128)S(1)} collective-permute-done((f32[2,32,1,128]{3,0,2,1:T(2,128)S(1)}, f32[2,32,1,128]{3,0,2,1:T(2,128)S(1)}, u32[]{:S(2)}, u32[]{:S(2)}) %collective-permute-start.23) | collective-permute-done | bytes 32800 | tf_op jit(solution)/shard_map/ppermute | solution.py:21
  192.3 41.1 %psum.30 = f32[]{:T(128)} all-reduce(f32[]{:T(128)} %multiply_reduce_fusion.1), channel_id=1, replica_groups=mesh['gx'=4,'gy'=8] {'gx','gy'}, use_global_device_ids=true, to_apply=%region_9.10 | all-reduce | flops 1 | bytes 8 | tf_op jit(solution)/shard_map/psum | solution.py:139
  237.4 4.5 %collective-permute-done.24 = f32[2,1,16,128]{3,0,2,1:T(2,128)S(1)} collective-permute-done((f32[2,1,16,128]{3,0,2,1:T(2,128)S(1)}, f32[2,1,16,128]{3,0,2,1:T(2,128)S(1)}, u32[]{:S(2)}, u32[]{:S(2)}) %collective-permute-start.24) | collective-permute-done | bytes 16416 | tf_op jit(solution)/shard_map/ppermute | solution.py:21
  241.9 2.8 collective-permute-start.27
  246.3 4.2 %collective-permute-done.26 = f32[2,34,1,128]{3,0,2,1:T(2,128)S(1)} collective-permute-done((f32[2,34,1,128]{3,0,2,1:T(2,128)S(1)}, f32[2,34,1,128]{3,0,2,1:T(2,128)S(1)}, u32[]{:S(2)}, u32[]{:S(2)}) %collective-permute-start.26) | collective-permute-done | bytes 34848 | tf_op jit(solution)/shard_map/ppermute | solution.py:21
  250.6 3.3 %select_maximum_fusion.10 = f32[2,34,18,130]{3,0,2,1:T(2,128)S(1)} fusion(f32[2,34,1,128]{3,0,2,1:T(2,128)S(1)} %collective-permute-done.26, f32[2,34,1,128]{3,0,2,1:T(2,128)S(1)} %collective-permute-done.27, f32[2,1,16,128]{3,0,2,1:T(2,128)S(1)} %collective-permute-done.24, f32[2,32,16,128]{3,0,2,1:T(2,128)S(1)} %bitcast.96, ...), kind=kLoop, calls=%fused_computation.42 | loop fusion | flops 1909440 | bytes 1263168 | tf_op jit(solution)/shard_map/concatenate | solution.py:22
  253.9 12.5 %fusion.51 = f32[2,32,16,128]{3,0,2,1:T(2,128)S(1)} fusion(f32[2,32,16,128]{3,0,2,1:T(2,128)S(1)} %bitcast.97, f32[2,34,18,130]{3,0,2,1:T(2,128)S(1)} %select_maximum_fusion.10, f32[2,34,1,128]{3,0,2,1:T(2,128)S(1)} %collective-permute-done.27, f32[2,1,16,128]{3,0,2,1:T(2,128)S(1)} %collective-permute-done.24, ...), kind=kLoop, calls=%fused_computation.76 | loop fusion | flops 5636096 | bytes 6262784 | tf_op jit(solution)/shard_map/add | solution.py:43
  266.4 6.8 %slice_add_fusion.1 = (f32[1,32,16,128]{3,0,2,1:T(1,128)S(1)}, f32[1,32,16,128]{3,0,2,1:T(1,128)S(1)}) fusion(f32[2,32,16,128]{3,0,2,1:T(2,128)S(1)} %fusion.51, f32[2,32,16,128]{3,0,2,1:T(2,128)S(1)} %bitcast.98, f32[5,34,18,130]{3,0,2,1:T(8,128)} %copy-done), kind=kLoop, calls=%fused_computation.138 | loop fusion | flops 524288 | bytes 2359296 | tf_op jit(solution)/shard_map/add | solution.py:44
  274.3 41.8 %psum.31 = f32[]{:T(128)} all-reduce(f32[]{:T(128)} %multiply_reduce_fusion), channel_id=1, replica_groups=mesh['gx'=4,'gy'=8] {'gx','gy'}, use_global_device_ids=true, to_apply=%region_11.12 | all-reduce | flops 1 | bytes 8 | tf_op jit(solution)/shard_map/psum | solution.py:147
  (140 shorter events, 71.0 us)
Async XLA Ops:
  1.4 21.6 %collective-permute-start.1 = (f32[2,1,16,128]{3,1,2,0:T(1,128)S(1)}, f32[2,1,16,128]{3,1,2,0:T(1,128)S(1)}, u32[]{:S(2)}, u32[]{:S(2)}) collective-permute-start(f32[2,1,16,128]{3,1,2,0:T(1,128)S(1)} %bitcast.109), channel_id=1, source_target_pairs={{8,0},{16,8},{24,16},{9,1},{17,9},{25,17},{10,2},{18,10},{26,18},{... | collective-permute-start | bytes 49160 | tf_op jit(solution)/shard_map/ppermute | solution.py:21
  2.7 20.3 %collective-permute-start = (f32[2,1,16,128]{3,1,2,0:T(1,128)S(1)}, f32[2,1,16,128]{3,1,2,0:T(1,128)S(1)}, u32[]{:S(2)}, u32[]{:S(2)}) collective-permute-start(f32[2,1,16,128]{3,1,2,0:T(1,128)S(1)} %bitcast.108), channel_id=1, source_target_pairs={{0,8},{8,16},{16,24},{1,9},{9,17},{17,25},{2,10},{10,18},{18,26},{... | collective-permute-start | bytes 49160 | tf_op jit(solution)/shard_map/ppermute | solution.py:18
  7.4 10.2 %collective-permute-start.4 = (s32[1,16,128]{2,1,0:T(8,128)S(1)}, s32[1,16,128]{2,1,0:T(8,128)S(1)}, u32[]{:S(2)}, u32[]{:S(2)}) collective-permute-start(s32[1,16,128]{2,1,0:T(8,128)S(1)} %get-tuple-element.140), channel_id=1, source_target_pairs={{0,8},{8,16},{16,24},{1,9},{9,17},{17,25},{2,10},{10,18},{18,26},{... | collective-permute-start | bytes 24584 | tf_op jit(solution)/shard_map/ppermute | solution.py:18
  11.9 5.7 %collective-permute-start.5 = (s32[1,16,128]{2,1,0:T(8,128)S(1)}, s32[1,16,128]{2,1,0:T(8,128)S(1)}, u32[]{:S(2)}, u32[]{:S(2)}) collective-permute-start(s32[1,16,128]{2,1,0:T(8,128)S(1)} %get-tuple-element.141), channel_id=1, source_target_pairs={{8,0},{16,8},{24,16},{9,1},{17,9},{25,17},{10,2},{18,10},{26,18},{... | collective-permute-start | bytes 24584 | tf_op jit(solution)/shard_map/ppermute | solution.py:21
  17.5 25.0 %copy-start.5 = (f32[36,18,144]{2,1,0:T(8,128)}, f32[36,18,144]{2,1,0:T(8,128)S(1)}, u32[]{:S(2)}) copy-start(f32[36,18,144]{2,1,0:T(8,128)S(1)} %copy.30) | copy-start | bytes 1119748
  17.5 11.9 %copy-start.7 = (f32[2,8]{1,0:T(2,128)S(1)}, f32[2,8]{1,0:T(2,128)}, u32[]{:S(2)}) copy-start(f32[2,8]{1,0:T(2,128)} %param.24) | copy-start | bytes 196
  18.2 10.8 %collective-permute-start.6 = (s32[34,1,128]{2,1,0:T(1,128)S(1)}, s32[34,1,128]{2,1,0:T(1,128)S(1)}, u32[]{:S(2)}, u32[]{:S(2)}) collective-permute-start(s32[34,1,128]{2,1,0:T(1,128)S(1)} %get-tuple-element.138), channel_id=1, source_target_pairs={{0,1},{1,2},{2,3},{3,4},{4,5},{5,6},{6,7},{8,9},{9,10},{10,11},{11... | collective-permute-start | bytes 52232 | tf_op jit(solution)/shard_map/ppermute | solution.py:18
  21.6 7.4 %collective-permute-start.7 = (s32[34,1,128]{2,1,0:T(1,128)S(1)}, s32[34,1,128]{2,1,0:T(1,128)S(1)}, u32[]{:S(2)}, u32[]{:S(2)}) collective-permute-start(s32[34,1,128]{2,1,0:T(1,128)S(1)} %get-tuple-element.139), channel_id=1, source_target_pairs={{1,0},{2,1},{3,2},{4,3},{5,4},{6,5},{7,6},{9,8},{10,9},{11,10},{12... | collective-permute-start | bytes 52232 | tf_op jit(solution)/shard_map/ppermute | solution.py:21
  23.0 13.3 %collective-permute-start.2 = (f32[2,34,1,128]{3,1,2,0:T(8,128)S(1)}, f32[2,34,1,128]{3,1,2,0:T(8,128)S(1)}, u32[]{:S(2)}, u32[]{:S(2)}) collective-permute-start(f32[2,34,1,128]{3,1,2,0:T(8,128)S(1)} %get-tuple-element.128), channel_id=1, source_target_pairs={{0,1},{1,2},{2,3},{3,4},{4,5},{5,6},{6,7},{8,9},{9,10},{10,11},{11... | collective-permute-start | bytes 104456 | tf_op jit(solution)/shard_map/ppermute | solution.py:18
  27.6 8.8 %collective-permute-start.3 = (f32[2,34,1,128]{3,1,2,0:T(8,128)S(1)}, f32[2,34,1,128]{3,1,2,0:T(8,128)S(1)}, u32[]{:S(2)}, u32[]{:S(2)}) collective-permute-start(f32[2,34,1,128]{3,1,2,0:T(8,128)S(1)} %get-tuple-element.129), channel_id=1, source_target_pairs={{1,0},{2,1},{3,2},{4,3},{5,4},{6,5},{7,6},{9,8},{10,9},{11,10},{12... | collective-permute-start | bytes 104456 | tf_op jit(solution)/shard_map/ppermute | solution.py:21
  45.0 45.6 %slice-start = ((s8[5013504]{0:T(1024)(128)(4,1)}), s8[4194304]{0:T(1024)(128)(4,1)S(1)}, s32[]{:S(2)}) async-start(s8[5013504]{0:T(1024)(128)(4,1)} %bitcast.91), calls=%async_computation | async-start | bytes 8388608
  48.6 42.1 %slice-start.1 = ((s8[5013504]{0:T(1024)(128)(4,1)}), s8[819200]{0:T(1024)(128)(4,1)S(1)}, s32[]{:S(2)}) async-start(s8[5013504]{0:T(1024)(128)(4,1)} %bitcast.91), calls=%async_computation.1 | async-start | bytes 1638400
  49.6 4.2 %collective-permute-start.8 = (f32[2,1,18,128]{3,0,2,1:T(2,128)S(1)}, f32[2,1,18,128]{3,0,2,1:T(2,128)S(1)}, u32[]{:S(2)}, u32[]{:S(2)}) collective-permute-start(f32[2,1,18,128]{3,0,2,1:T(2,128)S(1)} %get-tuple-element.117), channel_id=1, source_target_pairs={{0,8},{8,16},{16,24},{1,9},{9,17},{17,25},{2,10},{10,18},{18,26},{... | collective-permute-start | bytes 55304 | tf_op jit(solution)/shard_map/ppermute | solution.py:18
  52.5 5.2 %collective-permute-start.9 = (f32[2,1,18,128]{3,0,2,1:T(2,128)S(1)}, f32[2,1,18,128]{3,0,2,1:T(2,128)S(1)}, u32[]{:S(2)}, u32[]{:S(2)}) collective-permute-start(f32[2,1,18,128]{3,0,2,1:T(2,128)S(1)} %get-tuple-element.116), channel_id=1, source_target_pairs={{8,0},{16,8},{24,16},{9,1},{17,9},{25,17},{10,2},{18,10},{26,18},{... | collective-permute-start | bytes 55304 | tf_op jit(solution)/shard_map/ppermute | solution.py:21
  57.7 6.6 %collective-permute-start.10 = (f32[2,32,1,128]{3,0,2,1:T(2,128)S(1)}, f32[2,32,1,128]{3,0,2,1:T(2,128)S(1)}, u32[]{:S(2)}, u32[]{:S(2)}) collective-permute-start(f32[2,32,1,128]{3,0,2,1:T(2,128)S(1)} %get-tuple-element.121), channel_id=1, source_target_pairs={{0,1},{1,2},{2,3},{3,4},{4,5},{5,6},{6,7},{8,9},{9,10},{10,11},{11... | collective-permute-start | bytes 98312 | tf_op jit(solution)/shard_map/ppermute | solution.py:18
  62.8 6.7 %collective-permute-start.11 = (f32[2,32,1,128]{3,0,2,1:T(2,128)S(1)}, f32[2,32,1,128]{3,0,2,1:T(2,128)S(1)}, u32[]{:S(2)}, u32[]{:S(2)}) collective-permute-start(f32[2,32,1,128]{3,0,2,1:T(2,128)S(1)} %get-tuple-element.120), channel_id=1, source_target_pairs={{1,0},{2,1},{3,2},{4,3},{5,4},{6,5},{7,6},{9,8},{10,9},{11,10},{12... | collective-permute-start | bytes 98312 | tf_op jit(solution)/shard_map/ppermute | solution.py:21
  69.5 4.9 %collective-permute-start.13 = (f32[2,1,16,128]{3,0,2,1:T(2,128)S(1)}, f32[2,1,16,128]{3,0,2,1:T(2,128)S(1)}, u32[]{:S(2)}, u32[]{:S(2)}) collective-permute-start(f32[2,1,16,128]{3,0,2,1:T(2,128)S(1)} %get-tuple-element.134), channel_id=1, source_target_pairs={{0,8},{8,16},{16,24},{1,9},{9,17},{17,25},{2,10},{10,18},{18,26},{... | collective-permute-start | bytes 49160 | tf_op jit(solution)/shard_map/ppermute | solution.py:18
  72.8 3.8 %collective-permute-start.12 = (f32[2,1,16,128]{3,0,2,1:T(2,128)S(1)}, f32[2,1,16,128]{3,0,2,1:T(2,128)S(1)}, u32[]{:S(2)}, u32[]{:S(2)}) collective-permute-start(f32[2,1,16,128]{3,0,2,1:T(2,128)S(1)} %get-tuple-element.135), channel_id=1, source_target_pairs={{8,0},{16,8},{24,16},{9,1},{17,9},{25,17},{10,2},{18,10},{26,18},{... | collective-permute-start | bytes 49160 | tf_op jit(solution)/shard_map/ppermute | solution.py:21
  76.6 7.0 %collective-permute-start.15 = (f32[2,34,1,128]{3,0,2,1:T(2,128)S(1)}, f32[2,34,1,128]{3,0,2,1:T(2,128)S(1)}, u32[]{:S(2)}, u32[]{:S(2)}) collective-permute-start(f32[2,34,1,128]{3,0,2,1:T(2,128)S(1)} %get-tuple-element.126), channel_id=1, source_target_pairs={{0,1},{1,2},{2,3},{3,4},{4,5},{5,6},{6,7},{8,9},{9,10},{10,11},{11... | collective-permute-start | bytes 104456 | tf_op jit(solution)/shard_map/ppermute | solution.py:18
  81.4 5.8 %collective-permute-start.14 = (f32[2,34,1,128]{3,0,2,1:T(2,128)S(1)}, f32[2,34,1,128]{3,0,2,1:T(2,128)S(1)}, u32[]{:S(2)}, u32[]{:S(2)}) collective-permute-start(f32[2,34,1,128]{3,0,2,1:T(2,128)S(1)} %get-tuple-element.127), channel_id=1, source_target_pairs={{1,0},{2,1},{3,2},{4,3},{5,4},{6,5},{7,6},{9,8},{10,9},{11,10},{12... | collective-permute-start | bytes 104456 | tf_op jit(solution)/shard_map/ppermute | solution.py:21
  144.6 2.6 collective-permute-start.16
  145.9 5.8 %collective-permute-start.17 = (f32[2,1,16,128]{3,0,2,1:T(2,128)S(1)}, f32[2,1,16,128]{3,0,2,1:T(2,128)S(1)}, u32[]{:S(2)}, u32[]{:S(2)}) collective-permute-start(f32[2,1,16,128]{3,0,2,1:T(2,128)S(1)} %get-tuple-element.133), channel_id=1, source_target_pairs={{8,0},{16,8},{24,16},{9,1},{17,9},{25,17},{10,2},{18,10},{26,18},{... | collective-permute-start | bytes 49160 | tf_op jit(solution)/shard_map/ppermute | solution.py:21
  151.7 4.6 %collective-permute-start.18 = (f32[2,34,1,128]{3,0,2,1:T(2,128)S(1)}, f32[2,34,1,128]{3,0,2,1:T(2,128)S(1)}, u32[]{:S(2)}, u32[]{:S(2)}) collective-permute-start(f32[2,34,1,128]{3,0,2,1:T(2,128)S(1)} %get-tuple-element.124), channel_id=1, source_target_pairs={{0,1},{1,2},{2,3},{3,4},{4,5},{5,6},{6,7},{8,9},{9,10},{10,11},{11... | collective-permute-start | bytes 104456 | tf_op jit(solution)/shard_map/ppermute | solution.py:18
  154.7 5.8 %collective-permute-start.19 = (f32[2,34,1,128]{3,0,2,1:T(2,128)S(1)}, f32[2,34,1,128]{3,0,2,1:T(2,128)S(1)}, u32[]{:S(2)}, u32[]{:S(2)}) collective-permute-start(f32[2,34,1,128]{3,0,2,1:T(2,128)S(1)} %get-tuple-element.125), channel_id=1, source_target_pairs={{1,0},{2,1},{3,2},{4,3},{5,4},{6,5},{7,6},{9,8},{10,9},{11,10},{12... | collective-permute-start | bytes 104456 | tf_op jit(solution)/shard_map/ppermute | solution.py:21
  173.7 4.9 %collective-permute-start.20 = (f32[2,1,18,128]{3,0,2,1:T(2,128)S(1)}, f32[2,1,18,128]{3,0,2,1:T(2,128)S(1)}, u32[]{:S(2)}, u32[]{:S(2)}) collective-permute-start(f32[2,1,18,128]{3,0,2,1:T(2,128)S(1)} %get-tuple-element.115), channel_id=1, source_target_pairs={{0,8},{8,16},{16,24},{1,9},{9,17},{17,25},{2,10},{10,18},{18,26},{... | collective-permute-start | bytes 55304 | tf_op jit(solution)/shard_map/ppermute | solution.py:18
  177.3 4.0 %collective-permute-start.21 = (f32[2,1,18,128]{3,0,2,1:T(2,128)S(1)}, f32[2,1,18,128]{3,0,2,1:T(2,128)S(1)}, u32[]{:S(2)}, u32[]{:S(2)}) collective-permute-start(f32[2,1,18,128]{3,0,2,1:T(2,128)S(1)} %get-tuple-element.114), channel_id=1, source_target_pairs={{8,0},{16,8},{24,16},{9,1},{17,9},{25,17},{10,2},{18,10},{26,18},{... | collective-permute-start | bytes 55304 | tf_op jit(solution)/shard_map/ppermute | solution.py:21
  181.4 5.1 %collective-permute-start.22 = (f32[2,32,1,128]{3,0,2,1:T(2,128)S(1)}, f32[2,32,1,128]{3,0,2,1:T(2,128)S(1)}, u32[]{:S(2)}, u32[]{:S(2)}) collective-permute-start(f32[2,32,1,128]{3,0,2,1:T(2,128)S(1)} %get-tuple-element.119), channel_id=1, source_target_pairs={{0,1},{1,2},{2,3},{3,4},{4,5},{5,6},{6,7},{8,9},{9,10},{10,11},{11... | collective-permute-start | bytes 98312 | tf_op jit(solution)/shard_map/ppermute | solution.py:18
  185.0 5.8 %collective-permute-start.23 = (f32[2,32,1,128]{3,0,2,1:T(2,128)S(1)}, f32[2,32,1,128]{3,0,2,1:T(2,128)S(1)}, u32[]{:S(2)}, u32[]{:S(2)}) collective-permute-start(f32[2,32,1,128]{3,0,2,1:T(2,128)S(1)} %get-tuple-element.118), channel_id=1, source_target_pairs={{1,0},{2,1},{3,2},{4,3},{5,4},{6,5},{7,6},{9,8},{10,9},{11,10},{12... | collective-permute-start | bytes 98312 | tf_op jit(solution)/shard_map/ppermute | solution.py:21
  234.8 2.6 collective-permute-start.25
  236.1 5.8 %collective-permute-start.24 = (f32[2,1,16,128]{3,0,2,1:T(2,128)S(1)}, f32[2,1,16,128]{3,0,2,1:T(2,128)S(1)}, u32[]{:S(2)}, u32[]{:S(2)}) collective-permute-start(f32[2,1,16,128]{3,0,2,1:T(2,128)S(1)} %get-tuple-element.131), channel_id=1, source_target_pairs={{8,0},{16,8},{24,16},{9,1},{17,9},{25,17},{10,2},{18,10},{26,18},{... | collective-permute-start | bytes 49160 | tf_op jit(solution)/shard_map/ppermute | solution.py:21
  241.9 4.4 %collective-permute-start.27 = (f32[2,34,1,128]{3,0,2,1:T(2,128)S(1)}, f32[2,34,1,128]{3,0,2,1:T(2,128)S(1)}, u32[]{:S(2)}, u32[]{:S(2)}) collective-permute-start(f32[2,34,1,128]{3,0,2,1:T(2,128)S(1)} %get-tuple-element.122), channel_id=1, source_target_pairs={{0,1},{1,2},{2,3},{3,4},{4,5},{5,6},{6,7},{8,9},{9,10},{10,11},{11... | collective-permute-start | bytes 104456 | tf_op jit(solution)/shard_map/ppermute | solution.py:18
  244.7 5.8 %collective-permute-start.26 = (f32[2,34,1,128]{3,0,2,1:T(2,128)S(1)}, f32[2,34,1,128]{3,0,2,1:T(2,128)S(1)}, u32[]{:S(2)}, u32[]{:S(2)}) collective-permute-start(f32[2,34,1,128]{3,0,2,1:T(2,128)S(1)} %get-tuple-element.123), channel_id=1, source_target_pairs={{1,0},{2,1},{3,2},{4,3},{5,4},{6,5},{7,6},{9,8},{10,9},{11,10},{12... | collective-permute-start | bytes 104456 | tf_op jit(solution)/shard_map/ppermute | solution.py:21
  (7 other events, 25.5 us)
where the time goes:
time: 324 us; the launch traced here: 321 us
  blocking collectives  124 us (38%)
  starting transfers between devices  64.4 us (20%)
  other arithmetic  46.1 us (14%)
  waiting for transfers between devices  40 us (12%)
  matrix products  25.9 us (8%)
  local copies, waits for them, and re-layouts  14.6 us (5%)
  between operations  5.83 us (2%)
    psum x2, blocking collectives, shards(): product = lax.psum(jnp.sum(residual * precond), ('gx', 'gy'))  82.1 us
    ppermute x14, starting transfers between devices, with_halo(): lax.ppermute(lax.slice_in_dim(block, block.shape[dim] - width, None, axis...  45.6 us
    psum x1, blocking collectives, shards(): curvature = lax.psum(jnp.sum(direction * image), ('gx', 'gy'))  41.8 us
    ppermute x14, waiting for transfers between devices, with_halo(): lax.ppermute(lax.slice_in_dim(block, 0, width, axis=dim), axis, backward)  39.1 us
    add x2, other arithmetic, apply_operator(): flux + face * (field - neighbour(padded, offset_x, offset_y, offset_z))  19.7 us
    ppermute x14, starting transfers between devices, with_halo(): lax.ppermute(lax.slice_in_dim(block, 0, width, axis=dim), axis, backward)  18.8 us
    add x2, other arithmetic, apply_operator(): first = mass[0] * field[0] + mass[2] * field[1] + flux[0]  8.66 us
    unnamed x26, local copies, waits for them, and re-layouts  7.33 us
  transfers between devices with their start and end apart: 28, of which 14 were waited for; matrix products, arithmetic and copies ran while one was open for 4% of the time, Pallas kernels for 0%

commit v1 on v0

v1 whole, which is shorter than its diff:
```python
import functools
import math

import jax
import jax.numpy as jnp
import ml_dtypes
import numpy as np
from jax import lax
from jax.experimental import pallas as pl
from jax.experimental.pallas import tpu as pltpu
from jax.sharding import PartitionSpec as P

BOX = 16
SPAN = BOX + 2
F32 = jnp.float32
BF16 = jnp.bfloat16
AXES = ("gx", "gy")
ROW0 = 4


def split(matrix):
    high = matrix.astype(ml_dtypes.bfloat16)
    low = (matrix - high.astype(np.float64)).astype(ml_dtypes.bfloat16)
    return high, low


def round_up(value, step):
    return (value + step - 1) // step * step


def sine_basis():
    index = np.arange(SPAN)
    angle = np.pi * np.outer(index + 1, index + 1) / (SPAN + 1)
    return np.sqrt(2.0 / (SPAN + 1)) * np.sin(angle)


def eigenvalues():
    return 4.0 * np.sin(np.pi * (np.arange(SPAN) + 1) / (2 * (SPAN + 1))) ** 2


def plane_layout():
    places = [(x, y + 1) for x in range(SPAN) for y in range(BOX)]
    for y in (0, SPAN - 1):
        for position in range(24):
            x = position - (ROW0 - 1)
            places.append((x, y) if 0 <= x < SPAN else None)
    return places


def constants(size_z):
    basis = sine_basis()
    places = plane_layout()
    rows = len(places)
    modes = SPAN * SPAN
    padded_modes = round_up(modes, 16)
    plane = np.zeros((padded_modes, rows))
    for column, place in enumerate(places):
        if place is not None:
            plane[:modes, column] = np.outer(basis[:, place[0]], basis[:, place[1]]).reshape(-1)
    high, low = split(plane)
    forward = np.concatenate([high, high, low], axis=1)
    high, low = split(plane.T)
    inverse = np.concatenate([high, high, low], axis=1)
    boxes = size_z // BOX
    line = np.zeros((size_z, boxes * SPAN))
    means = np.zeros((size_z, boxes * SPAN))
    for box in range(boxes):
        for mode in range(SPAN):
            for offset in range(SPAN):
                cell = box * BOX + offset - 1
                if 0 <= cell < size_z:
                    line[cell, box * SPAN + mode] = basis[mode, offset]
        means[box * BOX : (box + 1) * BOX, box * SPAN : (box + 1) * SPAN] = 1.0 / BOX**3
    high, low = split(line)
    line_forward = np.concatenate([high, high, low], axis=0)
    high, low = split(line.T)
    line_inverse = np.concatenate([high, low], axis=1)
    eigen = eigenvalues()
    pair = np.zeros(padded_modes)
    pair[:modes] = (eigen[:, None] + eigen[None, :]).reshape(-1)
    summed = (pair[:, None] + np.tile(eigen, boxes)[None, :]).astype(np.float32)
    return forward, inverse, line_forward, line_inverse, summed, means.astype(np.float32)


def swap_pairs(mesh, axis, odd):
    sizes = [mesh.shape[name] for name in AXES]
    along = AXES.index(axis)
    pairs = []
    for i in range(sizes[0]):
        for j in range(sizes[1]):
            here = [i, j]
            there = [i, j]
            place = here[along]
            target = place ^ 1 if not odd else (place + 1 if place % 2 else place - 1)
            if 0 <= target < sizes[along]:
                there[along] = target
            elif along == 0:
                there[0] = sizes[0] - 1 - place
            else:
                there[0] = i ^ 1
            pairs.append((here[0] * sizes[1] + here[1], there[0] * sizes[1] + there[1]))
    return pairs


def swap(mesh, axis, even_part, odd_part):
    first = lax.ppermute(even_part, AXES, swap_pairs(mesh, axis, False))
    second = lax.ppermute(odd_part, AXES, swap_pairs(mesh, axis, True))
    return first, second


EVEN_X, EVEN_Y, LOW_X, HIGH_X, LOW_Y, HIGH_Y = range(6)


def chosen(flags, which, yes, no):
    return jnp.where(flags[which] > 0, yes, no)


def keep(flags, which, value):
    return jnp.where(flags[which] > 0, value, jnp.zeros_like(value))


def halves(value):
    high = value.astype(BF16)
    low = (value - high.astype(F32)).astype(BF16)
    return high, low


def dot(left, right):
    return jnp.dot(left, right, preferred_element_type=F32)


def solve(field_ref, rows_ref, inverse_ref, consts, stack_ref, out_ref, out_rows_ref):
    forward_ref, back_ref, line_forward_ref, line_back_ref = consts
    boxes = (field_ref.shape[1] - 2) // BOX
    size_y, size_z = field_ref.shape[2:]
    inner = SPAN * size_y
    rows = inner + 48
    line_rows = line_forward_ref.shape[0] // 3
    for field in range(2):
        for box in range(boxes):
            start = box * BOX
            main = field_ref[field, start : start + SPAN].reshape(inner, size_z)
            lanes = slice(box * size_z, (box + 1) * size_z)
            parts = (
                (0, main),
                (inner, rows_ref[field, 0, start : start + 24]),
                (inner + 24, rows_ref[field, 1, start : start + 24]),
            )
            whole = jnp.concatenate([part for _, part in parts], axis=0)
            high, low = halves(whole)
            stack_ref[0:rows, lanes] = high
            stack_ref[rows : 2 * rows, lanes] = low
            stack_ref[2 * rows : 3 * rows, lanes] = high
        spectral = dot(forward_ref[...], stack_ref[...])
        for box in range(boxes):
            lanes = slice(box * size_z, (box + 1) * size_z)
            high, low = halves(spectral[:, lanes])
            both = jnp.concatenate([high, low], axis=1)
            modes = dot(both, line_forward_ref[0 : 2 * line_rows]) + dot(high, line_forward_ref[2 * line_rows :])
            modes = modes * inverse_ref[field * boxes + box]
            high, low = halves(modes)
            cells = dot(high, line_back_ref[...])
            cells = cells[:, :size_z] + (cells[:, size_z:] + dot(low, line_back_ref[:, :size_z]))
            high, low = halves(cells)
            stack_ref[0:rows, lanes] = high
            stack_ref[rows : 2 * rows, lanes] = low
            stack_ref[2 * rows : 3 * rows, lanes] = high
        result = dot(back_ref[...], stack_ref[...])
        for box in range(boxes):
            lanes = slice(box * size_z, (box + 1) * size_z)
            start = box * BOX
            main = result[:inner, lanes].reshape(SPAN, size_y, size_z)
            if box == 0:
                out_ref[field, 0:SPAN] = main
            else:
                out_ref[field, start : start + 2] = out_ref[field, start : start + 2] + main[0:2]
                out_ref[field, start + 2 : start + SPAN] = main[2:]
            for side in range(2):
                strip = result[inner + 24 * side : inner + 24 * side + 24, lanes]
                if box == 0:
                    out_rows_ref[field, side, 0:24] = strip
                else:
                    out_rows_ref[field, side, start : start + 8] = (
                        out_rows_ref[field, side, start : start + 8] + strip[0:8]
                    )
                    out_rows_ref[field, side, start + 8 : start + 24] = strip[8:]


def pack_x(flags, part_ref, part_rows_ref, even_ref, odd_ref):
    last = part_ref.shape[1] - 1
    size_y = part_ref.shape[2]
    for field in range(2):
        for layer in range(3):
            low, high = layer, last - 2 + layer
            for side, place in ((None, slice(0, size_y)), (0, slice(size_y, size_y + 1)), (1, slice(size_y + 1, size_y + 2))):
                if side is None:
                    to_low, to_high = part_ref[field, low], part_ref[field, high]
                else:
                    shift = ROW0 - 1
                    to_low = part_rows_ref[field, side, low + shift : low + shift + 1]
                    to_high = part_rows_ref[field, side, high + shift : high + shift + 1]
                even_ref[field, layer, place] = chosen(flags, EVEN_X, to_high, to_low)
                odd_ref[field, layer, place] = chosen(flags, EVEN_X, to_low, to_high)
            rest = even_ref.shape[2] - size_y - 2
            blank = jnp.zeros((rest, even_ref.shape[3]), F32)
            even_ref[field, layer, size_y + 2 :] = blank
            odd_ref[field, layer, size_y + 2 :] = blank


def divisor_kernel(table_ref, zones_ref, summed_ref, means_ref, inverse_ref):
    size_x, size_y, size_z = zones_ref.shape
    boxes = size_x // BOX
    lines = []
    for which in (2, 3, 0, 1):
        for box in range(boxes):
            total = jnp.zeros((size_y, size_z), F32)
            for x in range(box * BOX, (box + 1) * BOX):
                zone = zones_ref[x]
                value = jnp.full((size_y, size_z), table_ref[which, 0], F32)
                for label in range(1, table_ref.shape[1]):
                    value = jnp.where(zone == label, table_ref[which, label], value)
                total = total + value
            lines.append(jnp.sum(total, axis=0, keepdims=True))
    sums = jnp.concatenate(lines, axis=0)
    means = jnp.dot(sums, means_ref[...], preferred_element_type=F32, precision=lax.Precision.HIGHEST)
    half = 2 * boxes
    for combo in range(half):
        cbar = means[combo : combo + 1]
        kbar = 2.0 * means[half + combo : half + combo + 1]
        inverse_ref[combo] = 1.0 / (cbar + kbar * summed_ref[...])


def edge_rows_kernel(flags, load_ref, zones_ref, first_ref, second_ref, even_ref, odd_ref):
    size_x, size_y, size_z = zones_ref.shape
    from_low = chosen(flags, EVEN_X, second_ref[...], first_ref[...])
    from_high = chosen(flags, EVEN_X, first_ref[...], second_ref[...])
    blank = jnp.zeros((8, size_z), F32)
    for channel in range(4):
        for ref in (even_ref, odd_ref):
            ref[channel, 0:8] = blank
            ref[channel, size_x : size_x + 8] = blank

    def put(channel, position, count, to_low, to_high):
        place = slice(position, position + count)
        even_ref[channel, place] = chosen(flags, EVEN_Y, to_high, to_low)
        odd_ref[channel, place] = chosen(flags, EVEN_Y, to_low, to_high)

    end = ROW0 + size_x
    for field in range(2):
        put(field, ROW0, size_x, load_ref[field, :, 0], load_ref[field, :, size_y - 1])
        low = keep(flags, LOW_X, from_low[field])
        high = keep(flags, HIGH_X, from_high[field])
        put(field, ROW0 - 1, 1, low[0:1], low[size_y - 1 : size_y])
        put(field, end, 1, high[0:1], high[size_y - 1 : size_y])
    for layer in range(2):
        channel = 2 + layer
        near, far = layer, size_y - 2 + layer
        put(channel, ROW0, size_x, zones_ref[:, near].astype(F32), zones_ref[:, far].astype(F32))
        for depth in range(2):
            low, high = from_low[2 + depth], from_high[2 + depth]
            put(channel, ROW0 - 2 + depth, 1, low[near : near + 1], low[far : far + 1])
            put(channel, end + depth, 1, high[near : near + 1], high[far : far + 1])


def looked_up(table_ref, which, zone):
    value = jnp.full(zone.shape, table_ref[which, 0], F32)
    for label in range(1, table_ref.shape[1]):
        value = jnp.where(zone == float(label), table_ref[which, label], value)
    return value


def coefficient_kernel(
    flags, table_ref, zones_ref, first_x, second_x, first_y, second_y, half_ref, mass_ref, half_rows_ref, mass_rows_ref
):
    size_x, size_y, size_z = zones_ref.shape
    low_x = chosen(flags, EVEN_X, second_x[2:4], first_x[2:4])
    high_x = chosen(flags, EVEN_X, first_x[2:4], second_x[2:4])
    low_y = chosen(flags, EVEN_Y, second_y[2:4], first_y[2:4])
    high_y = chosen(flags, EVEN_Y, first_y[2:4], second_y[2:4])
    inside = slice(8, 8 + size_y)
    for x in range(-2, size_x + 2):
        if x < 0:
            zone = low_x[x + 2]
        elif x >= size_x:
            zone = high_x[x - size_x]
        else:
            zone = zones_ref[x].astype(F32)
        for field in range(2):
            half_ref[field, x + 2, inside] = looked_up(table_ref, field, zone)
        if -1 <= x <= size_x:
            for which in range(3):
                mass_ref[which, x + 1] = looked_up(table_ref, 2 + which, zone)
    for field in range(2):
        for outer in (0, 1):
            half_ref[field, outer, inside] = chosen(
                flags, LOW_X, half_ref[field, outer, inside], half_ref[field, 2, inside]
            )
            place = size_x + 2 + outer
            half_ref[field, place, inside] = chosen(
                flags, HIGH_X, half_ref[field, place, inside], half_ref[field, size_x + 1, inside]
            )
    count = half_rows_ref.shape[2]
    position = lax.broadcasted_iota(jnp.int32, (count, size_z), 0)
    for line, (zone, flag) in enumerate(
        ((low_y[0], LOW_Y), (low_y[1], LOW_Y), (high_y[0], HIGH_Y), (high_y[1], HIGH_Y))
    ):
        for field in range(2):
            value = looked_up(table_ref, field, zone)
            below = value[ROW0 : ROW0 + 1]
            above = value[ROW0 + size_x - 1 : ROW0 + size_x]
            value = jnp.where((position < ROW0) & (flags[LOW_X] == 0), below, value)
            value = jnp.where((position >= ROW0 + size_x) & (flags[HIGH_X] == 0), above, value)
            near = half_ref[field, :, 8 if flag == LOW_Y else 8 + size_y - 1]
            half_rows_ref[field, line] = value
            half_rows_ref[field, line, ROW0 - 2 : ROW0 + size_x + 2] = chosen(
                flags, flag, half_rows_ref[field, line, ROW0 - 2 : ROW0 + size_x + 2], near
            )
            if line in (1, 2):
                row = 7 if line == 1 else 8 + size_y
                half_ref[field, :, row] = half_rows_ref[field, line, ROW0 - 2 : ROW0 + size_x + 2]
        if line in (1, 2):
            for which in range(3):
                mass_rows_ref[which, line - 1] = looked_up(table_ref, 2 + which, zone)
    for field in range(2):
        for line, row in ((4, 8), (5, 8 + size_y - 1)):
            half_rows_ref[field, line] = jnp.zeros((count, size_z), F32)
            half_rows_ref[field, line, ROW0 - 2 : ROW0 + size_x + 2] = half_ref[field, :, row]


def first_solve_kernel(
    flags, load_ref, first_x, second_x, first_y, second_y, inverse_ref, c0, c1, c2, c3,
    part_ref, part_rows_ref, even_ref, odd_ref, field_ref, rows_ref, stack_ref,
):
    size_x = load_ref.shape[1]
    for field in range(2):
        field_ref[field, 1 : 1 + size_x] = load_ref[field]
        field_ref[field, 0] = keep(flags, LOW_X, chosen(flags, EVEN_X, second_x[field], first_x[field]))
        field_ref[field, 1 + size_x] = keep(flags, HIGH_X, chosen(flags, EVEN_X, first_x[field], second_x[field]))
        rows_ref[field, 0] = keep(flags, LOW_Y, chosen(flags, EVEN_Y, second_y[field], first_y[field]))
        rows_ref[field, 1] = keep(flags, HIGH_Y, chosen(flags, EVEN_Y, first_y[field], second_y[field]))
    solve(field_ref, rows_ref, inverse_ref, (c0, c1, c2, c3), stack_ref, part_ref, part_rows_ref)
    pack_x(flags, part_ref, part_rows_ref, even_ref, odd_ref)


def merge_x_kernel(flags, part_ref, part_rows_ref, first_ref, second_ref, whole_ref, whole_rows_ref, even_ref, odd_ref):
    size_x = part_ref.shape[1] - 2
    size_y, size_z = part_ref.shape[2:]
    end = ROW0 + size_x
    for field in range(2):
        low = keep(flags, LOW_X, chosen(flags, EVEN_X, second_ref[field], first_ref[field]))
        high = keep(flags, HIGH_X, chosen(flags, EVEN_X, first_ref[field], second_ref[field]))
        whole_ref[field, 0] = low[0, :size_y]
        whole_ref[field, 1] = keep(flags, LOW_X, part_ref[field, 0]) + low[1, :size_y]
        whole_ref[field, 2] = part_ref[field, 1] + low[2, :size_y]
        whole_ref[field, 3 : size_x + 1] = part_ref[field, 2:size_x]
        whole_ref[field, size_x + 1] = part_ref[field, size_x] + high[0, :size_y]
        whole_ref[field, size_x + 2] = keep(flags, HIGH_X, part_ref[field, size_x + 1]) + high[1, :size_y]
        whole_ref[field, size_x + 3] = high[2, :size_y]
        for side in range(2):
            row = slice(size_y + side, size_y + side + 1)
            whole_rows_ref[field, side] = part_rows_ref[field, side]
            edge = ROW0 - 1
            whole_rows_ref[field, side, edge - 1 : edge] = low[0, row]
            whole_rows_ref[field, side, edge : edge + 1] = (
                keep(flags, LOW_X, part_rows_ref[field, side, edge : edge + 1]) + low[1, row]
            )
            whole_rows_ref[field, side, edge + 1 : edge + 2] = part_rows_ref[field, side, edge + 1 : edge + 2] + low[2, row]
            whole_rows_ref[field, side, end - 1 : end] = part_rows_ref[field, side, end - 1 : end] + high[0, row]
            whole_rows_ref[field, side, end : end + 1] = (
                keep(flags, HIGH_X, part_rows_ref[field, side, end : end + 1]) + high[1, row]
            )
            whole_rows_ref[field, side, end + 1 : end + 2] = high[2, row]
        blank = jnp.zeros((8, size_z), F32)
        spread = slice(ROW0 - 2, end + 2)

        def put(layer, to_low, to_high, place):
            even_ref[field, layer, place] = chosen(flags, EVEN_Y, to_high, to_low)
            odd_ref[field, layer, place] = chosen(flags, EVEN_Y, to_low, to_high)

        for layer in range(3):
            for ref in (even_ref, odd_ref):
                ref[field, layer, 0:8] = blank
                ref[field, layer, size_x : size_x + 8] = blank
        low_rows = whole_rows_ref[field, 0, spread]
        high_rows = whole_rows_ref[field, 1, spread]
        put(0, low_rows, whole_ref[field, :, size_y - 2], spread)
        put(1, whole_ref[field, :, 0], whole_ref[field, :, size_y - 1], spread)
        put(2, whole_ref[field, :, 1], high_rows, spread)


def assemble(flags, whole_ref, whole_rows_ref, first_ref, second_ref, field_ref, lines):
    size_x = whole_ref.shape[1] - 4
    size_y = whole_ref.shape[2]
    spread = slice(ROW0 - 2, ROW0 + size_x + 2)
    for field in range(2):
        low = keep(flags, LOW_Y, chosen(flags, EVEN_Y, second_ref[field], first_ref[field]))
        high = keep(flags, HIGH_Y, chosen(flags, EVEN_Y, first_ref[field], second_ref[field]))
        below = keep(flags, LOW_Y, whole_rows_ref[field, 0]) + low[1]
        above = keep(flags, HIGH_Y, whole_rows_ref[field, 1]) + high[1]
        lines[field, 0] = low[0]
        lines[field, 1] = below
        lines[field, 2] = above
        lines[field, 3] = high[2]
        lines[field, 4] = low[2]
        lines[field, 5] = high[0]
        field_ref[field, :, 8 : 8 + size_y] = whole_ref[field]
        field_ref[field, :, 7] = lines[field, 1, spread]
        field_ref[field, :, 8 + size_y] = lines[field, 2, spread]
        field_ref[field, :, 8] = field_ref[field, :, 8] + lines[field, 4, spread]
        field_ref[field, :, 7 + size_y] = field_ref[field, :, 7 + size_y] + lines[field, 5, spread]


def along_z(value, half):
    size_z = value.shape[-1]
    lane = lax.broadcasted_iota(jnp.int32, value.shape, value.ndim - 1)
    axis = value.ndim - 1
    last = lane == size_z - 1
    beside = jnp.where(last, 0.0, pltpu.roll(value, size_z - 1, axis))
    half_beside = jnp.where(last, half, pltpu.roll(half, size_z - 1, axis))
    upper = (half + half_beside) * (value - beside)
    lower = jnp.where(lane == 0, -2.0 * half * value, pltpu.roll(upper, 1, axis))
    return upper - lower


def operate(field_ref, half_ref, mass_ref, x):
    size_y = mass_ref.shape[2]
    inside = slice(8, 8 + size_y)
    values, images = [], []
    for field in range(2):
        value = field_ref[field, x + 2, inside]
        half = half_ref[field, x + 2, inside]
        flux = along_z(value, half)
        for place in (x + 1, x + 3):
            flux = flux + (half + half_ref[field, place, inside]) * (value - field_ref[field, place, inside])
        for shift in (-1, 1):
            moved = slice(8 + shift, 8 + shift + size_y)
            flux = flux + (half + half_ref[field, x + 2, moved]) * (value - field_ref[field, x + 2, moved])
        values.append(value)
        images.append(flux)
    first = mass_ref[0, x + 1] * values[0] + mass_ref[2, x + 1] * values[1] + images[0]
    second = mass_ref[2, x + 1] * values[0] + mass_ref[1, x + 1] * values[1] + images[1]
    return values, (first, second)


def operate_line(lines, half_lines, mass_lines, side, near):
    outer, center, inner = (0, 1, 4) if side == 0 else (3, 2, 5)
    values, images = [], []
    for field in range(2):
        value = lines[field, center]
        half = half_lines[field, center]
        count = value.shape[0]
        flux = along_z(value, half)
        for turn in (1, count - 1):
            flux = flux + (half + pltpu.roll(half, turn, 0)) * (value - pltpu.roll(value, turn, 0))
        flux = flux + (half + half_lines[field, outer]) * (value - lines[field, outer])
        flux = flux + (half + half_lines[field, inner]) * (value - near[field, side])
        values.append(value)
        images.append(flux)
    first = mass_lines[0, side] * values[0] + mass_lines[2, side] * values[1] + images[0]
    second = mass_lines[2, side] * values[0] + mass_lines[1, side] * values[1] + images[1]
    return first, second


def second_solve_kernel(
    flags, whole_ref, whole_rows_ref, first_ref, second_ref, half_ref, mass_ref, half_lines, mass_lines, load_ref,
    inverse_ref, c0, c1, c2, c3,
    precond_ref, image_ref, sums_ref, part_ref, part_rows_ref, even_ref, odd_ref,
    value_ref, lines, near, field_ref, rows_ref, stack_ref,
):
    size_x, size_y, size_z = load_ref.shape[1:]
    assemble(flags, whole_ref, whole_rows_ref, first_ref, second_ref, value_ref, lines)
    zero = jnp.zeros((size_y, size_z), F32)
    total_a, total_b = zero, zero
    for x in range(-1, size_x + 1):
        values, images = operate(value_ref, half_ref, mass_ref, x)
        for field in range(2):
            image = images[field]
            if x == -1:
                image = keep(flags, LOW_X, image)
            elif x == size_x:
                image = keep(flags, HIGH_X, image)
            else:
                precond_ref[field, x] = values[field]
                image_ref[field, x] = image
                total_a = total_a + load_ref[field, x] * values[field]
                total_b = total_b + image * values[field]
            field_ref[field, x + 1] = image
    sums_ref[0:1] = jnp.sum(total_a, axis=0, keepdims=True)
    sums_ref[1:2] = jnp.sum(total_b, axis=0, keepdims=True)
    sums_ref[2:8] = jnp.zeros((6, size_z), F32)
    count = rows_ref.shape[2]
    position = lax.broadcasted_iota(jnp.int32, (count, size_z), 0)
    begin = jnp.where(flags[LOW_X] > 0, ROW0 - 1, ROW0)
    end = jnp.where(flags[HIGH_X] > 0, ROW0 + size_x + 1, ROW0 + size_x)
    valid = (position >= begin) & (position < end)
    for field in range(2):
        for side, row in ((0, 8), (1, 7 + size_y)):
            near[field, side] = jnp.zeros((count, size_z), F32)
            near[field, side, ROW0 - 2 : ROW0 + size_x + 2] = value_ref[field, :, row]
    for side, flag in ((0, LOW_Y), (1, HIGH_Y)):
        images = operate_line(lines, half_lines, mass_lines, side, near)
        for field in range(2):
            rows_ref[field, side] = keep(flags, flag, jnp.where(valid, images[field], 0.0))
    solve(field_ref, rows_ref, inverse_ref, (c0, c1, c2, c3), stack_ref, part_ref, part_rows_ref)
    pack_x(flags, part_ref, part_rows_ref, even_ref, odd_ref)


def second_image_kernel(
    flags, whole_ref, whole_rows_ref, first_ref, second_ref, half_ref, mass_ref, old_image_ref, old_sums_ref,
    precond_ref, image_ref, sums_ref, value_ref, lines,
):
    size_x, size_y, size_z = old_image_ref.shape[1:]
    assemble(flags, whole_ref, whole_rows_ref, first_ref, second_ref, value_ref, lines)
    zero = jnp.zeros((size_y, size_z), F32)
    total_c, total_d = zero, zero
    for x in range(size_x):
        values, images = operate(value_ref, half_ref, mass_ref, x)
        for field in range(2):
            precond_ref[field, x] = values[field]
            image_ref[field, x] = images[field]
            total_c = total_c + old_image_ref[field, x] * values[field]
            total_d = total_d + images[field] * values[field]
    totals = [
        jnp.sum(old_sums_ref[0:1], axis=1, keepdims=True),
        jnp.sum(old_sums_ref[1:2], axis=1, keepdims=True),
        jnp.sum(jnp.sum(total_c, axis=0, keepdims=True), axis=1, keepdims=True),
        jnp.sum(jnp.sum(total_d, axis=0, keepdims=True), axis=1, keepdims=True),
    ]
    lane = lax.broadcasted_iota(jnp.int32, sums_ref.shape, 1)
    spread = jnp.zeros(sums_ref.shape, F32)
    for place, total in enumerate(totals):
        spread = jnp.where(lane == place, total, spread)
    sums_ref[...] = spread


def finish_kernel(sums_ref, load_ref, z_ref, q_ref, w_ref, s_ref, solution_ref, residual_ref):
    line = jnp.sum(sums_ref[...], axis=0, keepdims=True)
    lane = lax.broadcasted_iota(jnp.int32, line.shape, 1)
    rz, zq, qw, ws = [jnp.sum(jnp.where(lane == place, line, 0.0), axis=1, keepdims=True) for place in range(4)]
    alpha = rz / zq
    rz_next = rz - alpha * (2.0 * zq) + alpha * alpha * qw
    grown = 1.0 + rz_next / rz
    curvature = grown * grown * zq - 2.0 * grown * alpha * qw + alpha * alpha * ws
    alpha_next = rz_next / curvature
    along = alpha + alpha_next * grown
    against = alpha_next * alpha
    for field in range(2):
        for x in range(load_ref.shape[1]):
            solution_ref[field, x] = along * z_ref[field, x] - against * w_ref[field, x]
            residual_ref[field, x] = load_ref[field, x] - along * q_ref[field, x] + against * s_ref[field, x]


SMEM = pl.BlockSpec(memory_space=pltpu.SMEM)
VMEM = pl.BlockSpec(memory_space=pltpu.VMEM)


def call(kernel, scalars, arrays, outs, scratch=(), flops=0, limit=24):
    moved = sum(math.prod(a.shape) * a.dtype.itemsize for a in list(arrays) + list(outs))
    return pl.pallas_call(
        kernel,
        out_shape=tuple(outs),
        in_specs=[SMEM] * len(scalars) + [VMEM] * len(arrays),
        out_specs=tuple([VMEM] * len(outs)),
        scratch_shapes=list(scratch),
        compiler_params=pltpu.CompilerParams(vmem_limit_bytes=limit * 1024 * 1024),
        cost_estimate=pl.CostEstimate(flops=flops, bytes_accessed=moved, transcendentals=0),
    )(*scalars, *arrays)


def shards(mesh, load, zones, conductance, capacity, coupling):
    size_x, size_y, size_z = zones.shape
    assert size_x % BOX == 0 and size_y == BOX and size_z % BOX == 0
    boxes = size_x // BOX
    count = size_x + 8
    sds = lambda *shape: jax.ShapeDtypeStruct(shape, F32)
    forward, back, line_forward, line_back, summed, means = [jnp.asarray(c) for c in constants(size_z)]
    consts = (forward, back, line_forward, line_back)
    modes, lanes = summed.shape
    cross = coupling * jnp.sqrt(capacity[0] * capacity[1])
    table = jnp.concatenate([0.5 * conductance, capacity, cross[None]], axis=0)
    here_x, here_y = lax.axis_index("gx"), lax.axis_index("gy")
    even_x, even_y = here_x % 2 == 0, here_y % 2 == 0
    flags = jnp.stack(
        [even_x, even_y, here_x > 0, here_x < mesh.shape["gx"] - 1, here_y > 0, here_y < mesh.shape["gy"] - 1]
    ).astype(jnp.int32)

    to_low = jnp.concatenate([load[:, 0], zones[:2].astype(F32)], axis=0)
    to_high = jnp.concatenate([load[:, -1], zones[-2:].astype(F32)], axis=0)
    x_halo = swap(mesh, "gx", jnp.where(even_x, to_high, to_low), jnp.where(even_x, to_low, to_high))

    (inverse,) = call(
        divisor_kernel, [table], [zones, summed, means], [sds(2 * boxes, modes, lanes)], flops=40_000_000
    )
    y_halo = swap(
        mesh, "gy", *call(edge_rows_kernel, [flags], [load, zones, *x_halo], [sds(4, count, size_z)] * 2)
    )
    half, mass, half_lines, mass_lines = call(
        coefficient_kernel,
        [flags, table],
        [zones, *x_halo, *y_halo],
        [
            sds(2, size_x + 4, size_y + 16, size_z),
            sds(3, size_x + 2, size_y, size_z),
            sds(2, 6, count, size_z),
            sds(3, 2, count, size_z),
        ],
        flops=20_000_000,
    )
    parts = [sds(2, size_x + 2, size_y, size_z), sds(2, 2, count, size_z)]
    packed_x = [sds(2, 3, size_y + 8, size_z)] * 2
    wholes = [sds(2, size_x + 4, size_y, size_z), sds(2, 2, count, size_z)]
    packed_y = [sds(2, 3, count, size_z)] * 2
    rows = SPAN * size_y + 48
    work = [
        pltpu.VMEM((2, size_x + 2, size_y, size_z), F32),
        pltpu.VMEM((2, 2, count, size_z), F32),
        pltpu.VMEM((3 * rows, boxes * size_z), BF16),
    ]
    padded = [
        pltpu.VMEM((2, size_x + 4, size_y + 16, size_z), F32),
        pltpu.VMEM((2, 6, count, size_z), F32),
    ]
    own = sds(2, size_x, size_y, size_z)

    part, part_rows, *packed = call(
        first_solve_kernel, [flags], [load, *x_halo, *y_halo, inverse, *consts], parts + packed_x, work, 3_000_000_000
    )
    received = swap(mesh, "gx", *packed)
    whole, whole_rows, *packed = call(merge_x_kernel, [flags], [part, part_rows, *received], wholes + packed_y)
    received = swap(mesh, "gy", *packed)
    precond, image, sums, part, part_rows, *packed = call(
        second_solve_kernel,
        [flags],
        [whole, whole_rows, *received, half, mass, half_lines, mass_lines, load, inverse, *consts],
        [own, own, sds(8, size_z)] + parts + packed_x,
        padded + [pltpu.VMEM((2, 2, count, size_z), F32)] + work,
        3_000_000_000,
    )
    received = swap(mesh, "gx", *packed)
    whole, whole_rows, *packed = call(merge_x_kernel, [flags], [part, part_rows, *received], wholes + packed_y)
    received = swap(mesh, "gy", *packed)
    devices = mesh.shape["gx"] * mesh.shape["gy"]
    last_precond, last_image, sums = call(
        second_image_kernel,
        [flags],
        [whole, whole_rows, *received, half, mass, image, sums],
        [own, own, sds(devices, size_z)],
        padded,
        10_000_000,
    )
    sums = lax.all_to_all(sums, AXES, 0, 0, tiled=True)
    return call(finish_kernel, [], [sums, load, precond, image, last_precond, last_image], [own, own])


def solution(mesh):
    in_specs = (P(None, "gx", "gy", None), P("gx", "gy", None), P(), P(), P())
    out_specs = (P(None, "gx", "gy", None), P(None, "gx", "gy", None))
    return jax.shard_map(
        functools.partial(shards, mesh), mesh=mesh, in_specs=in_specs, out_specs=out_specs, check_vma=False
    )
```

time: 324 us -> 68.5 us (0.21)
  blocking collectives: 124 us -> 12.8 us
  starting transfers between devices: 64.4 us -> 13.9 us
  other arithmetic: 46.1 us -> 2.93 us
  matrix products: 25.9 us -> 0 us
  waiting for transfers between devices: 40 us -> 15.3 us
  Pallas kernels: 0 us -> 17.7 us
  local copies, waits for them, and re-layouts: 14.6 us -> 4.73 us
  between operations: 5.83 us -> 0.79 us
    psum x3 -> x0, blocking collectives: 124 us -> none  [the longest x2 82.1 us: shards(): product = lax.psum(jnp.sum(residual * precond), ('gx', 'gy'))]
    ppermute x28 -> x12, starting transfers between devices: 64.4 us -> 13.9 us  [the longest x6 8.25 us: swap(): first = lax.ppermute(even_part, AXES, swap_pairs(mesh, axis, False))]
    add x9 -> x0, other arithmetic: 29.6 us -> none  [the longest x2 19.7 us: apply_operator(): flux + face * (field - neighbour(padded, offset_x, offset_y, offset_z))]
    dot_general x13 -> x0, matrix products: 25.9 us -> none  [the longest x2 4.65 us: solve_boxes(): jnp.einsum('co,fabc->fabo', matrix_z, spectral, precision=highest)]
    ppermute x28 -> x12, waiting for transfers between devices: 40 us -> 15.3 us  [the longest x6 9.9 us: swap(): first = lax.ppermute(even_part, AXES, swap_pairs(mesh, axis, False))]
    pallas_call x0 -> x9, Pallas kernels: none -> 17.7 us  [call(): pl.pallas_call(kernel, out_shape=tuple(outs), in_specs=[SMEM] * len(scala...]
    all_to_all x0 -> x1, blocking collectives: none -> 12.8 us  [shards(): sums = lax.all_to_all(sums, AXES, 0, 0, tiled=True)]
    concatenate x6 -> x1, other arithmetic: 7.12 us -> 0.69 us  [shards(): table = jnp.concatenate([0.5 * conductance, capacity, cross[None]], axis=0)]
  transfers between devices with their start and end apart: 28 -> 12, of which waited for: 14 -> 4; matrix products, arithmetic and copies ran while one was open for 4% -> 3% of each run, Pallas kernels for 0% -> 4%
where the time goes in v1:
time: 68.5 us; the launch traced here: 68.1 us
  Pallas kernels  17.7 us (26%)
  waiting for transfers between devices  15.3 us (22%)
  starting transfers between devices  13.9 us (20%)
  blocking collectives  12.8 us (19%)
  local copies, waits for them, and re-layouts  4.73 us (7%)
  other arithmetic  2.93 us (4%)
  between operations  0.79 us (1%)
    pallas_call x9, Pallas kernels, call(): pl.pallas_call(kernel, out_shape=tuple(outs), in_specs=[SMEM] * len(scala...  17.7 us
    all_to_all x1, blocking collectives, shards(): sums = lax.all_to_all(sums, AXES, 0, 0, tiled=True)  12.8 us
    ppermute x6, waiting for transfers between devices, swap(): first = lax.ppermute(even_part, AXES, swap_pairs(mesh, axis, False))  9.9 us
    ppermute x6, starting transfers between devices, swap(): first = lax.ppermute(even_part, AXES, swap_pairs(mesh, axis, False))  8.25 us
    ppermute x6, starting transfers between devices, swap(): second = lax.ppermute(odd_part, AXES, swap_pairs(mesh, axis, True))  5.6 us
    ppermute x6, waiting for transfers between devices, swap(): second = lax.ppermute(odd_part, AXES, swap_pairs(mesh, axis, True))  5.4 us
    unnamed x20, local copies, waits for them, and re-layouts  3.89 us
  transfers between devices with their start and end apart: 12, of which 4 were waited for; matrix products, arithmetic and copies ran while one was open for 3% of the time, Pallas kernels for 4%

profile of v1, /device:TPU:0, one launch (start us, length us, event | category | flops | bytes accessed | tf_op | source)
XLA Modules:
  0.0 68.1 jit_solution(8198692050070388819)
XLA Ops:
  0.7 0.8 %slice_convert_fusion.1 = (f32[2,16,128]{2,1,0:T(8,128)S(1)}, f32[2,16,128]{2,1,0:T(8,128)S(1)}) fusion(s32[32,16,128]{2,1,0:T(8,128)} %zones_ref.5), kind=kLoop, calls=%fused_computation.6 | loop fusion | flops 8192 | bytes 65536 | tf_op jit(solution)/shard_map/convert_element_type | solution.py:588
  1.4 0.7 %slice_bitcast_fusion.1 = (f32[2,16,128]{2,1,0:T(8,128)S(1)}, f32[2,16,128]{2,1,0:T(8,128)S(1)}) fusion(f32[2,32,16,128]{3,2,1,0:T(8,128)} %load_ref.7), kind=kLoop, calls=%fused_computation.7 | loop fusion | bytes 65536 | tf_op jit(solution)/shard_map/squeeze | solution.py:588
  2.2 2.5 %collective-permute-start.1 = (f32[4,16,128]{2,1,0:T(8,128)S(1)}, f32[4,16,128]{2,1,0:T(8,128)S(1)}, u32[]{:S(2)}, u32[]{:S(2)}) collective-permute-start(f32[4,16,128]{2,1,0:T(8,128)S(1)} %get-tuple-element.62), channel_id=1, source_target_pairs={{0,24},{1,25},{2,26},{3,27},{4,28},{5,29},{6,30},{7,31},{8,16},{9,... | collective-permute-start | bytes 98312 | tf_op jit(solution)/shard_map/ppermute | solution.py:107
  4.7 0.7 collective-permute-start
  5.3 0.7 broadcast_multiply_fusion
  6.0 0.8 %fusion.2 = f32[1,8]{1,0:T(1,128)S(1)} fusion(f32[8]{0:T(128)} %param.15, f32[2,8]{1,0:T(2,128)} %param.14), kind=kLoop, calls=%fused_computation.10 | loop fusion | flops 16 | bytes 128 | tf_op jit(solution)/shard_map/broadcast_in_dim | solution.py:580
  6.8 0.1 stack.27
  6.9 0.9 %copy-done = s32[32,16,128]{2,1,0:T(8,128)S(1)} copy-done((s32[32,16,128]{2,1,0:T(8,128)S(1)}, s32[32,16,128]{2,1,0:T(8,128)}, u32[]{:S(2)}) %copy-start) | copy-done | bytes 262168
  7.9 1.0 %copy-done.2 = f32[2,32,16,128]{3,2,1,0:T(8,128)S(1)} copy-done((f32[2,32,16,128]{3,2,1,0:T(8,128)S(1)}, f32[2,32,16,128]{3,2,1,0:T(8,128)}, u32[]{:S(2)}) %copy-start.2) | copy-done | bytes 524312
  8.9 0.7 %shard_map.122 = (f32[4,40,128]{2,1,0:T(8,128)S(1)}, f32[4,40,128]{2,1,0:T(8,128)S(1)}) custom-call(s32[6]{0:T(128)S(1)} %convert_element_type.9.flags, f32[2,32,16,128]{3,2,1,0:T(8,128)S(1)} %copy-done.2, s32[32,16,128]{2,1,0:T(8,128)S(1)} %copy-done, f32[4,16,128]{2,1,0:T(8,128)S(1)} %collective-permute-done.first_ref.first_x, ...), custom_call_target="tpu_custom_call" | custom-call | bytes 1015808 | tf_op jit(solution)/shard_map/pallas_call | solution.py:559
  9.6 2.0 %collective-permute-start.2 = (f32[4,40,128]{2,1,0:T(8,128)S(1)}, f32[4,40,128]{2,1,0:T(8,128)S(1)}, u32[]{:S(2)}, u32[]{:S(2)}) collective-permute-start(f32[4,40,128]{2,1,0:T(8,128)S(1)} %get-tuple-element.30), channel_id=1, source_target_pairs={{0,1},{1,0},{2,3},{3,2},{4,5},{5,4},{6,7},{7,6},{8,9},{9,8},{10,11... | collective-permute-start | bytes 245768 | tf_op jit(solution)/shard_map/ppermute | solution.py:106
  11.6 0.7 %pad_maximum_fusion.2.table_ref = f32[5,8]{1,0:T(8,128)S(1)} fusion(f32[1,8]{1,0:T(1,128)S(1)} %fusion.2, f32[2,8]{1,0:T(2,128)} %param.14, f32[2,8]{1,0:T(2,128)S(1)} %broadcast_multiply_fusion), kind=kLoop, calls=%fused_computation.8 | loop fusion | flops 80 | bytes 320 | tf_op jit(solution)/shard_map/concatenate | solution.py:580
  12.3 1.0 %copy-done.4 = f32[336,144]{1,0:T(8,128)S(1)} copy-done((f32[336,144]{1,0:T(8,128)S(1)}, f32[336,144]{1,0:T(8,128)}, u32[]{:S(2)}) %copy-start.4) | copy-done | bytes 193560
  13.3 0.9 %copy-done.5 = f32[128,144]{1,0:T(8,128)S(1)} copy-done((f32[128,144]{1,0:T(8,128)S(1)}, f32[128,144]{1,0:T(8,128)}, u32[]{:S(2)}) %copy-start.5) | copy-done | bytes 73752
  14.2 1.5 %shard_map.123.inverse_ref = f32[4,336,144]{2,1,0:T(8,128)S(1)} custom-call(f32[5,8]{1,0:T(8,128)S(1)} %pad_maximum_fusion.2.table_ref, s32[32,16,128]{2,1,0:T(8,128)S(1)} %copy-done.1, f32[336,144]{1,0:T(8,128)S(1)} %copy-done.4, f32[128,144]{1,0:T(8,128)S(1)} %copy-done.5), custom_call_target="tpu_custom_call" | custom-call | flops 40000000 | bytes 1303552 | tf_op jit(solution)/shard_map/pallas_call | solution.py:559
  15.7 3.4 %shard_map.124 = (f32[2,34,16,128]{3,2,1,0:T(8,128)S(1)}, f32[2,2,40,128]{3,2,1,0:T(8,128)S(1)}, f32[2,3,24,128]{3,2,1,0:T(8,128)S(1)}, f32[2,3,24,128]{3,2,1,0:T(8,128)S(1)}) custom-call(s32[6]{0:T(128)S(1)} %convert_element_type.9.flags, f32[2,32,16,128]{3,2,1,0:T(8,128)S(1)} %copy-done.3, f32[4,16,128]{2,1,0:T(8,128)S(1)} %collective-permute-done.first_ref.first_x, ...), custom_call_target="tpu_custom_call" | custom-call | flops 3000000000 | bytes 3853312 | tf_op jit(solution)/shard_map/pallas_call | solution.py:559
  19.1 0.6 collective-permute-start.4
  19.7 1.3 %collective-permute-start.5 = (f32[2,3,24,128]{3,2,1,0:T(8,128)S(1)}, f32[2,3,24,128]{3,2,1,0:T(8,128)S(1)}, u32[]{:S(2)}, u32[]{:S(2)}) collective-permute-start(f32[2,3,24,128]{3,2,1,0:T(8,128)S(1)} %get-tuple-element.35), channel_id=1, source_target_pairs={{0,24},{1,25},{2,26},{3,27},{4,28},{5,29},{6,30},{7,31},{8,16},{9,... | collective-permute-start | bytes 221192 | tf_op jit(solution)/shard_map/ppermute | solution.py:107
  20.9 3.0 %collective-permute-done.5.second_ref = f32[2,3,24,128]{3,2,1,0:T(8,128)S(1)} collective-permute-done((f32[2,3,24,128]{3,2,1,0:T(8,128)S(1)}, f32[2,3,24,128]{3,2,1,0:T(8,128)S(1)}, u32[]{:S(2)}, u32[]{:S(2)}) %collective-permute-start.5) | collective-permute-done | bytes 73760 | tf_op jit(solution)/shard_map/ppermute | solution.py:107
  24.0 0.7 %shard_map.125 = (f32[2,36,16,128]{3,2,1,0:T(8,128)S(1)}, f32[2,2,40,128]{3,2,1,0:T(8,128)S(1)}, f32[2,3,40,128]{3,2,1,0:T(8,128)S(1)}, f32[2,3,40,128]{3,2,1,0:T(8,128)S(1)}) custom-call(s32[6]{0:T(128)S(1)} %convert_element_type.9.flags, f32[2,34,16,128]{3,2,1,0:T(8,128)S(1)} %get-tuple-element.32.part_ref, ...), custom_call_target="tpu_custom_call" | custom-call | bytes 1703936 | tf_op jit(solution)/shard_map/pallas_call | solution.py:559
  24.7 2.4 %collective-permute-start.6 = (f32[2,3,40,128]{3,2,1,0:T(8,128)S(1)}, f32[2,3,40,128]{3,2,1,0:T(8,128)S(1)}, u32[]{:S(2)}, u32[]{:S(2)}) collective-permute-start(f32[2,3,40,128]{3,2,1,0:T(8,128)S(1)} %get-tuple-element.38), channel_id=1, source_target_pairs={{0,1},{1,0},{2,3},{3,2},{4,5},{5,4},{6,7},{7,6},{8,9},{9,8},{10,11... | collective-permute-start | bytes 368648 | tf_op jit(solution)/shard_map/ppermute | solution.py:106
  27.2 1.4 %shard_map.126 = (f32[2,36,32,128]{3,2,1,0:T(8,128)S(1)}, f32[3,34,16,128]{3,2,1,0:T(8,128)S(1)}, f32[2,6,40,128]{3,2,1,0:T(8,128)S(1)}, f32[3,2,40,128]{3,2,1,0:T(8,128)S(1)}) custom-call(s32[6]{0:T(128)S(1)} %convert_element_type.9.flags, f32[5,8]{1,0:T(8,128)S(1)} %pad_maximum_fusion.2.table_ref, s32[32,16,128]{2,1,0:T(8,128)S(1)} %copy-done.1, ...), custom_call_target="tpu_custom_call" | custom-call | flops 20000000 | bytes 2875392 | tf_op jit(solution)/shard_map/pallas_call | solution.py:559
  28.6 4.2 %collective-permute-done.6.first_ref = f32[2,3,40,128]{3,2,1,0:T(8,128)S(1)} collective-permute-done((f32[2,3,40,128]{3,2,1,0:T(8,128)S(1)}, f32[2,3,40,128]{3,2,1,0:T(8,128)S(1)}, u32[]{:S(2)}, u32[]{:S(2)}) %collective-permute-start.6) | collective-permute-done | bytes 122912 | tf_op jit(solution)/shard_map/ppermute | solution.py:106
  32.9 4.6 %shard_map.127 = (f32[2,32,16,128]{3,2,1,0:T(8,128)S(1)}, f32[2,32,16,128]{3,2,1,0:T(8,128)S(1)}, f32[8,128]{1,0:T(8,128)S(1)}, f32[2,34,16,128]{3,2,1,0:T(8,128...) custom-call(s32[6]{0:T(128)S(1)} %convert_element_type.9.flags, ...), custom_call_target="tpu_custom_call" | custom-call | flops 3000000000 | bytes 7977984 | tf_op jit(solution)/shard_map/pallas_call | solution.py:559
  37.5 1.7 %collective-permute-start.9 = (f32[2,3,24,128]{3,2,1,0:T(8,128)S(1)}, f32[2,3,24,128]{3,2,1,0:T(8,128)S(1)}, u32[]{:S(2)}, u32[]{:S(2)}) collective-permute-start(f32[2,3,24,128]{3,2,1,0:T(8,128)S(1)} %get-tuple-element.47), channel_id=1, source_target_pairs={{0,24},{1,25},{2,26},{3,27},{4,28},{5,29},{6,30},{7,31},{8,16},{9,... | collective-permute-start | bytes 221192 | tf_op jit(solution)/shard_map/ppermute | solution.py:107
  39.3 2.4 %collective-permute-done.9.second_ref = f32[2,3,24,128]{3,2,1,0:T(8,128)S(1)} collective-permute-done((f32[2,3,24,128]{3,2,1,0:T(8,128)S(1)}, f32[2,3,24,128]{3,2,1,0:T(8,128)S(1)}, u32[]{:S(2)}, u32[]{:S(2)}) %collective-permute-start.9) | collective-permute-done | bytes 73760 | tf_op jit(solution)/shard_map/ppermute | solution.py:107
  41.6 0.7 %shard_map.128 = (f32[2,36,16,128]{3,2,1,0:T(8,128)S(1)}, f32[2,2,40,128]{3,2,1,0:T(8,128)S(1)}, f32[2,3,40,128]{3,2,1,0:T(8,128)S(1)}, f32[2,3,40,128]{3,2,1,0:T(8,128)S(1)}) custom-call(s32[6]{0:T(128)S(1)} %convert_element_type.9.flags, f32[2,34,16,128]{3,2,1,0:T(8,128)S(1)} %get-tuple-element.44.part_ref, ...), custom_call_target="tpu_custom_call" | custom-call | bytes 1703936 | tf_op jit(solution)/shard_map/pallas_call | solution.py:559
  42.3 2.6 %collective-permute-start.10 = (f32[2,3,40,128]{3,2,1,0:T(8,128)S(1)}, f32[2,3,40,128]{3,2,1,0:T(8,128)S(1)}, u32[]{:S(2)}, u32[]{:S(2)}) collective-permute-start(f32[2,3,40,128]{3,2,1,0:T(8,128)S(1)} %get-tuple-element.50), channel_id=1, source_target_pairs={{0,1},{1,0},{2,3},{3,2},{4,5},{5,4},{6,7},{7,6},{8,9},{9,8},{10,11... | collective-permute-start | bytes 368648 | tf_op jit(solution)/shard_map/ppermute | solution.py:106
  45.0 5.7 %collective-permute-done.10.first_ref = f32[2,3,40,128]{3,2,1,0:T(8,128)S(1)} collective-permute-done((f32[2,3,40,128]{3,2,1,0:T(8,128)S(1)}, f32[2,3,40,128]{3,2,1,0:T(8,128)S(1)}, u32[]{:S(2)}, u32[]{:S(2)}) %collective-permute-start.10) | collective-permute-done | bytes 122912 | tf_op jit(solution)/shard_map/ppermute | solution.py:106
  50.7 3.4 %shard_map.129 = (f32[2,32,16,128]{3,2,1,0:T(8,128)S(1)}, f32[2,32,16,128]{3,2,1,0:T(8,128)S(1)}, f32[32,128]{1,0:T(8,128)S(1)}) custom-call(s32[6]{0:T(128)S(1)} %convert_element_type.9.flags, f32[2,36,16,128]{3,2,1,0:T(8,128)S(1)} %get-tuple-element.48.whole_ref, f32[2,2,40,128]{3,2,1,0:T(8,128)S(1)} %get-tuple-element.49.whole_rows_ref, ...), custom_call_target="tpu_custom_call" | custom-call | flops 10000000 | bytes 4526080 | tf_op jit(solution)/shard_map/pallas_call | solution.py:559
  54.0 12.8 %all_to_all.11 = f32[32,1,128]{2,1,0:T(1,128)S(1)} all-to-all(f32[32,1,128]{2,1,0:T(1,128)S(1)} %bitcast.25), channel_id=1, replica_groups=mesh['gx'=4,'gy'=8] {'gx','gy'}, dimensions={0} | all-to-all | bytes 32768 | tf_op jit(solution)/shard_map/all_to_all | solution.py:651
  66.8 1.3 %shard_map.130 = (f32[2,32,16,128]{3,2,1,0:T(8,128)}, f32[2,32,16,128]{3,2,1,0:T(8,128)}) custom-call(f32[32,128]{1,0:T(8,128)S(1)} %bitcast.24, f32[2,32,16,128]{3,2,1,0:T(8,128)S(1)} %copy-done.3, f32[2,32,16,128]{3,2,1,0:T(8,128)S(1)} %get-tuple-element.55.z_ref, f32[2,32,16,128]{3,2,1,0:T(8,128)S(1)} %get-tuple-element.52.old_image_ref.q_ref, ...), custom_call_target="tpu_custom_call" | custom-call | bytes 3686400 | tf_op jit(solution)/shard_map/pallas_call | solution.py:559
  (30 shorter events, 0.3 us)
Async XLA Ops:
  0.6 11.6 %copy-start.1 = (s32[32,16,128]{2,1,0:T(8,128)S(1)}, s32[32,16,128]{2,1,0:T(8,128)}, u32[]{:S(2)}) copy-start(s32[32,16,128]{2,1,0:T(8,128)} %zones_ref.5) | copy-start | bytes 786436
  2.2 4.7 %collective-permute-start.1 = (f32[4,16,128]{2,1,0:T(8,128)S(1)}, f32[4,16,128]{2,1,0:T(8,128)S(1)}, u32[]{:S(2)}, u32[]{:S(2)}) collective-permute-start(f32[4,16,128]{2,1,0:T(8,128)S(1)} %get-tuple-element.62), channel_id=1, source_target_pairs={{0,24},{1,25},{2,26},{3,27},{4,28},{5,29},{6,30},{7,31},{8,16},{9,... | collective-permute-start | bytes 98312 | tf_op jit(solution)/shard_map/ppermute | solution.py:107
  4.7 2.2 %collective-permute-start = (f32[4,16,128]{2,1,0:T(8,128)S(1)}, f32[4,16,128]{2,1,0:T(8,128)S(1)}, u32[]{:S(2)}, u32[]{:S(2)}) collective-permute-start(f32[4,16,128]{2,1,0:T(8,128)S(1)} %get-tuple-element.63), channel_id=1, source_target_pairs={{0,8},{1,9},{2,10},{3,11},{4,12},{5,13},{6,14},{7,15},{8,0},{9,1},... | collective-permute-start | bytes 98312 | tf_op jit(solution)/shard_map/ppermute | solution.py:106
  6.9 1.0 %copy-start = (s32[32,16,128]{2,1,0:T(8,128)S(1)}, s32[32,16,128]{2,1,0:T(8,128)}, u32[]{:S(2)}) copy-start(s32[32,16,128]{2,1,0:T(8,128)} %zones_ref.5) | copy-start | bytes 786436
  7.9 1.0 %copy-start.2 = (f32[2,32,16,128]{3,2,1,0:T(8,128)S(1)}, f32[2,32,16,128]{3,2,1,0:T(8,128)}, u32[]{:S(2)}) copy-start(f32[2,32,16,128]{3,2,1,0:T(8,128)} %load_ref.7) | copy-start | bytes 1572868
  8.9 6.8 %copy-start.3 = (f32[2,32,16,128]{3,2,1,0:T(8,128)S(1)}, f32[2,32,16,128]{3,2,1,0:T(8,128)}, u32[]{:S(2)}) copy-start(f32[2,32,16,128]{3,2,1,0:T(8,128)} %load_ref.7) | copy-start | bytes 1572868
  8.9 6.8 %copy-start.8 = (bf16[384,144]{1,0:T(8,128)(2,1)S(1)}, bf16[384,144]{1,0:T(8,128)(2,1)}, u32[]{:S(2)}) copy-start(bf16[384,144]{1,0:T(8,128)(2,1)} %constant.46.clone.c2) | copy-start | bytes 331780
  8.9 6.8 %copy-start.9 = (bf16[144,256]{1,0:T(8,128)(2,1)S(1)}, bf16[144,256]{1,0:T(8,128)(2,1)}, u32[]{:S(2)}) copy-start(bf16[144,256]{1,0:T(8,128)(2,1)} %constant.47.clone.c3) | copy-start | bytes 221188
  9.6 6.0 %collective-permute-start.2 = (f32[4,40,128]{2,1,0:T(8,128)S(1)}, f32[4,40,128]{2,1,0:T(8,128)S(1)}, u32[]{:S(2)}, u32[]{:S(2)}) collective-permute-start(f32[4,40,128]{2,1,0:T(8,128)S(1)} %get-tuple-element.30), channel_id=1, source_target_pairs={{0,1},{1,0},{2,3},{3,2},{4,5},{5,4},{6,7},{7,6},{8,9},{9,8},{10,11... | collective-permute-start | bytes 245768 | tf_op jit(solution)/shard_map/ppermute | solution.py:106
  11.6 4.1 %collective-permute-start.3 = (f32[4,40,128]{2,1,0:T(8,128)S(1)}, f32[4,40,128]{2,1,0:T(8,128)S(1)}, u32[]{:S(2)}, u32[]{:S(2)}) collective-permute-start(f32[4,40,128]{2,1,0:T(8,128)S(1)} %get-tuple-element.31), channel_id=1, source_target_pairs={{0,8},{1,2},{2,1},{3,4},{4,3},{5,6},{6,5},{7,15},{8,0},{9,10},{10,... | collective-permute-start | bytes 245768 | tf_op jit(solution)/shard_map/ppermute | solution.py:107
  12.3 1.0 %copy-start.4 = (f32[336,144]{1,0:T(8,128)S(1)}, f32[336,144]{1,0:T(8,128)}, u32[]{:S(2)}) copy-start(f32[336,144]{1,0:T(8,128)} %constant.48.clone.summed_ref) | copy-start | bytes 580612
  13.2 0.9 %copy-start.5 = (f32[128,144]{1,0:T(8,128)S(1)}, f32[128,144]{1,0:T(8,128)}, u32[]{:S(2)}) copy-start(f32[128,144]{1,0:T(8,128)} %constant.49.clone.means_ref) | copy-start | bytes 221188
  14.2 1.5 %copy-start.6 = (bf16[336,1008]{1,0:T(8,128)(2,1)S(1)}, bf16[336,1008]{1,0:T(8,128)(2,1)}, u32[]{:S(2)}) copy-start(bf16[336,1008]{1,0:T(8,128)(2,1)} %constant.45.clone.c1) | copy-start | bytes 2032132
  14.2 1.5 %copy-start.7 = (bf16[336,1008]{1,0:T(8,128)(2,1)S(1)}, bf16[336,1008]{1,0:T(8,128)(2,1)}, u32[]{:S(2)}) copy-start(bf16[336,1008]{1,0:T(8,128)(2,1)} %constant.44.clone.c0) | copy-start | bytes 2032132
  19.1 1.8 %collective-permute-start.4 = (f32[2,3,24,128]{3,2,1,0:T(8,128)S(1)}, f32[2,3,24,128]{3,2,1,0:T(8,128)S(1)}, u32[]{:S(2)}, u32[]{:S(2)}) collective-permute-start(f32[2,3,24,128]{3,2,1,0:T(8,128)S(1)} %get-tuple-element.34), channel_id=1, source_target_pairs={{0,8},{1,9},{2,10},{3,11},{4,12},{5,13},{6,14},{7,15},{8,0},{9,1},... | collective-permute-start | bytes 221192 | tf_op jit(solution)/shard_map/ppermute | solution.py:106
  19.7 4.3 %collective-permute-start.5 = (f32[2,3,24,128]{3,2,1,0:T(8,128)S(1)}, f32[2,3,24,128]{3,2,1,0:T(8,128)S(1)}, u32[]{:S(2)}, u32[]{:S(2)}) collective-permute-start(f32[2,3,24,128]{3,2,1,0:T(8,128)S(1)} %get-tuple-element.35), channel_id=1, source_target_pairs={{0,24},{1,25},{2,26},{3,27},{4,28},{5,29},{6,30},{7,31},{8,16},{9,... | collective-permute-start | bytes 221192 | tf_op jit(solution)/shard_map/ppermute | solution.py:107
  24.7 8.1 %collective-permute-start.6 = (f32[2,3,40,128]{3,2,1,0:T(8,128)S(1)}, f32[2,3,40,128]{3,2,1,0:T(8,128)S(1)}, u32[]{:S(2)}, u32[]{:S(2)}) collective-permute-start(f32[2,3,40,128]{3,2,1,0:T(8,128)S(1)} %get-tuple-element.38), channel_id=1, source_target_pairs={{0,1},{1,0},{2,3},{3,2},{4,5},{5,4},{6,7},{7,6},{8,9},{9,8},{10,11... | collective-permute-start | bytes 368648 | tf_op jit(solution)/shard_map/ppermute | solution.py:106
  27.1 5.7 %collective-permute-start.7 = (f32[2,3,40,128]{3,2,1,0:T(8,128)S(1)}, f32[2,3,40,128]{3,2,1,0:T(8,128)S(1)}, u32[]{:S(2)}, u32[]{:S(2)}) collective-permute-start(f32[2,3,40,128]{3,2,1,0:T(8,128)S(1)} %get-tuple-element.39), channel_id=1, source_target_pairs={{0,8},{1,2},{2,1},{3,4},{4,3},{5,6},{6,5},{7,15},{8,0},{9,10},{10,... | collective-permute-start | bytes 368648 | tf_op jit(solution)/shard_map/ppermute | solution.py:107
  37.5 1.8 %collective-permute-start.8 = (f32[2,3,24,128]{3,2,1,0:T(8,128)S(1)}, f32[2,3,24,128]{3,2,1,0:T(8,128)S(1)}, u32[]{:S(2)}, u32[]{:S(2)}) collective-permute-start(f32[2,3,24,128]{3,2,1,0:T(8,128)S(1)} %get-tuple-element.46), channel_id=1, source_target_pairs={{0,8},{1,9},{2,10},{3,11},{4,12},{5,13},{6,14},{7,15},{8,0},{9,1},... | collective-permute-start | bytes 221192 | tf_op jit(solution)/shard_map/ppermute | solution.py:106
  37.5 4.1 %collective-permute-start.9 = (f32[2,3,24,128]{3,2,1,0:T(8,128)S(1)}, f32[2,3,24,128]{3,2,1,0:T(8,128)S(1)}, u32[]{:S(2)}, u32[]{:S(2)}) collective-permute-start(f32[2,3,24,128]{3,2,1,0:T(8,128)S(1)} %get-tuple-element.47), channel_id=1, source_target_pairs={{0,24},{1,25},{2,26},{3,27},{4,28},{5,29},{6,30},{7,31},{8,16},{9,... | collective-permute-start | bytes 221192 | tf_op jit(solution)/shard_map/ppermute | solution.py:107
  42.3 8.3 %collective-permute-start.10 = (f32[2,3,40,128]{3,2,1,0:T(8,128)S(1)}, f32[2,3,40,128]{3,2,1,0:T(8,128)S(1)}, u32[]{:S(2)}, u32[]{:S(2)}) collective-permute-start(f32[2,3,40,128]{3,2,1,0:T(8,128)S(1)} %get-tuple-element.50), channel_id=1, source_target_pairs={{0,1},{1,0},{2,3},{3,2},{4,5},{5,4},{6,7},{7,6},{8,9},{9,8},{10,11... | collective-permute-start | bytes 368648 | tf_op jit(solution)/shard_map/ppermute | solution.py:106
  44.9 5.7 %collective-permute-start.11 = (f32[2,3,40,128]{3,2,1,0:T(8,128)S(1)}, f32[2,3,40,128]{3,2,1,0:T(8,128)S(1)}, u32[]{:S(2)}, u32[]{:S(2)}) collective-permute-start(f32[2,3,40,128]{3,2,1,0:T(8,128)S(1)} %get-tuple-element.51), channel_id=1, source_target_pairs={{0,8},{1,2},{2,1},{3,4},{4,3},{5,6},{6,5},{7,15},{8,0},{9,10},{10,... | collective-permute-start | bytes 368648 | tf_op jit(solution)/shard_map/ppermute | solution.py:107

commit v2 on v1

--- a/solution.py
+++ b/solution.py
@@ -16,6 +16,7 @@
 BF16 = jnp.bfloat16
 AXES = ("gx", "gy")
 ROW0 = 4
+CHUNK = 4
 
 
 def split(matrix):
@@ -103,8 +104,12 @@
 
 
 def swap(mesh, axis, even_part, odd_part):
-    first = lax.ppermute(even_part, AXES, swap_pairs(mesh, axis, False))
-    second = lax.ppermute(odd_part, AXES, swap_pairs(mesh, axis, True))
+    if axis == "gx":
+        first = lax.ppermute(even_part, AXES, swap_pairs(mesh, axis, False))
+        second = lax.ppermute(odd_part, AXES, swap_pairs(mesh, axis, True))
+    else:
+        second = lax.ppermute(odd_part, AXES, swap_pairs(mesh, axis, True))
+        first = lax.ppermute(even_part, AXES, swap_pairs(mesh, axis, False))
     return first, second
 
 
@@ -188,10 +193,11 @@
 
 def pack_x(flags, part_ref, part_rows_ref, even_ref, odd_ref):
     last = part_ref.shape[1] - 1
+    depth = even_ref.shape[1]
     size_y = part_ref.shape[2]
     for field in range(2):
-        for layer in range(3):
-            low, high = layer, last - 2 + layer
+        for layer in range(depth):
+            low, high = layer, last + 1 - depth + layer
             for side, place in ((None, slice(0, size_y)), (0, slice(size_y, size_y + 1)), (1, slice(size_y + 1, size_y + 2))):
                 if side is None:
                     to_low, to_high = part_ref[field, low], part_ref[field, high]
@@ -270,7 +276,8 @@
 
 
 def coefficient_kernel(
-    flags, table_ref, zones_ref, first_x, second_x, first_y, second_y, half_ref, mass_ref, half_rows_ref, mass_rows_ref
+    flags, table_ref, zones_ref, first_x, second_x, first_y, second_y,
+    half_ref, mass_ref, face_ref, half_rows_ref, mass_rows_ref, face_rows_ref,
 ):
     size_x, size_y, size_z = zones_ref.shape
     low_x = chosen(flags, EVEN_X, second_x[2:4], first_x[2:4])
@@ -322,6 +329,14 @@
             for which in range(3):
                 mass_rows_ref[which, line - 1] = looked_up(table_ref, 2 + which, zone)
     for field in range(2):
+        for x in range(0, size_x + 2, 2):
+            faces = faces_z(half_ref[field, x + 1 : x + 3, inside])
+            for way in range(2):
+                face_ref[field, way, x : x + 2] = faces[way]
+        for side in range(2):
+            faces = faces_z(half_rows_ref[field, side + 1])
+            for way in range(2):
+                face_rows_ref[field, way, side] = faces[way]
         for line, row in ((4, 8), (5, 8 + size_y - 1)):
             half_rows_ref[field, line] = jnp.zeros((count, size_z), F32)
             half_rows_ref[field, line, ROW0 - 2 : ROW0 + size_x + 2] = half_ref[field, :, row]
@@ -345,47 +360,58 @@
 def merge_x_kernel(flags, part_ref, part_rows_ref, first_ref, second_ref, whole_ref, whole_rows_ref, even_ref, odd_ref):
     size_x = part_ref.shape[1] - 2
     size_y, size_z = part_ref.shape[2:]
+    depth = first_ref.shape[1]
+    count = part_rows_ref.shape[2]
     end = ROW0 + size_x
     for field in range(2):
         low = keep(flags, LOW_X, chosen(flags, EVEN_X, second_ref[field], first_ref[field]))
         high = keep(flags, HIGH_X, chosen(flags, EVEN_X, first_ref[field], second_ref[field]))
-        whole_ref[field, 0] = low[0, :size_y]
-        whole_ref[field, 1] = keep(flags, LOW_X, part_ref[field, 0]) + low[1, :size_y]
-        whole_ref[field, 2] = part_ref[field, 1] + low[2, :size_y]
+        whole_ref[field, 1] = keep(flags, LOW_X, part_ref[field, 0]) + low[depth - 2, :size_y]
+        whole_ref[field, 2] = part_ref[field, 1] + low[depth - 1, :size_y]
         whole_ref[field, 3 : size_x + 1] = part_ref[field, 2:size_x]
         whole_ref[field, size_x + 1] = part_ref[field, size_x] + high[0, :size_y]
         whole_ref[field, size_x + 2] = keep(flags, HIGH_X, part_ref[field, size_x + 1]) + high[1, :size_y]
-        whole_ref[field, size_x + 3] = high[2, :size_y]
+        if depth == 3:
+            whole_ref[field, 0] = low[0, :size_y]
+            whole_ref[field, size_x + 3] = high[2, :size_y]
         for side in range(2):
             row = slice(size_y + side, size_y + side + 1)
+            edge = ROW0 - 1
             whole_rows_ref[field, side] = part_rows_ref[field, side]
-            edge = ROW0 - 1
-            whole_rows_ref[field, side, edge - 1 : edge] = low[0, row]
             whole_rows_ref[field, side, edge : edge + 1] = (
-                keep(flags, LOW_X, part_rows_ref[field, side, edge : edge + 1]) + low[1, row]
+                keep(flags, LOW_X, part_rows_ref[field, side, edge : edge + 1]) + low[depth - 2, row]
             )
-            whole_rows_ref[field, side, edge + 1 : edge + 2] = part_rows_ref[field, side, edge + 1 : edge + 2] + low[2, row]
+            whole_rows_ref[field, side, edge + 1 : edge + 2] = (
+                part_rows_ref[field, side, edge + 1 : edge + 2] + low[depth - 1, row]
+            )
             whole_rows_ref[field, side, end - 1 : end] = part_rows_ref[field, side, end - 1 : end] + high[0, row]
             whole_rows_ref[field, side, end : end + 1] = (
                 keep(flags, HIGH_X, part_rows_ref[field, side, end : end + 1]) + high[1, row]
             )
-            whole_rows_ref[field, side, end + 1 : end + 2] = high[2, row]
-        blank = jnp.zeros((8, size_z), F32)
-        spread = slice(ROW0 - 2, end + 2)
-
-        def put(layer, to_low, to_high, place):
-            even_ref[field, layer, place] = chosen(flags, EVEN_Y, to_high, to_low)
-            odd_ref[field, layer, place] = chosen(flags, EVEN_Y, to_low, to_high)
-
-        for layer in range(3):
-            for ref in (even_ref, odd_ref):
-                ref[field, layer, 0:8] = blank
-                ref[field, layer, size_x : size_x + 8] = blank
-        low_rows = whole_rows_ref[field, 0, spread]
-        high_rows = whole_rows_ref[field, 1, spread]
-        put(0, low_rows, whole_ref[field, :, size_y - 2], spread)
-        put(1, whole_ref[field, :, 0], whole_ref[field, :, size_y - 1], spread)
-        put(2, whole_ref[field, :, 1], high_rows, spread)
+            if depth == 3:
+                whole_rows_ref[field, side, edge - 1 : edge] = low[0, row]
+                whole_rows_ref[field, side, end + 1 : end + 2] = high[2, row]
+
+        def put(at, to_low, to_high):
+            even_ref[(field, *at)] = chosen(flags, EVEN_Y, to_high, to_low)
+            odd_ref[(field, *at)] = chosen(flags, EVEN_Y, to_low, to_high)
+
+        if depth == 3:
+            blank = jnp.zeros((8, size_z), F32)
+            for layer in range(3):
+                for ref in (even_ref, odd_ref):
+                    ref[field, layer, 0:8] = blank
+                    ref[field, layer, count - 8 : count] = blank
+            rows = slice(ROW0 - 2, end + 2)
+            low_rows = whole_rows_ref[field, 0, rows]
+            high_rows = whole_rows_ref[field, 1, rows]
+            put((0, rows), low_rows, whole_ref[field, :, size_y - 2])
+            put((1, rows), whole_ref[field, :, 0], whole_ref[field, :, size_y - 1])
+            put((2, rows), whole_ref[field, :, 1], high_rows)
+        else:
+            own = slice(2, size_x + 2)
+            put((slice(0, size_x),), whole_ref[field, own, 0], whole_ref[field, own, size_y - 1])
+            put((slice(size_x, None),), whole_rows_ref[field, 0], whole_rows_ref[field, 1])
 
 
 def assemble(flags, whole_ref, whole_rows_ref, first_ref, second_ref, field_ref, lines):
@@ -410,46 +436,53 @@
         field_ref[field, :, 7 + size_y] = field_ref[field, :, 7 + size_y] + lines[field, 5, spread]
 
 
-def along_z(value, half):
-    size_z = value.shape[-1]
-    lane = lax.broadcasted_iota(jnp.int32, value.shape, value.ndim - 1)
-    axis = value.ndim - 1
-    last = lane == size_z - 1
-    beside = jnp.where(last, 0.0, pltpu.roll(value, size_z - 1, axis))
-    half_beside = jnp.where(last, half, pltpu.roll(half, size_z - 1, axis))
-    upper = (half + half_beside) * (value - beside)
-    lower = jnp.where(lane == 0, -2.0 * half * value, pltpu.roll(upper, 1, axis))
-    return upper - lower
-
-
-def operate(field_ref, half_ref, mass_ref, x):
+def faces_z(half):
+    size_z, axis = half.shape[-1], half.ndim - 1
+    lane = lax.broadcasted_iota(jnp.int32, half.shape, axis)
+    upper = half + jnp.where(lane == size_z - 1, half, pltpu.roll(half, size_z - 1, axis))
+    lower = half + jnp.where(lane == 0, half, pltpu.roll(half, 1, axis))
+    return upper, lower
+
+
+def along_z(value, upper, lower):
+    size_z, axis = value.shape[-1], value.ndim - 1
+    lane = lax.broadcasted_iota(jnp.int32, value.shape, axis)
+    above = jnp.where(lane == size_z - 1, 0.0, pltpu.roll(value, size_z - 1, axis))
+    below = jnp.where(lane == 0, 0.0, pltpu.roll(value, 1, axis))
+    return upper * (value - above) + lower * (value - below)
+
+
+def operate(field_ref, half_ref, mass_ref, face_ref, x, count):
     size_y = mass_ref.shape[2]
     inside = slice(8, 8 + size_y)
+    masses = slice(x + 1, x + 1 + count)
+    here = slice(x + 2, x + 2 + count)
     values, images = [], []
     for field in range(2):
-        value = field_ref[field, x + 2, inside]
-        half = half_ref[field, x + 2, inside]
-        flux = along_z(value, half)
-        for place in (x + 1, x + 3):
+        value = field_ref[field, here, inside]
+        half = half_ref[field, here, inside]
+        flux = along_z(value, face_ref[field, 0, masses], face_ref[field, 1, masses])
+        for start in (x + 1, x + 3):
+            place = slice(start, start + count)
             flux = flux + (half + half_ref[field, place, inside]) * (value - field_ref[field, place, inside])
         for shift in (-1, 1):
             moved = slice(8 + shift, 8 + shift + size_y)
-            flux = flux + (half + half_ref[field, x + 2, moved]) * (value - field_ref[field, x + 2, moved])
+            flux = flux + (half + half_ref[field, here, moved]) * (value - field_ref[field, here, moved])
         values.append(value)
         images.append(flux)
-    first = mass_ref[0, x + 1] * values[0] + mass_ref[2, x + 1] * values[1] + images[0]
-    second = mass_ref[2, x + 1] * values[0] + mass_ref[1, x + 1] * values[1] + images[1]
+    first = mass_ref[0, masses] * values[0] + mass_ref[2, masses] * values[1] + images[0]
+    second = mass_ref[2, masses] * values[0] + mass_ref[1, masses] * values[1] + images[1]
     return values, (first, second)
 
 
-def operate_line(lines, half_lines, mass_lines, side, near):
+def operate_line(lines, half_lines, mass_lines, face_lines, side, near):
     outer, center, inner = (0, 1, 4) if side == 0 else (3, 2, 5)
     values, images = [], []
     for field in range(2):
         value = lines[field, center]
         half = half_lines[field, center]
         count = value.shape[0]
-        flux = along_z(value, half)
+        flux = along_z(value, face_lines[field, 0, side], face_lines[field, 1, side])
         for turn in (1, count - 1):
             flux = flux + (half + pltpu.roll(half, turn, 0)) * (value - pltpu.roll(value, turn, 0))
         flux = flux + (half + half_lines[field, outer]) * (value - lines[field, outer])
@@ -462,31 +495,29 @@
 
 
 def second_solve_kernel(
-    flags, whole_ref, whole_rows_ref, first_ref, second_ref, half_ref, mass_ref, half_lines, mass_lines, load_ref,
-    inverse_ref, c0, c1, c2, c3,
+    flags, whole_ref, whole_rows_ref, first_ref, second_ref,
+    half_ref, mass_ref, face_ref, half_lines, mass_lines, face_lines, load_ref, inverse_ref, c0, c1, c2, c3,
     precond_ref, image_ref, sums_ref, part_ref, part_rows_ref, even_ref, odd_ref,
     value_ref, lines, near, field_ref, rows_ref, stack_ref,
 ):
     size_x, size_y, size_z = load_ref.shape[1:]
     assemble(flags, whole_ref, whole_rows_ref, first_ref, second_ref, value_ref, lines)
-    zero = jnp.zeros((size_y, size_z), F32)
-    total_a, total_b = zero, zero
-    for x in range(-1, size_x + 1):
-        values, images = operate(value_ref, half_ref, mass_ref, x)
+    for x, flag in ((-1, LOW_X), (size_x, HIGH_X)):
+        _, images = operate(value_ref, half_ref, mass_ref, face_ref, x, 1)
         for field in range(2):
-            image = images[field]
-            if x == -1:
-                image = keep(flags, LOW_X, image)
-            elif x == size_x:
-                image = keep(flags, HIGH_X, image)
-            else:
-                precond_ref[field, x] = values[field]
-                image_ref[field, x] = image
-                total_a = total_a + load_ref[field, x] * values[field]
-                total_b = total_b + image * values[field]
-            field_ref[field, x + 1] = image
-    sums_ref[0:1] = jnp.sum(total_a, axis=0, keepdims=True)
-    sums_ref[1:2] = jnp.sum(total_b, axis=0, keepdims=True)
+            field_ref[field, x + 1 : x + 2] = keep(flags, flag, images[field])
+    total_a = total_b = jnp.zeros((CHUNK, size_y, size_z), F32)
+    for x in range(0, size_x, CHUNK):
+        chunk = slice(x, x + CHUNK)
+        values, images = operate(value_ref, half_ref, mass_ref, face_ref, x, CHUNK)
+        for field in range(2):
+            precond_ref[field, chunk] = values[field]
+            image_ref[field, chunk] = images[field]
+            field_ref[field, x + 1 : x + 1 + CHUNK] = images[field]
+            total_a = total_a + load_ref[field, chunk] * values[field]
+            total_b = total_b + images[field] * values[field]
+    sums_ref[0:1] = jnp.sum(jnp.sum(total_a, axis=0), axis=0, keepdims=True)
+    sums_ref[1:2] = jnp.sum(jnp.sum(total_b, axis=0), axis=0, keepdims=True)
     sums_ref[2:8] = jnp.zeros((6, size_z), F32)
     count = rows_ref.shape[2]
     position = lax.broadcasted_iota(jnp.int32, (count, size_z), 0)
@@ -498,7 +529,7 @@
             near[field, side] = jnp.zeros((count, size_z), F32)
             near[field, side, ROW0 - 2 : ROW0 + size_x + 2] = value_ref[field, :, row]
     for side, flag in ((0, LOW_Y), (1, HIGH_Y)):
-        images = operate_line(lines, half_lines, mass_lines, side, near)
+        images = operate_line(lines, half_lines, mass_lines, face_lines, side, near)
         for field in range(2):
             rows_ref[field, side] = keep(flags, flag, jnp.where(valid, images[field], 0.0))
     solve(field_ref, rows_ref, inverse_ref, (c0, c1, c2, c3), stack_ref, part_ref, part_rows_ref)
@@ -506,20 +537,30 @@
 
 
 def second_image_kernel(
-    flags, whole_ref, whole_rows_ref, first_ref, second_ref, half_ref, mass_ref, old_image_ref, old_sums_ref,
-    precond_ref, image_ref, sums_ref, value_ref, lines,
+    flags, whole_ref, whole_rows_ref, first_ref, second_ref, half_ref, mass_ref, face_ref, old_image_ref, old_sums_ref,
+    precond_ref, image_ref, sums_ref, value_ref,
 ):
     size_x, size_y, size_z = old_image_ref.shape[1:]
-    assemble(flags, whole_ref, whole_rows_ref, first_ref, second_ref, value_ref, lines)
-    zero = jnp.zeros((size_y, size_z), F32)
-    total_c, total_d = zero, zero
-    for x in range(size_x):
-        values, images = operate(value_ref, half_ref, mass_ref, x)
+    own, wide = slice(2, size_x + 2), slice(1, size_x + 3)
+    rows, margins = slice(ROW0, ROW0 + size_x), slice(size_x + ROW0 - 1, 2 * size_x + ROW0 + 1)
+    for field in range(2):
+        low = keep(flags, LOW_Y, chosen(flags, EVEN_Y, second_ref[field], first_ref[field]))
+        high = keep(flags, HIGH_Y, chosen(flags, EVEN_Y, first_ref[field], second_ref[field]))
+        value_ref[field, wide, 8 : 8 + size_y] = whole_ref[field, wide]
+        value_ref[field, own, 7] = keep(flags, LOW_Y, whole_rows_ref[field, 0, rows]) + low[:size_x]
+        value_ref[field, wide, 8] = whole_ref[field, wide, 0] + low[margins]
+        value_ref[field, wide, 7 + size_y] = whole_ref[field, wide, size_y - 1] + high[margins]
+        value_ref[field, own, 8 + size_y] = keep(flags, HIGH_Y, whole_rows_ref[field, 1, rows]) + high[:size_x]
+    total_c = total_d = jnp.zeros((CHUNK, size_y, size_z), F32)
+    for x in range(0, size_x, CHUNK):
+        chunk = slice(x, x + CHUNK)
+        values, images = operate(value_ref, half_ref, mass_ref, face_ref, x, CHUNK)
         for field in range(2):
-            precond_ref[field, x] = values[field]
-            image_ref[field, x] = images[field]
-            total_c = total_c + old_image_ref[field, x] * values[field]
+            precond_ref[field, chunk] = values[field]
+            image_ref[field, chunk] = images[field]
+            total_c = total_c + old_image_ref[field, chunk] * values[field]
             total_d = total_d + images[field] * values[field]
+    total_c, total_d = jnp.sum(total_c, axis=0), jnp.sum(total_d, axis=0)
     totals = [
         jnp.sum(old_sums_ref[0:1], axis=1, keepdims=True),
         jnp.sum(old_sums_ref[1:2], axis=1, keepdims=True),
@@ -594,22 +635,24 @@
     y_halo = swap(
         mesh, "gy", *call(edge_rows_kernel, [flags], [load, zones, *x_halo], [sds(4, count, size_z)] * 2)
     )
-    half, mass, half_lines, mass_lines = call(
+    half, mass, face, half_lines, mass_lines, face_lines = call(
         coefficient_kernel,
         [flags, table],
         [zones, *x_halo, *y_halo],
         [
             sds(2, size_x + 4, size_y + 16, size_z),
             sds(3, size_x + 2, size_y, size_z),
+            sds(2, 2, size_x + 2, size_y, size_z),
             sds(2, 6, count, size_z),
             sds(3, 2, count, size_z),
+            sds(2, 2, 2, count, size_z),
         ],
         flops=20_000_000,
     )
     parts = [sds(2, size_x + 2, size_y, size_z), sds(2, 2, count, size_z)]
-    packed_x = [sds(2, 3, size_y + 8, size_z)] * 2
+    packed_x = [[sds(2, depth, size_y + 8, size_z)] * 2 for depth in (3, 2)]
     wholes = [sds(2, size_x + 4, size_y, size_z), sds(2, 2, count, size_z)]
-    packed_y = [sds(2, 3, count, size_z)] * 2
+    packed_y = [[sds(2, 3, count, size_z)] * 2, [sds(2, size_x + count, size_z)] * 2]
     rows = SPAN * size_y + 48
     work = [
         pltpu.VMEM((2, size_x + 2, size_y, size_z), F32),
@@ -623,29 +666,29 @@
     own = sds(2, size_x, size_y, size_z)
 
     part, part_rows, *packed = call(
-        first_solve_kernel, [flags], [load, *x_halo, *y_halo, inverse, *consts], parts + packed_x, work, 3_000_000_000
+        first_solve_kernel, [flags], [load, *x_halo, *y_halo, inverse, *consts], parts + packed_x[0], work, 3_000_000_000
     )
     received = swap(mesh, "gx", *packed)
-    whole, whole_rows, *packed = call(merge_x_kernel, [flags], [part, part_rows, *received], wholes + packed_y)
+    whole, whole_rows, *packed = call(merge_x_kernel, [flags], [part, part_rows, *received], wholes + packed_y[0])
     received = swap(mesh, "gy", *packed)
     precond, image, sums, part, part_rows, *packed = call(
         second_solve_kernel,
         [flags],
-        [whole, whole_rows, *received, half, mass, half_lines, mass_lines, load, inverse, *consts],
-        [own, own, sds(8, size_z)] + parts + packed_x,
+        [whole, whole_rows, *received, half, mass, face, half_lines, mass_lines, face_lines, load, inverse, *consts],
+        [own, own, sds(8, size_z)] + parts + packed_x[1],
         padded + [pltpu.VMEM((2, 2, count, size_z), F32)] + work,
         3_000_000_000,
     )
     received = swap(mesh, "gx", *packed)
-    whole, whole_rows, *packed = call(merge_x_kernel, [flags], [part, part_rows, *received], wholes + packed_y)
+    whole, whole_rows, *packed = call(merge_x_kernel, [flags], [part, part_rows, *received], wholes + packed_y[1])
     received = swap(mesh, "gy", *packed)
     devices = mesh.shape["gx"] * mesh.shape["gy"]
     last_precond, last_image, sums = call(
         second_image_kernel,
         [flags],
-        [whole, whole_rows, *received, half, mass, image, sums],
+        [whole, whole_rows, *received, half, mass, face, image, sums],
         [own, own, sds(devices, size_z)],
-        padded,
+        padded[:1],
         10_000_000,
     )
     sums = lax.all_to_all(sums, AXES, 0, 0, tiled=True)

time: 68.5 us -> 63.8 us (0.931)
  waiting for transfers between devices: 15.3 us -> 12.4 us
  Pallas kernels: 17.7 us -> 16.1 us
    ppermute x6, waiting for transfers between devices: 9.9 us -> 7.89 us  [swap(): first = lax.ppermute(even_part, AXES, swap_pairs(mesh, axis, False))]
    pallas_call x9, Pallas kernels: 17.7 us -> 16.1 us  [call(): pl.pallas_call(kernel, out_shape=tuple(outs), in_specs=[SMEM] * len(scala...]
    ppermute x6, waiting for transfers between devices: 5.4 us -> 4.5 us  [swap(): second = lax.ppermute(odd_part, AXES, swap_pairs(mesh, axis, True))]
    unnamed x20 -> x22, local copies, waits for them, and re-layouts: 3.89 us -> 3.9 us
  transfers between devices with their start and end apart: 12 -> 12, of which waited for: 4 -> 5; matrix products, arithmetic and copies ran while one was open for 3% -> 2% of each run, Pallas kernels for 4% -> 5%
where the time goes in v2:
time: 63.8 us; the launch traced here: 63.5 us
  Pallas kernels  16.1 us (25%)
  starting transfers between devices  14 us (22%)
  blocking collectives  13.2 us (21%)
  waiting for transfers between devices  12.4 us (19%)
  local copies, waits for them, and re-layouts  4.74 us (7%)
  other arithmetic  2.25 us (4%)
  between operations  0.77 us (1%)
    pallas_call x9, Pallas kernels, call(): pl.pallas_call(kernel, out_shape=tuple(outs), in_specs=[SMEM] * len(scala...  16.1 us
    all_to_all x1, blocking collectives, shards(): sums = lax.all_to_all(sums, AXES, 0, 0, tiled=True)  13.2 us
    ppermute x6, starting transfers between devices, swap(): first = lax.ppermute(even_part, AXES, swap_pairs(mesh, axis, False))  8.07 us
    ppermute x6, waiting for transfers between devices, swap(): first = lax.ppermute(even_part, AXES, swap_pairs(mesh, axis, False))  7.89 us
    ppermute x6, starting transfers between devices, swap(): second = lax.ppermute(odd_part, AXES, swap_pairs(mesh, axis, True))  5.95 us
    ppermute x6, waiting for transfers between devices, swap(): second = lax.ppermute(odd_part, AXES, swap_pairs(mesh, axis, True))  4.5 us
    unnamed x22, local copies, waits for them, and re-layouts  3.9 us
  transfers between devices with their start and end apart: 12, of which 5 were waited for; matrix products, arithmetic and copies ran while one was open for 2% of the time, Pallas kernels for 5%

profile of v2, /device:TPU:0, one launch (start us, length us, event | category | flops | bytes accessed | tf_op | source)
XLA Modules:
  0.0 63.5 jit_solution(16362415757613252592)
XLA Ops:
  0.7 0.8 %slice_convert_fusion.1 = (f32[2,16,128]{2,1,0:T(8,128)S(1)}, f32[2,16,128]{2,1,0:T(8,128)S(1)}) fusion(s32[32,16,128]{2,1,0:T(8,128)} %zones_ref.5), kind=kLoop, calls=%fused_computation.6 | loop fusion | flops 8192 | bytes 65536 | tf_op jit(solution)/shard_map/convert_element_type | solution.py:629
  1.4 0.7 %slice_bitcast_fusion.1 = (f32[2,16,128]{2,1,0:T(8,128)S(1)}, f32[2,16,128]{2,1,0:T(8,128)S(1)}) fusion(f32[2,32,16,128]{3,2,1,0:T(8,128)} %load_ref.7), kind=kLoop, calls=%fused_computation.7 | loop fusion | bytes 65536 | tf_op jit(solution)/shard_map/squeeze | solution.py:629
  2.2 2.5 %collective-permute-start.1 = (f32[4,16,128]{2,1,0:T(8,128)S(1)}, f32[4,16,128]{2,1,0:T(8,128)S(1)}, u32[]{:S(2)}, u32[]{:S(2)}) collective-permute-start(f32[4,16,128]{2,1,0:T(8,128)S(1)} %get-tuple-element.66), channel_id=1, source_target_pairs={{0,24},{1,25},{2,26},{3,27},{4,28},{5,29},{6,30},{7,31},{8,16},{9,... | collective-permute-start | bytes 98312 | tf_op jit(solution)/shard_map/ppermute | solution.py:109
  4.7 0.7 %collective-permute-start = (f32[4,16,128]{2,1,0:T(8,128)S(1)}, f32[4,16,128]{2,1,0:T(8,128)S(1)}, u32[]{:S(2)}, u32[]{:S(2)}) collective-permute-start(f32[4,16,128]{2,1,0:T(8,128)S(1)} %get-tuple-element.67), channel_id=1, source_target_pairs={{0,8},{1,9},{2,10},{3,11},{4,12},{5,13},{6,14},{7,15},{8,0},{9,1},... | collective-permute-start | bytes 98312 | tf_op jit(solution)/shard_map/ppermute | solution.py:108
  5.3 0.7 %broadcast_multiply_fusion = f32[2,8]{1,0:T(2,128)S(1)} fusion(f32[2,8]{1,0:T(2,128)} %param.13), kind=kLoop, calls=%fused_computation.11 | loop fusion | flops 16 | bytes 128 | tf_op jit(solution)/shard_map/mul | solution.py:621
  6.0 0.8 %fusion.2 = f32[1,8]{1,0:T(1,128)S(1)} fusion(f32[8]{0:T(128)} %param.15, f32[2,8]{1,0:T(2,128)} %param.14), kind=kLoop, calls=%fused_computation.10 | loop fusion | flops 16 | bytes 128 | tf_op jit(solution)/shard_map/broadcast_in_dim | solution.py:621
  6.9 0.9 %copy-done = s32[32,16,128]{2,1,0:T(8,128)S(1)} copy-done((s32[32,16,128]{2,1,0:T(8,128)S(1)}, s32[32,16,128]{2,1,0:T(8,128)}, u32[]{:S(2)}) %copy-start) | copy-done | bytes 262168
  7.9 1.0 %copy-done.2 = f32[2,32,16,128]{3,2,1,0:T(8,128)S(1)} copy-done((f32[2,32,16,128]{3,2,1,0:T(8,128)S(1)}, f32[2,32,16,128]{3,2,1,0:T(8,128)}, u32[]{:S(2)}) %copy-start.2) | copy-done | bytes 524312
  8.9 0.7 %shard_map.122 = (f32[4,40,128]{2,1,0:T(8,128)S(1)}, f32[4,40,128]{2,1,0:T(8,128)S(1)}) custom-call(s32[6]{0:T(128)S(1)} %convert_element_type.9.flags, f32[2,32,16,128]{3,2,1,0:T(8,128)S(1)} %copy-done.2, s32[32,16,128]{2,1,0:T(8,128)S(1)} %copy-done, f32[4,16,128]{2,1,0:T(8,128)S(1)} %collective-permute-done.first_ref.first_x, ...), custom_call_target="tpu_custom_call" | custom-call | bytes 1015808 | tf_op jit(solution)/shard_map/pallas_call | solution.py:600
  9.6 2.0 %collective-permute-start.2 = (f32[4,40,128]{2,1,0:T(8,128)S(1)}, f32[4,40,128]{2,1,0:T(8,128)S(1)}, u32[]{:S(2)}, u32[]{:S(2)}) collective-permute-start(f32[4,40,128]{2,1,0:T(8,128)S(1)} %get-tuple-element.32), channel_id=1, source_target_pairs={{0,1},{1,0},{2,3},{3,2},{4,5},{5,4},{6,7},{7,6},{8,9},{9,8},{10,11... | collective-permute-start | bytes 245768 | tf_op jit(solution)/shard_map/ppermute | solution.py:112
  11.6 1.0 %copy-done.4 = f32[336,144]{1,0:T(8,128)S(1)} copy-done((f32[336,144]{1,0:T(8,128)S(1)}, f32[336,144]{1,0:T(8,128)}, u32[]{:S(2)}) %copy-start.4) | copy-done | bytes 193560
  12.6 0.9 %copy-done.5 = f32[128,144]{1,0:T(8,128)S(1)} copy-done((f32[128,144]{1,0:T(8,128)S(1)}, f32[128,144]{1,0:T(8,128)}, u32[]{:S(2)}) %copy-start.5) | copy-done | bytes 73752
  13.5 1.5 %shard_map.123.inverse_ref = f32[4,336,144]{2,1,0:T(8,128)S(1)} custom-call(f32[5,8]{1,0:T(8,128)S(1)} %pad_maximum_fusion.2.table_ref, s32[32,16,128]{2,1,0:T(8,128)S(1)} %copy-done.1, f32[336,144]{1,0:T(8,128)S(1)} %copy-done.4, f32[128,144]{1,0:T(8,128)S(1)} %copy-done.5), custom_call_target="tpu_custom_call" | custom-call | flops 40000000 | bytes 1303552 | tf_op jit(solution)/shard_map/pallas_call | solution.py:600
  15.0 0.3 collective-permute-done.2.first_y
  15.4 3.4 %shard_map.124 = (f32[2,34,16,128]{3,2,1,0:T(8,128)S(1)}, f32[2,2,40,128]{3,2,1,0:T(8,128)S(1)}, f32[2,3,24,128]{3,2,1,0:T(8,128)S(1)}, f32[2,3,24,128]{3,2,1,0:T(8,128)S(1)}) custom-call(s32[6]{0:T(128)S(1)} %convert_element_type.9.flags, f32[2,32,16,128]{3,2,1,0:T(8,128)S(1)} %copy-done.3, f32[4,16,128]{2,1,0:T(8,128)S(1)} %collective-permute-done.first_ref.first_x, ...), custom_call_target="tpu_custom_call" | custom-call | flops 3000000000 | bytes 3853312 | tf_op jit(solution)/shard_map/pallas_call | solution.py:600
  18.8 0.3 collective-permute-start.4
  19.0 1.5 %collective-permute-start.5 = (f32[2,3,24,128]{3,2,1,0:T(8,128)S(1)}, f32[2,3,24,128]{3,2,1,0:T(8,128)S(1)}, u32[]{:S(2)}, u32[]{:S(2)}) collective-permute-start(f32[2,3,24,128]{3,2,1,0:T(8,128)S(1)} %get-tuple-element.37), channel_id=1, source_target_pairs={{0,24},{1,25},{2,26},{3,27},{4,28},{5,29},{6,30},{7,31},{8,16},{9,... | collective-permute-start | bytes 221192 | tf_op jit(solution)/shard_map/ppermute | solution.py:109
  20.6 2.6 %collective-permute-done.5.second_ref = f32[2,3,24,128]{3,2,1,0:T(8,128)S(1)} collective-permute-done((f32[2,3,24,128]{3,2,1,0:T(8,128)S(1)}, f32[2,3,24,128]{3,2,1,0:T(8,128)S(1)}, u32[]{:S(2)}, u32[]{:S(2)}) %collective-permute-start.5) | collective-permute-done | bytes 73760 | tf_op jit(solution)/shard_map/ppermute | solution.py:109
  23.2 0.7 %shard_map.125 = (f32[2,36,16,128]{3,2,1,0:T(8,128)S(1)}, f32[2,2,40,128]{3,2,1,0:T(8,128)S(1)}, f32[2,3,40,128]{3,2,1,0:T(8,128)S(1)}, f32[2,3,40,128]{3,2,1,0:T(8,128)S(1)}) custom-call(s32[6]{0:T(128)S(1)} %convert_element_type.9.flags, f32[2,34,16,128]{3,2,1,0:T(8,128)S(1)} %get-tuple-element.34.part_ref, ...), custom_call_target="tpu_custom_call" | custom-call | bytes 1703936 | tf_op jit(solution)/shard_map/pallas_call | solution.py:600
  23.9 2.6 %collective-permute-start.6 = (f32[2,3,40,128]{3,2,1,0:T(8,128)S(1)}, f32[2,3,40,128]{3,2,1,0:T(8,128)S(1)}, u32[]{:S(2)}, u32[]{:S(2)}) collective-permute-start(f32[2,3,40,128]{3,2,1,0:T(8,128)S(1)} %get-tuple-element.40), channel_id=1, source_target_pairs={{0,1},{1,0},{2,3},{3,2},{4,5},{5,4},{6,7},{7,6},{8,9},{9,8},{10,11... | collective-permute-start | bytes 368648 | tf_op jit(solution)/shard_map/ppermute | solution.py:112
  26.5 1.7 %shard_map.126 = (f32[2,36,32,128]{3,2,1,0:T(8,128)S(1)}, f32[3,34,16,128]{3,2,1,0:T(8,128)S(1)}, f32[2,2,34,16,128]{4,3,2,1,0:T(8,128)S(1)}, f32[2,6,40,128]{3,...) custom-call(s32[6]{0:T(128)S(1)} %convert_element_type.9.flags, ...), custom_call_target="tpu_custom_call" | custom-call | flops 20000000 | bytes 4153344 | tf_op jit(solution)/shard_map/pallas_call | solution.py:600
  28.3 4.0 %collective-permute-done.6.first_ref = f32[2,3,40,128]{3,2,1,0:T(8,128)S(1)} collective-permute-done((f32[2,3,40,128]{3,2,1,0:T(8,128)S(1)}, f32[2,3,40,128]{3,2,1,0:T(8,128)S(1)}, u32[]{:S(2)}, u32[]{:S(2)}) %collective-permute-start.6) | collective-permute-done | bytes 122912 | tf_op jit(solution)/shard_map/ppermute | solution.py:112
  32.2 4.6 %shard_map.127 = (f32[2,32,16,128]{3,2,1,0:T(8,128)S(1)}, f32[2,32,16,128]{3,2,1,0:T(8,128)S(1)}, f32[8,128]{1,0:T(8,128)S(1)}, f32[2,34,16,128]{3,2,1,0:T(8,128...) custom-call(s32[6]{0:T(128)S(1)} %convert_element_type.9.flags, ...), custom_call_target="tpu_custom_call" | custom-call | flops 3000000000 | bytes 9206784 | tf_op jit(solution)/shard_map/pallas_call | solution.py:600
  36.8 1.7 %collective-permute-start.9 = (f32[2,2,24,128]{3,2,1,0:T(8,128)S(1)}, f32[2,2,24,128]{3,2,1,0:T(8,128)S(1)}, u32[]{:S(2)}, u32[]{:S(2)}) collective-permute-start(f32[2,2,24,128]{3,2,1,0:T(8,128)S(1)} %get-tuple-element.51), channel_id=1, source_target_pairs={{0,24},{1,25},{2,26},{3,27},{4,28},{5,29},{6,30},{7,31},{8,16},{9,... | collective-permute-start | bytes 147464 | tf_op jit(solution)/shard_map/ppermute | solution.py:109
  38.5 1.9 %collective-permute-done.9.second_ref = f32[2,2,24,128]{3,2,1,0:T(8,128)S(1)} collective-permute-done((f32[2,2,24,128]{3,2,1,0:T(8,128)S(1)}, f32[2,2,24,128]{3,2,1,0:T(8,128)S(1)}, u32[]{:S(2)}, u32[]{:S(2)}) %collective-permute-start.9) | collective-permute-done | bytes 49184 | tf_op jit(solution)/shard_map/ppermute | solution.py:109
  40.4 0.7 %shard_map.128 = (f32[2,36,16,128]{3,2,1,0:T(8,128)S(1)}, f32[2,2,40,128]{3,2,1,0:T(8,128)S(1)}, f32[2,72,128]{2,1,0:T(8,128)S(1)}, f32[2,72,128]{2,1,0:T(8,128)S(1)}) custom-call(s32[6]{0:T(128)S(1)} %convert_element_type.9.flags, f32[2,34,16,128]{3,2,1,0:T(8,128)S(1)} %get-tuple-element.48.part_ref, f32[2,2,40,128]{3,2,1,0:T(8,128)S(1)} %get-tuple-element.49.part_rows_ref, ...), custom_call_target="tpu_custom_call" | custom-call | bytes 1556480 | tf_op jit(solution)/shard_map/pallas_call | solution.py:600
  41.1 2.5 %collective-permute-start.10 = (f32[2,72,128]{2,1,0:T(8,128)S(1)}, f32[2,72,128]{2,1,0:T(8,128)S(1)}, u32[]{:S(2)}, u32[]{:S(2)}) collective-permute-start(f32[2,72,128]{2,1,0:T(8,128)S(1)} %get-tuple-element.54), channel_id=1, source_target_pairs={{0,1},{1,0},{2,3},{3,2},{4,5},{5,4},{6,7},{7,6},{8,9},{9,8},{10,11... | collective-permute-start | bytes 221192 | tf_op jit(solution)/shard_map/ppermute | solution.py:112
  43.6 0.2 collective-permute-start.11
  43.8 3.6 %collective-permute-done.10.first_ref = f32[2,72,128]{2,1,0:T(8,128)S(1)} collective-permute-done((f32[2,72,128]{2,1,0:T(8,128)S(1)}, f32[2,72,128]{2,1,0:T(8,128)S(1)}, u32[]{:S(2)}, u32[]{:S(2)}) %collective-permute-start.10) | collective-permute-done | bytes 73760 | tf_op jit(solution)/shard_map/ppermute | solution.py:112
  47.4 1.6 %shard_map.129 = (f32[2,32,16,128]{3,2,1,0:T(8,128)S(1)}, f32[2,32,16,128]{3,2,1,0:T(8,128)S(1)}, f32[32,128]{1,0:T(8,128)S(1)}) custom-call(s32[6]{0:T(128)S(1)} %convert_element_type.9.flags, f32[2,36,16,128]{3,2,1,0:T(8,128)S(1)} %get-tuple-element.52.whole_ref, f32[2,2,40,128]{3,2,1,0:T(8,128)S(1)} %get-tuple-element.53.whole_rows_ref, ...), custom_call_target="tpu_custom_call" | custom-call | flops 10000000 | bytes 5541888 | tf_op jit(solution)/shard_map/pallas_call | solution.py:600
  49.0 13.2 %all_to_all.11 = f32[32,1,128]{2,1,0:T(1,128)S(1)} all-to-all(f32[32,1,128]{2,1,0:T(1,128)S(1)} %bitcast.25), channel_id=1, replica_groups=mesh['gx'=4,'gy'=8] {'gx','gy'}, dimensions={0} | all-to-all | bytes 32768 | tf_op jit(solution)/shard_map/all_to_all | solution.py:694
  62.2 1.3 %shard_map.130 = (f32[2,32,16,128]{3,2,1,0:T(8,128)}, f32[2,32,16,128]{3,2,1,0:T(8,128)}) custom-call(f32[32,128]{1,0:T(8,128)S(1)} %bitcast.24, f32[2,32,16,128]{3,2,1,0:T(8,128)S(1)} %copy-done.3, f32[2,32,16,128]{3,2,1,0:T(8,128)S(1)} %get-tuple-element.59.z_ref, f32[2,32,16,128]{3,2,1,0:T(8,128)S(1)} %get-tuple-element.56.old_image_ref.q_ref, ...), custom_call_target="tpu_custom_call" | custom-call | bytes 3686400 | tf_op jit(solution)/shard_map/pallas_call | solution.py:600
  (32 shorter events, 0.3 us)
Async XLA Ops:
  0.6 11.0 %copy-start.1 = (s32[32,16,128]{2,1,0:T(8,128)S(1)}, s32[32,16,128]{2,1,0:T(8,128)}, u32[]{:S(2)}) copy-start(s32[32,16,128]{2,1,0:T(8,128)} %zones_ref.5) | copy-start | bytes 786436
  0.6 11.0 %copy-start.10 = (f32[2,8]{1,0:T(2,128)S(1)}, f32[2,8]{1,0:T(2,128)}, u32[]{:S(2)}) copy-start(f32[2,8]{1,0:T(2,128)} %param.14) | copy-start | bytes 196
  2.2 4.7 %collective-permute-start.1 = (f32[4,16,128]{2,1,0:T(8,128)S(1)}, f32[4,16,128]{2,1,0:T(8,128)S(1)}, u32[]{:S(2)}, u32[]{:S(2)}) collective-permute-start(f32[4,16,128]{2,1,0:T(8,128)S(1)} %get-tuple-element.66), channel_id=1, source_target_pairs={{0,24},{1,25},{2,26},{3,27},{4,28},{5,29},{6,30},{7,31},{8,16},{9,... | collective-permute-start | bytes 98312 | tf_op jit(solution)/shard_map/ppermute | solution.py:109
  4.7 2.2 %collective-permute-start = (f32[4,16,128]{2,1,0:T(8,128)S(1)}, f32[4,16,128]{2,1,0:T(8,128)S(1)}, u32[]{:S(2)}, u32[]{:S(2)}) collective-permute-start(f32[4,16,128]{2,1,0:T(8,128)S(1)} %get-tuple-element.67), channel_id=1, source_target_pairs={{0,8},{1,9},{2,10},{3,11},{4,12},{5,13},{6,14},{7,15},{8,0},{9,1},... | collective-permute-start | bytes 98312 | tf_op jit(solution)/shard_map/ppermute | solution.py:108
  6.9 1.0 %copy-start = (s32[32,16,128]{2,1,0:T(8,128)S(1)}, s32[32,16,128]{2,1,0:T(8,128)}, u32[]{:S(2)}) copy-start(s32[32,16,128]{2,1,0:T(8,128)} %zones_ref.5) | copy-start | bytes 786436
  7.9 1.0 %copy-start.2 = (f32[2,32,16,128]{3,2,1,0:T(8,128)S(1)}, f32[2,32,16,128]{3,2,1,0:T(8,128)}, u32[]{:S(2)}) copy-start(f32[2,32,16,128]{3,2,1,0:T(8,128)} %load_ref.7) | copy-start | bytes 1572868
  8.9 6.4 %copy-start.6 = (bf16[336,1008]{1,0:T(8,128)(2,1)S(1)}, bf16[336,1008]{1,0:T(8,128)(2,1)}, u32[]{:S(2)}) copy-start(bf16[336,1008]{1,0:T(8,128)(2,1)} %constant.45.clone.c1) | copy-start | bytes 2032132
  8.9 6.4 %copy-start.9 = (bf16[144,256]{1,0:T(8,128)(2,1)S(1)}, bf16[144,256]{1,0:T(8,128)(2,1)}, u32[]{:S(2)}) copy-start(bf16[144,256]{1,0:T(8,128)(2,1)} %constant.47.clone.c3) | copy-start | bytes 221188
  9.6 5.7 %copy-start.3 = (f32[2,32,16,128]{3,2,1,0:T(8,128)S(1)}, f32[2,32,16,128]{3,2,1,0:T(8,128)}, u32[]{:S(2)}) copy-start(f32[2,32,16,128]{3,2,1,0:T(8,128)} %load_ref.7) | copy-start | bytes 1572868
  9.6 5.7 %collective-permute-start.2 = (f32[4,40,128]{2,1,0:T(8,128)S(1)}, f32[4,40,128]{2,1,0:T(8,128)S(1)}, u32[]{:S(2)}, u32[]{:S(2)}) collective-permute-start(f32[4,40,128]{2,1,0:T(8,128)S(1)} %get-tuple-element.32), channel_id=1, source_target_pairs={{0,1},{1,0},{2,3},{3,2},{4,5},{5,4},{6,7},{7,6},{8,9},{9,8},{10,11... | collective-permute-start | bytes 245768 | tf_op jit(solution)/shard_map/ppermute | solution.py:112
  11.6 3.7 %collective-permute-start.3 = (f32[4,40,128]{2,1,0:T(8,128)S(1)}, f32[4,40,128]{2,1,0:T(8,128)S(1)}, u32[]{:S(2)}, u32[]{:S(2)}) collective-permute-start(f32[4,40,128]{2,1,0:T(8,128)S(1)} %get-tuple-element.33), channel_id=1, source_target_pairs={{0,8},{1,2},{2,1},{3,4},{4,3},{5,6},{6,5},{7,15},{8,0},{9,10},{10,... | collective-permute-start | bytes 245768 | tf_op jit(solution)/shard_map/ppermute | solution.py:111
  11.6 1.0 %copy-start.4 = (f32[336,144]{1,0:T(8,128)S(1)}, f32[336,144]{1,0:T(8,128)}, u32[]{:S(2)}) copy-start(f32[336,144]{1,0:T(8,128)} %constant.48.clone.summed_ref) | copy-start | bytes 580612
  12.6 0.9 %copy-start.5 = (f32[128,144]{1,0:T(8,128)S(1)}, f32[128,144]{1,0:T(8,128)}, u32[]{:S(2)}) copy-start(f32[128,144]{1,0:T(8,128)} %constant.49.clone.means_ref) | copy-start | bytes 221188
  13.5 1.8 %copy-start.7 = (bf16[336,1008]{1,0:T(8,128)(2,1)S(1)}, bf16[336,1008]{1,0:T(8,128)(2,1)}, u32[]{:S(2)}) copy-start(bf16[336,1008]{1,0:T(8,128)(2,1)} %constant.44.clone.c0) | copy-start | bytes 2032132
  13.5 1.8 %copy-start.8 = (bf16[384,144]{1,0:T(8,128)(2,1)S(1)}, bf16[384,144]{1,0:T(8,128)(2,1)}, u32[]{:S(2)}) copy-start(bf16[384,144]{1,0:T(8,128)(2,1)} %constant.46.clone.c2) | copy-start | bytes 331780
  18.8 1.8 %collective-permute-start.4 = (f32[2,3,24,128]{3,2,1,0:T(8,128)S(1)}, f32[2,3,24,128]{3,2,1,0:T(8,128)S(1)}, u32[]{:S(2)}, u32[]{:S(2)}) collective-permute-start(f32[2,3,24,128]{3,2,1,0:T(8,128)S(1)} %get-tuple-element.36), channel_id=1, source_target_pairs={{0,8},{1,9},{2,10},{3,11},{4,12},{5,13},{6,14},{7,15},{8,0},{9,1},... | collective-permute-start | bytes 221192 | tf_op jit(solution)/shard_map/ppermute | solution.py:108
  19.0 4.1 %collective-permute-start.5 = (f32[2,3,24,128]{3,2,1,0:T(8,128)S(1)}, f32[2,3,24,128]{3,2,1,0:T(8,128)S(1)}, u32[]{:S(2)}, u32[]{:S(2)}) collective-permute-start(f32[2,3,24,128]{3,2,1,0:T(8,128)S(1)} %get-tuple-element.37), channel_id=1, source_target_pairs={{0,24},{1,25},{2,26},{3,27},{4,28},{5,29},{6,30},{7,31},{8,16},{9,... | collective-permute-start | bytes 221192 | tf_op jit(solution)/shard_map/ppermute | solution.py:109
  23.9 8.3 %collective-permute-start.6 = (f32[2,3,40,128]{3,2,1,0:T(8,128)S(1)}, f32[2,3,40,128]{3,2,1,0:T(8,128)S(1)}, u32[]{:S(2)}, u32[]{:S(2)}) collective-permute-start(f32[2,3,40,128]{3,2,1,0:T(8,128)S(1)} %get-tuple-element.40), channel_id=1, source_target_pairs={{0,1},{1,0},{2,3},{3,2},{4,5},{5,4},{6,7},{7,6},{8,9},{9,8},{10,11... | collective-permute-start | bytes 368648 | tf_op jit(solution)/shard_map/ppermute | solution.py:112
  26.5 5.7 %collective-permute-start.7 = (f32[2,3,40,128]{3,2,1,0:T(8,128)S(1)}, f32[2,3,40,128]{3,2,1,0:T(8,128)S(1)}, u32[]{:S(2)}, u32[]{:S(2)}) collective-permute-start(f32[2,3,40,128]{3,2,1,0:T(8,128)S(1)} %get-tuple-element.41), channel_id=1, source_target_pairs={{0,8},{1,2},{2,1},{3,4},{4,3},{5,6},{6,5},{7,15},{8,0},{9,10},{10,... | collective-permute-start | bytes 368648 | tf_op jit(solution)/shard_map/ppermute | solution.py:111
  36.8 1.8 %collective-permute-start.8 = (f32[2,2,24,128]{3,2,1,0:T(8,128)S(1)}, f32[2,2,24,128]{3,2,1,0:T(8,128)S(1)}, u32[]{:S(2)}, u32[]{:S(2)}) collective-permute-start(f32[2,2,24,128]{3,2,1,0:T(8,128)S(1)} %get-tuple-element.50), channel_id=1, source_target_pairs={{0,8},{1,9},{2,10},{3,11},{4,12},{5,13},{6,14},{7,15},{8,0},{9,1},... | collective-permute-start | bytes 147464 | tf_op jit(solution)/shard_map/ppermute | solution.py:108
  36.8 3.6 %collective-permute-start.9 = (f32[2,2,24,128]{3,2,1,0:T(8,128)S(1)}, f32[2,2,24,128]{3,2,1,0:T(8,128)S(1)}, u32[]{:S(2)}, u32[]{:S(2)}) collective-permute-start(f32[2,2,24,128]{3,2,1,0:T(8,128)S(1)} %get-tuple-element.51), channel_id=1, source_target_pairs={{0,24},{1,25},{2,26},{3,27},{4,28},{5,29},{6,30},{7,31},{8,16},{9,... | collective-permute-start | bytes 147464 | tf_op jit(solution)/shard_map/ppermute | solution.py:109
  41.1 6.3 %collective-permute-start.10 = (f32[2,72,128]{2,1,0:T(8,128)S(1)}, f32[2,72,128]{2,1,0:T(8,128)S(1)}, u32[]{:S(2)}, u32[]{:S(2)}) collective-permute-start(f32[2,72,128]{2,1,0:T(8,128)S(1)} %get-tuple-element.54), channel_id=1, source_target_pairs={{0,1},{1,0},{2,3},{3,2},{4,5},{5,4},{6,7},{7,6},{8,9},{9,8},{10,11... | collective-permute-start | bytes 221192 | tf_op jit(solution)/shard_map/ppermute | solution.py:112
  43.6 3.8 %collective-permute-start.11 = (f32[2,72,128]{2,1,0:T(8,128)S(1)}, f32[2,72,128]{2,1,0:T(8,128)S(1)}, u32[]{:S(2)}, u32[]{:S(2)}) collective-permute-start(f32[2,72,128]{2,1,0:T(8,128)S(1)} %get-tuple-element.55), channel_id=1, source_target_pairs={{0,8},{1,2},{2,1},{3,4},{4,3},{5,6},{6,5},{7,15},{8,0},{9,10},{10,... | collective-permute-start | bytes 221192 | tf_op jit(solution)/shard_map/ppermute | solution.py:111

commit v3 on v2

--- a/solution.py
+++ b/solution.py
@@ -114,6 +114,19 @@
 
 
 EVEN_X, EVEN_Y, LOW_X, HIGH_X, LOW_Y, HIGH_Y = range(6)
+
+
+def standing(mesh):
+    here_x, here_y = lax.axis_index("gx"), lax.axis_index("gy")
+    facts = (
+        lax.rem(here_x, 2) == 0,
+        lax.rem(here_y, 2) == 0,
+        here_x > 0,
+        here_x < mesh.shape["gx"] - 1,
+        here_y > 0,
+        here_y < mesh.shape["gy"] - 1,
+    )
+    return [fact.astype(jnp.int32) for fact in facts]
 
 
 def chosen(flags, which, yes, no):
@@ -213,11 +226,11 @@
             odd_ref[field, layer, size_y + 2 :] = blank
 
 
-def divisor_kernel(table_ref, zones_ref, summed_ref, means_ref, inverse_ref):
+def divisor_kernel(conductance_ref, capacity_ref, zones_ref, summed_ref, means_ref, inverse_ref):
     size_x, size_y, size_z = zones_ref.shape
     boxes = size_x // BOX
     lines = []
-    for which in (2, 3, 0, 1):
+    for table_ref, which in ((capacity_ref, 0), (capacity_ref, 1), (conductance_ref, 0), (conductance_ref, 1)):
         for box in range(boxes):
             total = jnp.zeros((size_y, size_z), F32)
             for x in range(box * BOX, (box + 1) * BOX):
@@ -232,11 +245,24 @@
     half = 2 * boxes
     for combo in range(half):
         cbar = means[combo : combo + 1]
-        kbar = 2.0 * means[half + combo : half + combo + 1]
+        kbar = means[half + combo : half + combo + 1]
         inverse_ref[combo] = 1.0 / (cbar + kbar * summed_ref[...])
 
 
-def edge_rows_kernel(flags, load_ref, zones_ref, first_ref, second_ref, even_ref, odd_ref):
+def edge_layers_kernel(mesh, load_ref, zones_ref, even_ref, odd_ref):
+    flags = standing(mesh)
+    last = zones_ref.shape[0] - 1
+    for channel in range(4):
+        if channel < 2:
+            low, high = load_ref[channel, 0], load_ref[channel, last]
+        else:
+            low, high = zones_ref[channel - 2].astype(F32), zones_ref[last - 3 + channel].astype(F32)
+        even_ref[channel] = chosen(flags, EVEN_X, high, low)
+        odd_ref[channel] = chosen(flags, EVEN_X, low, high)
+
+
+def edge_rows_kernel(mesh, load_ref, zones_ref, first_ref, second_ref, even_ref, odd_ref):
+    flags = standing(mesh)
     size_x, size_y, size_z = zones_ref.shape
     from_low = chosen(flags, EVEN_X, second_ref[...], first_ref[...])
     from_high = chosen(flags, EVEN_X, first_ref[...], second_ref[...])
@@ -268,17 +294,24 @@
             put(channel, end + depth, 1, high[near : near + 1], high[far : far + 1])
 
 
-def looked_up(table_ref, which, zone):
-    value = jnp.full(zone.shape, table_ref[which, 0], F32)
-    for label in range(1, table_ref.shape[1]):
-        value = jnp.where(zone == float(label), table_ref[which, label], value)
+def looked_up(entries, zone):
+    value = jnp.full(zone.shape, entries[0], F32)
+    for label in range(1, len(entries)):
+        value = jnp.where(zone == float(label), entries[label], value)
     return value
 
 
 def coefficient_kernel(
-    flags, table_ref, zones_ref, first_x, second_x, first_y, second_y,
+    mesh, conductance_ref, capacity_ref, coupling_ref, zones_ref, first_x, second_x, first_y, second_y,
     half_ref, mass_ref, face_ref, half_rows_ref, mass_rows_ref, face_rows_ref,
 ):
+    flags = standing(mesh)
+    labels = range(coupling_ref.shape[0])
+    halves_of = [[0.5 * conductance_ref[field, label] for label in labels] for field in range(2)]
+    masses = [[capacity_ref[field, label] for label in labels] for field in range(2)]
+    line = zones_ref.shape[2:]
+    roots = [jnp.sqrt(jnp.full((8, *line), capacity_ref[0, label] * capacity_ref[1, label], F32)) for label in labels]
+    masses.append([coupling_ref[label] * roots[label][0:1] for label in labels])
     size_x, size_y, size_z = zones_ref.shape
     low_x = chosen(flags, EVEN_X, second_x[2:4], first_x[2:4])
     high_x = chosen(flags, EVEN_X, first_x[2:4], second_x[2:4])
@@ -293,10 +326,10 @@
         else:
             zone = zones_ref[x].astype(F32)
         for field in range(2):
-            half_ref[field, x + 2, inside] = looked_up(table_ref, field, zone)
+            half_ref[field, x + 2, inside] = looked_up(halves_of[field], zone)
         if -1 <= x <= size_x:
             for which in range(3):
-                mass_ref[which, x + 1] = looked_up(table_ref, 2 + which, zone)
+                mass_ref[which, x + 1] = looked_up(masses[which], zone)
     for field in range(2):
         for outer in (0, 1):
             half_ref[field, outer, inside] = chosen(
@@ -312,7 +345,7 @@
         ((low_y[0], LOW_Y), (low_y[1], LOW_Y), (high_y[0], HIGH_Y), (high_y[1], HIGH_Y))
     ):
         for field in range(2):
-            value = looked_up(table_ref, field, zone)
+            value = looked_up(halves_of[field], zone)
             below = value[ROW0 : ROW0 + 1]
             above = value[ROW0 + size_x - 1 : ROW0 + size_x]
             value = jnp.where((position < ROW0) & (flags[LOW_X] == 0), below, value)
@@ -327,7 +360,7 @@
                 half_ref[field, :, row] = half_rows_ref[field, line, ROW0 - 2 : ROW0 + size_x + 2]
         if line in (1, 2):
             for which in range(3):
-                mass_rows_ref[which, line - 1] = looked_up(table_ref, 2 + which, zone)
+                mass_rows_ref[which, line - 1] = looked_up(masses[which], zone)
     for field in range(2):
         for x in range(0, size_x + 2, 2):
             faces = faces_z(half_ref[field, x + 1 : x + 3, inside])
@@ -343,9 +376,10 @@
 
 
 def first_solve_kernel(
-    flags, load_ref, first_x, second_x, first_y, second_y, inverse_ref, c0, c1, c2, c3,
+    mesh, load_ref, first_x, second_x, first_y, second_y, inverse_ref, c0, c1, c2, c3,
     part_ref, part_rows_ref, even_ref, odd_ref, field_ref, rows_ref, stack_ref,
 ):
+    flags = standing(mesh)
     size_x = load_ref.shape[1]
     for field in range(2):
         field_ref[field, 1 : 1 + size_x] = load_ref[field]
@@ -357,7 +391,8 @@
     pack_x(flags, part_ref, part_rows_ref, even_ref, odd_ref)
 
 
-def merge_x_kernel(flags, part_ref, part_rows_ref, first_ref, second_ref, whole_ref, whole_rows_ref, even_ref, odd_ref):
+def merge_x_kernel(mesh, part_ref, part_rows_ref, first_ref, second_ref, whole_ref, whole_rows_ref, even_ref, odd_ref):
+    flags = standing(mesh)
     size_x = part_ref.shape[1] - 2
     size_y, size_z = part_ref.shape[2:]
     depth = first_ref.shape[1]
@@ -495,11 +530,12 @@
 
 
 def second_solve_kernel(
-    flags, whole_ref, whole_rows_ref, first_ref, second_ref,
+    mesh, whole_ref, whole_rows_ref, first_ref, second_ref,
     half_ref, mass_ref, face_ref, half_lines, mass_lines, face_lines, load_ref, inverse_ref, c0, c1, c2, c3,
     precond_ref, image_ref, sums_ref, part_ref, part_rows_ref, even_ref, odd_ref,
     value_ref, lines, near, field_ref, rows_ref, stack_ref,
 ):
+    flags = standing(mesh)
     size_x, size_y, size_z = load_ref.shape[1:]
     assemble(flags, whole_ref, whole_rows_ref, first_ref, second_ref, value_ref, lines)
     for x, flag in ((-1, LOW_X), (size_x, HIGH_X)):
@@ -537,9 +573,10 @@
 
 
 def second_image_kernel(
-    flags, whole_ref, whole_rows_ref, first_ref, second_ref, half_ref, mass_ref, face_ref, old_image_ref, old_sums_ref,
+    mesh, whole_ref, whole_rows_ref, first_ref, second_ref, half_ref, mass_ref, face_ref, old_image_ref, old_sums_ref,
     precond_ref, image_ref, sums_ref, value_ref,
 ):
+    flags = standing(mesh)
     size_x, size_y, size_z = old_image_ref.shape[1:]
     own, wide = slice(2, size_x + 2), slice(1, size_x + 3)
     rows, margins = slice(ROW0, ROW0 + size_x), slice(size_x + ROW0 - 1, 2 * size_x + ROW0 + 1)
@@ -595,10 +632,10 @@
 VMEM = pl.BlockSpec(memory_space=pltpu.VMEM)
 
 
-def call(kernel, scalars, arrays, outs, scratch=(), flops=0, limit=24):
+def call(mesh, kernel, scalars, arrays, outs, scratch=(), flops=0, limit=24):
     moved = sum(math.prod(a.shape) * a.dtype.itemsize for a in list(arrays) + list(outs))
     return pl.pallas_call(
-        kernel,
+        kernel if mesh is None else functools.partial(kernel, mesh),
         out_shape=tuple(outs),
         in_specs=[SMEM] * len(scalars) + [VMEM] * len(arrays),
         out_specs=tuple([VMEM] * len(outs)),
@@ -617,27 +654,24 @@
     forward, back, line_forward, line_back, summed, means = [jnp.asarray(c) for c in constants(size_z)]
     consts = (forward, back, line_forward, line_back)
     modes, lanes = summed.shape
-    cross = coupling * jnp.sqrt(capacity[0] * capacity[1])
-    table = jnp.concatenate([0.5 * conductance, capacity, cross[None]], axis=0)
-    here_x, here_y = lax.axis_index("gx"), lax.axis_index("gy")
-    even_x, even_y = here_x % 2 == 0, here_y % 2 == 0
-    flags = jnp.stack(
-        [even_x, even_y, here_x > 0, here_x < mesh.shape["gx"] - 1, here_y > 0, here_y < mesh.shape["gy"] - 1]
-    ).astype(jnp.int32)
-
-    to_low = jnp.concatenate([load[:, 0], zones[:2].astype(F32)], axis=0)
-    to_high = jnp.concatenate([load[:, -1], zones[-2:].astype(F32)], axis=0)
-    x_halo = swap(mesh, "gx", jnp.where(even_x, to_high, to_low), jnp.where(even_x, to_low, to_high))
-
+    packed = call(
+        mesh, edge_layers_kernel, [], [load, zones], [sds(4, size_y, size_z)] * 2
+    )
+    x_halo = swap(mesh, "gx", *packed)
     (inverse,) = call(
-        divisor_kernel, [table], [zones, summed, means], [sds(2 * boxes, modes, lanes)], flops=40_000_000
+        None,
+        divisor_kernel,
+        [conductance, capacity],
+        [zones, summed, means],
+        [sds(2 * boxes, modes, lanes)],
+        flops=40_000_000,
     )
-    y_halo = swap(
-        mesh, "gy", *call(edge_rows_kernel, [flags], [load, zones, *x_halo], [sds(4, count, size_z)] * 2)
-    )
+    packed = call(mesh, edge_rows_kernel, [], [load, zones, *x_halo], [sds(4, count, size_z)] * 2)
+    y_halo = swap(mesh, "gy", *packed)
     half, mass, face, half_lines, mass_lines, face_lines = call(
+        mesh,
         coefficient_kernel,
-        [flags, table],
+        [conductance, capacity, coupling],
         [zones, *x_halo, *y_halo],
         [
             sds(2, size_x + 4, size_y + 16, size_z),
@@ -666,33 +700,35 @@
     own = sds(2, size_x, size_y, size_z)
 
     part, part_rows, *packed = call(
-        first_solve_kernel, [flags], [load, *x_halo, *y_halo, inverse, *consts], parts + packed_x[0], work, 3_000_000_000
+        mesh, first_solve_kernel, [], [load, *x_halo, *y_halo, inverse, *consts], parts + packed_x[0], work, 3_000_000_000
     )
     received = swap(mesh, "gx", *packed)
-    whole, whole_rows, *packed = call(merge_x_kernel, [flags], [part, part_rows, *received], wholes + packed_y[0])
+    whole, whole_rows, *packed = call(mesh, merge_x_kernel, [], [part, part_rows, *received], wholes + packed_y[0])
     received = swap(mesh, "gy", *packed)
     precond, image, sums, part, part_rows, *packed = call(
+        mesh,
         second_solve_kernel,
-        [flags],
+        [],
         [whole, whole_rows, *received, half, mass, face, half_lines, mass_lines, face_lines, load, inverse, *consts],
         [own, own, sds(8, size_z)] + parts + packed_x[1],
         padded + [pltpu.VMEM((2, 2, count, size_z), F32)] + work,
         3_000_000_000,
     )
     received = swap(mesh, "gx", *packed)
-    whole, whole_rows, *packed = call(merge_x_kernel, [flags], [part, part_rows, *received], wholes + packed_y[1])
+    whole, whole_rows, *packed = call(mesh, merge_x_kernel, [], [part, part_rows, *received], wholes + packed_y[1])
     received = swap(mesh, "gy", *packed)
     devices = mesh.shape["gx"] * mesh.shape["gy"]
     last_precond, last_image, sums = call(
+        mesh,
         second_image_kernel,
-        [flags],
+        [],
         [whole, whole_rows, *received, half, mass, face, image, sums],
         [own, own, sds(devices, size_z)],
         padded[:1],
         10_000_000,
     )
     sums = lax.all_to_all(sums, AXES, 0, 0, tiled=True)
-    return call(finish_kernel, [], [sums, load, precond, image, last_precond, last_image], [own, own])
+    return call(None, finish_kernel, [], [sums, load, precond, image, last_precond, last_image], [own, own])
 
 
 def solution(mesh):

time: 63.8 us -> 58.7 us (0.920)
  waiting for transfers between devices: 12.4 us -> 16.1 us
  Pallas kernels: 16.1 us -> 12.6 us
  local copies, waits for them, and re-layouts: 4.74 us -> 2.04 us
  other arithmetic: 2.25 us -> 0 us
    pallas_call x9 -> x10, Pallas kernels: 16.1 us -> 12.6 us  [call(): pl.pallas_call(kernel if mesh is None else functools.partial(kernel, mesh...]
    ppermute x6, waiting for transfers between devices: 7.89 us -> 10.1 us  [swap(): first = lax.ppermute(even_part, AXES, swap_pairs(mesh, axis, False))]
    unnamed x22 -> x26, local copies, waits for them, and re-layouts: 3.9 us -> 2.04 us
    ppermute x6, waiting for transfers between devices: 4.5 us -> 6.01 us  [swap(): second = lax.ppermute(odd_part, AXES, swap_pairs(mesh, axis, True))]
    convert_element_type x2 -> x0, other arithmetic: 0.78 us -> none  [the longest x1 0.78 us: shards(): to_high = jnp.concatenate([load[:, -1], zones[-2:].astype(F32)], axis=0)]
    broadcast_in_dim x1 -> x0, other arithmetic: 0.76 us -> none  [shards(): table = jnp.concatenate([0.5 * conductance, capacity, cross[None]], axis=0)]
    squeeze x1 -> x0, local copies, waits for them, and re-layouts: 0.74 us -> none  [shards(): to_high = jnp.concatenate([load[:, -1], zones[-2:].astype(F32)], axis=0)]
    mul x1 -> x0, other arithmetic: 0.68 us -> none  [shards(): table = jnp.concatenate([0.5 * conductance, capacity, cross[None]], axis=0)]
  transfers between devices with their start and end apart: 12 -> 12, of which waited for: 5 -> 6; matrix products, arithmetic and copies ran while one was open for 2% -> 0% of each run, Pallas kernels for 5% -> 5%
where the time goes in v3:
time: 58.7 us; the launch traced here: 58.5 us
  waiting for transfers between devices  16.1 us (27%)
  starting transfers between devices  13.8 us (24%)
  blocking collectives  13.2 us (22%)
  Pallas kernels  12.6 us (21%)
  local copies, waits for them, and re-layouts  2.04 us (3%)
  between operations  0.79 us (1%)
    all_to_all x1, blocking collectives, shards(): sums = lax.all_to_all(sums, AXES, 0, 0, tiled=True)  13.2 us
    pallas_call x10, Pallas kernels, call(): pl.pallas_call(kernel if mesh is None else functools.partial(kernel, mesh...  12.6 us
    ppermute x6, waiting for transfers between devices, swap(): first = lax.ppermute(even_part, AXES, swap_pairs(mesh, axis, False))  10.1 us
    ppermute x6, starting transfers between devices, swap(): first = lax.ppermute(even_part, AXES, swap_pairs(mesh, axis, False))  7.42 us
    ppermute x6, starting transfers between devices, swap(): second = lax.ppermute(odd_part, AXES, swap_pairs(mesh, axis, True))  6.36 us
    ppermute x6, waiting for transfers between devices, swap(): second = lax.ppermute(odd_part, AXES, swap_pairs(mesh, axis, True))  6.01 us
    unnamed x26, local copies, waits for them, and re-layouts  2.04 us
  transfers between devices with their start and end apart: 12, of which 6 were waited for; matrix products, arithmetic and copies ran while one was open for 0% of the time, Pallas kernels for 5%

profile of v3, /device:TPU:0, one launch (start us, length us, event | category | flops | bytes accessed | tf_op | source)
XLA Modules:
  0.0 58.5 jit_solution(1250911847739992847)
XLA Ops:
  0.6 1.0 %copy-done = f32[2,32,16,128]{3,2,1,0:T(8,128)S(1)} copy-done((f32[2,32,16,128]{3,2,1,0:T(8,128)S(1)}, f32[2,32,16,128]{3,2,1,0:T(8,128)}, u32[]{:S(2)}) %copy-start) | copy-done | bytes 524312
  1.7 0.9 %copy-done.2 = s32[32,16,128]{2,1,0:T(8,128)S(1)} copy-done((s32[32,16,128]{2,1,0:T(8,128)S(1)}, s32[32,16,128]{2,1,0:T(8,128)}, u32[]{:S(2)}) %copy-start.2) | copy-done | bytes 262168
  2.7 0.5 collective-permute-start
  3.2 2.6 %collective-permute-start.1 = (f32[4,16,128]{2,1,0:T(8,128)S(1)}, f32[4,16,128]{2,1,0:T(8,128)S(1)}, u32[]{:S(2)}, u32[]{:S(2)}) collective-permute-start(f32[4,16,128]{2,1,0:T(8,128)S(1)} %get-tuple-element.35), channel_id=1, source_target_pairs={{0,24},{1,25},{2,26},{3,27},{4,28},{5,29},{6,30},{7,31},{8,16},{9,... | collective-permute-start | bytes 98312 | tf_op jit(solution)/shard_map/ppermute | solution.py:109
  5.8 1.7 %collective-permute-done.1.second_ref.second_x = f32[4,16,128]{2,1,0:T(8,128)S(1)} collective-permute-done((f32[4,16,128]{2,1,0:T(8,128)S(1)}, f32[4,16,128]{2,1,0:T(8,128)S(1)}, u32[]{:S(2)}, u32[]{:S(2)}) %collective-permute-start.1) | collective-permute-done | bytes 32800 | tf_op jit(solution)/shard_map/ppermute | solution.py:109
  7.5 0.2 shard_map.123
  7.7 0.0 copy-start.9
  7.7 0.0 copy-start.10
  7.7 1.7 %collective-permute-start.2 = (f32[4,40,128]{2,1,0:T(8,128)S(1)}, f32[4,40,128]{2,1,0:T(8,128)S(1)}, u32[]{:S(2)}, u32[]{:S(2)}) collective-permute-start(f32[4,40,128]{2,1,0:T(8,128)S(1)} %get-tuple-element.36), channel_id=1, source_target_pairs={{0,1},{1,0},{2,3},{3,2},{4,5},{5,4},{6,7},{7,6},{8,9},{9,8},{10,11... | collective-permute-start | bytes 245768 | tf_op jit(solution)/shard_map/ppermute | solution.py:112
  9.4 0.2 collective-permute-start.3
  9.6 1.4 %shard_map.124.inverse_ref = f32[4,336,144]{2,1,0:T(8,128)S(1)} custom-call(f32[2,8]{1,0:T(2,128)S(1)} %copy-done.6, f32[2,8]{1,0:T(2,128)S(1)} %copy-done.7, s32[32,16,128]{2,1,0:T(8,128)S(1)} %copy-done.3, f32[336,144]{1,0:T(8,128)S(1)} %copy-done.4, f32[128,144]{1,0:T(8,128)S(1)} %copy-done.5), custom_call_target="tpu_custom_call" | custom-call | flops 40000000 | bytes 1303552 | tf_op jit(solution)/shard_map/pallas_call | solution.py:637
  11.0 2.4 %collective-permute-done.2.first_y = f32[4,40,128]{2,1,0:T(8,128)S(1)} collective-permute-done((f32[4,40,128]{2,1,0:T(8,128)S(1)}, f32[4,40,128]{2,1,0:T(8,128)S(1)}, u32[]{:S(2)}, u32[]{:S(2)}) %collective-permute-start.2) | collective-permute-done | bytes 81952 | tf_op jit(solution)/shard_map/ppermute | solution.py:112
  13.5 2.9 %shard_map.125 = (f32[2,34,16,128]{3,2,1,0:T(8,128)S(1)}, f32[2,2,40,128]{3,2,1,0:T(8,128)S(1)}, f32[2,3,24,128]{3,2,1,0:T(8,128)S(1)}, f32[2,3,24,128]{3,2,1,0:T(8,128)S(1)}) custom-call(f32[2,32,16,128]{3,2,1,0:T(8,128)S(1)} %copy-done.1, f32[4,16,128]{2,1,0:T(8,128)S(1)} %collective-permute-done.first_ref.first_x, ...), custom_call_target="tpu_custom_call" | custom-call | flops 3000000000 | bytes 3853312 | tf_op jit(solution)/shard_map/pallas_call | solution.py:637
  16.4 0.1 collective-permute-start.4
  16.4 1.7 %collective-permute-start.5 = (f32[2,3,24,128]{3,2,1,0:T(8,128)S(1)}, f32[2,3,24,128]{3,2,1,0:T(8,128)S(1)}, u32[]{:S(2)}, u32[]{:S(2)}) collective-permute-start(f32[2,3,24,128]{3,2,1,0:T(8,128)S(1)} %get-tuple-element.41), channel_id=1, source_target_pairs={{0,24},{1,25},{2,26},{3,27},{4,28},{5,29},{6,30},{7,31},{8,16},{9,... | collective-permute-start | bytes 221192 | tf_op jit(solution)/shard_map/ppermute | solution.py:109
  18.1 2.4 %collective-permute-done.5.second_ref = f32[2,3,24,128]{3,2,1,0:T(8,128)S(1)} collective-permute-done((f32[2,3,24,128]{3,2,1,0:T(8,128)S(1)}, f32[2,3,24,128]{3,2,1,0:T(8,128)S(1)}, u32[]{:S(2)}, u32[]{:S(2)}) %collective-permute-start.5) | collective-permute-done | bytes 73760 | tf_op jit(solution)/shard_map/ppermute | solution.py:109
  20.5 0.2 shard_map.126
  20.7 2.6 %collective-permute-start.6 = (f32[2,3,40,128]{3,2,1,0:T(8,128)S(1)}, f32[2,3,40,128]{3,2,1,0:T(8,128)S(1)}, u32[]{:S(2)}, u32[]{:S(2)}) collective-permute-start(f32[2,3,40,128]{3,2,1,0:T(8,128)S(1)} %get-tuple-element.44), channel_id=1, source_target_pairs={{0,1},{1,0},{2,3},{3,2},{4,5},{5,4},{6,7},{7,6},{8,9},{9,8},{10,11... | collective-permute-start | bytes 368648 | tf_op jit(solution)/shard_map/ppermute | solution.py:112
  23.3 0.1 collective-permute-start.7
  23.4 1.6 %shard_map.127 = (f32[2,36,32,128]{3,2,1,0:T(8,128)S(1)}, f32[3,34,16,128]{3,2,1,0:T(8,128)S(1)}, f32[2,2,34,16,128]{4,3,2,1,0:T(8,128)S(1)}, f32[2,6,40,128]{3,...) custom-call(f32[2,8]{1,0:T(2,128)S(1)} %copy-done.6, f32[2,8]{1,0:T(2,128)S(1)} %copy-done.7, ...), custom_call_target="tpu_custom_call" | custom-call | flops 20000000 | bytes 4153344 | tf_op jit(solution)/shard_map/pallas_call | solution.py:637
  25.0 4.0 %collective-permute-done.6.first_ref = f32[2,3,40,128]{3,2,1,0:T(8,128)S(1)} collective-permute-done((f32[2,3,40,128]{3,2,1,0:T(8,128)S(1)}, f32[2,3,40,128]{3,2,1,0:T(8,128)S(1)}, u32[]{:S(2)}, u32[]{:S(2)}) %collective-permute-start.6) | collective-permute-done | bytes 122912 | tf_op jit(solution)/shard_map/ppermute | solution.py:112
  29.0 3.9 %shard_map.128 = (f32[2,32,16,128]{3,2,1,0:T(8,128)S(1)}, f32[2,32,16,128]{3,2,1,0:T(8,128)S(1)}, f32[8,128]{1,0:T(8,128)S(1)}, f32[2,34,16,128]{3,2,1,0:T(8,128...) custom-call(f32[2,36,16,128]{3,2,1,0:T(8,128)S(1)} %get-tuple-element.42.whole_re, ...), custom_call_target="tpu_custom_call" | custom-call | flops 3000000000 | bytes 9206784 | tf_op jit(solution)/shard_map/pallas_call | solution.py:637
  32.9 0.1 collective-permute-start.8
  33.0 1.6 %collective-permute-start.9 = (f32[2,2,24,128]{3,2,1,0:T(8,128)S(1)}, f32[2,2,24,128]{3,2,1,0:T(8,128)S(1)}, u32[]{:S(2)}, u32[]{:S(2)}) collective-permute-start(f32[2,2,24,128]{3,2,1,0:T(8,128)S(1)} %get-tuple-element.55), channel_id=1, source_target_pairs={{0,24},{1,25},{2,26},{3,27},{4,28},{5,29},{6,30},{7,31},{8,16},{9,... | collective-permute-start | bytes 147464 | tf_op jit(solution)/shard_map/ppermute | solution.py:109
  34.7 1.9 %collective-permute-done.9.second_ref = f32[2,2,24,128]{3,2,1,0:T(8,128)S(1)} collective-permute-done((f32[2,2,24,128]{3,2,1,0:T(8,128)S(1)}, f32[2,2,24,128]{3,2,1,0:T(8,128)S(1)}, u32[]{:S(2)}, u32[]{:S(2)}) %collective-permute-start.9) | collective-permute-done | bytes 49184 | tf_op jit(solution)/shard_map/ppermute | solution.py:109
  36.6 0.1 shard_map.129
  36.7 2.5 %collective-permute-start.10 = (f32[2,72,128]{2,1,0:T(8,128)S(1)}, f32[2,72,128]{2,1,0:T(8,128)S(1)}, u32[]{:S(2)}, u32[]{:S(2)}) collective-permute-start(f32[2,72,128]{2,1,0:T(8,128)S(1)} %get-tuple-element.58), channel_id=1, source_target_pairs={{0,1},{1,0},{2,3},{3,2},{4,5},{5,4},{6,7},{7,6},{8,9},{9,8},{10,11... | collective-permute-start | bytes 221192 | tf_op jit(solution)/shard_map/ppermute | solution.py:112
  39.3 0.2 collective-permute-start.11
  39.4 3.6 %collective-permute-done.10.first_ref = f32[2,72,128]{2,1,0:T(8,128)S(1)} collective-permute-done((f32[2,72,128]{2,1,0:T(8,128)S(1)}, f32[2,72,128]{2,1,0:T(8,128)S(1)}, u32[]{:S(2)}, u32[]{:S(2)}) %collective-permute-start.10) | collective-permute-done | bytes 73760 | tf_op jit(solution)/shard_map/ppermute | solution.py:112
  43.0 1.0 %shard_map.130 = (f32[2,32,16,128]{3,2,1,0:T(8,128)S(1)}, f32[2,32,16,128]{3,2,1,0:T(8,128)S(1)}, f32[32,128]{1,0:T(8,128)S(1)}) custom-call(f32[2,36,16,128]{3,2,1,0:T(8,128)S(1)} %get-tuple-element.56.whole_ref, f32[2,2,40,128]{3,2,1,0:T(8,128)S(1)} %get-tuple-element.57.whole_rows_ref, f32[2,72,128]{2,1,0:T(8,128)S(1)} %collective-permute-done.10.first_ref, ...), custom_call_target="tpu_custom_call" | custom-call | flops 10000000 | bytes 5541888 | tf_op jit(solution)/shard_map/pallas_call | solution.py:637
  44.0 13.2 %all_to_all.11 = f32[32,1,128]{2,1,0:T(1,128)S(1)} all-to-all(f32[32,1,128]{2,1,0:T(1,128)S(1)} %bitcast.5), channel_id=1, replica_groups=mesh['gx'=4,'gy'=8] {'gx','gy'}, dimensions={0} | all-to-all | bytes 32768 | tf_op jit(solution)/shard_map/all_to_all | solution.py:730
  57.2 1.3 %shard_map.131 = (f32[2,32,16,128]{3,2,1,0:T(8,128)}, f32[2,32,16,128]{3,2,1,0:T(8,128)}) custom-call(f32[32,128]{1,0:T(8,128)S(1)} %bitcast.4, f32[2,32,16,128]{3,2,1,0:T(8,128)S(1)} %copy-done.1, f32[2,32,16,128]{3,2,1,0:T(8,128)S(1)} %get-tuple-element.63.z_ref, f32[2,32,16,128]{3,2,1,0:T(8,128)S(1)} %get-tuple-element.60.old_image_ref.q_ref, ...), custom_call_target="tpu_custom_call" | custom-call | bytes 3686400 | tf_op jit(solution)/shard_map/pallas_call | solution.py:637
  (29 shorter events, 0.1 us)
Async XLA Ops:
  0.6 1.0 %copy-start = (f32[2,32,16,128]{3,2,1,0:T(8,128)S(1)}, f32[2,32,16,128]{3,2,1,0:T(8,128)}, u32[]{:S(2)}) copy-start(f32[2,32,16,128]{3,2,1,0:T(8,128)} %load_ref.9) | copy-start | bytes 1572868
  1.7 0.9 %copy-start.2 = (s32[32,16,128]{2,1,0:T(8,128)S(1)}, s32[32,16,128]{2,1,0:T(8,128)}, u32[]{:S(2)}) copy-start(s32[32,16,128]{2,1,0:T(8,128)} %zones_ref.7) | copy-start | bytes 786436
  2.6 6.9 %copy-start.3 = (s32[32,16,128]{2,1,0:T(8,128)S(1)}, s32[32,16,128]{2,1,0:T(8,128)}, u32[]{:S(2)}) copy-start(s32[32,16,128]{2,1,0:T(8,128)} %zones_ref.7) | copy-start | bytes 786436
  2.6 6.9 %copy-start.4 = (f32[336,144]{1,0:T(8,128)S(1)}, f32[336,144]{1,0:T(8,128)}, u32[]{:S(2)}) copy-start(f32[336,144]{1,0:T(8,128)} %constant.16.clone.summed_ref) | copy-start | bytes 580612
  2.6 6.9 %copy-start.5 = (f32[128,144]{1,0:T(8,128)S(1)}, f32[128,144]{1,0:T(8,128)}, u32[]{:S(2)}) copy-start(f32[128,144]{1,0:T(8,128)} %constant.17.clone.means_ref) | copy-start | bytes 221188
  2.6 6.9 %copy-start.6 = (f32[2,8]{1,0:T(2,128)S(1)}, f32[2,8]{1,0:T(2,128)}, u32[]{:S(2)}) copy-start(f32[2,8]{1,0:T(2,128)} %conductance_ref.3) | copy-start | bytes 196
  2.6 6.9 %copy-start.7 = (f32[2,8]{1,0:T(2,128)S(1)}, f32[2,8]{1,0:T(2,128)}, u32[]{:S(2)}) copy-start(f32[2,8]{1,0:T(2,128)} %capacity_ref.3) | copy-start | bytes 196
  2.7 3.2 %collective-permute-start = (f32[4,16,128]{2,1,0:T(8,128)S(1)}, f32[4,16,128]{2,1,0:T(8,128)S(1)}, u32[]{:S(2)}, u32[]{:S(2)}) collective-permute-start(f32[4,16,128]{2,1,0:T(8,128)S(1)} %get-tuple-element.34), channel_id=1, source_target_pairs={{0,8},{1,9},{2,10},{3,11},{4,12},{5,13},{6,14},{7,15},{8,0},{9,1},... | collective-permute-start | bytes 98312 | tf_op jit(solution)/shard_map/ppermute | solution.py:108
  3.2 4.3 %collective-permute-start.1 = (f32[4,16,128]{2,1,0:T(8,128)S(1)}, f32[4,16,128]{2,1,0:T(8,128)S(1)}, u32[]{:S(2)}, u32[]{:S(2)}) collective-permute-start(f32[4,16,128]{2,1,0:T(8,128)S(1)} %get-tuple-element.35), channel_id=1, source_target_pairs={{0,24},{1,25},{2,26},{3,27},{4,28},{5,29},{6,30},{7,31},{8,16},{9,... | collective-permute-start | bytes 98312 | tf_op jit(solution)/shard_map/ppermute | solution.py:109
  7.5 5.9 %copy-start.12 = (bf16[144,256]{1,0:T(8,128)(2,1)S(1)}, bf16[144,256]{1,0:T(8,128)(2,1)}, u32[]{:S(2)}) copy-start(bf16[144,256]{1,0:T(8,128)(2,1)} %constant.15.clone.c3) | copy-start | bytes 221188
  7.7 5.8 %copy-start.1 = (f32[2,32,16,128]{3,2,1,0:T(8,128)S(1)}, f32[2,32,16,128]{3,2,1,0:T(8,128)}, u32[]{:S(2)}) copy-start(f32[2,32,16,128]{3,2,1,0:T(8,128)} %load_ref.9) | copy-start | bytes 1572868
  7.7 5.8 %copy-start.9 = (bf16[336,1008]{1,0:T(8,128)(2,1)S(1)}, bf16[336,1008]{1,0:T(8,128)(2,1)}, u32[]{:S(2)}) copy-start(bf16[336,1008]{1,0:T(8,128)(2,1)} %constant.13.clone.c1) | copy-start | bytes 2032132
  7.7 5.8 %copy-start.10 = (bf16[336,1008]{1,0:T(8,128)(2,1)S(1)}, bf16[336,1008]{1,0:T(8,128)(2,1)}, u32[]{:S(2)}) copy-start(bf16[336,1008]{1,0:T(8,128)(2,1)} %constant.12.clone.c0) | copy-start | bytes 2032132
  7.7 5.8 %copy-start.11 = (bf16[384,144]{1,0:T(8,128)(2,1)S(1)}, bf16[384,144]{1,0:T(8,128)(2,1)}, u32[]{:S(2)}) copy-start(bf16[384,144]{1,0:T(8,128)(2,1)} %constant.14.clone.c2) | copy-start | bytes 331780
  7.7 5.7 %collective-permute-start.2 = (f32[4,40,128]{2,1,0:T(8,128)S(1)}, f32[4,40,128]{2,1,0:T(8,128)S(1)}, u32[]{:S(2)}, u32[]{:S(2)}) collective-permute-start(f32[4,40,128]{2,1,0:T(8,128)S(1)} %get-tuple-element.36), channel_id=1, source_target_pairs={{0,1},{1,0},{2,3},{3,2},{4,5},{5,4},{6,7},{7,6},{8,9},{9,8},{10,11... | collective-permute-start | bytes 245768 | tf_op jit(solution)/shard_map/ppermute | solution.py:112
  9.4 4.1 %collective-permute-start.3 = (f32[4,40,128]{2,1,0:T(8,128)S(1)}, f32[4,40,128]{2,1,0:T(8,128)S(1)}, u32[]{:S(2)}, u32[]{:S(2)}) collective-permute-start(f32[4,40,128]{2,1,0:T(8,128)S(1)} %get-tuple-element.37), channel_id=1, source_target_pairs={{0,8},{1,2},{2,1},{3,4},{4,3},{5,6},{6,5},{7,15},{8,0},{9,10},{10,... | collective-permute-start | bytes 245768 | tf_op jit(solution)/shard_map/ppermute | solution.py:111
  11.0 12.3 %copy-start.8 = (f32[8]{0:T(128)S(1)}, f32[8]{0:T(128)}, u32[]{:S(2)}) copy-start(f32[8]{0:T(128)} %coupling_ref.1) | copy-start | bytes 100
  16.4 1.7 %collective-permute-start.4 = (f32[2,3,24,128]{3,2,1,0:T(8,128)S(1)}, f32[2,3,24,128]{3,2,1,0:T(8,128)S(1)}, u32[]{:S(2)}, u32[]{:S(2)}) collective-permute-start(f32[2,3,24,128]{3,2,1,0:T(8,128)S(1)} %get-tuple-element.40), channel_id=1, source_target_pairs={{0,8},{1,9},{2,10},{3,11},{4,12},{5,13},{6,14},{7,15},{8,0},{9,1},... | collective-permute-start | bytes 221192 | tf_op jit(solution)/shard_map/ppermute | solution.py:108
  16.4 4.1 %collective-permute-start.5 = (f32[2,3,24,128]{3,2,1,0:T(8,128)S(1)}, f32[2,3,24,128]{3,2,1,0:T(8,128)S(1)}, u32[]{:S(2)}, u32[]{:S(2)}) collective-permute-start(f32[2,3,24,128]{3,2,1,0:T(8,128)S(1)} %get-tuple-element.41), channel_id=1, source_target_pairs={{0,24},{1,25},{2,26},{3,27},{4,28},{5,29},{6,30},{7,31},{8,16},{9,... | collective-permute-start | bytes 221192 | tf_op jit(solution)/shard_map/ppermute | solution.py:109
  20.7 8.3 %collective-permute-start.6 = (f32[2,3,40,128]{3,2,1,0:T(8,128)S(1)}, f32[2,3,40,128]{3,2,1,0:T(8,128)S(1)}, u32[]{:S(2)}, u32[]{:S(2)}) collective-permute-start(f32[2,3,40,128]{3,2,1,0:T(8,128)S(1)} %get-tuple-element.44), channel_id=1, source_target_pairs={{0,1},{1,0},{2,3},{3,2},{4,5},{5,4},{6,7},{7,6},{8,9},{9,8},{10,11... | collective-permute-start | bytes 368648 | tf_op jit(solution)/shard_map/ppermute | solution.py:112
  23.3 5.7 %collective-permute-start.7 = (f32[2,3,40,128]{3,2,1,0:T(8,128)S(1)}, f32[2,3,40,128]{3,2,1,0:T(8,128)S(1)}, u32[]{:S(2)}, u32[]{:S(2)}) collective-permute-start(f32[2,3,40,128]{3,2,1,0:T(8,128)S(1)} %get-tuple-element.45), channel_id=1, source_target_pairs={{0,8},{1,2},{2,1},{3,4},{4,3},{5,6},{6,5},{7,15},{8,0},{9,10},{10,... | collective-permute-start | bytes 368648 | tf_op jit(solution)/shard_map/ppermute | solution.py:111
  32.9 1.7 %collective-permute-start.8 = (f32[2,2,24,128]{3,2,1,0:T(8,128)S(1)}, f32[2,2,24,128]{3,2,1,0:T(8,128)S(1)}, u32[]{:S(2)}, u32[]{:S(2)}) collective-permute-start(f32[2,2,24,128]{3,2,1,0:T(8,128)S(1)} %get-tuple-element.54), channel_id=1, source_target_pairs={{0,8},{1,9},{2,10},{3,11},{4,12},{5,13},{6,14},{7,15},{8,0},{9,1},... | collective-permute-start | bytes 147464 | tf_op jit(solution)/shard_map/ppermute | solution.py:108
  33.0 3.6 %collective-permute-start.9 = (f32[2,2,24,128]{3,2,1,0:T(8,128)S(1)}, f32[2,2,24,128]{3,2,1,0:T(8,128)S(1)}, u32[]{:S(2)}, u32[]{:S(2)}) collective-permute-start(f32[2,2,24,128]{3,2,1,0:T(8,128)S(1)} %get-tuple-element.55), channel_id=1, source_target_pairs={{0,24},{1,25},{2,26},{3,27},{4,28},{5,29},{6,30},{7,31},{8,16},{9,... | collective-permute-start | bytes 147464 | tf_op jit(solution)/shard_map/ppermute | solution.py:109
  36.7 6.3 %collective-permute-start.10 = (f32[2,72,128]{2,1,0:T(8,128)S(1)}, f32[2,72,128]{2,1,0:T(8,128)S(1)}, u32[]{:S(2)}, u32[]{:S(2)}) collective-permute-start(f32[2,72,128]{2,1,0:T(8,128)S(1)} %get-tuple-element.58), channel_id=1, source_target_pairs={{0,1},{1,0},{2,3},{3,2},{4,5},{5,4},{6,7},{7,6},{8,9},{9,8},{10,11... | collective-permute-start | bytes 221192 | tf_op jit(solution)/shard_map/ppermute | solution.py:112
  39.3 3.8 %collective-permute-start.11 = (f32[2,72,128]{2,1,0:T(8,128)S(1)}, f32[2,72,128]{2,1,0:T(8,128)S(1)}, u32[]{:S(2)}, u32[]{:S(2)}) collective-permute-start(f32[2,72,128]{2,1,0:T(8,128)S(1)} %get-tuple-element.59), channel_id=1, source_target_pairs={{0,8},{1,2},{2,1},{3,4},{4,3},{5,6},{6,5},{7,15},{8,0},{9,10},{10,... | collective-permute-start | bytes 221192 | tf_op jit(solution)/shard_map/ppermute | solution.py:111

commit v4 on v3

--- a/solution.py
+++ b/solution.py
@@ -147,54 +147,50 @@
     return jnp.dot(left, right, preferred_element_type=F32)
 
 
-def solve(field_ref, rows_ref, inverse_ref, consts, stack_ref, out_ref, out_rows_ref):
+def store_split(stack_ref, lanes, value):
+    rows = value.shape[0]
+    high, low = halves(value)
+    stack_ref[0:rows, lanes] = high
+    stack_ref[rows : 2 * rows, lanes] = low
+    stack_ref[2 * rows : 3 * rows, lanes] = high
+
+
+def solve(field_ref, rows_ref, inverse_ref, consts, before_ref, after_ref, out_ref, out_rows_ref):
     forward_ref, back_ref, line_forward_ref, line_back_ref = consts
     boxes = (field_ref.shape[1] - 2) // BOX
     size_y, size_z = field_ref.shape[2:]
     inner = SPAN * size_y
-    rows = inner + 48
     line_rows = line_forward_ref.shape[0] // 3
+    lanes = [slice(box * size_z, (box + 1) * size_z) for box in range(boxes)]
     for field in range(2):
         for box in range(boxes):
             start = box * BOX
             main = field_ref[field, start : start + SPAN].reshape(inner, size_z)
-            lanes = slice(box * size_z, (box + 1) * size_z)
-            parts = (
-                (0, main),
-                (inner, rows_ref[field, 0, start : start + 24]),
-                (inner + 24, rows_ref[field, 1, start : start + 24]),
-            )
-            whole = jnp.concatenate([part for _, part in parts], axis=0)
-            high, low = halves(whole)
-            stack_ref[0:rows, lanes] = high
-            stack_ref[rows : 2 * rows, lanes] = low
-            stack_ref[2 * rows : 3 * rows, lanes] = high
-        spectral = dot(forward_ref[...], stack_ref[...])
+            strips = [rows_ref[field, side, start : start + 24] for side in range(2)]
+            store_split(before_ref.at[field], lanes[box], jnp.concatenate([main, *strips], axis=0))
+    spectral = [dot(forward_ref[...], before_ref[field]) for field in range(2)]
+    for field in range(2):
         for box in range(boxes):
-            lanes = slice(box * size_z, (box + 1) * size_z)
-            high, low = halves(spectral[:, lanes])
+            high, low = halves(spectral[field][:, lanes[box]])
             both = jnp.concatenate([high, low], axis=1)
             modes = dot(both, line_forward_ref[0 : 2 * line_rows]) + dot(high, line_forward_ref[2 * line_rows :])
             modes = modes * inverse_ref[field * boxes + box]
             high, low = halves(modes)
             cells = dot(high, line_back_ref[...])
             cells = cells[:, :size_z] + (cells[:, size_z:] + dot(low, line_back_ref[:, :size_z]))
-            high, low = halves(cells)
-            stack_ref[0:rows, lanes] = high
-            stack_ref[rows : 2 * rows, lanes] = low
-            stack_ref[2 * rows : 3 * rows, lanes] = high
-        result = dot(back_ref[...], stack_ref[...])
+            store_split(after_ref.at[field], lanes[box], cells)
+    for field in range(2):
+        result = dot(back_ref[...], after_ref[field])
         for box in range(boxes):
-            lanes = slice(box * size_z, (box + 1) * size_z)
             start = box * BOX
-            main = result[:inner, lanes].reshape(SPAN, size_y, size_z)
+            main = result[:inner, lanes[box]].reshape(SPAN, size_y, size_z)
             if box == 0:
                 out_ref[field, 0:SPAN] = main
             else:
                 out_ref[field, start : start + 2] = out_ref[field, start : start + 2] + main[0:2]
                 out_ref[field, start + 2 : start + SPAN] = main[2:]
             for side in range(2):
-                strip = result[inner + 24 * side : inner + 24 * side + 24, lanes]
+                strip = result[inner + 24 * side : inner + 24 * side + 24, lanes[box]]
                 if box == 0:
                     out_rows_ref[field, side, 0:24] = strip
                 else:
@@ -249,10 +245,19 @@
         inverse_ref[combo] = 1.0 / (cbar + kbar * summed_ref[...])
 
 
-def edge_layers_kernel(mesh, load_ref, zones_ref, even_ref, odd_ref):
+def edge_layers_kernel(mesh, load_hbm, zones_hbm, load_ref, zones_ref, even_ref, odd_ref, sems):
+    copies = [
+        pltpu.make_async_copy(load_hbm.at[0], load_ref.at[0], sems.at[0]),
+        pltpu.make_async_copy(load_hbm.at[1], load_ref.at[1], sems.at[1]),
+        pltpu.make_async_copy(zones_hbm, zones_ref, sems.at[2]),
+    ]
+    for copy in copies:
+        copy.start()
     flags = standing(mesh)
     last = zones_ref.shape[0] - 1
     for channel in range(4):
+        if channel < 3:
+            copies[channel].wait()
         if channel < 2:
             low, high = load_ref[channel, 0], load_ref[channel, last]
         else:
@@ -267,8 +272,8 @@
     from_low = chosen(flags, EVEN_X, second_ref[...], first_ref[...])
     from_high = chosen(flags, EVEN_X, first_ref[...], second_ref[...])
     blank = jnp.zeros((8, size_z), F32)
-    for channel in range(4):
-        for ref in (even_ref, odd_ref):
+    for ref in (even_ref, odd_ref):
+        for channel in range(4):
             ref[channel, 0:8] = blank
             ref[channel, size_x : size_x + 8] = blank
 
@@ -377,7 +382,7 @@
 
 def first_solve_kernel(
     mesh, load_ref, first_x, second_x, first_y, second_y, inverse_ref, c0, c1, c2, c3,
-    part_ref, part_rows_ref, even_ref, odd_ref, field_ref, rows_ref, stack_ref,
+    part_ref, part_rows_ref, even_ref, odd_ref, field_ref, rows_ref, before_ref, after_ref,
 ):
     flags = standing(mesh)
     size_x = load_ref.shape[1]
@@ -387,7 +392,7 @@
         field_ref[field, 1 + size_x] = keep(flags, HIGH_X, chosen(flags, EVEN_X, first_x[field], second_x[field]))
         rows_ref[field, 0] = keep(flags, LOW_Y, chosen(flags, EVEN_Y, second_y[field], first_y[field]))
         rows_ref[field, 1] = keep(flags, HIGH_Y, chosen(flags, EVEN_Y, first_y[field], second_y[field]))
-    solve(field_ref, rows_ref, inverse_ref, (c0, c1, c2, c3), stack_ref, part_ref, part_rows_ref)
+    solve(field_ref, rows_ref, inverse_ref, (c0, c1, c2, c3), before_ref, after_ref, part_ref, part_rows_ref)
     pack_x(flags, part_ref, part_rows_ref, even_ref, odd_ref)
 
 
@@ -533,7 +538,7 @@
     mesh, whole_ref, whole_rows_ref, first_ref, second_ref,
     half_ref, mass_ref, face_ref, half_lines, mass_lines, face_lines, load_ref, inverse_ref, c0, c1, c2, c3,
     precond_ref, image_ref, sums_ref, part_ref, part_rows_ref, even_ref, odd_ref,
-    value_ref, lines, near, field_ref, rows_ref, stack_ref,
+    value_ref, lines, near, field_ref, rows_ref, before_ref, after_ref,
 ):
     flags = standing(mesh)
     size_x, size_y, size_z = load_ref.shape[1:]
@@ -568,7 +573,7 @@
         images = operate_line(lines, half_lines, mass_lines, face_lines, side, near)
         for field in range(2):
             rows_ref[field, side] = keep(flags, flag, jnp.where(valid, images[field], 0.0))
-    solve(field_ref, rows_ref, inverse_ref, (c0, c1, c2, c3), stack_ref, part_ref, part_rows_ref)
+    solve(field_ref, rows_ref, inverse_ref, (c0, c1, c2, c3), before_ref, after_ref, part_ref, part_rows_ref)
     pack_x(flags, part_ref, part_rows_ref, even_ref, odd_ref)
 
 
@@ -611,7 +616,9 @@
     sums_ref[...] = spread
 
 
-def finish_kernel(sums_ref, load_ref, z_ref, q_ref, w_ref, s_ref, solution_ref, residual_ref):
+def finish_kernel(
+    sums_ref, load_ref, z_ref, q_ref, w_ref, s_ref, solution_hbm, residual_hbm, solution_ref, residual_ref, sems
+):
     line = jnp.sum(sums_ref[...], axis=0, keepdims=True)
     lane = lax.broadcasted_iota(jnp.int32, line.shape, 1)
     rz, zq, qw, ws = [jnp.sum(jnp.where(lane == place, line, 0.0), axis=1, keepdims=True) for place in range(4)]
@@ -622,23 +629,35 @@
     alpha_next = rz_next / curvature
     along = alpha + alpha_next * grown
     against = alpha_next * alpha
-    for field in range(2):
-        for x in range(load_ref.shape[1]):
-            solution_ref[field, x] = along * z_ref[field, x] - against * w_ref[field, x]
-            residual_ref[field, x] = load_ref[field, x] - along * q_ref[field, x] + against * s_ref[field, x]
+    copies = []
+    step = load_ref.shape[1] // 2
+    for field in range(2):
+        for start in range(0, 2 * step, step):
+            part = pl.ds(start, step)
+            for x in range(start, start + step):
+                solution_ref[field, x] = along * z_ref[field, x] - against * w_ref[field, x]
+                residual_ref[field, x] = load_ref[field, x] - along * q_ref[field, x] + against * s_ref[field, x]
+            for here, there in ((solution_ref, solution_hbm), (residual_ref, residual_hbm)):
+                copies.append(
+                    pltpu.make_async_copy(here.at[field, part], there.at[field, part], sems.at[len(copies)])
+                )
+                copies[-1].start()
+    for copy in copies:
+        copy.wait()
 
 
 SMEM = pl.BlockSpec(memory_space=pltpu.SMEM)
 VMEM = pl.BlockSpec(memory_space=pltpu.VMEM)
-
-
-def call(mesh, kernel, scalars, arrays, outs, scratch=(), flops=0, limit=24):
+HBM = pl.BlockSpec(memory_space=pltpu.HBM)
+
+
+def call(mesh, kernel, scalars, arrays, outs, scratch=(), flops=0, limit=24, in_hbm=False, outs_in_hbm=False):
     moved = sum(math.prod(a.shape) * a.dtype.itemsize for a in list(arrays) + list(outs))
     return pl.pallas_call(
         kernel if mesh is None else functools.partial(kernel, mesh),
         out_shape=tuple(outs),
-        in_specs=[SMEM] * len(scalars) + [VMEM] * len(arrays),
-        out_specs=tuple([VMEM] * len(outs)),
+        in_specs=[SMEM] * len(scalars) + [HBM if in_hbm else VMEM] * len(arrays),
+        out_specs=tuple([HBM if outs_in_hbm else VMEM] * len(outs)),
         scratch_shapes=list(scratch),
         compiler_params=pltpu.CompilerParams(vmem_limit_bytes=limit * 1024 * 1024),
         cost_estimate=pl.CostEstimate(flops=flops, bytes_accessed=moved, transcendentals=0),
@@ -654,8 +673,14 @@
     forward, back, line_forward, line_back, summed, means = [jnp.asarray(c) for c in constants(size_z)]
     consts = (forward, back, line_forward, line_back)
     modes, lanes = summed.shape
-    packed = call(
-        mesh, edge_layers_kernel, [], [load, zones], [sds(4, size_y, size_z)] * 2
+    load, zones, *packed = call(
+        mesh,
+        edge_layers_kernel,
+        [],
+        [load, zones],
+        [sds(*load.shape), jax.ShapeDtypeStruct(zones.shape, zones.dtype)] + [sds(4, size_y, size_z)] * 2,
+        [pltpu.SemaphoreType.DMA((3,))],
+        in_hbm=True,
     )
     x_halo = swap(mesh, "gx", *packed)
     (inverse,) = call(
@@ -691,7 +716,8 @@
     work = [
         pltpu.VMEM((2, size_x + 2, size_y, size_z), F32),
         pltpu.VMEM((2, 2, count, size_z), F32),
-        pltpu.VMEM((3 * rows, boxes * size_z), BF16),
+        pltpu.VMEM((2, 3 * rows, boxes * size_z), BF16),
+        pltpu.VMEM((2, 3 * rows, boxes * size_z), BF16),
     ]
     padded = [
         pltpu.VMEM((2, size_x + 4, size_y + 16, size_z), F32),
@@ -728,7 +754,16 @@
         10_000_000,
     )
     sums = lax.all_to_all(sums, AXES, 0, 0, tiled=True)
-    return call(None, finish_kernel, [], [sums, load, precond, image, last_precond, last_image], [own, own])
+    whole_block = pltpu.VMEM((2, size_x, size_y, size_z), F32)
+    return call(
+        None,
+        finish_kernel,
+        [],
+        [sums, load, precond, image, last_precond, last_image],
+        [own, own],
+        [whole_block, whole_block, pltpu.SemaphoreType.DMA((8,))],
+        outs_in_hbm=True,
+    )
 
 
 def solution(mesh):

time: 58.7 us -> 57.2 us (0.974)
  Pallas kernels: 12.6 us -> 11.1 us
    pallas_call x10, Pallas kernels: 12.6 us -> 11.1 us  [call(): pl.pallas_call(kernel if mesh is None else functools.partial(kernel, mesh...]
    unnamed x26 -> x22, local copies, waits for them, and re-layouts: 2.04 us -> 2.03 us
where the time goes in v4:
time: 57.2 us; the launch traced here: 57 us
  waiting for transfers between devices  16.1 us (28%)
  starting transfers between devices  13.8 us (24%)
  blocking collectives  13.1 us (23%)
  Pallas kernels  11.1 us (19%)
  local copies, waits for them, and re-layouts  2.03 us (4%)
  between operations  0.77 us (1%)
    all_to_all x1, blocking collectives, shards(): sums = lax.all_to_all(sums, AXES, 0, 0, tiled=True)  13.1 us
    pallas_call x10, Pallas kernels, call(): pl.pallas_call(kernel if mesh is None else functools.partial(kernel, mesh...  11.1 us
    ppermute x6, waiting for transfers between devices, swap(): first = lax.ppermute(even_part, AXES, swap_pairs(mesh, axis, False))  10.1 us
    ppermute x6, starting transfers between devices, swap(): first = lax.ppermute(even_part, AXES, swap_pairs(mesh, axis, False))  7.45 us
    ppermute x6, starting transfers between devices, swap(): second = lax.ppermute(odd_part, AXES, swap_pairs(mesh, axis, True))  6.36 us
    ppermute x6, waiting for transfers between devices, swap(): second = lax.ppermute(odd_part, AXES, swap_pairs(mesh, axis, True))  6.01 us
    unnamed x22, local copies, waits for them, and re-layouts  2.03 us
  transfers between devices with their start and end apart: 12, of which 6 were waited for; matrix products, arithmetic and copies ran while one was open for 0% of the time, Pallas kernels for 5%

profile of v4, /device:TPU:0, one launch (start us, length us, event | category | flops | bytes accessed | tf_op | source)
XLA Modules:
  0.0 57.0 jit_solution(2933915899664712924)
XLA Ops:
  0.6 1.0 %copy-done = f32[2,32,16,128]{3,2,1,0:T(8,128)S(1)} copy-done((f32[2,32,16,128]{3,2,1,0:T(8,128)S(1)}, f32[2,32,16,128]{3,2,1,0:T(8,128)}, u32[]{:S(2)}) %copy-start) | copy-done | bytes 524312
  1.7 0.9 %copy-done.2 = s32[32,16,128]{2,1,0:T(8,128)S(1)} copy-done((s32[32,16,128]{2,1,0:T(8,128)S(1)}, s32[32,16,128]{2,1,0:T(8,128)}, u32[]{:S(2)}) %copy-start.2) | copy-done | bytes 262168
  2.6 0.1 shard_map.122
  2.8 0.5 collective-permute-start
  3.3 2.6 %collective-permute-start.1 = (f32[4,16,128]{2,1,0:T(8,128)S(1)}, f32[4,16,128]{2,1,0:T(8,128)S(1)}, u32[]{:S(2)}, u32[]{:S(2)}) collective-permute-start(f32[4,16,128]{2,1,0:T(8,128)S(1)} %get-tuple-element.38), channel_id=1, source_target_pairs={{0,24},{1,25},{2,26},{3,27},{4,28},{5,29},{6,30},{7,31},{8,16},{9,... | collective-permute-start | bytes 98312 | tf_op jit(solution)/shard_map/ppermute | solution.py:109
  5.9 1.7 %collective-permute-done.1.second_ref.second_x = f32[4,16,128]{2,1,0:T(8,128)S(1)} collective-permute-done((f32[4,16,128]{2,1,0:T(8,128)S(1)}, f32[4,16,128]{2,1,0:T(8,128)S(1)}, u32[]{:S(2)}, u32[]{:S(2)}) %collective-permute-start.1) | collective-permute-done | bytes 32800 | tf_op jit(solution)/shard_map/ppermute | solution.py:109
  7.6 0.2 shard_map.123
  7.8 0.0 copy-start.8
  7.8 1.7 %collective-permute-start.2 = (f32[4,40,128]{2,1,0:T(8,128)S(1)}, f32[4,40,128]{2,1,0:T(8,128)S(1)}, u32[]{:S(2)}, u32[]{:S(2)}) collective-permute-start(f32[4,40,128]{2,1,0:T(8,128)S(1)} %get-tuple-element.40), channel_id=1, source_target_pairs={{0,1},{1,0},{2,3},{3,2},{4,5},{5,4},{6,7},{7,6},{8,9},{9,8},{10,11... | collective-permute-start | bytes 245768 | tf_op jit(solution)/shard_map/ppermute | solution.py:112
  9.5 0.2 collective-permute-start.3
  9.6 1.4 %shard_map.124.inverse_ref = f32[4,336,144]{2,1,0:T(8,128)S(1)} custom-call(f32[2,8]{1,0:T(2,128)S(1)} %copy-done.4, f32[2,8]{1,0:T(2,128)S(1)} %copy-done.5, s32[32,16,128]{2,1,0:T(8,128)S(1)} %get-tuple-element.39.zones_ref, f32[336,144]{1,0:T(8,128)S(1)} %copy-done.1, f32[128,144]{1,0:T(8,128)S(1)} %copy-done.3), custom_call_target="tpu_custom_call" | custom-call | flops 40000000 | bytes 1303552 | tf_op jit(solution)/shard_map/pallas_call | solution.py:656
  11.1 2.4 %collective-permute-done.2.first_y = f32[4,40,128]{2,1,0:T(8,128)S(1)} collective-permute-done((f32[4,40,128]{2,1,0:T(8,128)S(1)}, f32[4,40,128]{2,1,0:T(8,128)S(1)}, u32[]{:S(2)}, u32[]{:S(2)}) %collective-permute-start.2) | collective-permute-done | bytes 81952 | tf_op jit(solution)/shard_map/ppermute | solution.py:112
  13.6 2.1 %shard_map.125 = (f32[2,34,16,128]{3,2,1,0:T(8,128)S(1)}, f32[2,2,40,128]{3,2,1,0:T(8,128)S(1)}, f32[2,3,24,128]{3,2,1,0:T(8,128)S(1)}, f32[2,3,24,128]{3,2,1,0:T(8,128)S(1)}) custom-call(f32[2,32,16,128]{3,2,1,0:T(8,128)S(1)} %get-tuple-element.36.load_ref, f32[4,16,128]{2,1,0:T(8,128)S(1)} %collective-permute-done.first_ref.first_x, ...), custom_call_target="tpu_custom_call" | custom-call | flops 3000000000 | bytes 3853312 | tf_op jit(solution)/shard_map/pallas_call | solution.py:656
  15.7 0.1 collective-permute-start.4
  15.7 1.7 %collective-permute-start.5 = (f32[2,3,24,128]{3,2,1,0:T(8,128)S(1)}, f32[2,3,24,128]{3,2,1,0:T(8,128)S(1)}, u32[]{:S(2)}, u32[]{:S(2)}) collective-permute-start(f32[2,3,24,128]{3,2,1,0:T(8,128)S(1)} %get-tuple-element.45), channel_id=1, source_target_pairs={{0,24},{1,25},{2,26},{3,27},{4,28},{5,29},{6,30},{7,31},{8,16},{9,... | collective-permute-start | bytes 221192 | tf_op jit(solution)/shard_map/ppermute | solution.py:109
  17.4 2.4 %collective-permute-done.5.second_ref = f32[2,3,24,128]{3,2,1,0:T(8,128)S(1)} collective-permute-done((f32[2,3,24,128]{3,2,1,0:T(8,128)S(1)}, f32[2,3,24,128]{3,2,1,0:T(8,128)S(1)}, u32[]{:S(2)}, u32[]{:S(2)}) %collective-permute-start.5) | collective-permute-done | bytes 73760 | tf_op jit(solution)/shard_map/ppermute | solution.py:109
  19.8 0.2 shard_map.126
  20.0 2.6 %collective-permute-start.6 = (f32[2,3,40,128]{3,2,1,0:T(8,128)S(1)}, f32[2,3,40,128]{3,2,1,0:T(8,128)S(1)}, u32[]{:S(2)}, u32[]{:S(2)}) collective-permute-start(f32[2,3,40,128]{3,2,1,0:T(8,128)S(1)} %get-tuple-element.48), channel_id=1, source_target_pairs={{0,1},{1,0},{2,3},{3,2},{4,5},{5,4},{6,7},{7,6},{8,9},{9,8},{10,11... | collective-permute-start | bytes 368648 | tf_op jit(solution)/shard_map/ppermute | solution.py:112
  22.6 0.1 collective-permute-start.7
  22.7 1.6 %shard_map.127 = (f32[2,36,32,128]{3,2,1,0:T(8,128)S(1)}, f32[3,34,16,128]{3,2,1,0:T(8,128)S(1)}, f32[2,2,34,16,128]{4,3,2,1,0:T(8,128)S(1)}, f32[2,6,40,128]{3,...) custom-call(f32[2,8]{1,0:T(2,128)S(1)} %copy-done.4, f32[2,8]{1,0:T(2,128)S(1)} %copy-done.5, ...), custom_call_target="tpu_custom_call" | custom-call | flops 20000000 | bytes 4153344 | tf_op jit(solution)/shard_map/pallas_call | solution.py:656
  24.3 4.0 %collective-permute-done.6.first_ref = f32[2,3,40,128]{3,2,1,0:T(8,128)S(1)} collective-permute-done((f32[2,3,40,128]{3,2,1,0:T(8,128)S(1)}, f32[2,3,40,128]{3,2,1,0:T(8,128)S(1)}, u32[]{:S(2)}, u32[]{:S(2)}) %collective-permute-start.6) | collective-permute-done | bytes 122912 | tf_op jit(solution)/shard_map/ppermute | solution.py:112
  28.3 3.2 %shard_map.128 = (f32[2,32,16,128]{3,2,1,0:T(8,128)S(1)}, f32[2,32,16,128]{3,2,1,0:T(8,128)S(1)}, f32[8,128]{1,0:T(8,128)S(1)}, f32[2,34,16,128]{3,2,1,0:T(8,128...) custom-call(f32[2,36,16,128]{3,2,1,0:T(8,128)S(1)} %get-tuple-element.46.whole_re, ...), custom_call_target="tpu_custom_call" | custom-call | flops 3000000000 | bytes 9206784 | tf_op jit(solution)/shard_map/pallas_call | solution.py:656
  31.5 0.1 collective-permute-start.8
  31.6 1.6 %collective-permute-start.9 = (f32[2,2,24,128]{3,2,1,0:T(8,128)S(1)}, f32[2,2,24,128]{3,2,1,0:T(8,128)S(1)}, u32[]{:S(2)}, u32[]{:S(2)}) collective-permute-start(f32[2,2,24,128]{3,2,1,0:T(8,128)S(1)} %get-tuple-element.59), channel_id=1, source_target_pairs={{0,24},{1,25},{2,26},{3,27},{4,28},{5,29},{6,30},{7,31},{8,16},{9,... | collective-permute-start | bytes 147464 | tf_op jit(solution)/shard_map/ppermute | solution.py:109
  33.2 1.9 %collective-permute-done.9.second_ref = f32[2,2,24,128]{3,2,1,0:T(8,128)S(1)} collective-permute-done((f32[2,2,24,128]{3,2,1,0:T(8,128)S(1)}, f32[2,2,24,128]{3,2,1,0:T(8,128)S(1)}, u32[]{:S(2)}, u32[]{:S(2)}) %collective-permute-start.9) | collective-permute-done | bytes 49184 | tf_op jit(solution)/shard_map/ppermute | solution.py:109
  35.2 0.1 shard_map.129
  35.3 2.5 %collective-permute-start.10 = (f32[2,72,128]{2,1,0:T(8,128)S(1)}, f32[2,72,128]{2,1,0:T(8,128)S(1)}, u32[]{:S(2)}, u32[]{:S(2)}) collective-permute-start(f32[2,72,128]{2,1,0:T(8,128)S(1)} %get-tuple-element.62), channel_id=1, source_target_pairs={{0,1},{1,0},{2,3},{3,2},{4,5},{5,4},{6,7},{7,6},{8,9},{9,8},{10,11... | collective-permute-start | bytes 221192 | tf_op jit(solution)/shard_map/ppermute | solution.py:112
  37.9 0.2 collective-permute-start.11
  38.0 3.6 %collective-permute-done.10.first_ref = f32[2,72,128]{2,1,0:T(8,128)S(1)} collective-permute-done((f32[2,72,128]{2,1,0:T(8,128)S(1)}, f32[2,72,128]{2,1,0:T(8,128)S(1)}, u32[]{:S(2)}, u32[]{:S(2)}) %collective-permute-start.10) | collective-permute-done | bytes 73760 | tf_op jit(solution)/shard_map/ppermute | solution.py:112
  41.6 1.0 %shard_map.130 = (f32[2,32,16,128]{3,2,1,0:T(8,128)S(1)}, f32[2,32,16,128]{3,2,1,0:T(8,128)S(1)}, f32[32,128]{1,0:T(8,128)S(1)}) custom-call(f32[2,36,16,128]{3,2,1,0:T(8,128)S(1)} %get-tuple-element.60.whole_ref, f32[2,2,40,128]{3,2,1,0:T(8,128)S(1)} %get-tuple-element.61.whole_rows_ref, f32[2,72,128]{2,1,0:T(8,128)S(1)} %collective-permute-done.10.first_ref, ...), custom_call_target="tpu_custom_call" | custom-call | flops 10000000 | bytes 5541888 | tf_op jit(solution)/shard_map/pallas_call | solution.py:656
  42.6 13.1 %all_to_all.11 = f32[32,1,128]{2,1,0:T(1,128)S(1)} all-to-all(f32[32,1,128]{2,1,0:T(1,128)S(1)} %bitcast.5), channel_id=1, replica_groups=mesh['gx'=4,'gy'=8] {'gx','gy'}, dimensions={0} | all-to-all | bytes 32768 | tf_op jit(solution)/shard_map/all_to_all | solution.py:756
  55.8 1.2 %shard_map.131 = (f32[2,32,16,128]{3,2,1,0:T(8,128)}, f32[2,32,16,128]{3,2,1,0:T(8,128)}) custom-call(f32[32,128]{1,0:T(8,128)S(1)} %bitcast.4, f32[2,32,16,128]{3,2,1,0:T(8,128)S(1)} %get-tuple-element.36.load_ref, f32[2,32,16,128]{3,2,1,0:T(8,128)S(1)} %get-tuple-element.67.z_ref, f32[2,32,16,128]{3,2,1,0:T(8,128)S(1)} %get-tuple-element.64.old_image_ref.q_ref, ...), custom_call_target="tpu_custom_call" | custom-call | bytes 3686400 | tf_op jit(solution)/shard_map/pallas_call | solution.py:656
  (25 shorter events, 0.1 us)
Async XLA Ops:
  0.6 1.0 %copy-start = (f32[2,32,16,128]{3,2,1,0:T(8,128)S(1)}, f32[2,32,16,128]{3,2,1,0:T(8,128)}, u32[]{:S(2)}) copy-start(f32[2,32,16,128]{3,2,1,0:T(8,128)} %load_hbm.1) | copy-start | bytes 1572868
  1.7 0.9 %copy-start.2 = (s32[32,16,128]{2,1,0:T(8,128)S(1)}, s32[32,16,128]{2,1,0:T(8,128)}, u32[]{:S(2)}) copy-start(s32[32,16,128]{2,1,0:T(8,128)} %zones_hbm.1) | copy-start | bytes 786436
  2.6 7.0 %copy-start.1 = (f32[336,144]{1,0:T(8,128)S(1)}, f32[336,144]{1,0:T(8,128)}, u32[]{:S(2)}) copy-start(f32[336,144]{1,0:T(8,128)} %constant.16.clone.summed_ref) | copy-start | bytes 580612
  2.6 7.0 %copy-start.3 = (f32[128,144]{1,0:T(8,128)S(1)}, f32[128,144]{1,0:T(8,128)}, u32[]{:S(2)}) copy-start(f32[128,144]{1,0:T(8,128)} %constant.17.clone.means_ref) | copy-start | bytes 221188
  2.6 7.0 %copy-start.4 = (f32[2,8]{1,0:T(2,128)S(1)}, f32[2,8]{1,0:T(2,128)}, u32[]{:S(2)}) copy-start(f32[2,8]{1,0:T(2,128)} %conductance_ref.3) | copy-start | bytes 196
  2.6 7.0 %copy-start.5 = (f32[2,8]{1,0:T(2,128)S(1)}, f32[2,8]{1,0:T(2,128)}, u32[]{:S(2)}) copy-start(f32[2,8]{1,0:T(2,128)} %capacity_ref.3) | copy-start | bytes 196
  2.8 3.2 %collective-permute-start = (f32[4,16,128]{2,1,0:T(8,128)S(1)}, f32[4,16,128]{2,1,0:T(8,128)S(1)}, u32[]{:S(2)}, u32[]{:S(2)}) collective-permute-start(f32[4,16,128]{2,1,0:T(8,128)S(1)} %get-tuple-element.37), channel_id=1, source_target_pairs={{0,8},{1,9},{2,10},{3,11},{4,12},{5,13},{6,14},{7,15},{8,0},{9,1},... | collective-permute-start | bytes 98312 | tf_op jit(solution)/shard_map/ppermute | solution.py:108
  3.3 4.3 %collective-permute-start.1 = (f32[4,16,128]{2,1,0:T(8,128)S(1)}, f32[4,16,128]{2,1,0:T(8,128)S(1)}, u32[]{:S(2)}, u32[]{:S(2)}) collective-permute-start(f32[4,16,128]{2,1,0:T(8,128)S(1)} %get-tuple-element.38), channel_id=1, source_target_pairs={{0,24},{1,25},{2,26},{3,27},{4,28},{5,29},{6,30},{7,31},{8,16},{9,... | collective-permute-start | bytes 98312 | tf_op jit(solution)/shard_map/ppermute | solution.py:109
  7.7 5.8 %copy-start.7 = (bf16[336,1008]{1,0:T(8,128)(2,1)S(1)}, bf16[336,1008]{1,0:T(8,128)(2,1)}, u32[]{:S(2)}) copy-start(bf16[336,1008]{1,0:T(8,128)(2,1)} %constant.13.clone.c1) | copy-start | bytes 2032132
  7.8 5.8 %copy-start.8 = (bf16[336,1008]{1,0:T(8,128)(2,1)S(1)}, bf16[336,1008]{1,0:T(8,128)(2,1)}, u32[]{:S(2)}) copy-start(bf16[336,1008]{1,0:T(8,128)(2,1)} %constant.12.clone.c0) | copy-start | bytes 2032132
  7.8 5.8 %copy-start.9 = (bf16[384,144]{1,0:T(8,128)(2,1)S(1)}, bf16[384,144]{1,0:T(8,128)(2,1)}, u32[]{:S(2)}) copy-start(bf16[384,144]{1,0:T(8,128)(2,1)} %constant.14.clone.c2) | copy-start | bytes 331780
  7.8 5.8 %copy-start.10 = (bf16[144,256]{1,0:T(8,128)(2,1)S(1)}, bf16[144,256]{1,0:T(8,128)(2,1)}, u32[]{:S(2)}) copy-start(bf16[144,256]{1,0:T(8,128)(2,1)} %constant.15.clone.c3) | copy-start | bytes 221188
  7.8 5.7 %collective-permute-start.2 = (f32[4,40,128]{2,1,0:T(8,128)S(1)}, f32[4,40,128]{2,1,0:T(8,128)S(1)}, u32[]{:S(2)}, u32[]{:S(2)}) collective-permute-start(f32[4,40,128]{2,1,0:T(8,128)S(1)} %get-tuple-element.40), channel_id=1, source_target_pairs={{0,1},{1,0},{2,3},{3,2},{4,5},{5,4},{6,7},{7,6},{8,9},{9,8},{10,11... | collective-permute-start | bytes 245768 | tf_op jit(solution)/shard_map/ppermute | solution.py:112
  9.5 4.1 %collective-permute-start.3 = (f32[4,40,128]{2,1,0:T(8,128)S(1)}, f32[4,40,128]{2,1,0:T(8,128)S(1)}, u32[]{:S(2)}, u32[]{:S(2)}) collective-permute-start(f32[4,40,128]{2,1,0:T(8,128)S(1)} %get-tuple-element.41), channel_id=1, source_target_pairs={{0,8},{1,2},{2,1},{3,4},{4,3},{5,6},{6,5},{7,15},{8,0},{9,10},{10,... | collective-permute-start | bytes 245768 | tf_op jit(solution)/shard_map/ppermute | solution.py:111
  11.1 11.6 %copy-start.6 = (f32[8]{0:T(128)S(1)}, f32[8]{0:T(128)}, u32[]{:S(2)}) copy-start(f32[8]{0:T(128)} %coupling_ref.1) | copy-start | bytes 100
  15.7 1.7 %collective-permute-start.4 = (f32[2,3,24,128]{3,2,1,0:T(8,128)S(1)}, f32[2,3,24,128]{3,2,1,0:T(8,128)S(1)}, u32[]{:S(2)}, u32[]{:S(2)}) collective-permute-start(f32[2,3,24,128]{3,2,1,0:T(8,128)S(1)} %get-tuple-element.44), channel_id=1, source_target_pairs={{0,8},{1,9},{2,10},{3,11},{4,12},{5,13},{6,14},{7,15},{8,0},{9,1},... | collective-permute-start | bytes 221192 | tf_op jit(solution)/shard_map/ppermute | solution.py:108
  15.7 4.1 %collective-permute-start.5 = (f32[2,3,24,128]{3,2,1,0:T(8,128)S(1)}, f32[2,3,24,128]{3,2,1,0:T(8,128)S(1)}, u32[]{:S(2)}, u32[]{:S(2)}) collective-permute-start(f32[2,3,24,128]{3,2,1,0:T(8,128)S(1)} %get-tuple-element.45), channel_id=1, source_target_pairs={{0,24},{1,25},{2,26},{3,27},{4,28},{5,29},{6,30},{7,31},{8,16},{9,... | collective-permute-start | bytes 221192 | tf_op jit(solution)/shard_map/ppermute | solution.py:109
  20.0 8.3 %collective-permute-start.6 = (f32[2,3,40,128]{3,2,1,0:T(8,128)S(1)}, f32[2,3,40,128]{3,2,1,0:T(8,128)S(1)}, u32[]{:S(2)}, u32[]{:S(2)}) collective-permute-start(f32[2,3,40,128]{3,2,1,0:T(8,128)S(1)} %get-tuple-element.48), channel_id=1, source_target_pairs={{0,1},{1,0},{2,3},{3,2},{4,5},{5,4},{6,7},{7,6},{8,9},{9,8},{10,11... | collective-permute-start | bytes 368648 | tf_op jit(solution)/shard_map/ppermute | solution.py:112
  22.6 5.7 %collective-permute-start.7 = (f32[2,3,40,128]{3,2,1,0:T(8,128)S(1)}, f32[2,3,40,128]{3,2,1,0:T(8,128)S(1)}, u32[]{:S(2)}, u32[]{:S(2)}) collective-permute-start(f32[2,3,40,128]{3,2,1,0:T(8,128)S(1)} %get-tuple-element.49), channel_id=1, source_target_pairs={{0,8},{1,2},{2,1},{3,4},{4,3},{5,6},{6,5},{7,15},{8,0},{9,10},{10,... | collective-permute-start | bytes 368648 | tf_op jit(solution)/shard_map/ppermute | solution.py:111
  31.5 1.7 %collective-permute-start.8 = (f32[2,2,24,128]{3,2,1,0:T(8,128)S(1)}, f32[2,2,24,128]{3,2,1,0:T(8,128)S(1)}, u32[]{:S(2)}, u32[]{:S(2)}) collective-permute-start(f32[2,2,24,128]{3,2,1,0:T(8,128)S(1)} %get-tuple-element.58), channel_id=1, source_target_pairs={{0,8},{1,9},{2,10},{3,11},{4,12},{5,13},{6,14},{7,15},{8,0},{9,1},... | collective-permute-start | bytes 147464 | tf_op jit(solution)/shard_map/ppermute | solution.py:108
  31.6 3.6 %collective-permute-start.9 = (f32[2,2,24,128]{3,2,1,0:T(8,128)S(1)}, f32[2,2,24,128]{3,2,1,0:T(8,128)S(1)}, u32[]{:S(2)}, u32[]{:S(2)}) collective-permute-start(f32[2,2,24,128]{3,2,1,0:T(8,128)S(1)} %get-tuple-element.59), channel_id=1, source_target_pairs={{0,24},{1,25},{2,26},{3,27},{4,28},{5,29},{6,30},{7,31},{8,16},{9,... | collective-permute-start | bytes 147464 | tf_op jit(solution)/shard_map/ppermute | solution.py:109
  35.3 6.3 %collective-permute-start.10 = (f32[2,72,128]{2,1,0:T(8,128)S(1)}, f32[2,72,128]{2,1,0:T(8,128)S(1)}, u32[]{:S(2)}, u32[]{:S(2)}) collective-permute-start(f32[2,72,128]{2,1,0:T(8,128)S(1)} %get-tuple-element.62), channel_id=1, source_target_pairs={{0,1},{1,0},{2,3},{3,2},{4,5},{5,4},{6,7},{7,6},{8,9},{9,8},{10,11... | collective-permute-start | bytes 221192 | tf_op jit(solution)/shard_map/ppermute | solution.py:112
  37.9 3.8 %collective-permute-start.11 = (f32[2,72,128]{2,1,0:T(8,128)S(1)}, f32[2,72,128]{2,1,0:T(8,128)S(1)}, u32[]{:S(2)}, u32[]{:S(2)}) collective-permute-start(f32[2,72,128]{2,1,0:T(8,128)S(1)} %get-tuple-element.63), channel_id=1, source_target_pairs={{0,8},{1,2},{2,1},{3,4},{4,3},{5,6},{6,5},{7,15},{8,0},{9,10},{10,... | collective-permute-start | bytes 221192 | tf_op jit(solution)/shard_map/ppermute | solution.py:111

commit v5 on v4

--- a/solution.py
+++ b/solution.py
@@ -64,23 +64,17 @@
     inverse = np.concatenate([high, high, low], axis=1)
     boxes = size_z // BOX
     line = np.zeros((size_z, boxes * SPAN))
-    means = np.zeros((size_z, boxes * SPAN))
     for box in range(boxes):
         for mode in range(SPAN):
             for offset in range(SPAN):
                 cell = box * BOX + offset - 1
                 if 0 <= cell < size_z:
                     line[cell, box * SPAN + mode] = basis[mode, offset]
-        means[box * BOX : (box + 1) * BOX, box * SPAN : (box + 1) * SPAN] = 1.0 / BOX**3
     high, low = split(line)
     line_forward = np.concatenate([high, high, low], axis=0)
     high, low = split(line.T)
     line_inverse = np.concatenate([high, low], axis=1)
-    eigen = eigenvalues()
-    pair = np.zeros(padded_modes)
-    pair[:modes] = (eigen[:, None] + eigen[None, :]).reshape(-1)
-    summed = (pair[:, None] + np.tile(eigen, boxes)[None, :]).astype(np.float32)
-    return forward, inverse, line_forward, line_inverse, summed, means.astype(np.float32)
+    return forward, inverse, line_forward, line_inverse
 
 
 def swap_pairs(mesh, axis, odd):
@@ -222,7 +216,49 @@
             odd_ref[field, layer, size_y + 2 :] = blank
 
 
-def divisor_kernel(conductance_ref, capacity_ref, zones_ref, summed_ref, means_ref, inverse_ref):
+def line_pairs(whole_ref, whole_rows_ref, field, layers, rows, depth):
+    size_y = whole_ref.shape[2]
+    if depth == 3:
+        return (
+            (whole_rows_ref[field, 0, rows], whole_ref[field, layers, size_y - 2]),
+            (whole_ref[field, layers, 0], whole_ref[field, layers, size_y - 1]),
+            (whole_ref[field, layers, 1], whole_rows_ref[field, 1, rows]),
+        )
+    return (
+        (whole_ref[field, layers, 0], whole_ref[field, layers, size_y - 1]),
+        (whole_rows_ref[field, 0, rows], whole_rows_ref[field, 1, rows]),
+    )
+
+
+def pack_lines(flags, part_ref, part_rows_ref, even_ref, odd_ref):
+    size_x = part_ref.shape[1] - 2
+    depth = even_ref.shape[1] // size_x
+    for field in range(2):
+        pairs = line_pairs(
+            part_ref, part_rows_ref, field, slice(1, size_x + 1), slice(ROW0, ROW0 + size_x), depth
+        )
+        for line, (to_low, to_high) in enumerate(pairs):
+            place = slice(line * size_x, (line + 1) * size_x)
+            even_ref[field, place] = chosen(flags, EVEN_Y, to_high, to_low)
+            odd_ref[field, place] = chosen(flags, EVEN_Y, to_low, to_high)
+
+
+def unpack_lines(flags, lines_refs, ends_refs, out_ref, field):
+    size_x = out_ref.shape[2] - 8
+    depth = lines_refs[0].shape[1] // size_x
+    blank = jnp.zeros((8, out_ref.shape[3]), F32)
+    for side, flag, (even, odd) in ((0, LOW_Y, (1, 0)), (1, HIGH_Y, (0, 1))):
+        lines = keep(flags, flag, chosen(flags, EVEN_Y, lines_refs[even][field], lines_refs[odd][field]))
+        ends = keep(flags, flag, chosen(flags, EVEN_Y, ends_refs[even][field], ends_refs[odd][field]))
+        for line in range(depth):
+            out_ref[side, line, 0:8] = blank
+            out_ref[side, line, size_x : size_x + 8] = blank
+            out_ref[side, line, ROW0 : ROW0 + size_x] = lines[line * size_x : (line + 1) * size_x]
+            out_ref[side, line, ROW0 - 2 : ROW0 + 1] = ends[8 * line : 8 * line + 3]
+            out_ref[side, line, ROW0 + size_x - 1 : ROW0 + size_x + 2] = ends[8 * line + 3 : 8 * line + 6]
+
+
+def divisor_kernel(conductance_ref, capacity_ref, zones_ref, inverse_ref):
     size_x, size_y, size_z = zones_ref.shape
     boxes = size_x // BOX
     lines = []
@@ -237,15 +273,40 @@
                 total = total + value
             lines.append(jnp.sum(total, axis=0, keepdims=True))
     sums = jnp.concatenate(lines, axis=0)
-    means = jnp.dot(sums, means_ref[...], preferred_element_type=F32, precision=lax.Precision.HIGHEST)
+    modes, lanes = inverse_ref.shape[1:]
+    cell = lax.broadcasted_iota(jnp.int32, (size_z, lanes), 0)
+    lane = lax.broadcasted_iota(jnp.int32, (size_z, lanes), 1)
+    spread = jnp.zeros((size_z, lanes), F32)
+    for box in range(size_z // BOX):
+        here = (cell >= box * BOX) & (cell < (box + 1) * BOX) & (lane >= box * SPAN) & (lane < (box + 1) * SPAN)
+        spread = jnp.where(here, 1.0 / BOX**3, spread)
+    means = jnp.dot(sums, spread, preferred_element_type=F32, precision=lax.Precision.HIGHEST)
+    eigen = [float(value) for value in eigenvalues()]
+    row = lax.broadcasted_iota(jnp.int32, (modes, 128), 0)
+    first = jnp.zeros(row.shape, jnp.int32)
+    for mode in range(1, SPAN):
+        first = first + (row >= mode * SPAN).astype(jnp.int32)
+    second = row - SPAN * first
+    pair = jnp.zeros(row.shape, F32)
+    for mode in range(SPAN):
+        pair = pair + jnp.where(first == mode, eigen[mode], 0.0) + jnp.where(second == mode, eigen[mode], 0.0)
+    lane = lax.broadcasted_iota(jnp.int32, (8, lanes), 1)
+    for box in range(1, size_z // BOX):
+        lane = lane - SPAN * (lax.broadcasted_iota(jnp.int32, (8, lanes), 1) >= box * SPAN).astype(jnp.int32)
+    third = jnp.zeros(lane.shape, F32)
+    for mode in range(SPAN):
+        third = jnp.where(lane == mode, eigen[mode], third)
+    summed = jnp.concatenate([pair, pair[:, : lanes - 128]], axis=1) + third[0:1]
     half = 2 * boxes
     for combo in range(half):
         cbar = means[combo : combo + 1]
         kbar = means[half + combo : half + combo + 1]
-        inverse_ref[combo] = 1.0 / (cbar + kbar * summed_ref[...])
-
-
-def edge_layers_kernel(mesh, load_hbm, zones_hbm, load_ref, zones_ref, even_ref, odd_ref, sems):
+        inverse_ref[combo] = 1.0 / (cbar + kbar * summed)
+
+
+def edge_layers_kernel(
+    mesh, load_hbm, zones_hbm, load_ref, zones_ref, even_ref, odd_ref, even_lines, odd_lines, sems
+):
     copies = [
         pltpu.make_async_copy(load_hbm.at[0], load_ref.at[0], sems.at[0]),
         pltpu.make_async_copy(load_hbm.at[1], load_ref.at[1], sems.at[1]),
@@ -255,48 +316,43 @@
         copy.start()
     flags = standing(mesh)
     last = zones_ref.shape[0] - 1
+    size_y = zones_ref.shape[1]
     for channel in range(4):
         if channel < 3:
             copies[channel].wait()
         if channel < 2:
             low, high = load_ref[channel, 0], load_ref[channel, last]
+            low_line, high_line = load_ref[channel, :, 0], load_ref[channel, :, size_y - 1]
         else:
             low, high = zones_ref[channel - 2].astype(F32), zones_ref[last - 3 + channel].astype(F32)
+            low_line = zones_ref[:, channel - 2].astype(F32)
+            high_line = zones_ref[:, size_y - 4 + channel].astype(F32)
         even_ref[channel] = chosen(flags, EVEN_X, high, low)
         odd_ref[channel] = chosen(flags, EVEN_X, low, high)
-
-
-def edge_rows_kernel(mesh, load_ref, zones_ref, first_ref, second_ref, even_ref, odd_ref):
+        even_lines[channel] = chosen(flags, EVEN_Y, high_line, low_line)
+        odd_lines[channel] = chosen(flags, EVEN_Y, low_line, high_line)
+
+
+def edge_ends_kernel(mesh, first_ref, second_ref, inverse_ref, even_ref, odd_ref):
     flags = standing(mesh)
-    size_x, size_y, size_z = zones_ref.shape
+    size_y = first_ref.shape[1]
     from_low = chosen(flags, EVEN_X, second_ref[...], first_ref[...])
     from_high = chosen(flags, EVEN_X, first_ref[...], second_ref[...])
-    blank = jnp.zeros((8, size_z), F32)
+
+    def put(row, layer, near, far):
+        to_low, to_high = layer[near : near + 1], layer[far : far + 1]
+        even_ref[row : row + 1] = chosen(flags, EVEN_Y, to_high, to_low)
+        odd_ref[row : row + 1] = chosen(flags, EVEN_Y, to_low, to_high)
+
     for ref in (even_ref, odd_ref):
-        for channel in range(4):
-            ref[channel, 0:8] = blank
-            ref[channel, size_x : size_x + 8] = blank
-
-    def put(channel, position, count, to_low, to_high):
-        place = slice(position, position + count)
-        even_ref[channel, place] = chosen(flags, EVEN_Y, to_high, to_low)
-        odd_ref[channel, place] = chosen(flags, EVEN_Y, to_low, to_high)
-
-    end = ROW0 + size_x
-    for field in range(2):
-        put(field, ROW0, size_x, load_ref[field, :, 0], load_ref[field, :, size_y - 1])
-        low = keep(flags, LOW_X, from_low[field])
-        high = keep(flags, HIGH_X, from_high[field])
-        put(field, ROW0 - 1, 1, low[0:1], low[size_y - 1 : size_y])
-        put(field, end, 1, high[0:1], high[size_y - 1 : size_y])
-    for layer in range(2):
-        channel = 2 + layer
-        near, far = layer, size_y - 2 + layer
-        put(channel, ROW0, size_x, zones_ref[:, near].astype(F32), zones_ref[:, far].astype(F32))
+        ref[8:16] = jnp.zeros((8, ref.shape[1]), F32)
+    for field in range(2):
+        put(2 * field, keep(flags, LOW_X, from_low[field]), 0, size_y - 1)
+        put(2 * field + 1, keep(flags, HIGH_X, from_high[field]), 0, size_y - 1)
+    for line in range(2):
         for depth in range(2):
-            low, high = from_low[2 + depth], from_high[2 + depth]
-            put(channel, ROW0 - 2 + depth, 1, low[near : near + 1], low[far : far + 1])
-            put(channel, end + depth, 1, high[near : near + 1], high[far : far + 1])
+            put(4 + 4 * line + depth, from_low[2 + depth], line, size_y - 2 + line)
+            put(6 + 4 * line + depth, from_high[2 + depth], line, size_y - 2 + line)
 
 
 def looked_up(entries, zone):
@@ -308,7 +364,8 @@
 
 def coefficient_kernel(
     mesh, conductance_ref, capacity_ref, coupling_ref, zones_ref, first_x, second_x, first_y, second_y,
-    half_ref, mass_ref, face_ref, half_rows_ref, mass_rows_ref, face_rows_ref,
+    first_end, second_end,
+    half_ref, mass_ref, face_ref, half_rows_ref, mass_rows_ref, face_rows_ref, line_ref,
 ):
     flags = standing(mesh)
     labels = range(coupling_ref.shape[0])
@@ -320,8 +377,19 @@
     size_x, size_y, size_z = zones_ref.shape
     low_x = chosen(flags, EVEN_X, second_x[2:4], first_x[2:4])
     high_x = chosen(flags, EVEN_X, first_x[2:4], second_x[2:4])
-    low_y = chosen(flags, EVEN_Y, second_y[2:4], first_y[2:4])
-    high_y = chosen(flags, EVEN_Y, first_y[2:4], second_y[2:4])
+    for side, (lines, ends) in enumerate(
+        (
+            (chosen(flags, EVEN_Y, second_y[2:4], first_y[2:4]), chosen(flags, EVEN_Y, second_end[...], first_end[...])),
+            (chosen(flags, EVEN_Y, first_y[2:4], second_y[2:4]), chosen(flags, EVEN_Y, first_end[...], second_end[...])),
+        )
+    ):
+        for line in range(2):
+            place = 2 * side + line
+            line_ref[place, 0:8] = jnp.zeros((8, size_z), F32)
+            line_ref[place, size_x : size_x + 8] = jnp.zeros((8, size_z), F32)
+            line_ref[place, ROW0 - 2 : ROW0] = ends[4 + 4 * line : 6 + 4 * line]
+            line_ref[place, ROW0 : ROW0 + size_x] = lines[line]
+            line_ref[place, ROW0 + size_x : ROW0 + size_x + 2] = ends[6 + 4 * line : 8 + 4 * line]
     inside = slice(8, 8 + size_y)
     for x in range(-2, size_x + 2):
         if x < 0:
@@ -346,9 +414,8 @@
             )
     count = half_rows_ref.shape[2]
     position = lax.broadcasted_iota(jnp.int32, (count, size_z), 0)
-    for line, (zone, flag) in enumerate(
-        ((low_y[0], LOW_Y), (low_y[1], LOW_Y), (high_y[0], HIGH_Y), (high_y[1], HIGH_Y))
-    ):
+    for line, flag in enumerate((LOW_Y, LOW_Y, HIGH_Y, HIGH_Y)):
+        zone = line_ref[line]
         for field in range(2):
             value = looked_up(halves_of[field], zone)
             below = value[ROW0 : ROW0 + 1]
@@ -381,8 +448,8 @@
 
 
 def first_solve_kernel(
-    mesh, load_ref, first_x, second_x, first_y, second_y, inverse_ref, c0, c1, c2, c3,
-    part_ref, part_rows_ref, even_ref, odd_ref, field_ref, rows_ref, before_ref, after_ref,
+    mesh, load_ref, first_x, second_x, first_y, second_y, first_end, second_end, inverse_ref, c0, c1, c2, c3,
+    part_ref, part_rows_ref, even_ref, odd_ref, even_lines, odd_lines, field_ref, rows_ref, before_ref, after_ref,
 ):
     flags = standing(mesh)
     size_x = load_ref.shape[1]
@@ -390,10 +457,20 @@
         field_ref[field, 1 : 1 + size_x] = load_ref[field]
         field_ref[field, 0] = keep(flags, LOW_X, chosen(flags, EVEN_X, second_x[field], first_x[field]))
         field_ref[field, 1 + size_x] = keep(flags, HIGH_X, chosen(flags, EVEN_X, first_x[field], second_x[field]))
-        rows_ref[field, 0] = keep(flags, LOW_Y, chosen(flags, EVEN_Y, second_y[field], first_y[field]))
-        rows_ref[field, 1] = keep(flags, HIGH_Y, chosen(flags, EVEN_Y, first_y[field], second_y[field]))
+        for side, flag, (even, odd), (even_end, odd_end) in (
+            (0, LOW_Y, (second_y, first_y), (second_end, first_end)),
+            (1, HIGH_Y, (first_y, second_y), (first_end, second_end)),
+        ):
+            line = keep(flags, flag, chosen(flags, EVEN_Y, even[field], odd[field]))
+            ends = keep(flags, flag, chosen(flags, EVEN_Y, even_end[0:8], odd_end[0:8]))
+            rows_ref[field, side, 0:8] = jnp.zeros((8, line.shape[1]), F32)
+            rows_ref[field, side, size_x : size_x + 8] = jnp.zeros((8, line.shape[1]), F32)
+            rows_ref[field, side, ROW0 - 1 : ROW0] = ends[2 * field : 2 * field + 1]
+            rows_ref[field, side, ROW0 : ROW0 + size_x] = line
+            rows_ref[field, side, ROW0 + size_x : ROW0 + size_x + 1] = ends[2 * field + 1 : 2 * field + 2]
     solve(field_ref, rows_ref, inverse_ref, (c0, c1, c2, c3), before_ref, after_ref, part_ref, part_rows_ref)
     pack_x(flags, part_ref, part_rows_ref, even_ref, odd_ref)
+    pack_lines(flags, part_ref, part_rows_ref, even_lines, odd_lines)
 
 
 def merge_x_kernel(mesh, part_ref, part_rows_ref, first_ref, second_ref, whole_ref, whole_rows_ref, even_ref, odd_ref):
@@ -401,7 +478,6 @@
     size_x = part_ref.shape[1] - 2
     size_y, size_z = part_ref.shape[2:]
     depth = first_ref.shape[1]
-    count = part_rows_ref.shape[2]
     end = ROW0 + size_x
     for field in range(2):
         low = keep(flags, LOW_X, chosen(flags, EVEN_X, second_ref[field], first_ref[field]))
@@ -411,9 +487,8 @@
         whole_ref[field, 3 : size_x + 1] = part_ref[field, 2:size_x]
         whole_ref[field, size_x + 1] = part_ref[field, size_x] + high[0, :size_y]
         whole_ref[field, size_x + 2] = keep(flags, HIGH_X, part_ref[field, size_x + 1]) + high[1, :size_y]
-        if depth == 3:
-            whole_ref[field, 0] = low[0, :size_y]
-            whole_ref[field, size_x + 3] = high[2, :size_y]
+        whole_ref[field, 0] = low[0, :size_y] if depth == 3 else jnp.zeros((size_y, size_z), F32)
+        whole_ref[field, size_x + 3] = high[2, :size_y] if depth == 3 else jnp.zeros((size_y, size_z), F32)
         for side in range(2):
             row = slice(size_y + side, size_y + side + 1)
             edge = ROW0 - 1
@@ -432,35 +507,25 @@
                 whole_rows_ref[field, side, edge - 1 : edge] = low[0, row]
                 whole_rows_ref[field, side, end + 1 : end + 2] = high[2, row]
 
-        def put(at, to_low, to_high):
-            even_ref[(field, *at)] = chosen(flags, EVEN_Y, to_high, to_low)
-            odd_ref[(field, *at)] = chosen(flags, EVEN_Y, to_low, to_high)
-
-        if depth == 3:
-            blank = jnp.zeros((8, size_z), F32)
-            for layer in range(3):
-                for ref in (even_ref, odd_ref):
-                    ref[field, layer, 0:8] = blank
-                    ref[field, layer, count - 8 : count] = blank
-            rows = slice(ROW0 - 2, end + 2)
-            low_rows = whole_rows_ref[field, 0, rows]
-            high_rows = whole_rows_ref[field, 1, rows]
-            put((0, rows), low_rows, whole_ref[field, :, size_y - 2])
-            put((1, rows), whole_ref[field, :, 0], whole_ref[field, :, size_y - 1])
-            put((2, rows), whole_ref[field, :, 1], high_rows)
-        else:
-            own = slice(2, size_x + 2)
-            put((slice(0, size_x),), whole_ref[field, own, 0], whole_ref[field, own, size_y - 1])
-            put((slice(size_x, None),), whole_rows_ref[field, 0], whole_rows_ref[field, 1])
-
-
-def assemble(flags, whole_ref, whole_rows_ref, first_ref, second_ref, field_ref, lines):
+        for line in range(depth):
+            for ref in (even_ref, odd_ref):
+                ref[field, 8 * line : 8 * line + 8] = jnp.zeros((8, size_z), F32)
+        for start, x in ((0, -2), (3, size_x - 1)):
+            layers, rows = slice(x + 2, x + 5), slice(x + ROW0, x + ROW0 + 3)
+            pairs = line_pairs(whole_ref, whole_rows_ref, field, layers, rows, depth)
+            for line, (to_low, to_high) in enumerate(pairs):
+                place = slice(8 * line + start, 8 * line + start + 3)
+                even_ref[field, place] = chosen(flags, EVEN_Y, to_high, to_low)
+                odd_ref[field, place] = chosen(flags, EVEN_Y, to_low, to_high)
+
+
+def assemble(flags, whole_ref, whole_rows_ref, lines_refs, ends_refs, came_ref, field_ref, lines):
     size_x = whole_ref.shape[1] - 4
     size_y = whole_ref.shape[2]
     spread = slice(ROW0 - 2, ROW0 + size_x + 2)
     for field in range(2):
-        low = keep(flags, LOW_Y, chosen(flags, EVEN_Y, second_ref[field], first_ref[field]))
-        high = keep(flags, HIGH_Y, chosen(flags, EVEN_Y, first_ref[field], second_ref[field]))
+        unpack_lines(flags, lines_refs, ends_refs, came_ref, field)
+        low, high = came_ref[0], came_ref[1]
         below = keep(flags, LOW_Y, whole_rows_ref[field, 0]) + low[1]
         above = keep(flags, HIGH_Y, whole_rows_ref[field, 1]) + high[1]
         lines[field, 0] = low[0]
@@ -535,14 +600,15 @@
 
 
 def second_solve_kernel(
-    mesh, whole_ref, whole_rows_ref, first_ref, second_ref,
+    mesh, whole_ref, whole_rows_ref, first_lines, second_lines, first_ends, second_ends,
     half_ref, mass_ref, face_ref, half_lines, mass_lines, face_lines, load_ref, inverse_ref, c0, c1, c2, c3,
-    precond_ref, image_ref, sums_ref, part_ref, part_rows_ref, even_ref, odd_ref,
-    value_ref, lines, near, field_ref, rows_ref, before_ref, after_ref,
+    precond_ref, image_ref, sums_ref, part_ref, part_rows_ref, even_ref, odd_ref, even_lines, odd_lines,
+    came_ref, value_ref, lines, near, field_ref, rows_ref, before_ref, after_ref,
 ):
     flags = standing(mesh)
     size_x, size_y, size_z = load_ref.shape[1:]
-    assemble(flags, whole_ref, whole_rows_ref, first_ref, second_ref, value_ref, lines)
+    lines_refs, ends_refs = (first_lines, second_lines), (first_ends, second_ends)
+    assemble(flags, whole_ref, whole_rows_ref, lines_refs, ends_refs, came_ref, value_ref, lines)
     for x, flag in ((-1, LOW_X), (size_x, HIGH_X)):
         _, images = operate(value_ref, half_ref, mass_ref, face_ref, x, 1)
         for field in range(2):
@@ -575,24 +641,25 @@
             rows_ref[field, side] = keep(flags, flag, jnp.where(valid, images[field], 0.0))
     solve(field_ref, rows_ref, inverse_ref, (c0, c1, c2, c3), before_ref, after_ref, part_ref, part_rows_ref)
     pack_x(flags, part_ref, part_rows_ref, even_ref, odd_ref)
+    pack_lines(flags, part_ref, part_rows_ref, even_lines, odd_lines)
 
 
 def second_image_kernel(
-    mesh, whole_ref, whole_rows_ref, first_ref, second_ref, half_ref, mass_ref, face_ref, old_image_ref, old_sums_ref,
-    precond_ref, image_ref, sums_ref, value_ref,
+    mesh, whole_ref, whole_rows_ref, first_lines, second_lines, first_ends, second_ends,
+    half_ref, mass_ref, face_ref, old_image_ref, old_sums_ref,
+    precond_ref, image_ref, sums_ref, came_ref, value_ref,
 ):
     flags = standing(mesh)
     size_x, size_y, size_z = old_image_ref.shape[1:]
     own, wide = slice(2, size_x + 2), slice(1, size_x + 3)
-    rows, margins = slice(ROW0, ROW0 + size_x), slice(size_x + ROW0 - 1, 2 * size_x + ROW0 + 1)
-    for field in range(2):
-        low = keep(flags, LOW_Y, chosen(flags, EVEN_Y, second_ref[field], first_ref[field]))
-        high = keep(flags, HIGH_Y, chosen(flags, EVEN_Y, first_ref[field], second_ref[field]))
+    rows, margins = slice(ROW0, ROW0 + size_x), slice(ROW0 - 1, ROW0 + size_x + 1)
+    for field in range(2):
+        unpack_lines(flags, (first_lines, second_lines), (first_ends, second_ends), came_ref, field)
         value_ref[field, wide, 8 : 8 + size_y] = whole_ref[field, wide]
-        value_ref[field, own, 7] = keep(flags, LOW_Y, whole_rows_ref[field, 0, rows]) + low[:size_x]
-        value_ref[field, wide, 8] = whole_ref[field, wide, 0] + low[margins]
-        value_ref[field, wide, 7 + size_y] = whole_ref[field, wide, size_y - 1] + high[margins]
-        value_ref[field, own, 8 + size_y] = keep(flags, HIGH_Y, whole_rows_ref[field, 1, rows]) + high[:size_x]
+        value_ref[field, own, 7] = keep(flags, LOW_Y, whole_rows_ref[field, 0, rows]) + came_ref[0, 0, rows]
+        value_ref[field, wide, 8] = whole_ref[field, wide, 0] + came_ref[0, 1, margins]
+        value_ref[field, wide, 7 + size_y] = whole_ref[field, wide, size_y - 1] + came_ref[1, 1, margins]
+        value_ref[field, own, 8 + size_y] = keep(flags, HIGH_Y, whole_rows_ref[field, 1, rows]) + came_ref[1, 0, rows]
     total_c = total_d = jnp.zeros((CHUNK, size_y, size_z), F32)
     for x in range(0, size_x, CHUNK):
         chunk = slice(x, x + CHUNK)
@@ -670,34 +737,35 @@
     boxes = size_x // BOX
     count = size_x + 8
     sds = lambda *shape: jax.ShapeDtypeStruct(shape, F32)
-    forward, back, line_forward, line_back, summed, means = [jnp.asarray(c) for c in constants(size_z)]
-    consts = (forward, back, line_forward, line_back)
-    modes, lanes = summed.shape
+    consts = [jnp.asarray(c) for c in constants(size_z)]
+    modes, lanes = consts[0].shape[0], size_z // BOX * SPAN
+    assert size_z == 128
     load, zones, *packed = call(
         mesh,
         edge_layers_kernel,
         [],
         [load, zones],
-        [sds(*load.shape), jax.ShapeDtypeStruct(zones.shape, zones.dtype)] + [sds(4, size_y, size_z)] * 2,
+        [sds(*load.shape), jax.ShapeDtypeStruct(zones.shape, zones.dtype)] + [sds(4, size_y, size_z)] * 2 + [sds(4, size_x, size_z)] * 2,
         [pltpu.SemaphoreType.DMA((3,))],
         in_hbm=True,
     )
-    x_halo = swap(mesh, "gx", *packed)
+    x_halo = swap(mesh, "gx", *packed[:2])
+    y_halo = swap(mesh, "gy", *packed[2:])
     (inverse,) = call(
         None,
         divisor_kernel,
         [conductance, capacity],
-        [zones, summed, means],
+        [zones],
         [sds(2 * boxes, modes, lanes)],
         flops=40_000_000,
     )
-    packed = call(mesh, edge_rows_kernel, [], [load, zones, *x_halo], [sds(4, count, size_z)] * 2)
-    y_halo = swap(mesh, "gy", *packed)
+    packed = call(mesh, edge_ends_kernel, [], [*x_halo, inverse], [sds(16, size_z)] * 2)
+    y_ends = swap(mesh, "gy", *packed)
     half, mass, face, half_lines, mass_lines, face_lines = call(
         mesh,
         coefficient_kernel,
         [conductance, capacity, coupling],
-        [zones, *x_halo, *y_halo],
+        [zones, *x_halo, *y_halo, *y_ends],
         [
             sds(2, size_x + 4, size_y + 16, size_z),
             sds(3, size_x + 2, size_y, size_z),
@@ -706,12 +774,14 @@
             sds(3, 2, count, size_z),
             sds(2, 2, 2, count, size_z),
         ],
+        [pltpu.VMEM((4, count, size_z), F32)],
         flops=20_000_000,
     )
     parts = [sds(2, size_x + 2, size_y, size_z), sds(2, 2, count, size_z)]
     packed_x = [[sds(2, depth, size_y + 8, size_z)] * 2 for depth in (3, 2)]
     wholes = [sds(2, size_x + 4, size_y, size_z), sds(2, 2, count, size_z)]
-    packed_y = [[sds(2, 3, count, size_z)] * 2, [sds(2, size_x + count, size_z)] * 2]
+    packed_lines = [[sds(2, depth * size_x, size_z)] * 2 for depth in (3, 2)]
+    packed_ends = [[sds(2, depth * 8, size_z)] * 2 for depth in (3, 2)]
     rows = SPAN * size_y + 48
     work = [
         pltpu.VMEM((2, size_x + 2, size_y, size_z), F32),
@@ -726,31 +796,39 @@
     own = sds(2, size_x, size_y, size_z)
 
     part, part_rows, *packed = call(
-        mesh, first_solve_kernel, [], [load, *x_halo, *y_halo, inverse, *consts], parts + packed_x[0], work, 3_000_000_000
-    )
-    received = swap(mesh, "gx", *packed)
-    whole, whole_rows, *packed = call(mesh, merge_x_kernel, [], [part, part_rows, *received], wholes + packed_y[0])
-    received = swap(mesh, "gy", *packed)
+        mesh,
+        first_solve_kernel,
+        [],
+        [load, *x_halo, *y_halo, *y_ends, inverse, *consts],
+        parts + packed_x[0] + packed_lines[0],
+        work,
+        3_000_000_000,
+    )
+    lines = swap(mesh, "gy", *packed[2:])
+    received = swap(mesh, "gx", *packed[:2])
+    whole, whole_rows, *packed = call(mesh, merge_x_kernel, [], [part, part_rows, *received], wholes + packed_ends[0])
+    ends = swap(mesh, "gy", *packed)
     precond, image, sums, part, part_rows, *packed = call(
         mesh,
         second_solve_kernel,
         [],
-        [whole, whole_rows, *received, half, mass, face, half_lines, mass_lines, face_lines, load, inverse, *consts],
-        [own, own, sds(8, size_z)] + parts + packed_x[1],
-        padded + [pltpu.VMEM((2, 2, count, size_z), F32)] + work,
+        [whole, whole_rows, *lines, *ends, half, mass, face, half_lines, mass_lines, face_lines, load, inverse, *consts],
+        [own, own, sds(8, size_z)] + parts + packed_x[1] + packed_lines[1],
+        [pltpu.VMEM((2, 3, count, size_z), F32)] + padded + [pltpu.VMEM((2, 2, count, size_z), F32)] + work,
         3_000_000_000,
     )
-    received = swap(mesh, "gx", *packed)
-    whole, whole_rows, *packed = call(mesh, merge_x_kernel, [], [part, part_rows, *received], wholes + packed_y[1])
-    received = swap(mesh, "gy", *packed)
+    lines = swap(mesh, "gy", *packed[2:])
+    received = swap(mesh, "gx", *packed[:2])
+    whole, whole_rows, *packed = call(mesh, merge_x_kernel, [], [part, part_rows, *received], wholes + packed_ends[1])
+    ends = swap(mesh, "gy", *packed)
     devices = mesh.shape["gx"] * mesh.shape["gy"]
     last_precond, last_image, sums = call(
         mesh,
         second_image_kernel,
         [],
-        [whole, whole_rows, *received, half, mass, face, image, sums],
+        [whole, whole_rows, *lines, *ends, half, mass, face, image, sums],
         [own, own, sds(devices, size_z)],
-        padded[:1],
+        [pltpu.VMEM((2, 2, count, size_z), F32), padded[0]],
         10_000_000,
     )
     sums = lax.all_to_all(sums, AXES, 0, 0, tiled=True)

time: 57.2 us -> 55.6 us (0.972)
  waiting for transfers between devices: 16.1 us -> 3.81 us
  starting transfers between devices: 13.8 us -> 23.4 us
  local copies, waits for them, and re-layouts: 2.03 us -> 3.36 us
    ppermute x6 -> x9, starting transfers between devices: 7.45 us -> 20.1 us  [swap(): first = lax.ppermute(even_part, AXES, swap_pairs(mesh, axis, False))]
    ppermute x6 -> x9, waiting for transfers between devices: 10.1 us -> 3.38 us  [swap(): first = lax.ppermute(even_part, AXES, swap_pairs(mesh, axis, False))]
    ppermute x6 -> x9, waiting for transfers between devices: 6.01 us -> 0.43 us  [swap(): second = lax.ppermute(odd_part, AXES, swap_pairs(mesh, axis, True))]
    ppermute x6 -> x9, starting transfers between devices: 6.36 us -> 3.25 us  [swap(): second = lax.ppermute(odd_part, AXES, swap_pairs(mesh, axis, True))]
    unnamed x22 -> x18, local copies, waits for them, and re-layouts: 2.03 us -> 3.36 us
  transfers between devices with their start and end apart: 12 -> 18, of which waited for: 6 -> 3; matrix products, arithmetic and copies ran while one was open for 0% -> 0% of each run, Pallas kernels for 5% -> 6%
where the time goes in v5:
time: 55.6 us; the launch traced here: 55.3 us
  starting transfers between devices  23.4 us (42%)
  blocking collectives  12.7 us (23%)
  Pallas kernels  11.3 us (20%)
  waiting for transfers between devices  3.81 us (7%)
  local copies, waits for them, and re-layouts  3.36 us (6%)
  between operations  0.79 us (1%)
    ppermute x9, starting transfers between devices, swap(): first = lax.ppermute(even_part, AXES, swap_pairs(mesh, axis, False))  20.1 us
    all_to_all x1, blocking collectives, shards(): sums = lax.all_to_all(sums, AXES, 0, 0, tiled=True)  12.7 us
    pallas_call x10, Pallas kernels, call(): pl.pallas_call(kernel if mesh is None else functools.partial(kernel, mesh...  11.3 us
    ppermute x9, waiting for transfers between devices, swap(): first = lax.ppermute(even_part, AXES, swap_pairs(mesh, axis, False))  3.38 us
    unnamed x18, local copies, waits for them, and re-layouts  3.36 us
    ppermute x9, starting transfers between devices, swap(): second = lax.ppermute(odd_part, AXES, swap_pairs(mesh, axis, True))  3.25 us
  transfers between devices with their start and end apart: 18, of which 3 were waited for; matrix products, arithmetic and copies ran while one was open for 0% of the time, Pallas kernels for 6%

profile of v5, /device:TPU:0, one launch (start us, length us, event | category | flops | bytes accessed | tf_op | source)
XLA Modules:
  0.0 55.3 jit_solution(17532404606312890748)
XLA Ops:
  0.6 1.0 %copy-done = f32[2,32,16,128]{3,2,1,0:T(8,128)S(1)} copy-done((f32[2,32,16,128]{3,2,1,0:T(8,128)S(1)}, f32[2,32,16,128]{3,2,1,0:T(8,128)}, u32[]{:S(2)}) %copy-start) | copy-done | bytes 524312
  1.7 0.9 %copy-done.1 = s32[32,16,128]{2,1,0:T(8,128)S(1)} copy-done((s32[32,16,128]{2,1,0:T(8,128)S(1)}, s32[32,16,128]{2,1,0:T(8,128)}, u32[]{:S(2)}) %copy-start.1) | copy-done | bytes 262168
  2.6 0.2 shard_map.104
  2.9 3.0 %collective-permute-start.2 = (f32[4,32,128]{2,1,0:T(8,128)S(1)}, f32[4,32,128]{2,1,0:T(8,128)S(1)}, u32[]{:S(2)}, u32[]{:S(2)}) collective-permute-start(f32[4,32,128]{2,1,0:T(8,128)S(1)} %get-tuple-element.45), channel_id=1, source_target_pairs={{0,1},{1,0},{2,3},{3,2},{4,5},{5,4},{6,7},{7,6},{8,9},{9,8},{10,11... | collective-permute-start | bytes 196616 | tf_op jit(solution)/shard_map/ppermute | solution.py:106
  5.9 0.5 collective-permute-start
  6.4 1.1 %collective-permute-start.1 = (f32[4,16,128]{2,1,0:T(8,128)S(1)}, f32[4,16,128]{2,1,0:T(8,128)S(1)}, u32[]{:S(2)}, u32[]{:S(2)}) collective-permute-start(f32[4,16,128]{2,1,0:T(8,128)S(1)} %get-tuple-element.44), channel_id=1, source_target_pairs={{0,24},{1,25},{2,26},{3,27},{4,28},{5,29},{6,30},{7,31},{8,16},{9,... | collective-permute-start | bytes 98312 | tf_op jit(solution)/shard_map/ppermute | solution.py:103
  7.5 0.7 %copy-done.2 = f32[2,8]{1,0:T(2,128)S(1)} copy-done((f32[2,8]{1,0:T(2,128)S(1)}, f32[2,8]{1,0:T(2,128)}, u32[]{:S(2)}) %copy-start.2) | copy-done | bytes 88
  8.2 0.7 %copy-done.3 = f32[2,8]{1,0:T(2,128)S(1)} copy-done((f32[2,8]{1,0:T(2,128)S(1)}, f32[2,8]{1,0:T(2,128)}, u32[]{:S(2)}) %copy-start.3) | copy-done | bytes 88
  8.9 1.6 %shard_map.105.inverse_ref = f32[4,336,144]{2,1,0:T(8,128)S(1)} custom-call(f32[2,8]{1,0:T(2,128)S(1)} %copy-done.2, f32[2,8]{1,0:T(2,128)S(1)} %copy-done.3, s32[32,16,128]{2,1,0:T(8,128)S(1)} %get-tuple-element.47.zones_ref), custom_call_target="tpu_custom_call" | custom-call | flops 40000000 | bytes 1036288 | tf_op jit(solution)/shard_map/pallas_call | solution.py:723
  10.5 3.1 %collective-permute-start.4 = (f32[16,128]{1,0:T(8,128)S(1)}, f32[16,128]{1,0:T(8,128)S(1)}, u32[]{:S(2)}, u32[]{:S(2)}) collective-permute-start(f32[16,128]{1,0:T(8,128)S(1)} %get-tuple-element.48), channel_id=1, source_target_pairs={{0,1},{1,0},{2,3},{3,2},{4,5},{5,4},{6,7},{7,6},{8,9},{9,8},{10,11... | collective-permute-start | bytes 24584 | tf_op jit(solution)/shard_map/ppermute | solution.py:106
  13.6 1.6 %collective-permute-done.4.first_end = f32[16,128]{1,0:T(8,128)S(1)} collective-permute-done((f32[16,128]{1,0:T(8,128)S(1)}, f32[16,128]{1,0:T(8,128)S(1)}, u32[]{:S(2)}, u32[]{:S(2)}) %collective-permute-start.4) | collective-permute-done | bytes 8224 | tf_op jit(solution)/shard_map/ppermute | solution.py:106
  15.3 0.0 copy-start.4
  15.3 2.2 %shard_map.107 = (f32[2,34,16,128]{3,2,1,0:T(8,128)S(1)}, f32[2,2,40,128]{3,2,1,0:T(8,128)S(1)}, f32[2,3,24,128]{3,2,1,0:T(8,128)S(1)}, f32[2,3,24,128]{3,2,1,0:...) custom-call(f32[2,32,16,128]{3,2,1,0:T(8,128)S(1)} %get-tuple-element.42.load_ref, ...), custom_call_target="tpu_custom_call" | custom-call | flops 3000000000 | bytes 4033536 | tf_op jit(solution)/shard_map/pallas_call | solution.py:723
  17.5 0.1 collective-permute-start.6
  17.6 0.6 %collective-permute-start.7 = (f32[2,3,24,128]{3,2,1,0:T(8,128)S(1)}, f32[2,3,24,128]{3,2,1,0:T(8,128)S(1)}, u32[]{:S(2)}, u32[]{:S(2)}) collective-permute-start(f32[2,3,24,128]{3,2,1,0:T(8,128)S(1)} %get-tuple-element.53), channel_id=1, source_target_pairs={{0,24},{1,25},{2,26},{3,27},{4,28},{5,29},{6,30},{7,31},{8,16},{9,... | collective-permute-start | bytes 221192 | tf_op jit(solution)/shard_map/ppermute | solution.py:103
  18.2 3.0 %collective-permute-start.8 = (f32[2,96,128]{2,1,0:T(8,128)S(1)}, f32[2,96,128]{2,1,0:T(8,128)S(1)}, u32[]{:S(2)}, u32[]{:S(2)}) collective-permute-start(f32[2,96,128]{2,1,0:T(8,128)S(1)} %get-tuple-element.56), channel_id=1, source_target_pairs={{0,1},{1,0},{2,3},{3,2},{4,5},{5,4},{6,7},{7,6},{8,9},{9,8},{10,11... | collective-permute-start | bytes 294920 | tf_op jit(solution)/shard_map/ppermute | solution.py:106
  21.2 0.4 collective-permute-done.7.second_ref
  21.7 0.1 shard_map.108
  21.7 3.1 %collective-permute-start.10 = (f32[2,24,128]{2,1,0:T(8,128)S(1)}, f32[2,24,128]{2,1,0:T(8,128)S(1)}, u32[]{:S(2)}, u32[]{:S(2)}) collective-permute-start(f32[2,24,128]{2,1,0:T(8,128)S(1)} %get-tuple-element.58), channel_id=1, source_target_pairs={{0,1},{1,0},{2,3},{3,2},{4,5},{5,4},{6,7},{7,6},{8,9},{9,8},{10,11... | collective-permute-start | bytes 73736 | tf_op jit(solution)/shard_map/ppermute | solution.py:106
  24.8 0.4 collective-permute-start.11
  25.2 1.6 %shard_map.109 = (f32[2,36,32,128]{3,2,1,0:T(8,128)S(1)}, f32[3,34,16,128]{3,2,1,0:T(8,128)S(1)}, f32[2,2,34,16,128]{4,3,2,1,0:T(8,128)S(1)}, f32[2,6,40,128]{3,...) custom-call(f32[2,8]{1,0:T(2,128)S(1)} %copy-done.2, f32[2,8]{1,0:T(2,128)S(1)} %copy-done.3, ...), custom_call_target="tpu_custom_call" | custom-call | flops 20000000 | bytes 4136960 | tf_op jit(solution)/shard_map/pallas_call | solution.py:723
  26.9 0.0 collective-permute-done.10.first_ends
  26.9 3.3 %shard_map.110 = (f32[2,32,16,128]{3,2,1,0:T(8,128)S(1)}, f32[2,32,16,128]{3,2,1,0:T(8,128)S(1)}, f32[8,128]{1,0:T(8,128)S(1)}, f32[2,34,16,128]{3,2,1,0:T(8,128...) custom-call(f32[2,36,16,128]{3,2,1,0:T(8,128)S(1)} %get-tuple-elemen, ...), custom_call_target="tpu_custom_call" | custom-call | flops 3000000000 | bytes 9337856 | tf_op jit(solution)/shard_map/pallas_call | solution.py:723
  30.2 0.2 collective-permute-start.12
  30.4 1.1 %collective-permute-start.13 = (f32[2,2,24,128]{3,2,1,0:T(8,128)S(1)}, f32[2,2,24,128]{3,2,1,0:T(8,128)S(1)}, u32[]{:S(2)}, u32[]{:S(2)}) collective-permute-start(f32[2,2,24,128]{3,2,1,0:T(8,128)S(1)} %get-tuple-element.69), channel_id=1, source_target_pairs={{0,24},{1,25},{2,26},{3,27},{4,28},{5,29},{6,30},{7,31},{8,16},{9,... | collective-permute-start | bytes 147464 | tf_op jit(solution)/shard_map/ppermute | solution.py:103
  31.4 2.8 %collective-permute-start.14 = (f32[2,64,128]{2,1,0:T(8,128)S(1)}, f32[2,64,128]{2,1,0:T(8,128)S(1)}, u32[]{:S(2)}, u32[]{:S(2)}) collective-permute-start(f32[2,64,128]{2,1,0:T(8,128)S(1)} %get-tuple-element.72), channel_id=1, source_target_pairs={{0,1},{1,0},{2,3},{3,2},{4,5},{5,4},{6,7},{7,6},{8,9},{9,8},{10,11... | collective-permute-start | bytes 196616 | tf_op jit(solution)/shard_map/ppermute | solution.py:106
  34.2 0.1 shard_map.111
  34.3 4.3 %collective-permute-start.16 = (f32[2,16,128]{2,1,0:T(8,128)S(1)}, f32[2,16,128]{2,1,0:T(8,128)S(1)}, u32[]{:S(2)}, u32[]{:S(2)}) collective-permute-start(f32[2,16,128]{2,1,0:T(8,128)S(1)} %get-tuple-element.74), channel_id=1, source_target_pairs={{0,1},{1,0},{2,3},{3,2},{4,5},{5,4},{6,7},{7,6},{8,9},{9,8},{10,11... | collective-permute-start | bytes 49160 | tf_op jit(solution)/shard_map/ppermute | solution.py:106
  38.7 1.7 %collective-permute-done.16.first_ends = f32[2,16,128]{2,1,0:T(8,128)S(1)} collective-permute-done((f32[2,16,128]{2,1,0:T(8,128)S(1)}, f32[2,16,128]{2,1,0:T(8,128)S(1)}, u32[]{:S(2)}, u32[]{:S(2)}) %collective-permute-start.16) | collective-permute-done | bytes 16416 | tf_op jit(solution)/shard_map/ppermute | solution.py:106
  40.4 1.1 %shard_map.112 = (f32[2,32,16,128]{3,2,1,0:T(8,128)S(1)}, f32[2,32,16,128]{3,2,1,0:T(8,128)S(1)}, f32[32,128]{1,0:T(8,128)S(1)}) custom-call(f32[2,36,16,128]{3,2,1,0:T(8,128)S(1)} %get-tuple-element.70.whole_ref, f32[2,2,40,128]{3,2,1,0:T(8,128)S(1)} %get-tuple-element.71.whole_rows_ref, f32[2,64,128]{2,1,0:T(8,128)S(1)} %collective-permute-done.14.first_lines, ...), custom_call_target="tpu_custom_call" | custom-call | flops 10000000 | bytes 5558272 | tf_op jit(solution)/shard_map/pallas_call | solution.py:723
  41.4 12.7 %all_to_all.11 = f32[32,1,128]{2,1,0:T(1,128)S(1)} all-to-all(f32[32,1,128]{2,1,0:T(1,128)S(1)} %bitcast.5), channel_id=1, replica_groups=mesh['gx'=4,'gy'=8] {'gx','gy'}, dimensions={0} | all-to-all | bytes 32768 | tf_op jit(solution)/shard_map/all_to_all | solution.py:834
  54.1 1.2 %shard_map.113 = (f32[2,32,16,128]{3,2,1,0:T(8,128)}, f32[2,32,16,128]{3,2,1,0:T(8,128)}) custom-call(f32[32,128]{1,0:T(8,128)S(1)} %bitcast.4, f32[2,32,16,128]{3,2,1,0:T(8,128)S(1)} %get-tuple-element.42.load_ref, f32[2,32,16,128]{3,2,1,0:T(8,128)S(1)} %get-tuple-element.79.z_ref, f32[2,32,16,128]{3,2,1,0:T(8,128)S(1)} %get-tuple-element.76.old_image_ref.q_ref, ...), custom_call_target="tpu_custom_call" | custom-call | bytes 3686400 | tf_op jit(solution)/shard_map/pallas_call | solution.py:723
  (33 shorter events, 0.1 us)
Async XLA Ops:
  0.6 1.0 %copy-start = (f32[2,32,16,128]{3,2,1,0:T(8,128)S(1)}, f32[2,32,16,128]{3,2,1,0:T(8,128)}, u32[]{:S(2)}) copy-start(f32[2,32,16,128]{3,2,1,0:T(8,128)} %load_hbm.1) | copy-start | bytes 1572868
  1.7 0.9 %copy-start.1 = (s32[32,16,128]{2,1,0:T(8,128)S(1)}, s32[32,16,128]{2,1,0:T(8,128)}, u32[]{:S(2)}) copy-start(s32[32,16,128]{2,1,0:T(8,128)} %zones_hbm.1) | copy-start | bytes 786436
  2.9 12.4 %collective-permute-start.2 = (f32[4,32,128]{2,1,0:T(8,128)S(1)}, f32[4,32,128]{2,1,0:T(8,128)S(1)}, u32[]{:S(2)}, u32[]{:S(2)}) collective-permute-start(f32[4,32,128]{2,1,0:T(8,128)S(1)} %get-tuple-element.45), channel_id=1, source_target_pairs={{0,1},{1,0},{2,3},{3,2},{4,5},{5,4},{6,7},{7,6},{8,9},{9,8},{10,11... | collective-permute-start | bytes 196616 | tf_op jit(solution)/shard_map/ppermute | solution.py:106
  5.9 9.4 %collective-permute-start.3 = (f32[4,32,128]{2,1,0:T(8,128)S(1)}, f32[4,32,128]{2,1,0:T(8,128)S(1)}, u32[]{:S(2)}, u32[]{:S(2)}) collective-permute-start(f32[4,32,128]{2,1,0:T(8,128)S(1)} %get-tuple-element.46), channel_id=1, source_target_pairs={{0,8},{1,2},{2,1},{3,4},{4,3},{5,6},{6,5},{7,15},{8,0},{9,10},{10,... | collective-permute-start | bytes 196616 | tf_op jit(solution)/shard_map/ppermute | solution.py:105
  5.9 4.6 %collective-permute-start = (f32[4,16,128]{2,1,0:T(8,128)S(1)}, f32[4,16,128]{2,1,0:T(8,128)S(1)}, u32[]{:S(2)}, u32[]{:S(2)}) collective-permute-start(f32[4,16,128]{2,1,0:T(8,128)S(1)} %get-tuple-element.43), channel_id=1, source_target_pairs={{0,8},{1,9},{2,10},{3,11},{4,12},{5,13},{6,14},{7,15},{8,0},{9,1},... | collective-permute-start | bytes 98312 | tf_op jit(solution)/shard_map/ppermute | solution.py:102
  6.4 4.1 %collective-permute-start.1 = (f32[4,16,128]{2,1,0:T(8,128)S(1)}, f32[4,16,128]{2,1,0:T(8,128)S(1)}, u32[]{:S(2)}, u32[]{:S(2)}) collective-permute-start(f32[4,16,128]{2,1,0:T(8,128)S(1)} %get-tuple-element.44), channel_id=1, source_target_pairs={{0,24},{1,25},{2,26},{3,27},{4,28},{5,29},{6,30},{7,31},{8,16},{9,... | collective-permute-start | bytes 98312 | tf_op jit(solution)/shard_map/ppermute | solution.py:103
  7.5 0.7 %copy-start.2 = (f32[2,8]{1,0:T(2,128)S(1)}, f32[2,8]{1,0:T(2,128)}, u32[]{:S(2)}) copy-start(f32[2,8]{1,0:T(2,128)} %conductance_ref.3) | copy-start | bytes 196
  8.2 0.7 %copy-start.3 = (f32[2,8]{1,0:T(2,128)S(1)}, f32[2,8]{1,0:T(2,128)}, u32[]{:S(2)}) copy-start(f32[2,8]{1,0:T(2,128)} %capacity_ref.3) | copy-start | bytes 196
  8.9 6.4 %copy-start.5 = (bf16[336,1008]{1,0:T(8,128)(2,1)S(1)}, bf16[336,1008]{1,0:T(8,128)(2,1)}, u32[]{:S(2)}) copy-start(bf16[336,1008]{1,0:T(8,128)(2,1)} %constant.9.clone.c1) | copy-start | bytes 2032132
  8.9 6.4 %copy-start.6 = (bf16[336,1008]{1,0:T(8,128)(2,1)S(1)}, bf16[336,1008]{1,0:T(8,128)(2,1)}, u32[]{:S(2)}) copy-start(bf16[336,1008]{1,0:T(8,128)(2,1)} %constant.8.clone.c0) | copy-start | bytes 2032132
  8.9 6.4 %copy-start.7 = (bf16[384,144]{1,0:T(8,128)(2,1)S(1)}, bf16[384,144]{1,0:T(8,128)(2,1)}, u32[]{:S(2)}) copy-start(bf16[384,144]{1,0:T(8,128)(2,1)} %constant.10.clone.c2) | copy-start | bytes 331780
  8.9 6.4 %copy-start.8 = (bf16[144,256]{1,0:T(8,128)(2,1)S(1)}, bf16[144,256]{1,0:T(8,128)(2,1)}, u32[]{:S(2)}) copy-start(bf16[144,256]{1,0:T(8,128)(2,1)} %constant.11.clone.c3) | copy-start | bytes 221188
  10.5 4.7 %collective-permute-start.4 = (f32[16,128]{1,0:T(8,128)S(1)}, f32[16,128]{1,0:T(8,128)S(1)}, u32[]{:S(2)}, u32[]{:S(2)}) collective-permute-start(f32[16,128]{1,0:T(8,128)S(1)} %get-tuple-element.48), channel_id=1, source_target_pairs={{0,1},{1,0},{2,3},{3,2},{4,5},{5,4},{6,7},{7,6},{8,9},{9,8},{10,11... | collective-permute-start | bytes 24584 | tf_op jit(solution)/shard_map/ppermute | solution.py:106
  13.6 1.6 %collective-permute-start.5 = (f32[16,128]{1,0:T(8,128)S(1)}, f32[16,128]{1,0:T(8,128)S(1)}, u32[]{:S(2)}, u32[]{:S(2)}) collective-permute-start(f32[16,128]{1,0:T(8,128)S(1)} %get-tuple-element.49), channel_id=1, source_target_pairs={{0,8},{1,2},{2,1},{3,4},{4,3},{5,6},{6,5},{7,15},{8,0},{9,10},{10,... | collective-permute-start | bytes 24584 | tf_op jit(solution)/shard_map/ppermute | solution.py:105
  15.3 9.9 %copy-start.4 = (f32[8]{0:T(128)S(1)}, f32[8]{0:T(128)}, u32[]{:S(2)}) copy-start(f32[8]{0:T(128)} %coupling_ref.1) | copy-start | bytes 100
  17.5 3.7 %collective-permute-start.6 = (f32[2,3,24,128]{3,2,1,0:T(8,128)S(1)}, f32[2,3,24,128]{3,2,1,0:T(8,128)S(1)}, u32[]{:S(2)}, u32[]{:S(2)}) collective-permute-start(f32[2,3,24,128]{3,2,1,0:T(8,128)S(1)} %get-tuple-element.52), channel_id=1, source_target_pairs={{0,8},{1,9},{2,10},{3,11},{4,12},{5,13},{6,14},{7,15},{8,0},{9,1},... | collective-permute-start | bytes 221192 | tf_op jit(solution)/shard_map/ppermute | solution.py:102
  17.6 4.1 %collective-permute-start.7 = (f32[2,3,24,128]{3,2,1,0:T(8,128)S(1)}, f32[2,3,24,128]{3,2,1,0:T(8,128)S(1)}, u32[]{:S(2)}, u32[]{:S(2)}) collective-permute-start(f32[2,3,24,128]{3,2,1,0:T(8,128)S(1)} %get-tuple-element.53), channel_id=1, source_target_pairs={{0,24},{1,25},{2,26},{3,27},{4,28},{5,29},{6,30},{7,31},{8,16},{9,... | collective-permute-start | bytes 221192 | tf_op jit(solution)/shard_map/ppermute | solution.py:103
  18.2 8.7 %collective-permute-start.8 = (f32[2,96,128]{2,1,0:T(8,128)S(1)}, f32[2,96,128]{2,1,0:T(8,128)S(1)}, u32[]{:S(2)}, u32[]{:S(2)}) collective-permute-start(f32[2,96,128]{2,1,0:T(8,128)S(1)} %get-tuple-element.56), channel_id=1, source_target_pairs={{0,1},{1,0},{2,3},{3,2},{4,5},{5,4},{6,7},{7,6},{8,9},{9,8},{10,11... | collective-permute-start | bytes 294920 | tf_op jit(solution)/shard_map/ppermute | solution.py:106
  21.2 5.7 %collective-permute-start.9 = (f32[2,96,128]{2,1,0:T(8,128)S(1)}, f32[2,96,128]{2,1,0:T(8,128)S(1)}, u32[]{:S(2)}, u32[]{:S(2)}) collective-permute-start(f32[2,96,128]{2,1,0:T(8,128)S(1)} %get-tuple-element.57), channel_id=1, source_target_pairs={{0,8},{1,2},{2,1},{3,4},{4,3},{5,6},{6,5},{7,15},{8,0},{9,10},{10,... | collective-permute-start | bytes 294920 | tf_op jit(solution)/shard_map/ppermute | solution.py:105
  21.7 5.2 %collective-permute-start.10 = (f32[2,24,128]{2,1,0:T(8,128)S(1)}, f32[2,24,128]{2,1,0:T(8,128)S(1)}, u32[]{:S(2)}, u32[]{:S(2)}) collective-permute-start(f32[2,24,128]{2,1,0:T(8,128)S(1)} %get-tuple-element.58), channel_id=1, source_target_pairs={{0,1},{1,0},{2,3},{3,2},{4,5},{5,4},{6,7},{7,6},{8,9},{9,8},{10,11... | collective-permute-start | bytes 73736 | tf_op jit(solution)/shard_map/ppermute | solution.py:106
  24.8 2.1 %collective-permute-start.11 = (f32[2,24,128]{2,1,0:T(8,128)S(1)}, f32[2,24,128]{2,1,0:T(8,128)S(1)}, u32[]{:S(2)}, u32[]{:S(2)}) collective-permute-start(f32[2,24,128]{2,1,0:T(8,128)S(1)} %get-tuple-element.59), channel_id=1, source_target_pairs={{0,8},{1,2},{2,1},{3,4},{4,3},{5,6},{6,5},{7,15},{8,0},{9,10},{10,... | collective-permute-start | bytes 73736 | tf_op jit(solution)/shard_map/ppermute | solution.py:105
  30.2 4.1 %collective-permute-start.12 = (f32[2,2,24,128]{3,2,1,0:T(8,128)S(1)}, f32[2,2,24,128]{3,2,1,0:T(8,128)S(1)}, u32[]{:S(2)}, u32[]{:S(2)}) collective-permute-start(f32[2,2,24,128]{3,2,1,0:T(8,128)S(1)} %get-tuple-element.68), channel_id=1, source_target_pairs={{0,8},{1,9},{2,10},{3,11},{4,12},{5,13},{6,14},{7,15},{8,0},{9,1},... | collective-permute-start | bytes 147464 | tf_op jit(solution)/shard_map/ppermute | solution.py:102
  30.4 3.9 %collective-permute-start.13 = (f32[2,2,24,128]{3,2,1,0:T(8,128)S(1)}, f32[2,2,24,128]{3,2,1,0:T(8,128)S(1)}, u32[]{:S(2)}, u32[]{:S(2)}) collective-permute-start(f32[2,2,24,128]{3,2,1,0:T(8,128)S(1)} %get-tuple-element.69), channel_id=1, source_target_pairs={{0,24},{1,25},{2,26},{3,27},{4,28},{5,29},{6,30},{7,31},{8,16},{9,... | collective-permute-start | bytes 147464 | tf_op jit(solution)/shard_map/ppermute | solution.py:103
  31.4 8.9 %collective-permute-start.14 = (f32[2,64,128]{2,1,0:T(8,128)S(1)}, f32[2,64,128]{2,1,0:T(8,128)S(1)}, u32[]{:S(2)}, u32[]{:S(2)}) collective-permute-start(f32[2,64,128]{2,1,0:T(8,128)S(1)} %get-tuple-element.72), channel_id=1, source_target_pairs={{0,1},{1,0},{2,3},{3,2},{4,5},{5,4},{6,7},{7,6},{8,9},{9,8},{10,11... | collective-permute-start | bytes 196616 | tf_op jit(solution)/shard_map/ppermute | solution.py:106
  34.2 6.2 %collective-permute-start.15 = (f32[2,64,128]{2,1,0:T(8,128)S(1)}, f32[2,64,128]{2,1,0:T(8,128)S(1)}, u32[]{:S(2)}, u32[]{:S(2)}) collective-permute-start(f32[2,64,128]{2,1,0:T(8,128)S(1)} %get-tuple-element.73), channel_id=1, source_target_pairs={{0,8},{1,2},{2,1},{3,4},{4,3},{5,6},{6,5},{7,15},{8,0},{9,10},{10,... | collective-permute-start | bytes 196616 | tf_op jit(solution)/shard_map/ppermute | solution.py:105
  34.3 6.1 %collective-permute-start.16 = (f32[2,16,128]{2,1,0:T(8,128)S(1)}, f32[2,16,128]{2,1,0:T(8,128)S(1)}, u32[]{:S(2)}, u32[]{:S(2)}) collective-permute-start(f32[2,16,128]{2,1,0:T(8,128)S(1)} %get-tuple-element.74), channel_id=1, source_target_pairs={{0,1},{1,0},{2,3},{3,2},{4,5},{5,4},{6,7},{7,6},{8,9},{9,8},{10,11... | collective-permute-start | bytes 49160 | tf_op jit(solution)/shard_map/ppermute | solution.py:106
  38.7 1.7 %collective-permute-start.17 = (f32[2,16,128]{2,1,0:T(8,128)S(1)}, f32[2,16,128]{2,1,0:T(8,128)S(1)}, u32[]{:S(2)}, u32[]{:S(2)}) collective-permute-start(f32[2,16,128]{2,1,0:T(8,128)S(1)} %get-tuple-element.75), channel_id=1, source_target_pairs={{0,8},{1,2},{2,1},{3,4},{4,3},{5,6},{6,5},{7,15},{8,0},{9,10},{10,... | collective-permute-start | bytes 49160 | tf_op jit(solution)/shard_map/ppermute | solution.py:105

commit v6 on v5

--- a/solution.py
+++ b/solution.py
@@ -304,9 +304,7 @@
         inverse_ref[combo] = 1.0 / (cbar + kbar * summed)
 
 
-def edge_layers_kernel(
-    mesh, load_hbm, zones_hbm, load_ref, zones_ref, even_ref, odd_ref, even_lines, odd_lines, sems
-):
+def edge_layers_kernel(mesh, load_hbm, zones_hbm, load_ref, zones_ref, even_ref, odd_ref, sems):
     copies = [
         pltpu.make_async_copy(load_hbm.at[0], load_ref.at[0], sems.at[0]),
         pltpu.make_async_copy(load_hbm.at[1], load_ref.at[1], sems.at[1]),
@@ -316,43 +314,43 @@
         copy.start()
     flags = standing(mesh)
     last = zones_ref.shape[0] - 1
-    size_y = zones_ref.shape[1]
     for channel in range(4):
         if channel < 3:
             copies[channel].wait()
         if channel < 2:
             low, high = load_ref[channel, 0], load_ref[channel, last]
-            low_line, high_line = load_ref[channel, :, 0], load_ref[channel, :, size_y - 1]
         else:
             low, high = zones_ref[channel - 2].astype(F32), zones_ref[last - 3 + channel].astype(F32)
-            low_line = zones_ref[:, channel - 2].astype(F32)
-            high_line = zones_ref[:, size_y - 4 + channel].astype(F32)
         even_ref[channel] = chosen(flags, EVEN_X, high, low)
         odd_ref[channel] = chosen(flags, EVEN_X, low, high)
-        even_lines[channel] = chosen(flags, EVEN_Y, high_line, low_line)
-        odd_lines[channel] = chosen(flags, EVEN_Y, low_line, high_line)
-
-
-def edge_ends_kernel(mesh, first_ref, second_ref, inverse_ref, even_ref, odd_ref):
+
+
+def edge_lines_kernel(mesh, load_ref, zones_ref, first_ref, second_ref, even_ref, odd_ref):
     flags = standing(mesh)
-    size_y = first_ref.shape[1]
+    size_x, size_y = zones_ref.shape[:2]
     from_low = chosen(flags, EVEN_X, second_ref[...], first_ref[...])
     from_high = chosen(flags, EVEN_X, first_ref[...], second_ref[...])
 
-    def put(row, layer, near, far):
-        to_low, to_high = layer[near : near + 1], layer[far : far + 1]
-        even_ref[row : row + 1] = chosen(flags, EVEN_Y, to_high, to_low)
-        odd_ref[row : row + 1] = chosen(flags, EVEN_Y, to_low, to_high)
-
-    for ref in (even_ref, odd_ref):
-        ref[8:16] = jnp.zeros((8, ref.shape[1]), F32)
-    for field in range(2):
-        put(2 * field, keep(flags, LOW_X, from_low[field]), 0, size_y - 1)
-        put(2 * field + 1, keep(flags, HIGH_X, from_high[field]), 0, size_y - 1)
+    def put(row, to_low, to_high):
+        place = slice(row, row + to_low.shape[0])
+        even_ref[place] = chosen(flags, EVEN_Y, to_high, to_low)
+        odd_ref[place] = chosen(flags, EVEN_Y, to_low, to_high)
+
+    def put_end(row, layer, near, far):
+        put(4 * size_x + row, layer[near : near + 1], layer[far : far + 1])
+
+    blank = jnp.zeros((8, even_ref.shape[1]), F32)
+    put(4 * size_x + 8, blank, blank)
+    for field in range(2):
+        put(field * size_x, load_ref[field, :, 0], load_ref[field, :, size_y - 1])
+        put_end(2 * field, keep(flags, LOW_X, from_low[field]), 0, size_y - 1)
+        put_end(2 * field + 1, keep(flags, HIGH_X, from_high[field]), 0, size_y - 1)
     for line in range(2):
+        far = size_y - 2 + line
+        put((2 + line) * size_x, zones_ref[:, line].astype(F32), zones_ref[:, far].astype(F32))
         for depth in range(2):
-            put(4 + 4 * line + depth, from_low[2 + depth], line, size_y - 2 + line)
-            put(6 + 4 * line + depth, from_high[2 + depth], line, size_y - 2 + line)
+            put_end(4 + 4 * line + depth, from_low[2 + depth], line, far)
+            put_end(6 + 4 * line + depth, from_high[2 + depth], line, far)
 
 
 def looked_up(entries, zone):
@@ -364,7 +362,6 @@
 
 def coefficient_kernel(
     mesh, conductance_ref, capacity_ref, coupling_ref, zones_ref, first_x, second_x, first_y, second_y,
-    first_end, second_end,
     half_ref, mass_ref, face_ref, half_rows_ref, mass_rows_ref, face_rows_ref, line_ref,
 ):
     flags = standing(mesh)
@@ -377,12 +374,9 @@
     size_x, size_y, size_z = zones_ref.shape
     low_x = chosen(flags, EVEN_X, second_x[2:4], first_x[2:4])
     high_x = chosen(flags, EVEN_X, first_x[2:4], second_x[2:4])
-    for side, (lines, ends) in enumerate(
-        (
-            (chosen(flags, EVEN_Y, second_y[2:4], first_y[2:4]), chosen(flags, EVEN_Y, second_end[...], first_end[...])),
-            (chosen(flags, EVEN_Y, first_y[2:4], second_y[2:4]), chosen(flags, EVEN_Y, first_end[...], second_end[...])),
-        )
-    ):
+    for side, (even, odd) in enumerate(((second_y, first_y), (first_y, second_y))):
+        came = chosen(flags, EVEN_Y, even[2 * size_x :], odd[2 * size_x :])
+        lines, ends = (came[:size_x], came[size_x : 2 * size_x]), came[2 * size_x :]
         for line in range(2):
             place = 2 * side + line
             line_ref[place, 0:8] = jnp.zeros((8, size_z), F32)
@@ -448,7 +442,7 @@
 
 
 def first_solve_kernel(
-    mesh, load_ref, first_x, second_x, first_y, second_y, first_end, second_end, inverse_ref, c0, c1, c2, c3,
+    mesh, load_ref, first_x, second_x, first_y, second_y, inverse_ref, c0, c1, c2, c3,
     part_ref, part_rows_ref, even_ref, odd_ref, even_lines, odd_lines, field_ref, rows_ref, before_ref, after_ref,
 ):
     flags = standing(mesh)
@@ -457,12 +451,10 @@
         field_ref[field, 1 : 1 + size_x] = load_ref[field]
         field_ref[field, 0] = keep(flags, LOW_X, chosen(flags, EVEN_X, second_x[field], first_x[field]))
         field_ref[field, 1 + size_x] = keep(flags, HIGH_X, chosen(flags, EVEN_X, first_x[field], second_x[field]))
-        for side, flag, (even, odd), (even_end, odd_end) in (
-            (0, LOW_Y, (second_y, first_y), (second_end, first_end)),
-            (1, HIGH_Y, (first_y, second_y), (first_end, second_end)),
-        ):
-            line = keep(flags, flag, chosen(flags, EVEN_Y, even[field], odd[field]))
-            ends = keep(flags, flag, chosen(flags, EVEN_Y, even_end[0:8], odd_end[0:8]))
+        for side, flag, even, odd in ((0, LOW_Y, second_y, first_y), (1, HIGH_Y, first_y, second_y)):
+            place, after = slice(field * size_x, (field + 1) * size_x), slice(4 * size_x, 4 * size_x + 8)
+            line = keep(flags, flag, chosen(flags, EVEN_Y, even[place], odd[place]))
+            ends = keep(flags, flag, chosen(flags, EVEN_Y, even[after], odd[after]))
             rows_ref[field, side, 0:8] = jnp.zeros((8, line.shape[1]), F32)
             rows_ref[field, side, size_x : size_x + 8] = jnp.zeros((8, line.shape[1]), F32)
             rows_ref[field, side, ROW0 - 1 : ROW0] = ends[2 * field : 2 * field + 1]
@@ -745,12 +737,11 @@
         edge_layers_kernel,
         [],
         [load, zones],
-        [sds(*load.shape), jax.ShapeDtypeStruct(zones.shape, zones.dtype)] + [sds(4, size_y, size_z)] * 2 + [sds(4, size_x, size_z)] * 2,
+        [sds(*load.shape), jax.ShapeDtypeStruct(zones.shape, zones.dtype)] + [sds(4, size_y, size_z)] * 2,
         [pltpu.SemaphoreType.DMA((3,))],
         in_hbm=True,
     )
-    x_halo = swap(mesh, "gx", *packed[:2])
-    y_halo = swap(mesh, "gy", *packed[2:])
+    x_halo = swap(mesh, "gx", *packed)
     (inverse,) = call(
         None,
         divisor_kernel,
@@ -759,13 +750,13 @@
         [sds(2 * boxes, modes, lanes)],
         flops=40_000_000,
     )
-    packed = call(mesh, edge_ends_kernel, [], [*x_halo, inverse], [sds(16, size_z)] * 2)
-    y_ends = swap(mesh, "gy", *packed)
+    packed = call(mesh, edge_lines_kernel, [], [load, zones, *x_halo], [sds(4 * size_x + 16, size_z)] * 2)
+    y_halo = swap(mesh, "gy", *packed)
     half, mass, face, half_lines, mass_lines, face_lines = call(
         mesh,
         coefficient_kernel,
         [conductance, capacity, coupling],
-        [zones, *x_halo, *y_halo, *y_ends],
+        [zones, *x_halo, *y_halo],
         [
             sds(2, size_x + 4, size_y + 16, size_z),
             sds(3, size_x + 2, size_y, size_z),
@@ -799,7 +790,7 @@
         mesh,
         first_solve_kernel,
         [],
-        [load, *x_halo, *y_halo, *y_ends, inverse, *consts],
+        [load, *x_halo, *y_halo, inverse, *consts],
         parts + packed_x[0] + packed_lines[0],
         work,
         3_000_000_000,

time: 55.6 us -> 53.3 us (0.959)
  starting transfers between devices: 23.4 us -> 20.3 us
  waiting for transfers between devices: 3.81 us -> 5.73 us
  local copies, waits for them, and re-layouts: 3.36 us -> 2.01 us
    ppermute x9 -> x8, starting transfers between devices: 20.1 us -> 14.9 us  [swap(): first = lax.ppermute(even_part, AXES, swap_pairs(mesh, axis, False))]
    ppermute x9 -> x8, starting transfers between devices: 3.25 us -> 5.39 us  [swap(): second = lax.ppermute(odd_part, AXES, swap_pairs(mesh, axis, True))]
    unnamed x18, local copies, waits for them, and re-layouts: 3.36 us -> 2.01 us
    ppermute x9 -> x8, waiting for transfers between devices: 0.43 us -> 1.68 us  [swap(): second = lax.ppermute(odd_part, AXES, swap_pairs(mesh, axis, True))]
    ppermute x9 -> x8, waiting for transfers between devices: 3.38 us -> 4.04 us  [swap(): first = lax.ppermute(even_part, AXES, swap_pairs(mesh, axis, False))]
  transfers between devices with their start and end apart: 18 -> 16, of which waited for: 3 -> 5; matrix products, arithmetic and copies ran while one was open for 0% -> 0% of each run, Pallas kernels for 6% -> 6%
where the time goes in v6:
time: 53.3 us; the launch traced here: 53.1 us
  starting transfers between devices  20.3 us (38%)
  blocking collectives  13 us (24%)
  Pallas kernels  11.3 us (21%)
  waiting for transfers between devices  5.73 us (11%)
  local copies, waits for them, and re-layouts  2.01 us (4%)
  between operations  0.74 us (1%)
    ppermute x8, starting transfers between devices, swap(): first = lax.ppermute(even_part, AXES, swap_pairs(mesh, axis, False))  14.9 us
    all_to_all x1, blocking collectives, shards(): sums = lax.all_to_all(sums, AXES, 0, 0, tiled=True)  13 us
    pallas_call x10, Pallas kernels, call(): pl.pallas_call(kernel if mesh is None else functools.partial(kernel, mesh...  11.3 us
    ppermute x8, starting transfers between devices, swap(): second = lax.ppermute(odd_part, AXES, swap_pairs(mesh, axis, True))  5.39 us
    ppermute x8, waiting for transfers between devices, swap(): first = lax.ppermute(even_part, AXES, swap_pairs(mesh, axis, False))  4.04 us
    unnamed x18, local copies, waits for them, and re-layouts  2.01 us
    ppermute x8, waiting for transfers between devices, swap(): second = lax.ppermute(odd_part, AXES, swap_pairs(mesh, axis, True))  1.68 us
  transfers between devices with their start and end apart: 16, of which 5 were waited for; matrix products, arithmetic and copies ran while one was open for 0% of the time, Pallas kernels for 6%

profile of v6, /device:TPU:0, one launch (start us, length us, event | category | flops | bytes accessed | tf_op | source)
XLA Modules:
  0.0 53.1 jit_solution(8715229666433628723)
XLA Ops:
  0.6 1.0 %copy-done = f32[2,32,16,128]{3,2,1,0:T(8,128)S(1)} copy-done((f32[2,32,16,128]{3,2,1,0:T(8,128)S(1)}, f32[2,32,16,128]{3,2,1,0:T(8,128)}, u32[]{:S(2)}) %copy-start) | copy-done | bytes 524312
  1.7 0.9 %copy-done.1 = s32[32,16,128]{2,1,0:T(8,128)S(1)} copy-done((s32[32,16,128]{2,1,0:T(8,128)S(1)}, s32[32,16,128]{2,1,0:T(8,128)}, u32[]{:S(2)}) %copy-start.1) | copy-done | bytes 262168
  2.6 0.1 shard_map.104
  2.7 0.5 collective-permute-start
  3.3 2.6 %collective-permute-start.1 = (f32[4,16,128]{2,1,0:T(8,128)S(1)}, f32[4,16,128]{2,1,0:T(8,128)S(1)}, u32[]{:S(2)}, u32[]{:S(2)}) collective-permute-start(f32[4,16,128]{2,1,0:T(8,128)S(1)} %get-tuple-element.42), channel_id=1, source_target_pairs={{0,24},{1,25},{2,26},{3,27},{4,28},{5,29},{6,30},{7,31},{8,16},{9,... | collective-permute-start | bytes 98312 | tf_op jit(solution)/shard_map/ppermute | solution.py:103
  5.9 0.0 collective-permute-done.first_ref.first_x
  5.9 1.7 %collective-permute-done.1.second_ref.second_x = f32[4,16,128]{2,1,0:T(8,128)S(1)} collective-permute-done((f32[4,16,128]{2,1,0:T(8,128)S(1)}, f32[4,16,128]{2,1,0:T(8,128)S(1)}, u32[]{:S(2)}, u32[]{:S(2)}) %collective-permute-start.1) | collective-permute-done | bytes 32800 | tf_op jit(solution)/shard_map/ppermute | solution.py:103
  7.6 0.2 shard_map.105
  7.8 1.7 %collective-permute-start.2 = (f32[144,128]{1,0:T(8,128)S(1)}, f32[144,128]{1,0:T(8,128)S(1)}, u32[]{:S(2)}, u32[]{:S(2)}) collective-permute-start(f32[144,128]{1,0:T(8,128)S(1)} %get-tuple-element.44), channel_id=1, source_target_pairs={{0,1},{1,0},{2,3},{3,2},{4,5},{5,4},{6,7},{7,6},{8,9},{9,8},{10,11... | collective-permute-start | bytes 221192 | tf_op jit(solution)/shard_map/ppermute | solution.py:106
  9.4 0.2 collective-permute-start.3
  9.6 1.6 %shard_map.106.inverse_ref = f32[4,336,144]{2,1,0:T(8,128)S(1)} custom-call(f32[2,8]{1,0:T(2,128)S(1)} %copy-done.2, f32[2,8]{1,0:T(2,128)S(1)} %copy-done.3, s32[32,16,128]{2,1,0:T(8,128)S(1)} %get-tuple-element.43.zones_ref), custom_call_target="tpu_custom_call" | custom-call | flops 40000000 | bytes 1036288 | tf_op jit(solution)/shard_map/pallas_call | solution.py:715
  11.2 0.0 copy-start.4
  11.2 2.0 %collective-permute-done.2.first_y = f32[144,128]{1,0:T(8,128)S(1)} collective-permute-done((f32[144,128]{1,0:T(8,128)S(1)}, f32[144,128]{1,0:T(8,128)S(1)}, u32[]{:S(2)}, u32[]{:S(2)}) %collective-permute-start.2) | collective-permute-done | bytes 73760 | tf_op jit(solution)/shard_map/ppermute | solution.py:106
  13.2 2.2 %shard_map.107 = (f32[2,34,16,128]{3,2,1,0:T(8,128)S(1)}, f32[2,2,40,128]{3,2,1,0:T(8,128)S(1)}, f32[2,3,24,128]{3,2,1,0:T(8,128)S(1)}, f32[2,3,24,128]{3,2,1,0:...) custom-call(f32[2,32,16,128]{3,2,1,0:T(8,128)S(1)} %get-tuple-element.40.load_ref, ...), custom_call_target="tpu_custom_call" | custom-call | flops 3000000000 | bytes 4033536 | tf_op jit(solution)/shard_map/pallas_call | solution.py:715
  15.4 0.1 collective-permute-start.4
  15.4 1.6 %collective-permute-start.5 = (f32[2,3,24,128]{3,2,1,0:T(8,128)S(1)}, f32[2,3,24,128]{3,2,1,0:T(8,128)S(1)}, u32[]{:S(2)}, u32[]{:S(2)}) collective-permute-start(f32[2,3,24,128]{3,2,1,0:T(8,128)S(1)} %get-tuple-element.49), channel_id=1, source_target_pairs={{0,24},{1,25},{2,26},{3,27},{4,28},{5,29},{6,30},{7,31},{8,16},{9,... | collective-permute-start | bytes 221192 | tf_op jit(solution)/shard_map/ppermute | solution.py:103
  17.1 2.5 %collective-permute-start.6 = (f32[2,96,128]{2,1,0:T(8,128)S(1)}, f32[2,96,128]{2,1,0:T(8,128)S(1)}, u32[]{:S(2)}, u32[]{:S(2)}) collective-permute-start(f32[2,96,128]{2,1,0:T(8,128)S(1)} %get-tuple-element.52), channel_id=1, source_target_pairs={{0,1},{1,0},{2,3},{3,2},{4,5},{5,4},{6,7},{7,6},{8,9},{9,8},{10,11... | collective-permute-start | bytes 294920 | tf_op jit(solution)/shard_map/ppermute | solution.py:106
  19.5 0.1 shard_map.108
  19.6 3.1 %collective-permute-start.8 = (f32[2,24,128]{2,1,0:T(8,128)S(1)}, f32[2,24,128]{2,1,0:T(8,128)S(1)}, u32[]{:S(2)}, u32[]{:S(2)}) collective-permute-start(f32[2,24,128]{2,1,0:T(8,128)S(1)} %get-tuple-element.54), channel_id=1, source_target_pairs={{0,1},{1,0},{2,3},{3,2},{4,5},{5,4},{6,7},{7,6},{8,9},{9,8},{10,11... | collective-permute-start | bytes 73736 | tf_op jit(solution)/shard_map/ppermute | solution.py:106
  22.7 1.6 %shard_map.109 = (f32[2,36,32,128]{3,2,1,0:T(8,128)S(1)}, f32[3,34,16,128]{3,2,1,0:T(8,128)S(1)}, f32[2,2,34,16,128]{4,3,2,1,0:T(8,128)S(1)}, f32[2,6,40,128]{3,...) custom-call(f32[2,8]{1,0:T(2,128)S(1)} %copy-done.2, f32[2,8]{1,0:T(2,128)S(1)} %copy-done.3, ...), custom_call_target="tpu_custom_call" | custom-call | flops 20000000 | bytes 4136960 | tf_op jit(solution)/shard_map/pallas_call | solution.py:715
  24.4 0.1 collective-permute-done.6.first_lines
  24.5 0.2 collective-permute-done.8.first_ends
  24.7 3.3 %shard_map.110 = (f32[2,32,16,128]{3,2,1,0:T(8,128)S(1)}, f32[2,32,16,128]{3,2,1,0:T(8,128)S(1)}, f32[8,128]{1,0:T(8,128)S(1)}, f32[2,34,16,128]{3,2,1,0:T(8,128...) custom-call(f32[2,36,16,128]{3,2,1,0:T(8,128)S(1)} %get-tuple-elemen, ...), custom_call_target="tpu_custom_call" | custom-call | flops 3000000000 | bytes 9337856 | tf_op jit(solution)/shard_map/pallas_call | solution.py:715
  28.0 0.3 collective-permute-start.10
  28.2 0.9 %collective-permute-start.11 = (f32[2,2,24,128]{3,2,1,0:T(8,128)S(1)}, f32[2,2,24,128]{3,2,1,0:T(8,128)S(1)}, u32[]{:S(2)}, u32[]{:S(2)}) collective-permute-start(f32[2,2,24,128]{3,2,1,0:T(8,128)S(1)} %get-tuple-element.65), channel_id=1, source_target_pairs={{0,24},{1,25},{2,26},{3,27},{4,28},{5,29},{6,30},{7,31},{8,16},{9,... | collective-permute-start | bytes 147464 | tf_op jit(solution)/shard_map/ppermute | solution.py:103
  29.2 2.8 %collective-permute-start.12 = (f32[2,64,128]{2,1,0:T(8,128)S(1)}, f32[2,64,128]{2,1,0:T(8,128)S(1)}, u32[]{:S(2)}, u32[]{:S(2)}) collective-permute-start(f32[2,64,128]{2,1,0:T(8,128)S(1)} %get-tuple-element.68), channel_id=1, source_target_pairs={{0,1},{1,0},{2,3},{3,2},{4,5},{5,4},{6,7},{7,6},{8,9},{9,8},{10,11... | collective-permute-start | bytes 196616 | tf_op jit(solution)/shard_map/ppermute | solution.py:106
  31.9 0.1 shard_map.111
  32.0 4.0 %collective-permute-start.14 = (f32[2,16,128]{2,1,0:T(8,128)S(1)}, f32[2,16,128]{2,1,0:T(8,128)S(1)}, u32[]{:S(2)}, u32[]{:S(2)}) collective-permute-start(f32[2,16,128]{2,1,0:T(8,128)S(1)} %get-tuple-element.70), channel_id=1, source_target_pairs={{0,1},{1,0},{2,3},{3,2},{4,5},{5,4},{6,7},{7,6},{8,9},{9,8},{10,11... | collective-permute-start | bytes 49160 | tf_op jit(solution)/shard_map/ppermute | solution.py:106
  36.1 1.7 %collective-permute-done.14.first_ends = f32[2,16,128]{2,1,0:T(8,128)S(1)} collective-permute-done((f32[2,16,128]{2,1,0:T(8,128)S(1)}, f32[2,16,128]{2,1,0:T(8,128)S(1)}, u32[]{:S(2)}, u32[]{:S(2)}) %collective-permute-start.14) | collective-permute-done | bytes 16416 | tf_op jit(solution)/shard_map/ppermute | solution.py:106
  37.8 1.1 %shard_map.112 = (f32[2,32,16,128]{3,2,1,0:T(8,128)S(1)}, f32[2,32,16,128]{3,2,1,0:T(8,128)S(1)}, f32[32,128]{1,0:T(8,128)S(1)}) custom-call(f32[2,36,16,128]{3,2,1,0:T(8,128)S(1)} %get-tuple-element.66.whole_ref, f32[2,2,40,128]{3,2,1,0:T(8,128)S(1)} %get-tuple-element.67.whole_rows_ref, f32[2,64,128]{2,1,0:T(8,128)S(1)} %collective-permute-done.12.first_lines, ...), custom_call_target="tpu_custom_call" | custom-call | flops 10000000 | bytes 5558272 | tf_op jit(solution)/shard_map/pallas_call | solution.py:715
  38.9 13.0 %all_to_all.11 = f32[32,1,128]{2,1,0:T(1,128)S(1)} all-to-all(f32[32,1,128]{2,1,0:T(1,128)S(1)} %bitcast.5), channel_id=1, replica_groups=mesh['gx'=4,'gy'=8] {'gx','gy'}, dimensions={0} | all-to-all | bytes 32768 | tf_op jit(solution)/shard_map/all_to_all | solution.py:825
  51.9 1.2 %shard_map.113 = (f32[2,32,16,128]{3,2,1,0:T(8,128)}, f32[2,32,16,128]{3,2,1,0:T(8,128)}) custom-call(f32[32,128]{1,0:T(8,128)S(1)} %bitcast.4, f32[2,32,16,128]{3,2,1,0:T(8,128)S(1)} %get-tuple-element.40.load_ref, f32[2,32,16,128]{3,2,1,0:T(8,128)S(1)} %get-tuple-element.75.z_ref, f32[2,32,16,128]{3,2,1,0:T(8,128)S(1)} %get-tuple-element.72.old_image_ref.q_ref, ...), custom_call_target="tpu_custom_call" | custom-call | bytes 3686400 | tf_op jit(solution)/shard_map/pallas_call | solution.py:715
  (29 shorter events, 0.1 us)
Async XLA Ops:
  0.6 1.0 %copy-start = (f32[2,32,16,128]{3,2,1,0:T(8,128)S(1)}, f32[2,32,16,128]{3,2,1,0:T(8,128)}, u32[]{:S(2)}) copy-start(f32[2,32,16,128]{3,2,1,0:T(8,128)} %load_hbm.1) | copy-start | bytes 1572868
  1.7 0.9 %copy-start.1 = (s32[32,16,128]{2,1,0:T(8,128)S(1)}, s32[32,16,128]{2,1,0:T(8,128)}, u32[]{:S(2)}) copy-start(s32[32,16,128]{2,1,0:T(8,128)} %zones_hbm.1) | copy-start | bytes 786436
  2.6 7.0 %copy-start.2 = (f32[2,8]{1,0:T(2,128)S(1)}, f32[2,8]{1,0:T(2,128)}, u32[]{:S(2)}) copy-start(f32[2,8]{1,0:T(2,128)} %conductance_ref.3) | copy-start | bytes 196
  2.6 7.0 %copy-start.3 = (f32[2,8]{1,0:T(2,128)S(1)}, f32[2,8]{1,0:T(2,128)}, u32[]{:S(2)}) copy-start(f32[2,8]{1,0:T(2,128)} %capacity_ref.3) | copy-start | bytes 196
  2.7 3.2 %collective-permute-start = (f32[4,16,128]{2,1,0:T(8,128)S(1)}, f32[4,16,128]{2,1,0:T(8,128)S(1)}, u32[]{:S(2)}, u32[]{:S(2)}) collective-permute-start(f32[4,16,128]{2,1,0:T(8,128)S(1)} %get-tuple-element.41), channel_id=1, source_target_pairs={{0,8},{1,9},{2,10},{3,11},{4,12},{5,13},{6,14},{7,15},{8,0},{9,1},... | collective-permute-start | bytes 98312 | tf_op jit(solution)/shard_map/ppermute | solution.py:102
  3.3 4.3 %collective-permute-start.1 = (f32[4,16,128]{2,1,0:T(8,128)S(1)}, f32[4,16,128]{2,1,0:T(8,128)S(1)}, u32[]{:S(2)}, u32[]{:S(2)}) collective-permute-start(f32[4,16,128]{2,1,0:T(8,128)S(1)} %get-tuple-element.42), channel_id=1, source_target_pairs={{0,24},{1,25},{2,26},{3,27},{4,28},{5,29},{6,30},{7,31},{8,16},{9,... | collective-permute-start | bytes 98312 | tf_op jit(solution)/shard_map/ppermute | solution.py:103
  7.6 5.6 %copy-start.5 = (bf16[336,1008]{1,0:T(8,128)(2,1)S(1)}, bf16[336,1008]{1,0:T(8,128)(2,1)}, u32[]{:S(2)}) copy-start(bf16[336,1008]{1,0:T(8,128)(2,1)} %constant.9.clone.c1) | copy-start | bytes 2032132
  7.6 5.6 %copy-start.6 = (bf16[336,1008]{1,0:T(8,128)(2,1)S(1)}, bf16[336,1008]{1,0:T(8,128)(2,1)}, u32[]{:S(2)}) copy-start(bf16[336,1008]{1,0:T(8,128)(2,1)} %constant.8.clone.c0) | copy-start | bytes 2032132
  7.6 5.6 %copy-start.7 = (bf16[384,144]{1,0:T(8,128)(2,1)S(1)}, bf16[384,144]{1,0:T(8,128)(2,1)}, u32[]{:S(2)}) copy-start(bf16[384,144]{1,0:T(8,128)(2,1)} %constant.10.clone.c2) | copy-start | bytes 331780
  7.6 5.6 %copy-start.8 = (bf16[144,256]{1,0:T(8,128)(2,1)S(1)}, bf16[144,256]{1,0:T(8,128)(2,1)}, u32[]{:S(2)}) copy-start(bf16[144,256]{1,0:T(8,128)(2,1)} %constant.11.clone.c3) | copy-start | bytes 221188
  7.8 5.4 %collective-permute-start.2 = (f32[144,128]{1,0:T(8,128)S(1)}, f32[144,128]{1,0:T(8,128)S(1)}, u32[]{:S(2)}, u32[]{:S(2)}) collective-permute-start(f32[144,128]{1,0:T(8,128)S(1)} %get-tuple-element.44), channel_id=1, source_target_pairs={{0,1},{1,0},{2,3},{3,2},{4,5},{5,4},{6,7},{7,6},{8,9},{9,8},{10,11... | collective-permute-start | bytes 221192 | tf_op jit(solution)/shard_map/ppermute | solution.py:106
  9.4 3.8 %collective-permute-start.3 = (f32[144,128]{1,0:T(8,128)S(1)}, f32[144,128]{1,0:T(8,128)S(1)}, u32[]{:S(2)}, u32[]{:S(2)}) collective-permute-start(f32[144,128]{1,0:T(8,128)S(1)} %get-tuple-element.45), channel_id=1, source_target_pairs={{0,8},{1,2},{2,1},{3,4},{4,3},{5,6},{6,5},{7,15},{8,0},{9,10},{10,... | collective-permute-start | bytes 221192 | tf_op jit(solution)/shard_map/ppermute | solution.py:105
  11.2 11.6 %copy-start.4 = (f32[8]{0:T(128)S(1)}, f32[8]{0:T(128)}, u32[]{:S(2)}) copy-start(f32[8]{0:T(128)} %coupling_ref.1) | copy-start | bytes 100
  15.4 4.2 %collective-permute-start.4 = (f32[2,3,24,128]{3,2,1,0:T(8,128)S(1)}, f32[2,3,24,128]{3,2,1,0:T(8,128)S(1)}, u32[]{:S(2)}, u32[]{:S(2)}) collective-permute-start(f32[2,3,24,128]{3,2,1,0:T(8,128)S(1)} %get-tuple-element.48), channel_id=1, source_target_pairs={{0,8},{1,9},{2,10},{3,11},{4,12},{5,13},{6,14},{7,15},{8,0},{9,1},... | collective-permute-start | bytes 221192 | tf_op jit(solution)/shard_map/ppermute | solution.py:102
  15.4 4.1 %collective-permute-start.5 = (f32[2,3,24,128]{3,2,1,0:T(8,128)S(1)}, f32[2,3,24,128]{3,2,1,0:T(8,128)S(1)}, u32[]{:S(2)}, u32[]{:S(2)}) collective-permute-start(f32[2,3,24,128]{3,2,1,0:T(8,128)S(1)} %get-tuple-element.49), channel_id=1, source_target_pairs={{0,24},{1,25},{2,26},{3,27},{4,28},{5,29},{6,30},{7,31},{8,16},{9,... | collective-permute-start | bytes 221192 | tf_op jit(solution)/shard_map/ppermute | solution.py:103
  17.1 7.4 %collective-permute-start.6 = (f32[2,96,128]{2,1,0:T(8,128)S(1)}, f32[2,96,128]{2,1,0:T(8,128)S(1)}, u32[]{:S(2)}, u32[]{:S(2)}) collective-permute-start(f32[2,96,128]{2,1,0:T(8,128)S(1)} %get-tuple-element.52), channel_id=1, source_target_pairs={{0,1},{1,0},{2,3},{3,2},{4,5},{5,4},{6,7},{7,6},{8,9},{9,8},{10,11... | collective-permute-start | bytes 294920 | tf_op jit(solution)/shard_map/ppermute | solution.py:106
  19.5 5.0 %collective-permute-start.7 = (f32[2,96,128]{2,1,0:T(8,128)S(1)}, f32[2,96,128]{2,1,0:T(8,128)S(1)}, u32[]{:S(2)}, u32[]{:S(2)}) collective-permute-start(f32[2,96,128]{2,1,0:T(8,128)S(1)} %get-tuple-element.53), channel_id=1, source_target_pairs={{0,8},{1,2},{2,1},{3,4},{4,3},{5,6},{6,5},{7,15},{8,0},{9,10},{10,... | collective-permute-start | bytes 294920 | tf_op jit(solution)/shard_map/ppermute | solution.py:105
  19.6 5.1 %collective-permute-start.8 = (f32[2,24,128]{2,1,0:T(8,128)S(1)}, f32[2,24,128]{2,1,0:T(8,128)S(1)}, u32[]{:S(2)}, u32[]{:S(2)}) collective-permute-start(f32[2,24,128]{2,1,0:T(8,128)S(1)} %get-tuple-element.54), channel_id=1, source_target_pairs={{0,1},{1,0},{2,3},{3,2},{4,5},{5,4},{6,7},{7,6},{8,9},{9,8},{10,11... | collective-permute-start | bytes 73736 | tf_op jit(solution)/shard_map/ppermute | solution.py:106
  22.7 2.0 %collective-permute-start.9 = (f32[2,24,128]{2,1,0:T(8,128)S(1)}, f32[2,24,128]{2,1,0:T(8,128)S(1)}, u32[]{:S(2)}, u32[]{:S(2)}) collective-permute-start(f32[2,24,128]{2,1,0:T(8,128)S(1)} %get-tuple-element.55), channel_id=1, source_target_pairs={{0,8},{1,2},{2,1},{3,4},{4,3},{5,6},{6,5},{7,15},{8,0},{9,10},{10,... | collective-permute-start | bytes 73736 | tf_op jit(solution)/shard_map/ppermute | solution.py:105
  28.0 4.0 %collective-permute-start.10 = (f32[2,2,24,128]{3,2,1,0:T(8,128)S(1)}, f32[2,2,24,128]{3,2,1,0:T(8,128)S(1)}, u32[]{:S(2)}, u32[]{:S(2)}) collective-permute-start(f32[2,2,24,128]{3,2,1,0:T(8,128)S(1)} %get-tuple-element.64), channel_id=1, source_target_pairs={{0,8},{1,9},{2,10},{3,11},{4,12},{5,13},{6,14},{7,15},{8,0},{9,1},... | collective-permute-start | bytes 147464 | tf_op jit(solution)/shard_map/ppermute | solution.py:102
  28.2 3.7 %collective-permute-start.11 = (f32[2,2,24,128]{3,2,1,0:T(8,128)S(1)}, f32[2,2,24,128]{3,2,1,0:T(8,128)S(1)}, u32[]{:S(2)}, u32[]{:S(2)}) collective-permute-start(f32[2,2,24,128]{3,2,1,0:T(8,128)S(1)} %get-tuple-element.65), channel_id=1, source_target_pairs={{0,24},{1,25},{2,26},{3,27},{4,28},{5,29},{6,30},{7,31},{8,16},{9,... | collective-permute-start | bytes 147464 | tf_op jit(solution)/shard_map/ppermute | solution.py:103
  29.2 8.6 %collective-permute-start.12 = (f32[2,64,128]{2,1,0:T(8,128)S(1)}, f32[2,64,128]{2,1,0:T(8,128)S(1)}, u32[]{:S(2)}, u32[]{:S(2)}) collective-permute-start(f32[2,64,128]{2,1,0:T(8,128)S(1)} %get-tuple-element.68), channel_id=1, source_target_pairs={{0,1},{1,0},{2,3},{3,2},{4,5},{5,4},{6,7},{7,6},{8,9},{9,8},{10,11... | collective-permute-start | bytes 196616 | tf_op jit(solution)/shard_map/ppermute | solution.py:106
  31.9 5.9 %collective-permute-start.13 = (f32[2,64,128]{2,1,0:T(8,128)S(1)}, f32[2,64,128]{2,1,0:T(8,128)S(1)}, u32[]{:S(2)}, u32[]{:S(2)}) collective-permute-start(f32[2,64,128]{2,1,0:T(8,128)S(1)} %get-tuple-element.69), channel_id=1, source_target_pairs={{0,8},{1,2},{2,1},{3,4},{4,3},{5,6},{6,5},{7,15},{8,0},{9,10},{10,... | collective-permute-start | bytes 196616 | tf_op jit(solution)/shard_map/ppermute | solution.py:105
  32.0 5.8 %collective-permute-start.14 = (f32[2,16,128]{2,1,0:T(8,128)S(1)}, f32[2,16,128]{2,1,0:T(8,128)S(1)}, u32[]{:S(2)}, u32[]{:S(2)}) collective-permute-start(f32[2,16,128]{2,1,0:T(8,128)S(1)} %get-tuple-element.70), channel_id=1, source_target_pairs={{0,1},{1,0},{2,3},{3,2},{4,5},{5,4},{6,7},{7,6},{8,9},{9,8},{10,11... | collective-permute-start | bytes 49160 | tf_op jit(solution)/shard_map/ppermute | solution.py:106
  36.1 1.7 %collective-permute-start.15 = (f32[2,16,128]{2,1,0:T(8,128)S(1)}, f32[2,16,128]{2,1,0:T(8,128)S(1)}, u32[]{:S(2)}, u32[]{:S(2)}) collective-permute-start(f32[2,16,128]{2,1,0:T(8,128)S(1)} %get-tuple-element.71), channel_id=1, source_target_pairs={{0,8},{1,2},{2,1},{3,4},{4,3},{5,6},{6,5},{7,15},{8,0},{9,10},{10,... | collective-permute-start | bytes 49160 | tf_op jit(solution)/shard_map/ppermute | solution.py:105

commit v7 on v6

--- a/solution.py
+++ b/solution.py
@@ -39,29 +39,35 @@
     return 4.0 * np.sin(np.pi * (np.arange(SPAN) + 1) / (2 * (SPAN + 1))) ** 2
 
 
-def plane_layout():
-    places = [(x, y + 1) for x in range(SPAN) for y in range(BOX)]
-    for y in (0, SPAN - 1):
-        for position in range(24):
-            x = position - (ROW0 - 1)
-            places.append((x, y) if 0 <= x < SPAN else None)
-    return places
-
-
-def constants(size_z):
+def line_places(y):
+    return [(x, y) if 0 <= x < SPAN else None for x in range(1 - ROW0, 25 - ROW0)]
+
+
+def layer_places(x):
+    return [(x, y + 1) for y in range(BOX)]
+
+
+def plane_matrix(places):
     basis = sine_basis()
-    places = plane_layout()
-    rows = len(places)
     modes = SPAN * SPAN
-    padded_modes = round_up(modes, 16)
-    plane = np.zeros((padded_modes, rows))
+    plane = np.zeros((round_up(modes, 16), len(places)))
     for column, place in enumerate(places):
         if place is not None:
             plane[:modes, column] = np.outer(basis[:, place[0]], basis[:, place[1]]).reshape(-1)
-    high, low = split(plane)
-    forward = np.concatenate([high, high, low], axis=1)
-    high, low = split(plane.T)
-    inverse = np.concatenate([high, high, low], axis=1)
+    return plane
+
+
+def three_products(matrix):
+    high, low = split(matrix)
+    return np.concatenate([high, high, low], axis=1)
+
+
+def constants(size_z):
+    basis = sine_basis()
+    outer = line_places(0) + line_places(SPAN - 1)
+    plane = plane_matrix(sum([layer_places(x) for x in range(SPAN)], []) + outer)
+    ends = plane_matrix(layer_places(0) + layer_places(SPAN - 1) + outer)
+    lines = plane_matrix(sum([line_places(y) for y in (1, 2, BOX - 1, BOX)], []) + outer)
     boxes = size_z // BOX
     line = np.zeros((size_z, boxes * SPAN))
     for box in range(boxes):
@@ -74,7 +80,7 @@
     line_forward = np.concatenate([high, high, low], axis=0)
     high, low = split(line.T)
     line_inverse = np.concatenate([high, low], axis=1)
-    return forward, inverse, line_forward, line_inverse
+    return three_products(plane), three_products(plane.T), line_forward, line_inverse, three_products(ends), three_products(lines)
 
 
 def swap_pairs(mesh, axis, odd):
@@ -149,20 +155,29 @@
     stack_ref[2 * rows : 3 * rows, lanes] = high
 
 
-def solve(field_ref, rows_ref, inverse_ref, consts, before_ref, after_ref, out_ref, out_rows_ref):
-    forward_ref, back_ref, line_forward_ref, line_back_ref = consts
+def stacked(before_ref, lanes, parts):
+    store_split(before_ref, lanes, jnp.concatenate(parts, axis=0))
+
+
+def forward_own(field_ref, forward_ref, before_ref, spectral_ref):
     boxes = (field_ref.shape[1] - 2) // BOX
     size_y, size_z = field_ref.shape[2:]
+    blank = jnp.zeros((48, size_z), F32)
+    for field in range(2):
+        for box in range(boxes):
+            main = field_ref[field, box * BOX : box * BOX + SPAN].reshape(SPAN * size_y, size_z)
+            stacked(before_ref.at[field], slice(box * size_z, (box + 1) * size_z), [main, blank])
+    for field in range(2):
+        spectral_ref[field] = dot(forward_ref[...], before_ref[field])
+
+
+def solve(spectral, inverse_ref, consts, after_ref, out_ref, out_rows_ref):
+    back_ref, line_forward_ref, line_back_ref = consts
+    boxes = (out_ref.shape[1] - 2) // BOX
+    size_y, size_z = out_ref.shape[2:]
     inner = SPAN * size_y
     line_rows = line_forward_ref.shape[0] // 3
     lanes = [slice(box * size_z, (box + 1) * size_z) for box in range(boxes)]
-    for field in range(2):
-        for box in range(boxes):
-            start = box * BOX
-            main = field_ref[field, start : start + SPAN].reshape(inner, size_z)
-            strips = [rows_ref[field, side, start : start + 24] for side in range(2)]
-            store_split(before_ref.at[field], lanes[box], jnp.concatenate([main, *strips], axis=0))
-    spectral = [dot(forward_ref[...], before_ref[field]) for field in range(2)]
     for field in range(2):
         for box in range(boxes):
             high, low = halves(spectral[field][:, lanes[box]])
@@ -304,28 +319,33 @@
         inverse_ref[combo] = 1.0 / (cbar + kbar * summed)
 
 
-def edge_layers_kernel(mesh, load_hbm, zones_hbm, load_ref, zones_ref, even_ref, odd_ref, sems):
+def edge_layers_kernel(mesh, load_hbm, zones_hbm, even_ref, odd_ref, load_ref, zones_ref, sems):
+    last = zones_hbm.shape[0] - 1
     copies = [
-        pltpu.make_async_copy(load_hbm.at[0], load_ref.at[0], sems.at[0]),
-        pltpu.make_async_copy(load_hbm.at[1], load_ref.at[1], sems.at[1]),
-        pltpu.make_async_copy(zones_hbm, zones_ref, sems.at[2]),
+        pltpu.make_async_copy(load_hbm.at[:, 0], load_ref.at[0], sems.at[0]),
+        pltpu.make_async_copy(load_hbm.at[:, last], load_ref.at[1], sems.at[1]),
+        pltpu.make_async_copy(zones_hbm.at[pl.ds(0, 2)], zones_ref.at[0], sems.at[2]),
+        pltpu.make_async_copy(zones_hbm.at[pl.ds(last - 1, 2)], zones_ref.at[1], sems.at[3]),
     ]
     for copy in copies:
         copy.start()
     flags = standing(mesh)
-    last = zones_ref.shape[0] - 1
+    for copy in copies:
+        copy.wait()
     for channel in range(4):
-        if channel < 3:
-            copies[channel].wait()
         if channel < 2:
-            low, high = load_ref[channel, 0], load_ref[channel, last]
+            low, high = load_ref[0, channel], load_ref[1, channel]
         else:
-            low, high = zones_ref[channel - 2].astype(F32), zones_ref[last - 3 + channel].astype(F32)
+            low, high = zones_ref[0, channel - 2].astype(F32), zones_ref[1, channel - 2].astype(F32)
         even_ref[channel] = chosen(flags, EVEN_X, high, low)
         odd_ref[channel] = chosen(flags, EVEN_X, low, high)
 
 
-def edge_lines_kernel(mesh, load_ref, zones_ref, first_ref, second_ref, even_ref, odd_ref):
+def fetched_kernel(load_ref, zones_ref, token_ref):
+    token_ref[...] = load_ref[0, 0, 0:8] + zones_ref[0, 0:8].astype(F32)
+
+
+def edge_lines_kernel(mesh, load_ref, zones_ref, token_ref, first_ref, second_ref, even_ref, odd_ref):
     flags = standing(mesh)
     size_x, size_y = zones_ref.shape[:2]
     from_low = chosen(flags, EVEN_X, second_ref[...], first_ref[...])
@@ -353,6 +373,15 @@
             put_end(6 + 4 * line + depth, from_high[2 + depth], line, far)
 
 
+def tables(conductance_ref, capacity_ref, coupling_ref, size_z):
+    labels = range(coupling_ref.shape[0])
+    halves_of = [[0.5 * conductance_ref[field, label] for label in labels] for field in range(2)]
+    masses = [[capacity_ref[field, label] for label in labels] for field in range(2)]
+    products = [jnp.full((8, size_z), capacity_ref[0, label] * capacity_ref[1, label], F32) for label in labels]
+    masses.append([coupling_ref[label] * jnp.sqrt(products[label])[0:1] for label in labels])
+    return halves_of, masses
+
+
 def looked_up(entries, zone):
     value = jnp.full(zone.shape, entries[0], F32)
     for label in range(1, len(entries)):
@@ -361,29 +390,13 @@
 
 
 def coefficient_kernel(
-    mesh, conductance_ref, capacity_ref, coupling_ref, zones_ref, first_x, second_x, first_y, second_y,
-    half_ref, mass_ref, face_ref, half_rows_ref, mass_rows_ref, face_rows_ref, line_ref,
+    mesh, conductance_ref, capacity_ref, coupling_ref, zones_ref, first_x, second_x, half_ref, mass_ref, face_ref
 ):
     flags = standing(mesh)
-    labels = range(coupling_ref.shape[0])
-    halves_of = [[0.5 * conductance_ref[field, label] for label in labels] for field in range(2)]
-    masses = [[capacity_ref[field, label] for label in labels] for field in range(2)]
-    line = zones_ref.shape[2:]
-    roots = [jnp.sqrt(jnp.full((8, *line), capacity_ref[0, label] * capacity_ref[1, label], F32)) for label in labels]
-    masses.append([coupling_ref[label] * roots[label][0:1] for label in labels])
     size_x, size_y, size_z = zones_ref.shape
+    halves_of, masses = tables(conductance_ref, capacity_ref, coupling_ref, size_z)
     low_x = chosen(flags, EVEN_X, second_x[2:4], first_x[2:4])
     high_x = chosen(flags, EVEN_X, first_x[2:4], second_x[2:4])
-    for side, (even, odd) in enumerate(((second_y, first_y), (first_y, second_y))):
-        came = chosen(flags, EVEN_Y, even[2 * size_x :], odd[2 * size_x :])
-        lines, ends = (came[:size_x], came[size_x : 2 * size_x]), came[2 * size_x :]
-        for line in range(2):
-            place = 2 * side + line
-            line_ref[place, 0:8] = jnp.zeros((8, size_z), F32)
-            line_ref[place, size_x : size_x + 8] = jnp.zeros((8, size_z), F32)
-            line_ref[place, ROW0 - 2 : ROW0] = ends[4 + 4 * line : 6 + 4 * line]
-            line_ref[place, ROW0 : ROW0 + size_x] = lines[line]
-            line_ref[place, ROW0 + size_x : ROW0 + size_x + 2] = ends[6 + 4 * line : 8 + 4 * line]
     inside = slice(8, 8 + size_y)
     for x in range(-2, size_x + 2):
         if x < 0:
@@ -406,6 +419,30 @@
             half_ref[field, place, inside] = chosen(
                 flags, HIGH_X, half_ref[field, place, inside], half_ref[field, size_x + 1, inside]
             )
+    for field in range(2):
+        for x in range(0, size_x + 2, 2):
+            faces = faces_z(half_ref[field, x + 1 : x + 3, inside])
+            for way in range(2):
+                face_ref[field, way, x : x + 2] = faces[way]
+
+
+def coefficient_lines_kernel(
+    mesh, conductance_ref, capacity_ref, coupling_ref, old_half_ref, mass_ref, face_ref, first_y, second_y,
+    half_ref, half_rows_ref, mass_rows_ref, face_rows_ref, line_ref,
+):
+    flags = standing(mesh)
+    size_x, size_y, size_z = mass_ref.shape[1] - 2, mass_ref.shape[2], mass_ref.shape[3]
+    halves_of, masses = tables(conductance_ref, capacity_ref, coupling_ref, size_z)
+    for side, (even, odd) in enumerate(((second_y, first_y), (first_y, second_y))):
+        came = chosen(flags, EVEN_Y, even[2 * size_x :], odd[2 * size_x :])
+        lines, ends = (came[:size_x], came[size_x : 2 * size_x]), came[2 * size_x :]
+        for line in range(2):
+            place = 2 * side + line
+            line_ref[place, 0:8] = jnp.zeros((8, size_z), F32)
+            line_ref[place, size_x : size_x + 8] = jnp.zeros((8, size_z), F32)
+            line_ref[place, ROW0 - 2 : ROW0] = ends[4 + 4 * line : 6 + 4 * line]
+            line_ref[place, ROW0 : ROW0 + size_x] = lines[line]
+            line_ref[place, ROW0 + size_x : ROW0 + size_x + 2] = ends[6 + 4 * line : 8 + 4 * line]
     count = half_rows_ref.shape[2]
     position = lax.broadcasted_iota(jnp.int32, (count, size_z), 0)
     for line, flag in enumerate((LOW_Y, LOW_Y, HIGH_Y, HIGH_Y)):
@@ -416,7 +453,7 @@
             above = value[ROW0 + size_x - 1 : ROW0 + size_x]
             value = jnp.where((position < ROW0) & (flags[LOW_X] == 0), below, value)
             value = jnp.where((position >= ROW0 + size_x) & (flags[HIGH_X] == 0), above, value)
-            near = half_ref[field, :, 8 if flag == LOW_Y else 8 + size_y - 1]
+            near = old_half_ref[field, :, 8 if flag == LOW_Y else 8 + size_y - 1]
             half_rows_ref[field, line] = value
             half_rows_ref[field, line, ROW0 - 2 : ROW0 + size_x + 2] = chosen(
                 flags, flag, half_rows_ref[field, line, ROW0 - 2 : ROW0 + size_x + 2], near
@@ -428,39 +465,61 @@
             for which in range(3):
                 mass_rows_ref[which, line - 1] = looked_up(masses[which], zone)
     for field in range(2):
-        for x in range(0, size_x + 2, 2):
-            faces = faces_z(half_ref[field, x + 1 : x + 3, inside])
-            for way in range(2):
-                face_ref[field, way, x : x + 2] = faces[way]
         for side in range(2):
             faces = faces_z(half_rows_ref[field, side + 1])
             for way in range(2):
                 face_rows_ref[field, way, side] = faces[way]
-        for line, row in ((4, 8), (5, 8 + size_y - 1)):
+        for line, row in ((4, 0), (5, size_y - 1), (6, 1), (7, size_y - 2)):
             half_rows_ref[field, line] = jnp.zeros((count, size_z), F32)
-            half_rows_ref[field, line, ROW0 - 2 : ROW0 + size_x + 2] = half_ref[field, :, row]
+            half_rows_ref[field, line, ROW0 - 2 : ROW0 + size_x + 2] = old_half_ref[field, :, 8 + row]
+    for line, row in ((2, 0), (3, size_y - 1)):
+        spread = slice(ROW0 - 1, ROW0 + size_x + 1)
+        for which in range(3):
+            mass_rows_ref[which, line] = jnp.zeros((count, size_z), F32)
+            mass_rows_ref[which, line, spread] = mass_ref[which, :, row]
+        for field in range(2):
+            for way in range(2):
+                face_rows_ref[field, way, line] = jnp.zeros((count, size_z), F32)
+                face_rows_ref[field, way, line, spread] = face_ref[field, way, :, row]
+
+
+def own_transform_kernel(load_ref, forward_ref, spectral_ref, field_ref, before_ref):
+    size_x = load_ref.shape[1]
+    for field in range(2):
+        field_ref[field, 0] = jnp.zeros(load_ref.shape[2:], F32)
+        field_ref[field, 1 : 1 + size_x] = load_ref[field]
+        field_ref[field, 1 + size_x] = jnp.zeros(load_ref.shape[2:], F32)
+    forward_own(field_ref, forward_ref, before_ref, spectral_ref)
 
 
 def first_solve_kernel(
-    mesh, load_ref, first_x, second_x, first_y, second_y, inverse_ref, c0, c1, c2, c3,
-    part_ref, part_rows_ref, even_ref, odd_ref, even_lines, odd_lines, field_ref, rows_ref, before_ref, after_ref,
+    mesh, spectral_ref, mass_ref, first_x, second_x, first_y, second_y, inverse_ref, c1, c2, c3, ends_ref,
+    part_ref, part_rows_ref, even_ref, odd_ref, even_lines, odd_lines, rows_ref, before_ref, after_ref,
 ):
     flags = standing(mesh)
-    size_x = load_ref.shape[1]
-    for field in range(2):
-        field_ref[field, 1 : 1 + size_x] = load_ref[field]
-        field_ref[field, 0] = keep(flags, LOW_X, chosen(flags, EVEN_X, second_x[field], first_x[field]))
-        field_ref[field, 1 + size_x] = keep(flags, HIGH_X, chosen(flags, EVEN_X, first_x[field], second_x[field]))
+    size_x, size_y, size_z = part_ref.shape[1] - 2, part_ref.shape[2], part_ref.shape[3]
+    boxes = size_x // BOX
+    blank = jnp.zeros((size_y, size_z), F32)
+    spectral = []
+    for field in range(2):
+        low = keep(flags, LOW_X, chosen(flags, EVEN_X, second_x[field], first_x[field]))
+        high = keep(flags, HIGH_X, chosen(flags, EVEN_X, first_x[field], second_x[field]))
         for side, flag, even, odd in ((0, LOW_Y, second_y, first_y), (1, HIGH_Y, first_y, second_y)):
             place, after = slice(field * size_x, (field + 1) * size_x), slice(4 * size_x, 4 * size_x + 8)
             line = keep(flags, flag, chosen(flags, EVEN_Y, even[place], odd[place]))
             ends = keep(flags, flag, chosen(flags, EVEN_Y, even[after], odd[after]))
-            rows_ref[field, side, 0:8] = jnp.zeros((8, line.shape[1]), F32)
-            rows_ref[field, side, size_x : size_x + 8] = jnp.zeros((8, line.shape[1]), F32)
+            rows_ref[field, side, 0:8] = blank[0:8]
+            rows_ref[field, side, size_x : size_x + 8] = blank[0:8]
             rows_ref[field, side, ROW0 - 1 : ROW0] = ends[2 * field : 2 * field + 1]
             rows_ref[field, side, ROW0 : ROW0 + size_x] = line
             rows_ref[field, side, ROW0 + size_x : ROW0 + size_x + 1] = ends[2 * field + 1 : 2 * field + 2]
-    solve(field_ref, rows_ref, inverse_ref, (c0, c1, c2, c3), before_ref, after_ref, part_ref, part_rows_ref)
+        for box in range(boxes):
+            parts = [low if box == 0 else blank, high if box == boxes - 1 else blank]
+            parts += [rows_ref[field, side, box * BOX : box * BOX + 24] for side in range(2)]
+            stacked(before_ref.at[field], slice(box * size_z, (box + 1) * size_z), parts)
+    for field in range(2):
+        spectral.append(spectral_ref[field] + dot(ends_ref[...], before_ref[field]))
+    solve(spectral, inverse_ref, (c1, c2, c3), after_ref, part_ref, part_rows_ref)
     pack_x(flags, part_ref, part_rows_ref, even_ref, odd_ref)
     pack_lines(flags, part_ref, part_rows_ref, even_lines, odd_lines)
 
@@ -511,28 +570,6 @@
                 odd_ref[field, place] = chosen(flags, EVEN_Y, to_low, to_high)
 
 
-def assemble(flags, whole_ref, whole_rows_ref, lines_refs, ends_refs, came_ref, field_ref, lines):
-    size_x = whole_ref.shape[1] - 4
-    size_y = whole_ref.shape[2]
-    spread = slice(ROW0 - 2, ROW0 + size_x + 2)
-    for field in range(2):
-        unpack_lines(flags, lines_refs, ends_refs, came_ref, field)
-        low, high = came_ref[0], came_ref[1]
-        below = keep(flags, LOW_Y, whole_rows_ref[field, 0]) + low[1]
-        above = keep(flags, HIGH_Y, whole_rows_ref[field, 1]) + high[1]
-        lines[field, 0] = low[0]
-        lines[field, 1] = below
-        lines[field, 2] = above
-        lines[field, 3] = high[2]
-        lines[field, 4] = low[2]
-        lines[field, 5] = high[0]
-        field_ref[field, :, 8 : 8 + size_y] = whole_ref[field]
-        field_ref[field, :, 7] = lines[field, 1, spread]
-        field_ref[field, :, 8 + size_y] = lines[field, 2, spread]
-        field_ref[field, :, 8] = field_ref[field, :, 8] + lines[field, 4, spread]
-        field_ref[field, :, 7 + size_y] = field_ref[field, :, 7 + size_y] + lines[field, 5, spread]
-
-
 def faces_z(half):
     size_z, axis = half.shape[-1], half.ndim - 1
     lane = lax.broadcasted_iota(jnp.int32, half.shape, axis)
@@ -572,101 +609,177 @@
     return values, (first, second)
 
 
-def operate_line(lines, half_lines, mass_lines, face_lines, side, near):
-    outer, center, inner = (0, 1, 4) if side == 0 else (3, 2, 5)
-    values, images = [], []
-    for field in range(2):
-        value = lines[field, center]
-        half = half_lines[field, center]
+def fill(flags, whole_ref, whole_rows_ref, value_ref):
+    size_x, size_y = whole_ref.shape[1] - 4, whole_ref.shape[2]
+    spread = slice(ROW0 - 2, ROW0 + size_x + 2)
+    for field in range(2):
+        value_ref[field, :, 8 : 8 + size_y] = whole_ref[field]
+        value_ref[field, :, 7] = keep(flags, LOW_Y, whole_rows_ref[field, 0, spread])
+        value_ref[field, :, 8 + size_y] = keep(flags, HIGH_Y, whole_rows_ref[field, 1, spread])
+
+
+def line_image(values, outers, inners, half_lines, places, mass_lines, face_lines, place):
+    center, outer, inner = places
+    images = []
+    for field in range(2):
+        value, half = values[field], half_lines[field, center]
         count = value.shape[0]
-        flux = along_z(value, face_lines[field, 0, side], face_lines[field, 1, side])
+        flux = along_z(value, face_lines[field, 0, place], face_lines[field, 1, place])
         for turn in (1, count - 1):
             flux = flux + (half + pltpu.roll(half, turn, 0)) * (value - pltpu.roll(value, turn, 0))
-        flux = flux + (half + half_lines[field, outer]) * (value - lines[field, outer])
-        flux = flux + (half + half_lines[field, inner]) * (value - near[field, side])
-        values.append(value)
+        flux = flux + (half + half_lines[field, outer]) * (value - outers[field])
+        flux = flux + (half + half_lines[field, inner]) * (value - inners[field])
         images.append(flux)
-    first = mass_lines[0, side] * values[0] + mass_lines[2, side] * values[1] + images[0]
-    second = mass_lines[2, side] * values[0] + mass_lines[1, side] * values[1] + images[1]
+    first = mass_lines[0, place] * values[0] + mass_lines[2, place] * values[1] + images[0]
+    second = mass_lines[2, place] * values[0] + mass_lines[1, place] * values[1] + images[1]
     return first, second
 
 
-def second_solve_kernel(
-    mesh, whole_ref, whole_rows_ref, first_lines, second_lines, first_ends, second_ends,
-    half_ref, mass_ref, face_ref, half_lines, mass_lines, face_lines, load_ref, inverse_ref, c0, c1, c2, c3,
-    precond_ref, image_ref, sums_ref, part_ref, part_rows_ref, even_ref, odd_ref, even_lines, odd_lines,
-    came_ref, value_ref, lines, near, field_ref, rows_ref, before_ref, after_ref,
+SIDES = (((4, 1, 6, 0), (2, 0)), ((5, 2, 7, 3), (3, 1)))
+
+
+def line_changes(delta, outer, half_lines, mass_lines, face_lines, side):
+    (edge, out, inner, _), (place, _) = SIDES[side]
+    nothing = [jnp.zeros_like(line) for line in delta]
+    at_edge = line_image(delta, outer, nothing, half_lines, (edge, out, inner), mass_lines, face_lines, place)
+    at_next = [-(half_lines[field, edge] + half_lines[field, inner]) * delta[field] for field in range(2)]
+    return at_edge, at_next
+
+
+def own_image_kernel(
+    mesh, whole_ref, whole_rows_ref, half_ref, mass_ref, face_ref, forward_ref, image_ref, spectral_ref,
+    value_ref, before_ref,
 ):
     flags = standing(mesh)
-    size_x, size_y, size_z = load_ref.shape[1:]
-    lines_refs, ends_refs = (first_lines, second_lines), (first_ends, second_ends)
-    assemble(flags, whole_ref, whole_rows_ref, lines_refs, ends_refs, came_ref, value_ref, lines)
+    size_x = whole_ref.shape[1] - 4
+    fill(flags, whole_ref, whole_rows_ref, value_ref)
     for x, flag in ((-1, LOW_X), (size_x, HIGH_X)):
         _, images = operate(value_ref, half_ref, mass_ref, face_ref, x, 1)
         for field in range(2):
-            field_ref[field, x + 1 : x + 2] = keep(flags, flag, images[field])
-    total_a = total_b = jnp.zeros((CHUNK, size_y, size_z), F32)
+            image_ref[field, x + 1 : x + 2] = keep(flags, flag, images[field])
     for x in range(0, size_x, CHUNK):
-        chunk = slice(x, x + CHUNK)
-        values, images = operate(value_ref, half_ref, mass_ref, face_ref, x, CHUNK)
+        _, images = operate(value_ref, half_ref, mass_ref, face_ref, x, CHUNK)
         for field in range(2):
-            precond_ref[field, chunk] = values[field]
-            image_ref[field, chunk] = images[field]
-            field_ref[field, x + 1 : x + 1 + CHUNK] = images[field]
-            total_a = total_a + load_ref[field, chunk] * values[field]
-            total_b = total_b + images[field] * values[field]
-    sums_ref[0:1] = jnp.sum(jnp.sum(total_a, axis=0), axis=0, keepdims=True)
-    sums_ref[1:2] = jnp.sum(jnp.sum(total_b, axis=0), axis=0, keepdims=True)
-    sums_ref[2:8] = jnp.zeros((6, size_z), F32)
-    count = rows_ref.shape[2]
+            image_ref[field, x + 1 : x + 1 + CHUNK] = images[field]
+    forward_own(image_ref, forward_ref, before_ref, spectral_ref)
+
+
+def second_solve_kernel(
+    mesh, whole_ref, whole_rows_ref, first_lines, second_lines, first_ends, second_ends,
+    half_lines, mass_lines, face_lines, spectral_ref, inverse_ref, c1, c2, c3, lines_ref,
+    deltas_ref, changes_ref, part_ref, part_rows_ref, even_ref, odd_ref, even_lines, odd_lines,
+    came_ref, near, before_ref, after_ref,
+):
+    flags = standing(mesh)
+    size_x, size_y, size_z = part_ref.shape[1] - 2, part_ref.shape[2], part_ref.shape[3]
+    boxes = size_x // BOX
+    count = near.shape[2]
     position = lax.broadcasted_iota(jnp.int32, (count, size_z), 0)
     begin = jnp.where(flags[LOW_X] > 0, ROW0 - 1, ROW0)
     end = jnp.where(flags[HIGH_X] > 0, ROW0 + size_x + 1, ROW0 + size_x)
     valid = (position >= begin) & (position < end)
     for field in range(2):
-        for side, row in ((0, 8), (1, 7 + size_y)):
+        unpack_lines(flags, (first_lines, second_lines), (first_ends, second_ends), came_ref.at[field], field)
+        for side, row in ((0, 0), (1, size_y - 1)):
             near[field, side] = jnp.zeros((count, size_z), F32)
-            near[field, side, ROW0 - 2 : ROW0 + size_x + 2] = value_ref[field, :, row]
-    for side, flag in ((0, LOW_Y), (1, HIGH_Y)):
-        images = operate_line(lines, half_lines, mass_lines, face_lines, side, near)
+            near[field, side, ROW0 - 2 : ROW0 + size_x + 2] = whole_ref[field, :, row]
+    for side, flag, order in ((0, LOW_Y, (2, 1, 0)), (1, HIGH_Y, (0, 1, 2))):
+        delta, outer, far = [[came_ref[field, side, line] for field in range(2)] for line in order]
+        at_edge, at_next = line_changes(delta, outer, half_lines, mass_lines, face_lines, side)
+        (edge, out, _, beyond), (_, place) = SIDES[side]
+        at_outer = line_image(
+            [keep(flags, flag, whole_rows_ref[field, side]) + outer[field] for field in range(2)],
+            far,
+            [near[field, side] + delta[field] for field in range(2)],
+            half_lines,
+            (out, beyond, edge),
+            mass_lines,
+            face_lines,
+            place,
+        )
         for field in range(2):
-            rows_ref[field, side] = keep(flags, flag, jnp.where(valid, images[field], 0.0))
-    solve(field_ref, rows_ref, inverse_ref, (c0, c1, c2, c3), before_ref, after_ref, part_ref, part_rows_ref)
+            deltas_ref[field, side] = delta[field]
+            changes_ref[field, 3 * side] = jnp.where(valid, at_edge[field], 0.0)
+            changes_ref[field, 1 + side] = jnp.where(valid, at_next[field], 0.0)
+            changes_ref[field, 4 + side] = keep(flags, flag, jnp.where(valid, at_outer[field], 0.0))
+    spectral = []
+    for field in range(2):
+        for box in range(boxes):
+            parts = [changes_ref[field, line, box * BOX : box * BOX + 24] for line in range(6)]
+            stacked(before_ref.at[field], slice(box * size_z, (box + 1) * size_z), parts)
+    for field in range(2):
+        spectral.append(spectral_ref[field] + dot(lines_ref[...], before_ref[field]))
+    solve(spectral, inverse_ref, (c1, c2, c3), after_ref, part_ref, part_rows_ref)
     pack_x(flags, part_ref, part_rows_ref, even_ref, odd_ref)
     pack_lines(flags, part_ref, part_rows_ref, even_lines, odd_lines)
 
 
-def second_image_kernel(
-    mesh, whole_ref, whole_rows_ref, first_lines, second_lines, first_ends, second_ends,
-    half_ref, mass_ref, face_ref, old_image_ref, old_sums_ref,
-    precond_ref, image_ref, sums_ref, came_ref, value_ref,
+def first_sums_kernel(load_ref, whole_ref, image_ref, deltas_ref, changes_ref, precond_ref, out_ref, sums_ref):
+    size_x, size_y, size_z = load_ref.shape[1:]
+    rows = slice(ROW0, ROW0 + size_x)
+    total_a = total_b = jnp.zeros((size_y, size_z), F32)
+    for field in range(2):
+        precond_ref[field] = whole_ref[field, 2 : size_x + 2]
+        out_ref[field] = image_ref[field, 1 : size_x + 1]
+        for side, row in ((0, 0), (1, size_y - 1)):
+            precond_ref[field, :, row] = precond_ref[field, :, row] + deltas_ref[field, side, rows]
+        for line, row in enumerate((0, 1, size_y - 2, size_y - 1)):
+            out_ref[field, :, row] = out_ref[field, :, row] + changes_ref[field, line, rows]
+        for x in range(size_x):
+            total_a = total_a + load_ref[field, x] * precond_ref[field, x]
+            total_b = total_b + out_ref[field, x] * precond_ref[field, x]
+    sums_ref[0:1] = jnp.sum(total_a, axis=0, keepdims=True)
+    sums_ref[1:2] = jnp.sum(total_b, axis=0, keepdims=True)
+    sums_ref[2:8] = jnp.zeros((6, size_z), F32)
+
+
+def own_second_image_kernel(
+    mesh, whole_ref, whole_rows_ref, half_ref, mass_ref, face_ref, old_image_ref, image_ref, sums_ref, value_ref
 ):
     flags = standing(mesh)
     size_x, size_y, size_z = old_image_ref.shape[1:]
-    own, wide = slice(2, size_x + 2), slice(1, size_x + 3)
-    rows, margins = slice(ROW0, ROW0 + size_x), slice(ROW0 - 1, ROW0 + size_x + 1)
-    for field in range(2):
-        unpack_lines(flags, (first_lines, second_lines), (first_ends, second_ends), came_ref, field)
-        value_ref[field, wide, 8 : 8 + size_y] = whole_ref[field, wide]
-        value_ref[field, own, 7] = keep(flags, LOW_Y, whole_rows_ref[field, 0, rows]) + came_ref[0, 0, rows]
-        value_ref[field, wide, 8] = whole_ref[field, wide, 0] + came_ref[0, 1, margins]
-        value_ref[field, wide, 7 + size_y] = whole_ref[field, wide, size_y - 1] + came_ref[1, 1, margins]
-        value_ref[field, own, 8 + size_y] = keep(flags, HIGH_Y, whole_rows_ref[field, 1, rows]) + came_ref[1, 0, rows]
+    fill(flags, whole_ref, whole_rows_ref, value_ref)
     total_c = total_d = jnp.zeros((CHUNK, size_y, size_z), F32)
     for x in range(0, size_x, CHUNK):
         chunk = slice(x, x + CHUNK)
         values, images = operate(value_ref, half_ref, mass_ref, face_ref, x, CHUNK)
         for field in range(2):
-            precond_ref[field, chunk] = values[field]
             image_ref[field, chunk] = images[field]
             total_c = total_c + old_image_ref[field, chunk] * values[field]
             total_d = total_d + images[field] * values[field]
-    total_c, total_d = jnp.sum(total_c, axis=0), jnp.sum(total_d, axis=0)
+    sums_ref[0:1] = jnp.sum(jnp.sum(total_c, axis=0), axis=0, keepdims=True)
+    sums_ref[1:2] = jnp.sum(jnp.sum(total_d, axis=0), axis=0, keepdims=True)
+    sums_ref[2:8] = jnp.zeros((6, size_z), F32)
+
+
+def second_image_kernel(
+    mesh, whole_ref, image_ref, first_lines, second_lines, first_ends, second_ends,
+    half_lines, mass_lines, face_lines, old_image_ref, old_sums_ref, own_sums_ref,
+    deltas_ref, changes_ref, sums_ref, came_ref,
+):
+    flags = standing(mesh)
+    size_x, size_y, size_z = old_image_ref.shape[1:]
+    own = slice(2, size_x + 2)
+    rows = slice(ROW0, ROW0 + size_x)
+    total_c = total_d = jnp.zeros((size_x, size_z), F32)
+    for field in range(2):
+        unpack_lines(flags, (first_lines, second_lines), (first_ends, second_ends), came_ref.at[field], field)
+    for side, row, beside in ((0, 0, 1), (1, size_y - 1, size_y - 2)):
+        outer, delta = [[came_ref[field, side, line] for field in range(2)] for line in range(2)]
+        at_edge, at_next = line_changes(delta, outer, half_lines, mass_lines, face_lines, side)
+        for field in range(2):
+            changed, edge, inner = delta[field][rows], at_edge[field][rows], at_next[field][rows]
+            deltas_ref[field, side] = changed
+            changes_ref[field, 3 * side] = edge
+            changes_ref[field, 1 + side] = inner
+            total_c = total_c + old_image_ref[field, :, row] * changed
+            total_d = total_d + (image_ref[field, :, row] + edge) * changed
+            total_d = total_d + whole_ref[field, own, row] * edge + whole_ref[field, own, beside] * inner
     totals = [
         jnp.sum(old_sums_ref[0:1], axis=1, keepdims=True),
         jnp.sum(old_sums_ref[1:2], axis=1, keepdims=True),
-        jnp.sum(jnp.sum(total_c, axis=0, keepdims=True), axis=1, keepdims=True),
-        jnp.sum(jnp.sum(total_d, axis=0, keepdims=True), axis=1, keepdims=True),
+        jnp.sum(jnp.sum(total_c, axis=0, keepdims=True) + own_sums_ref[0:1], axis=1, keepdims=True),
+        jnp.sum(jnp.sum(total_d, axis=0, keepdims=True) + own_sums_ref[1:2], axis=1, keepdims=True),
     ]
     lane = lax.broadcasted_iota(jnp.int32, sums_ref.shape, 1)
     spread = jnp.zeros(sums_ref.shape, F32)
@@ -676,7 +789,8 @@
 
 
 def finish_kernel(
-    sums_ref, load_ref, z_ref, q_ref, w_ref, s_ref, solution_hbm, residual_hbm, solution_ref, residual_ref, sems
+    sums_ref, load_ref, z_ref, q_ref, w_ref, s_ref, deltas_ref, changes_ref,
+    solution_hbm, residual_hbm, solution_ref, residual_ref, sems,
 ):
     line = jnp.sum(sums_ref[...], axis=0, keepdims=True)
     lane = lax.broadcasted_iota(jnp.int32, line.shape, 1)
@@ -694,8 +808,18 @@
         for start in range(0, 2 * step, step):
             part = pl.ds(start, step)
             for x in range(start, start + step):
-                solution_ref[field, x] = along * z_ref[field, x] - against * w_ref[field, x]
+                solution_ref[field, x] = along * z_ref[field, x] - against * w_ref[field, x + 2]
                 residual_ref[field, x] = load_ref[field, x] - along * q_ref[field, x] + against * s_ref[field, x]
+            size_y = load_ref.shape[2]
+            chunk = slice(start, start + step)
+            for side, row in ((0, 0), (1, size_y - 1)):
+                solution_ref[field, chunk, row] = (
+                    solution_ref[field, chunk, row] - against * deltas_ref[field, side, chunk]
+                )
+            for line, row in enumerate((0, 1, size_y - 2, size_y - 1)):
+                residual_ref[field, chunk, row] = (
+                    residual_ref[field, chunk, row] + against * changes_ref[field, line, chunk]
+                )
             for here, there in ((solution_ref, solution_hbm), (residual_ref, residual_hbm)):
                 copies.append(
                     pltpu.make_async_copy(here.at[field, part], there.at[field, part], sems.at[len(copies)])
@@ -710,7 +834,7 @@
 HBM = pl.BlockSpec(memory_space=pltpu.HBM)
 
 
-def call(mesh, kernel, scalars, arrays, outs, scratch=(), flops=0, limit=24, in_hbm=False, outs_in_hbm=False):
+def call(mesh, kernel, scalars, arrays, outs, scratch=(), flops=0, limit=24, in_hbm=False, outs_in_hbm=False, aliases=()):
     moved = sum(math.prod(a.shape) * a.dtype.itemsize for a in list(arrays) + list(outs))
     return pl.pallas_call(
         kernel if mesh is None else functools.partial(kernel, mesh),
@@ -718,6 +842,7 @@
         in_specs=[SMEM] * len(scalars) + [HBM if in_hbm else VMEM] * len(arrays),
         out_specs=tuple([HBM if outs_in_hbm else VMEM] * len(outs)),
         scratch_shapes=list(scratch),
+        input_output_aliases=dict(aliases),
         compiler_params=pltpu.CompilerParams(vmem_limit_bytes=limit * 1024 * 1024),
         cost_estimate=pl.CostEstimate(flops=flops, bytes_accessed=moved, transcendentals=0),
     )(*scalars, *arrays)
@@ -729,18 +854,25 @@
     boxes = size_x // BOX
     count = size_x + 8
     sds = lambda *shape: jax.ShapeDtypeStruct(shape, F32)
-    consts = [jnp.asarray(c) for c in constants(size_z)]
-    modes, lanes = consts[0].shape[0], size_z // BOX * SPAN
+    forward, back, line_forward, line_back, ends_forward, lines_forward = [jnp.asarray(c) for c in constants(size_z)]
+    consts = (back, line_forward, line_back)
+    modes, lanes = forward.shape[0], size_z // BOX * SPAN
     assert size_z == 128
-    load, zones, *packed = call(
+    packed = call(
         mesh,
         edge_layers_kernel,
         [],
         [load, zones],
-        [sds(*load.shape), jax.ShapeDtypeStruct(zones.shape, zones.dtype)] + [sds(4, size_y, size_z)] * 2,
-        [pltpu.SemaphoreType.DMA((3,))],
+        [sds(4, size_y, size_z)] * 2,
+        [
+            pltpu.VMEM((2, 2, size_y, size_z), F32),
+            pltpu.VMEM((2, 2, size_y, size_z), zones.dtype),
+            pltpu.SemaphoreType.DMA((4,)),
+        ],
         in_hbm=True,
-    )
+        limit=56,
+    )
+    (token,) = call(None, fetched_kernel, [], [load, zones], [sds(8, size_z)])
     x_halo = swap(mesh, "gx", *packed)
     (inverse,) = call(
         None,
@@ -750,23 +882,27 @@
         [sds(2 * boxes, modes, lanes)],
         flops=40_000_000,
     )
-    packed = call(mesh, edge_lines_kernel, [], [load, zones, *x_halo], [sds(4 * size_x + 16, size_z)] * 2)
+    packed = call(mesh, edge_lines_kernel, [], [load, zones, token, *x_halo], [sds(4 * size_x + 16, size_z)] * 2)
     y_halo = swap(mesh, "gy", *packed)
-    half, mass, face, half_lines, mass_lines, face_lines = call(
+    laws = [conductance, capacity, coupling]
+    padded_shape = sds(2, size_x + 4, size_y + 16, size_z)
+    half, mass, face = call(
         mesh,
         coefficient_kernel,
-        [conductance, capacity, coupling],
-        [zones, *x_halo, *y_halo],
-        [
-            sds(2, size_x + 4, size_y + 16, size_z),
-            sds(3, size_x + 2, size_y, size_z),
-            sds(2, 2, size_x + 2, size_y, size_z),
-            sds(2, 6, count, size_z),
-            sds(3, 2, count, size_z),
-            sds(2, 2, 2, count, size_z),
-        ],
+        laws,
+        [zones, *x_halo],
+        [padded_shape, sds(3, size_x + 2, size_y, size_z), sds(2, 2, size_x + 2, size_y, size_z)],
+        flops=20_000_000,
+    )
+    half, half_lines, mass_lines, face_lines = call(
+        mesh,
+        coefficient_lines_kernel,
+        laws,
+        [half, mass, face, *y_halo],
+        [padded_shape, sds(2, 8, count, size_z), sds(3, 4, count, size_z), sds(2, 2, 4, count, size_z)],
         [pltpu.VMEM((4, count, size_z), F32)],
-        flops=20_000_000,
+        flops=2_000_000,
+        aliases={3: 0},
     )
     parts = [sds(2, size_x + 2, size_y, size_z), sds(2, 2, count, size_z)]
     packed_x = [[sds(2, depth, size_y + 8, size_z)] * 2 for depth in (3, 2)]
@@ -774,53 +910,75 @@
     packed_lines = [[sds(2, depth * size_x, size_z)] * 2 for depth in (3, 2)]
     packed_ends = [[sds(2, depth * 8, size_z)] * 2 for depth in (3, 2)]
     rows = SPAN * size_y + 48
-    work = [
-        pltpu.VMEM((2, size_x + 2, size_y, size_z), F32),
-        pltpu.VMEM((2, 2, count, size_z), F32),
-        pltpu.VMEM((2, 3 * rows, boxes * size_z), BF16),
-        pltpu.VMEM((2, 3 * rows, boxes * size_z), BF16),
-    ]
-    padded = [
-        pltpu.VMEM((2, size_x + 4, size_y + 16, size_z), F32),
-        pltpu.VMEM((2, 6, count, size_z), F32),
-    ]
+    wide = boxes * size_z
+    spectrum = sds(2, modes, wide)
+    stack = lambda depth: pltpu.VMEM((2, depth, wide), BF16)
+    halo = pltpu.VMEM((2, size_x + 2, size_y, size_z), F32)
+    padded = pltpu.VMEM((2, size_x + 4, size_y + 16, size_z), F32)
     own = sds(2, size_x, size_y, size_z)
 
+    (spectral,) = call(None, own_transform_kernel, [], [load, forward], [spectrum], [halo, stack(3 * rows)], 700_000_000)
     part, part_rows, *packed = call(
         mesh,
         first_solve_kernel,
         [],
-        [load, *x_halo, *y_halo, inverse, *consts],
+        [spectral, mass, *x_halo, *y_halo, inverse, *consts, ends_forward],
         parts + packed_x[0] + packed_lines[0],
-        work,
-        3_000_000_000,
+        [pltpu.VMEM((2, 2, count, size_z), F32), stack(ends_forward.shape[1]), stack(3 * rows)],
+        2_000_000_000,
     )
     lines = swap(mesh, "gy", *packed[2:])
     received = swap(mesh, "gx", *packed[:2])
     whole, whole_rows, *packed = call(mesh, merge_x_kernel, [], [part, part_rows, *received], wholes + packed_ends[0])
     ends = swap(mesh, "gy", *packed)
-    precond, image, sums, part, part_rows, *packed = call(
+    own_image, spectral = call(
+        mesh,
+        own_image_kernel,
+        [],
+        [whole, whole_rows, half, mass, face, forward],
+        [sds(2, size_x + 2, size_y, size_z), spectrum],
+        [padded, stack(3 * rows)],
+        700_000_000,
+    )
+    deltas, changes, part, part_rows, *packed = call(
         mesh,
         second_solve_kernel,
         [],
-        [whole, whole_rows, *lines, *ends, half, mass, face, half_lines, mass_lines, face_lines, load, inverse, *consts],
-        [own, own, sds(8, size_z)] + parts + packed_x[1] + packed_lines[1],
-        [pltpu.VMEM((2, 3, count, size_z), F32)] + padded + [pltpu.VMEM((2, 2, count, size_z), F32)] + work,
-        3_000_000_000,
+        [whole, whole_rows, *lines, *ends, half_lines, mass_lines, face_lines, spectral, inverse, *consts, lines_forward],
+        [sds(2, 2, count, size_z), sds(2, 6, count, size_z)] + parts + packed_x[1] + packed_lines[1],
+        [
+            pltpu.VMEM((2, 2, 3, count, size_z), F32),
+            pltpu.VMEM((2, 2, count, size_z), F32),
+            stack(lines_forward.shape[1]),
+            stack(3 * rows),
+        ],
+        2_000_000_000,
     )
     lines = swap(mesh, "gy", *packed[2:])
     received = swap(mesh, "gx", *packed[:2])
+    precond, image, sums = call(
+        None, first_sums_kernel, [], [load, whole, own_image, deltas, changes], [own, own, sds(8, size_z)], flops=1_000_000
+    )
     whole, whole_rows, *packed = call(mesh, merge_x_kernel, [], [part, part_rows, *received], wholes + packed_ends[1])
     ends = swap(mesh, "gy", *packed)
+    last_image, own_sums = call(
+        mesh,
+        own_second_image_kernel,
+        [],
+        [whole, whole_rows, half, mass, face, image],
+        [own, sds(8, size_z)],
+        [padded],
+        10_000_000,
+    )
     devices = mesh.shape["gx"] * mesh.shape["gy"]
-    last_precond, last_image, sums = call(
+    deltas, changes, sums = call(
         mesh,
         second_image_kernel,
         [],
-        [whole, whole_rows, *lines, *ends, half, mass, face, image, sums],
-        [own, own, sds(devices, size_z)],
-        [pltpu.VMEM((2, 2, count, size_z), F32), padded[0]],
-        10_000_000,
+        [whole, last_image, *lines, *ends, half_lines, mass_lines, face_lines, image, sums, own_sums],
+        [sds(2, 2, size_x, size_z), sds(2, 4, size_x, size_z), sds(devices, size_z)],
+        [pltpu.VMEM((2, 2, 2, count, size_z), F32)],
+        1_000_000,
     )
     sums = lax.all_to_all(sums, AXES, 0, 0, tiled=True)
     whole_block = pltpu.VMEM((2, size_x, size_y, size_z), F32)
@@ -828,7 +986,7 @@
         None,
         finish_kernel,
         [],
-        [sums, load, precond, image, last_precond, last_image],
+        [sums, load, precond, image, whole, last_image, deltas, changes],
         [own, own],
         [whole_block, whole_block, pltpu.SemaphoreType.DMA((8,))],
         outs_in_hbm=True,

time: 53.3 us -> 52.3 us (0.981)
  waiting for transfers between devices: 5.73 us -> 0.89 us
  Pallas kernels: 11.3 us -> 14.8 us
  starting transfers between devices: 20.3 us -> 19.4 us
  blocking collectives: 13 us -> 13.9 us
    pallas_call x10 -> x16, Pallas kernels: 11.3 us -> 14.8 us  [call(): pl.pallas_call(kernel if mesh is None else functools.partial(kernel, mesh...]
    ppermute x8, waiting for transfers between devices: 4.04 us -> 0.87 us  [swap(): first = lax.ppermute(even_part, AXES, swap_pairs(mesh, axis, False))]
    ppermute x8, waiting for transfers between devices: 1.68 us -> 0.02 us  [swap(): second = lax.ppermute(odd_part, AXES, swap_pairs(mesh, axis, True))]
    all_to_all x1, blocking collectives: 13 us -> 13.9 us  [shards(): sums = lax.all_to_all(sums, AXES, 0, 0, tiled=True)]
    ppermute x8, starting transfers between devices: 5.39 us -> 4.71 us  [swap(): second = lax.ppermute(odd_part, AXES, swap_pairs(mesh, axis, True))]
    unnamed x18 -> x26, local copies, waits for them, and re-layouts: 2.01 us -> 2.05 us
  transfers between devices with their start and end apart: 16 -> 16, of which waited for: 5 -> 2; matrix products, arithmetic and copies ran while one was open for 0% -> 0% of each run, Pallas kernels for 6% -> 14%
where the time goes in v7:
time: 52.3 us; the launch traced here: 52 us
  starting transfers between devices  19.4 us (37%)
  Pallas kernels  14.8 us (28%)
  blocking collectives  13.9 us (27%)
  local copies, waits for them, and re-layouts  2.05 us (4%)
  waiting for transfers between devices  0.89 us (2%)
  between operations  0.89 us (2%)
    pallas_call x16, Pallas kernels, call(): pl.pallas_call(kernel if mesh is None else functools.partial(kernel, mesh...  14.8 us
    ppermute x8, starting transfers between devices, swap(): first = lax.ppermute(even_part, AXES, swap_pairs(mesh, axis, False))  14.7 us
    all_to_all x1, blocking collectives, shards(): sums = lax.all_to_all(sums, AXES, 0, 0, tiled=True)  13.9 us
    ppermute x8, starting transfers between devices, swap(): second = lax.ppermute(odd_part, AXES, swap_pairs(mesh, axis, True))  4.71 us
    unnamed x26, local copies, waits for them, and re-layouts  2.05 us
  transfers between devices with their start and end apart: 16, of which 2 were waited for; matrix products, arithmetic and copies ran while one was open for 0% of the time, Pallas kernels for 14%

profile of v7, /device:TPU:0, one launch (start us, length us, event | category | flops | bytes accessed | tf_op | source)
XLA Modules:
  0.0 52.0 jit_solution(3217840837979030657)
XLA Ops:
  0.7 1.5 %shard_map.123 = (f32[4,16,128]{2,1,0:T(8,128)}, f32[4,16,128]{2,1,0:T(8,128)}) custom-call(f32[2,32,16,128]{3,2,1,0:T(8,128)} %load_ref.9, s32[32,16,128]{2,1,0:T(8,128)} %zones_ref.7), custom_call_target="tpu_custom_call" | custom-call | bytes 851968 | tf_op jit(solution)/shard_map/pallas_call | solution.py:839
  2.1 0.5 collective-permute-start
  2.7 2.6 %collective-permute-start.1 = (f32[4,16,128]{2,1,0:T(8,128)}, f32[4,16,128]{2,1,0:T(8,128)S(1)}, u32[]{:S(2)}, u32[]{:S(2)}) collective-permute-start(f32[4,16,128]{2,1,0:T(8,128)} %get-tuple-element.46), channel_id=1, source_target_pairs={{0,24},{1,25},{2,26},{3,27},{4,28},{5,29},{6,30},{7,31},{8,16},{9,... | collective-permute-start | bytes 98312 | tf_op jit(solution)/shard_map/ppermute | solution.py:109
  5.3 1.0 %copy-done = f32[2,32,16,128]{3,2,1,0:T(8,128)S(1)} copy-done((f32[2,32,16,128]{3,2,1,0:T(8,128)S(1)}, f32[2,32,16,128]{3,2,1,0:T(8,128)}, u32[]{:S(2)}) %copy-start) | copy-done | bytes 524312
  6.3 0.9 %copy-done.2 = s32[32,16,128]{2,1,0:T(8,128)S(1)} copy-done((s32[32,16,128]{2,1,0:T(8,128)S(1)}, s32[32,16,128]{2,1,0:T(8,128)}, u32[]{:S(2)}) %copy-start.2) | copy-done | bytes 262168
  7.3 0.2 shard_map.126
  7.5 1.6 %collective-permute-start.2 = (f32[144,128]{1,0:T(8,128)S(1)}, f32[144,128]{1,0:T(8,128)S(1)}, u32[]{:S(2)}, u32[]{:S(2)}) collective-permute-start(f32[144,128]{1,0:T(8,128)S(1)} %get-tuple-element.48), channel_id=1, source_target_pairs={{0,1},{1,0},{2,3},{3,2},{4,5},{5,4},{6,7},{7,6},{8,9},{9,8},{10,11... | collective-permute-start | bytes 221192 | tf_op jit(solution)/shard_map/ppermute | solution.py:112
  9.0 0.1 collective-permute-start.3
  9.2 1.6 %shard_map.127.inverse_ref = f32[4,336,144]{2,1,0:T(8,128)S(1)} custom-call(f32[2,8]{1,0:T(2,128)S(1)} %copy-done.5, f32[2,8]{1,0:T(2,128)S(1)} %copy-done.6, s32[32,16,128]{2,1,0:T(8,128)S(1)} %copy-done.3), custom_call_target="tpu_custom_call" | custom-call | flops 40000000 | bytes 1036288 | tf_op jit(solution)/shard_map/pallas_call | solution.py:839
  10.9 0.6 %shard_map.122.spectral_ref = f32[2,336,256]{2,1,0:T(8,128)S(1)} custom-call(f32[2,32,16,128]{3,2,1,0:T(8,128)S(1)} %copy-done.1, bf16[336,1008]{1,0:T(8,128)(2,1)S(1)} %copy-done.4), custom_call_target="tpu_custom_call" | custom-call | flops 700000000 | bytes 1889792 | tf_op jit(solution)/shard_map/pallas_call | solution.py:839
  11.5 1.2 %shard_map.124 = (f32[2,36,32,128]{3,2,1,0:T(8,128)S(1)}, f32[3,34,16,128]{3,2,1,0:T(8,128)S(1)}, f32[2,2,34,16,128]{4,3,2,1,0:T(8,128)S(1)}) custom-call(f32[2,8]{1,0:T(2,128)S(1)} %copy-done.5, f32[2,8]{1,0:T(2,128)S(1)} %copy-done.6, f32[8]{0:T(128)S(1)} %copy-done.7, s32[32,16,128]{2,1,0:T(8,128)S(1)} %copy-done.3, ...), custom_call_target="tpu_custom_call" | custom-call | flops 20000000 | bytes 3457024 | tf_op jit(solution)/shard_map/pallas_call | solution.py:839
  12.8 1.8 %shard_map.128 = (f32[2,34,16,128]{3,2,1,0:T(8,128)S(1)}, f32[2,2,40,128]{3,2,1,0:T(8,128)S(1)}, f32[2,3,24,128]{3,2,1,0:T(8,128)S(1)}, f32[2,3,24,128]{3,2,1,0:...) custom-call(f32[2,336,256]{2,1,0:T(8,128)S(1)} %shard_map.122.spectral_ref, ...), custom_call_target="tpu_custom_call" | custom-call | flops 2000000000 | bytes 4516864 | tf_op jit(solution)/shard_map/pallas_call | solution.py:839
  14.7 0.4 collective-permute-start.4
  15.1 1.2 %collective-permute-start.5 = (f32[2,3,24,128]{3,2,1,0:T(8,128)S(1)}, f32[2,3,24,128]{3,2,1,0:T(8,128)S(1)}, u32[]{:S(2)}, u32[]{:S(2)}) collective-permute-start(f32[2,3,24,128]{3,2,1,0:T(8,128)S(1)} %get-tuple-element.53), channel_id=1, source_target_pairs={{0,24},{1,25},{2,26},{3,27},{4,28},{5,29},{6,30},{7,31},{8,16},{9,... | collective-permute-start | bytes 221192 | tf_op jit(solution)/shard_map/ppermute | solution.py:109
  16.4 2.9 %collective-permute-start.6 = (f32[2,96,128]{2,1,0:T(8,128)S(1)}, f32[2,96,128]{2,1,0:T(8,128)S(1)}, u32[]{:S(2)}, u32[]{:S(2)}) collective-permute-start(f32[2,96,128]{2,1,0:T(8,128)S(1)} %get-tuple-element.56), channel_id=1, source_target_pairs={{0,1},{1,0},{2,3},{3,2},{4,5},{5,4},{6,7},{7,6},{8,9},{9,8},{10,11... | collective-permute-start | bytes 294920 | tf_op jit(solution)/shard_map/ppermute | solution.py:112
  19.2 1.3 %shard_map.130 = (f32[2,36,32,128]{3,2,1,0:T(8,128)S(1)}, f32[2,8,40,128]{3,2,1,0:T(8,128)S(1)}, f32[3,4,40,128]{3,2,1,0:T(8,128)S(1)}, f32[2,2,4,40,128]{4,3,2,1,0:T(8,128)S(1)}) custom-call(f32[2,8]{1,0:T(2,128)S(1)} %copy-done.5, f32[2,8]{1,0:T(2,128)S(1)} %copy-done.6, f32[8]{0:T(128)S(1)} %copy-done.7, ...), custom_call_target="tpu_custom_call", output_to_operand_aliasing={{0}: (3, {})} | custom-call | flops 2000000 | bytes 5357568 | tf_op jit(solution)/shard_map/pallas_call | solution.py:839
  20.6 0.1 shard_map.129
  20.7 3.1 %collective-permute-start.8 = (f32[2,24,128]{2,1,0:T(8,128)S(1)}, f32[2,24,128]{2,1,0:T(8,128)S(1)}, u32[]{:S(2)}, u32[]{:S(2)}) collective-permute-start(f32[2,24,128]{2,1,0:T(8,128)S(1)} %get-tuple-element.58), channel_id=1, source_target_pairs={{0,1},{1,0},{2,3},{3,2},{4,5},{5,4},{6,7},{7,6},{8,9},{9,8},{10,11... | collective-permute-start | bytes 73736 | tf_op jit(solution)/shard_map/ppermute | solution.py:112
  23.8 1.3 %shard_map.131 = (f32[2,34,16,128]{3,2,1,0:T(8,128)S(1)}, f32[2,336,256]{2,1,0:T(8,128)S(1)}) custom-call(f32[2,36,16,128]{3,2,1,0:T(8,128)S(1)} %get-tuple-element.54.whole_ref, f32[2,2,40,128]{3,2,1,0:T(8,128)S(1)} %get-tuple-element.55.whole_rows_ref, f32[2,36,32,128]{3,2,1,0:T(8,128)S(1)} %get-tuple-element.65.half_ref, ...), custom_call_target="tpu_custom_call" | custom-call | flops 700000000 | bytes 5723648 | tf_op jit(solution)/shard_map/pallas_call | solution.py:839
  25.1 0.4 collective-permute-done.8.first_ends
  25.6 2.2 %shard_map.132 = (f32[2,2,40,128]{3,2,1,0:T(8,128)S(1)}, f32[2,6,40,128]{3,2,1,0:T(8,128)S(1)}, f32[2,34,16,128]{3,2,1,0:T(8,128)S(1)}, f32[2,2,40,128]{3,2,1,0:...) custom-call(f32[2,36,16,128]{3,2,1,0:T(8,128)S(1)} %get-tuple-elemen, ...), custom_call_target="tpu_custom_call" | custom-call | flops 2000000000 | bytes 5628928 | tf_op jit(solution)/shard_map/pallas_call | solution.py:839
  27.8 0.2 collective-permute-start.10
  27.9 0.6 %collective-permute-start.11 = (f32[2,2,24,128]{3,2,1,0:T(8,128)S(1)}, f32[2,2,24,128]{3,2,1,0:T(8,128)S(1)}, u32[]{:S(2)}, u32[]{:S(2)}) collective-permute-start(f32[2,2,24,128]{3,2,1,0:T(8,128)S(1)} %get-tuple-element.70), channel_id=1, source_target_pairs={{0,24},{1,25},{2,26},{3,27},{4,28},{5,29},{6,30},{7,31},{8,16},{9,... | collective-permute-start | bytes 147464 | tf_op jit(solution)/shard_map/ppermute | solution.py:109
  28.5 3.0 %collective-permute-start.12 = (f32[2,64,128]{2,1,0:T(8,128)S(1)}, f32[2,64,128]{2,1,0:T(8,128)S(1)}, u32[]{:S(2)}, u32[]{:S(2)}) collective-permute-start(f32[2,64,128]{2,1,0:T(8,128)S(1)} %get-tuple-element.78), channel_id=1, source_target_pairs={{0,1},{1,0},{2,3},{3,2},{4,5},{5,4},{6,7},{7,6},{8,9},{9,8},{10,11... | collective-permute-start | bytes 196616 | tf_op jit(solution)/shard_map/ppermute | solution.py:112
  31.6 3.1 %collective-permute-start.14 = (f32[2,16,128]{2,1,0:T(8,128)S(1)}, f32[2,16,128]{2,1,0:T(8,128)S(1)}, u32[]{:S(2)}, u32[]{:S(2)}) collective-permute-start(f32[2,16,128]{2,1,0:T(8,128)S(1)} %get-tuple-element.80), channel_id=1, source_target_pairs={{0,1},{1,0},{2,3},{3,2},{4,5},{5,4},{6,7},{7,6},{8,9},{9,8},{10,11... | collective-permute-start | bytes 49160 | tf_op jit(solution)/shard_map/ppermute | solution.py:112
  34.7 0.1 collective-permute-start.15
  34.8 0.4 shard_map.134
  35.1 0.8 %shard_map.135 = (f32[2,32,16,128]{3,2,1,0:T(8,128)S(1)}, f32[8,128]{1,0:T(8,128)S(1)}) custom-call(f32[2,36,16,128]{3,2,1,0:T(8,128)S(1)} %get-tuple-element.71.whole_ref.w_ref, f32[2,2,40,128]{3,2,1,0:T(8,128)S(1)} %get-tuple-element.72.whole_rows_ref, f32[2,36,32,128]{3,2,1,0:T(8,128)S(1)} %get-tuple-element.65.half_ref, ...), custom_call_target="tpu_custom_call" | custom-call | flops 10000000 | bytes 4853760 | tf_op jit(solution)/shard_map/pallas_call | solution.py:839
  36.0 0.4 collective-permute-done.14.first_ends
  36.4 0.4 shard_map.136
  36.8 13.9 %all_to_all.11 = f32[32,1,128]{2,1,0:T(1,128)S(1)} all-to-all(f32[32,1,128]{2,1,0:T(1,128)S(1)} %bitcast.5), channel_id=1, replica_groups=mesh['gx'=4,'gy'=8] {'gx','gy'}, dimensions={0} | all-to-all | bytes 32768 | tf_op jit(solution)/shard_map/all_to_all | solution.py:983
  50.8 1.2 %shard_map.137 = (f32[2,32,16,128]{3,2,1,0:T(8,128)}, f32[2,32,16,128]{3,2,1,0:T(8,128)}) custom-call(f32[32,128]{1,0:T(8,128)S(1)} %bitcast.4, f32[2,32,16,128]{3,2,1,0:T(8,128)S(1)} %copy-done.1, f32[2,32,16,128]{3,2,1,0:T(8,128)S(1)} %get-tuple-element.85.z_ref, f32[2,32,16,128]{3,2,1,0:T(8,128)S(1)} %get-tuple-element.76.old_image_ref.q_ref, ...), custom_call_target="tpu_custom_call" | custom-call | bytes 3948544 | tf_op jit(solution)/shard_map/pallas_call | solution.py:839
  (43 shorter events, 0.2 us)
Async XLA Ops:
  0.6 8.6 %copy-start.3 = (s32[32,16,128]{2,1,0:T(8,128)S(1)}, s32[32,16,128]{2,1,0:T(8,128)}, u32[]{:S(2)}) copy-start(s32[32,16,128]{2,1,0:T(8,128)} %zones_ref.7) | copy-start | bytes 786436
  0.6 8.6 %copy-start.6 = (f32[2,8]{1,0:T(2,128)S(1)}, f32[2,8]{1,0:T(2,128)}, u32[]{:S(2)}) copy-start(f32[2,8]{1,0:T(2,128)} %capacity_ref.5) | copy-start | bytes 196
  0.7 8.5 %copy-start.5 = (f32[2,8]{1,0:T(2,128)S(1)}, f32[2,8]{1,0:T(2,128)}, u32[]{:S(2)}) copy-start(f32[2,8]{1,0:T(2,128)} %conductance_ref.5) | copy-start | bytes 196
  2.1 5.2 %collective-permute-start = (f32[4,16,128]{2,1,0:T(8,128)}, f32[4,16,128]{2,1,0:T(8,128)S(1)}, u32[]{:S(2)}, u32[]{:S(2)}) collective-permute-start(f32[4,16,128]{2,1,0:T(8,128)} %get-tuple-element.45), channel_id=1, source_target_pairs={{0,8},{1,9},{2,10},{3,11},{4,12},{5,13},{6,14},{7,15},{8,0},{9,1},... | collective-permute-start | bytes 98312 | tf_op jit(solution)/shard_map/ppermute | solution.py:108
  2.7 4.7 %collective-permute-start.1 = (f32[4,16,128]{2,1,0:T(8,128)}, f32[4,16,128]{2,1,0:T(8,128)S(1)}, u32[]{:S(2)}, u32[]{:S(2)}) collective-permute-start(f32[4,16,128]{2,1,0:T(8,128)} %get-tuple-element.46), channel_id=1, source_target_pairs={{0,24},{1,25},{2,26},{3,27},{4,28},{5,29},{6,30},{7,31},{8,16},{9,... | collective-permute-start | bytes 98312 | tf_op jit(solution)/shard_map/ppermute | solution.py:109
  5.3 1.0 %copy-start = (f32[2,32,16,128]{3,2,1,0:T(8,128)S(1)}, f32[2,32,16,128]{3,2,1,0:T(8,128)}, u32[]{:S(2)}) copy-start(f32[2,32,16,128]{3,2,1,0:T(8,128)} %load_ref.9) | copy-start | bytes 1572868
  6.3 0.9 %copy-start.2 = (s32[32,16,128]{2,1,0:T(8,128)S(1)}, s32[32,16,128]{2,1,0:T(8,128)}, u32[]{:S(2)}) copy-start(s32[32,16,128]{2,1,0:T(8,128)} %zones_ref.7) | copy-start | bytes 786436
  7.3 3.5 %copy-start.1 = (f32[2,32,16,128]{3,2,1,0:T(8,128)S(1)}, f32[2,32,16,128]{3,2,1,0:T(8,128)}, u32[]{:S(2)}) copy-start(f32[2,32,16,128]{3,2,1,0:T(8,128)} %load_ref.9) | copy-start | bytes 1572868
  7.3 3.5 %copy-start.4 = (bf16[336,1008]{1,0:T(8,128)(2,1)S(1)}, bf16[336,1008]{1,0:T(8,128)(2,1)}, u32[]{:S(2)}) copy-start(bf16[336,1008]{1,0:T(8,128)(2,1)} %constant.12.clone.forward_ref) | copy-start | bytes 2032132
  7.5 5.3 %collective-permute-start.2 = (f32[144,128]{1,0:T(8,128)S(1)}, f32[144,128]{1,0:T(8,128)S(1)}, u32[]{:S(2)}, u32[]{:S(2)}) collective-permute-start(f32[144,128]{1,0:T(8,128)S(1)} %get-tuple-element.48), channel_id=1, source_target_pairs={{0,1},{1,0},{2,3},{3,2},{4,5},{5,4},{6,7},{7,6},{8,9},{9,8},{10,11... | collective-permute-start | bytes 221192 | tf_op jit(solution)/shard_map/ppermute | solution.py:112
  9.0 3.7 %collective-permute-start.3 = (f32[144,128]{1,0:T(8,128)S(1)}, f32[144,128]{1,0:T(8,128)S(1)}, u32[]{:S(2)}, u32[]{:S(2)}) collective-permute-start(f32[144,128]{1,0:T(8,128)S(1)} %get-tuple-element.49), channel_id=1, source_target_pairs={{0,8},{1,2},{2,1},{3,4},{4,3},{5,6},{6,5},{7,15},{8,0},{9,10},{10,... | collective-permute-start | bytes 221192 | tf_op jit(solution)/shard_map/ppermute | solution.py:111
  10.8 0.7 %copy-start.7 = (f32[8]{0:T(128)S(1)}, f32[8]{0:T(128)}, u32[]{:S(2)}) copy-start(f32[8]{0:T(128)} %coupling_ref.3) | copy-start | bytes 100
  10.8 2.0 %copy-start.8 = (bf16[336,1008]{1,0:T(8,128)(2,1)S(1)}, bf16[336,1008]{1,0:T(8,128)(2,1)}, u32[]{:S(2)}) copy-start(bf16[336,1008]{1,0:T(8,128)(2,1)} %constant.13.clone.c1) | copy-start | bytes 2032132
  10.8 2.0 %copy-start.10 = (bf16[384,144]{1,0:T(8,128)(2,1)S(1)}, bf16[384,144]{1,0:T(8,128)(2,1)}, u32[]{:S(2)}) copy-start(bf16[384,144]{1,0:T(8,128)(2,1)} %constant.14.clone.c2) | copy-start | bytes 331780
  10.9 2.0 %copy-start.11 = (bf16[336,240]{1,0:T(8,128)(2,1)S(1)}, bf16[336,240]{1,0:T(8,128)(2,1)}, u32[]{:S(2)}) copy-start(bf16[336,240]{1,0:T(8,128)(2,1)} %constant.16.clone.ends_ref) | copy-start | bytes 483844
  10.9 1.9 %copy-start.12 = (bf16[144,256]{1,0:T(8,128)(2,1)S(1)}, bf16[144,256]{1,0:T(8,128)(2,1)}, u32[]{:S(2)}) copy-start(bf16[144,256]{1,0:T(8,128)(2,1)} %constant.15.clone.c3) | copy-start | bytes 221188
  14.7 5.9 %collective-permute-start.4 = (f32[2,3,24,128]{3,2,1,0:T(8,128)S(1)}, f32[2,3,24,128]{3,2,1,0:T(8,128)S(1)}, u32[]{:S(2)}, u32[]{:S(2)}) collective-permute-start(f32[2,3,24,128]{3,2,1,0:T(8,128)S(1)} %get-tuple-element.52), channel_id=1, source_target_pairs={{0,8},{1,9},{2,10},{3,11},{4,12},{5,13},{6,14},{7,15},{8,0},{9,1},... | collective-permute-start | bytes 221192 | tf_op jit(solution)/shard_map/ppermute | solution.py:108
  15.1 5.5 %collective-permute-start.5 = (f32[2,3,24,128]{3,2,1,0:T(8,128)S(1)}, f32[2,3,24,128]{3,2,1,0:T(8,128)S(1)}, u32[]{:S(2)}, u32[]{:S(2)}) collective-permute-start(f32[2,3,24,128]{3,2,1,0:T(8,128)S(1)} %get-tuple-element.53), channel_id=1, source_target_pairs={{0,24},{1,25},{2,26},{3,27},{4,28},{5,29},{6,30},{7,31},{8,16},{9,... | collective-permute-start | bytes 221192 | tf_op jit(solution)/shard_map/ppermute | solution.py:109
  16.4 8.8 %collective-permute-start.6 = (f32[2,96,128]{2,1,0:T(8,128)S(1)}, f32[2,96,128]{2,1,0:T(8,128)S(1)}, u32[]{:S(2)}, u32[]{:S(2)}) collective-permute-start(f32[2,96,128]{2,1,0:T(8,128)S(1)} %get-tuple-element.56), channel_id=1, source_target_pairs={{0,1},{1,0},{2,3},{3,2},{4,5},{5,4},{6,7},{7,6},{8,9},{9,8},{10,11... | collective-permute-start | bytes 294920 | tf_op jit(solution)/shard_map/ppermute | solution.py:112
  19.2 5.9 %collective-permute-start.7 = (f32[2,96,128]{2,1,0:T(8,128)S(1)}, f32[2,96,128]{2,1,0:T(8,128)S(1)}, u32[]{:S(2)}, u32[]{:S(2)}) collective-permute-start(f32[2,96,128]{2,1,0:T(8,128)S(1)} %get-tuple-element.57), channel_id=1, source_target_pairs={{0,8},{1,2},{2,1},{3,4},{4,3},{5,6},{6,5},{7,15},{8,0},{9,10},{10,... | collective-permute-start | bytes 294920 | tf_op jit(solution)/shard_map/ppermute | solution.py:111
  20.7 4.9 %collective-permute-start.8 = (f32[2,24,128]{2,1,0:T(8,128)S(1)}, f32[2,24,128]{2,1,0:T(8,128)S(1)}, u32[]{:S(2)}, u32[]{:S(2)}) collective-permute-start(f32[2,24,128]{2,1,0:T(8,128)S(1)} %get-tuple-element.58), channel_id=1, source_target_pairs={{0,1},{1,0},{2,3},{3,2},{4,5},{5,4},{6,7},{7,6},{8,9},{9,8},{10,11... | collective-permute-start | bytes 73736 | tf_op jit(solution)/shard_map/ppermute | solution.py:112
  23.8 1.8 %collective-permute-start.9 = (f32[2,24,128]{2,1,0:T(8,128)S(1)}, f32[2,24,128]{2,1,0:T(8,128)S(1)}, u32[]{:S(2)}, u32[]{:S(2)}) collective-permute-start(f32[2,24,128]{2,1,0:T(8,128)S(1)} %get-tuple-element.59), channel_id=1, source_target_pairs={{0,8},{1,2},{2,1},{3,4},{4,3},{5,6},{6,5},{7,15},{8,0},{9,10},{10,... | collective-permute-start | bytes 73736 | tf_op jit(solution)/shard_map/ppermute | solution.py:111
  23.8 1.8 %copy-start.9 = (bf16[336,432]{1,0:T(8,128)(2,1)S(1)}, bf16[336,432]{1,0:T(8,128)(2,1)}, u32[]{:S(2)}) copy-start(bf16[336,432]{1,0:T(8,128)(2,1)} %constant.17.clone.lines_ref) | copy-start | bytes 870916
  27.8 3.8 %collective-permute-start.10 = (f32[2,2,24,128]{3,2,1,0:T(8,128)S(1)}, f32[2,2,24,128]{3,2,1,0:T(8,128)S(1)}, u32[]{:S(2)}, u32[]{:S(2)}) collective-permute-start(f32[2,2,24,128]{3,2,1,0:T(8,128)S(1)} %get-tuple-element.69), channel_id=1, source_target_pairs={{0,8},{1,9},{2,10},{3,11},{4,12},{5,13},{6,14},{7,15},{8,0},{9,1},... | collective-permute-start | bytes 147464 | tf_op jit(solution)/shard_map/ppermute | solution.py:108
  27.9 3.6 %collective-permute-start.11 = (f32[2,2,24,128]{3,2,1,0:T(8,128)S(1)}, f32[2,2,24,128]{3,2,1,0:T(8,128)S(1)}, u32[]{:S(2)}, u32[]{:S(2)}) collective-permute-start(f32[2,2,24,128]{3,2,1,0:T(8,128)S(1)} %get-tuple-element.70), channel_id=1, source_target_pairs={{0,24},{1,25},{2,26},{3,27},{4,28},{5,29},{6,30},{7,31},{8,16},{9,... | collective-permute-start | bytes 147464 | tf_op jit(solution)/shard_map/ppermute | solution.py:109
  28.5 7.9 %collective-permute-start.12 = (f32[2,64,128]{2,1,0:T(8,128)S(1)}, f32[2,64,128]{2,1,0:T(8,128)S(1)}, u32[]{:S(2)}, u32[]{:S(2)}) collective-permute-start(f32[2,64,128]{2,1,0:T(8,128)S(1)} %get-tuple-element.78), channel_id=1, source_target_pairs={{0,1},{1,0},{2,3},{3,2},{4,5},{5,4},{6,7},{7,6},{8,9},{9,8},{10,11... | collective-permute-start | bytes 196616 | tf_op jit(solution)/shard_map/ppermute | solution.py:112
  31.5 4.9 %collective-permute-start.13 = (f32[2,64,128]{2,1,0:T(8,128)S(1)}, f32[2,64,128]{2,1,0:T(8,128)S(1)}, u32[]{:S(2)}, u32[]{:S(2)}) collective-permute-start(f32[2,64,128]{2,1,0:T(8,128)S(1)} %get-tuple-element.79), channel_id=1, source_target_pairs={{0,8},{1,2},{2,1},{3,4},{4,3},{5,6},{6,5},{7,15},{8,0},{9,10},{10,... | collective-permute-start | bytes 196616 | tf_op jit(solution)/shard_map/ppermute | solution.py:111
  31.6 4.8 %collective-permute-start.14 = (f32[2,16,128]{2,1,0:T(8,128)S(1)}, f32[2,16,128]{2,1,0:T(8,128)S(1)}, u32[]{:S(2)}, u32[]{:S(2)}) collective-permute-start(f32[2,16,128]{2,1,0:T(8,128)S(1)} %get-tuple-element.80), channel_id=1, source_target_pairs={{0,1},{1,0},{2,3},{3,2},{4,5},{5,4},{6,7},{7,6},{8,9},{9,8},{10,11... | collective-permute-start | bytes 49160 | tf_op jit(solution)/shard_map/ppermute | solution.py:112
  34.7 1.7 %collective-permute-start.15 = (f32[2,16,128]{2,1,0:T(8,128)S(1)}, f32[2,16,128]{2,1,0:T(8,128)S(1)}, u32[]{:S(2)}, u32[]{:S(2)}) collective-permute-start(f32[2,16,128]{2,1,0:T(8,128)S(1)} %get-tuple-element.81), channel_id=1, source_target_pairs={{0,8},{1,2},{2,1},{3,4},{4,3},{5,6},{6,5},{7,15},{8,0},{9,10},{10,... | collective-permute-start | bytes 49160 | tf_op jit(solution)/shard_map/ppermute | solution.py:111

commit v8 on v7

--- a/solution.py
+++ b/solution.py
@@ -16,6 +16,7 @@
 BF16 = jnp.bfloat16
 AXES = ("gx", "gy")
 ROW0 = 4
+EDGE_LAYERS = (0, 1, 2, SPAN - 3, SPAN - 2, SPAN - 1)
 CHUNK = 4
 
 
@@ -80,7 +81,16 @@
     line_forward = np.concatenate([high, high, low], axis=0)
     high, low = split(line.T)
     line_inverse = np.concatenate([high, low], axis=1)
-    return three_products(plane), three_products(plane.T), line_forward, line_inverse, three_products(ends), three_products(lines)
+    edges = plane_matrix(sum([layer_places(x) for x in EDGE_LAYERS], []) + outer)
+    return (
+        three_products(plane),
+        three_products(plane.T),
+        line_forward,
+        line_inverse,
+        three_products(ends),
+        three_products(lines),
+        three_products(edges.T),
+    )
 
 
 def swap_pairs(mesh, axis, odd):
@@ -171,12 +181,11 @@
         spectral_ref[field] = dot(forward_ref[...], before_ref[field])
 
 
-def solve(spectral, inverse_ref, consts, after_ref, out_ref, out_rows_ref):
-    back_ref, line_forward_ref, line_back_ref = consts
-    boxes = (out_ref.shape[1] - 2) // BOX
-    size_y, size_z = out_ref.shape[2:]
-    inner = SPAN * size_y
+def solve(spectral, inverse_ref, consts, after_ref):
+    line_forward_ref, line_back_ref = consts
     line_rows = line_forward_ref.shape[0] // 3
+    size_z = line_rows
+    boxes = spectral[0].shape[1] // size_z
     lanes = [slice(box * size_z, (box + 1) * size_z) for box in range(boxes)]
     for field in range(2):
         for box in range(boxes):
@@ -188,6 +197,12 @@
             cells = dot(high, line_back_ref[...])
             cells = cells[:, :size_z] + (cells[:, size_z:] + dot(low, line_back_ref[:, :size_z]))
             store_split(after_ref.at[field], lanes[box], cells)
+
+def solved_kernel(mesh, after_ref, back_ref, out_ref, out_rows_ref, *lines_refs):
+    boxes = (out_ref.shape[1] - 2) // BOX
+    size_y, size_z = out_ref.shape[2:]
+    inner = SPAN * size_y
+    lanes = [slice(box * size_z, (box + 1) * size_z) for box in range(boxes)]
     for field in range(2):
         result = dot(back_ref[...], after_ref[field])
         for box in range(boxes):
@@ -207,26 +222,30 @@
                         out_rows_ref[field, side, start : start + 8] + strip[0:8]
                     )
                     out_rows_ref[field, side, start + 8 : start + 24] = strip[8:]
-
-
-def pack_x(flags, part_ref, part_rows_ref, even_ref, odd_ref):
-    last = part_ref.shape[1] - 1
-    depth = even_ref.shape[1]
-    size_y = part_ref.shape[2]
-    for field in range(2):
+    if lines_refs:
+        pack_lines(standing(mesh), out_ref, out_rows_ref, *lines_refs)
+
+
+def pack_x(flags, after_ref, edges_ref, even_ref, odd_ref):
+    depth, size_z = even_ref.shape[1], even_ref.shape[3]
+    size_y = BOX
+    after = len(EDGE_LAYERS) * size_y
+    for field in range(2):
+        result = dot(edges_ref[...], after_ref[field])
+        low, high = result[:, :size_z], result[:, result.shape[1] - size_z :]
         for layer in range(depth):
-            low, high = layer, last + 1 - depth + layer
-            for side, place in ((None, slice(0, size_y)), (0, slice(size_y, size_y + 1)), (1, slice(size_y + 1, size_y + 2))):
-                if side is None:
-                    to_low, to_high = part_ref[field, low], part_ref[field, high]
-                else:
-                    shift = ROW0 - 1
-                    to_low = part_rows_ref[field, side, low + shift : low + shift + 1]
-                    to_high = part_rows_ref[field, side, high + shift : high + shift + 1]
+            far = len(EDGE_LAYERS) - depth + layer
+            pairs = [(slice(0, size_y), low[layer * size_y : (layer + 1) * size_y], high[far * size_y : (far + 1) * size_y])]
+            for side in range(2):
+                near_row = after + 24 * side + ROW0 - 1 + layer
+                far_row = after + 24 * side + ROW0 - 1 + SPAN - depth + layer
+                pairs.append(
+                    (slice(size_y + side, size_y + side + 1), low[near_row : near_row + 1], high[far_row : far_row + 1])
+                )
+            for place, to_low, to_high in pairs:
                 even_ref[field, layer, place] = chosen(flags, EVEN_X, to_high, to_low)
                 odd_ref[field, layer, place] = chosen(flags, EVEN_X, to_low, to_high)
-            rest = even_ref.shape[2] - size_y - 2
-            blank = jnp.zeros((rest, even_ref.shape[3]), F32)
+            blank = jnp.zeros((even_ref.shape[2] - size_y - 2, size_z), F32)
             even_ref[field, layer, size_y + 2 :] = blank
             odd_ref[field, layer, size_y + 2 :] = blank
 
@@ -269,8 +288,12 @@
             out_ref[side, line, 0:8] = blank
             out_ref[side, line, size_x : size_x + 8] = blank
             out_ref[side, line, ROW0 : ROW0 + size_x] = lines[line * size_x : (line + 1) * size_x]
-            out_ref[side, line, ROW0 - 2 : ROW0 + 1] = ends[8 * line : 8 * line + 3]
-            out_ref[side, line, ROW0 + size_x - 1 : ROW0 + size_x + 2] = ends[8 * line + 3 : 8 * line + 6]
+            if depth == 3:
+                out_ref[side, line, ROW0 - 2 : ROW0 + 1] = ends[8 * line : 8 * line + 3]
+                out_ref[side, line, ROW0 + size_x - 1 : ROW0 + size_x + 2] = ends[8 * line + 3 : 8 * line + 6]
+            elif line == 1:
+                out_ref[side, line, ROW0 - 1 : ROW0] = ends[0:1]
+                out_ref[side, line, ROW0 + size_x : ROW0 + size_x + 1] = ends[1:2]
 
 
 def divisor_kernel(conductance_ref, capacity_ref, zones_ref, inverse_ref):
@@ -383,18 +406,22 @@
 
 
 def looked_up(entries, zone):
-    value = jnp.full(zone.shape, entries[0], F32)
+    value = jnp.broadcast_to(entries[0], zone.shape)
     for label in range(1, len(entries)):
         value = jnp.where(zone == float(label), entries[label], value)
     return value
 
 
 def coefficient_kernel(
-    mesh, conductance_ref, capacity_ref, coupling_ref, zones_ref, first_x, second_x, half_ref, mass_ref, face_ref
+    mesh, conductance_ref, capacity_ref, coupling_ref, zones_ref, first_x, second_x,
+    half_ref, mass_ref, face_ref, table_ref,
 ):
     flags = standing(mesh)
     size_x, size_y, size_z = zones_ref.shape
     halves_of, masses = tables(conductance_ref, capacity_ref, coupling_ref, size_z)
+    for which, entries in enumerate(halves_of + masses):
+        for label, entry in enumerate(entries):
+            table_ref[which, label : label + 1] = jnp.broadcast_to(entry, (1, size_z))
     low_x = chosen(flags, EVEN_X, second_x[2:4], first_x[2:4])
     high_x = chosen(flags, EVEN_X, first_x[2:4], second_x[2:4])
     inside = slice(8, 8 + size_y)
@@ -427,12 +454,13 @@
 
 
 def coefficient_lines_kernel(
-    mesh, conductance_ref, capacity_ref, coupling_ref, old_half_ref, mass_ref, face_ref, first_y, second_y,
+    mesh, old_half_ref, mass_ref, face_ref, table_ref, first_y, second_y, after_ref,
     half_ref, half_rows_ref, mass_rows_ref, face_rows_ref, line_ref,
 ):
     flags = standing(mesh)
     size_x, size_y, size_z = mass_ref.shape[1] - 2, mass_ref.shape[2], mass_ref.shape[3]
-    halves_of, masses = tables(conductance_ref, capacity_ref, coupling_ref, size_z)
+    rows_of = [[table_ref[which, label : label + 1] for label in range(table_ref.shape[1])] for which in range(5)]
+    halves_of, masses = rows_of[:2], rows_of[2:]
     for side, (even, odd) in enumerate(((second_y, first_y), (first_y, second_y))):
         came = chosen(flags, EVEN_Y, even[2 * size_x :], odd[2 * size_x :])
         lines, ends = (came[:size_x], came[size_x : 2 * size_x]), came[2 * size_x :]
@@ -493,11 +521,11 @@
 
 
 def first_solve_kernel(
-    mesh, spectral_ref, mass_ref, first_x, second_x, first_y, second_y, inverse_ref, c1, c2, c3, ends_ref,
-    part_ref, part_rows_ref, even_ref, odd_ref, even_lines, odd_lines, rows_ref, before_ref, after_ref,
+    mesh, spectral_ref, mass_ref, first_x, second_x, first_y, second_y, inverse_ref, c2, c3, ends_ref, edges_ref,
+    after_ref, even_ref, odd_ref, rows_ref, before_ref,
 ):
     flags = standing(mesh)
-    size_x, size_y, size_z = part_ref.shape[1] - 2, part_ref.shape[2], part_ref.shape[3]
+    size_x, size_y, size_z = mass_ref.shape[1] - 2, mass_ref.shape[2], mass_ref.shape[3]
     boxes = size_x // BOX
     blank = jnp.zeros((size_y, size_z), F32)
     spectral = []
@@ -519,9 +547,8 @@
             stacked(before_ref.at[field], slice(box * size_z, (box + 1) * size_z), parts)
     for field in range(2):
         spectral.append(spectral_ref[field] + dot(ends_ref[...], before_ref[field]))
-    solve(spectral, inverse_ref, (c1, c2, c3), after_ref, part_ref, part_rows_ref)
-    pack_x(flags, part_ref, part_rows_ref, even_ref, odd_ref)
-    pack_lines(flags, part_ref, part_rows_ref, even_lines, odd_lines)
+    solve(spectral, inverse_ref, (c2, c3), after_ref)
+    pack_x(flags, after_ref, edges_ref, even_ref, odd_ref)
 
 
 def merge_x_kernel(mesh, part_ref, part_rows_ref, first_ref, second_ref, whole_ref, whole_rows_ref, even_ref, odd_ref):
@@ -558,10 +585,24 @@
                 whole_rows_ref[field, side, edge - 1 : edge] = low[0, row]
                 whole_rows_ref[field, side, end + 1 : end + 2] = high[2, row]
 
-        for line in range(depth):
-            for ref in (even_ref, odd_ref):
-                ref[field, 8 * line : 8 * line + 8] = jnp.zeros((8, size_z), F32)
-        for start, x in ((0, -2), (3, size_x - 1)):
+        base = 2 * size_x if depth == 2 else 0
+        for ref in (even_ref, odd_ref):
+            ref[field, base:] = jnp.zeros((ref.shape[1] - base, size_z), F32)
+        if base:
+            own, rows = slice(2, size_x + 2), slice(ROW0, ROW0 + size_x)
+            pairs = line_pairs(whole_ref, whole_rows_ref, field, own, rows, depth)
+            for line, (to_low, to_high) in enumerate(pairs):
+                place = slice(line * size_x, (line + 1) * size_x)
+                even_ref[field, place] = chosen(flags, EVEN_Y, to_high, to_low)
+                odd_ref[field, place] = chosen(flags, EVEN_Y, to_low, to_high)
+            for row, x in ((base, -1), (base + 1, size_x)):
+                pairs = line_pairs(
+                    whole_ref, whole_rows_ref, field, slice(x + 2, x + 3), slice(x + ROW0, x + ROW0 + 1), depth
+                )
+                even_ref[field, row : row + 1] = chosen(flags, EVEN_Y, pairs[1][1], pairs[1][0])
+                odd_ref[field, row : row + 1] = chosen(flags, EVEN_Y, pairs[1][0], pairs[1][1])
+            continue
+        for start, x in ((base, -2), (base + 3, size_x - 1)):
             layers, rows = slice(x + 2, x + 5), slice(x + ROW0, x + ROW0 + 3)
             pairs = line_pairs(whole_ref, whole_rows_ref, field, layers, rows, depth)
             for line, (to_low, to_high) in enumerate(pairs):
@@ -666,12 +707,11 @@
 
 def second_solve_kernel(
     mesh, whole_ref, whole_rows_ref, first_lines, second_lines, first_ends, second_ends,
-    half_lines, mass_lines, face_lines, spectral_ref, inverse_ref, c1, c2, c3, lines_ref,
-    deltas_ref, changes_ref, part_ref, part_rows_ref, even_ref, odd_ref, even_lines, odd_lines,
-    came_ref, near, before_ref, after_ref,
+    half_lines, mass_lines, face_lines, spectral_ref, inverse_ref, c2, c3, lines_ref, edges_ref,
+    deltas_ref, changes_ref, after_ref, even_ref, odd_ref, came_ref, near, before_ref,
 ):
     flags = standing(mesh)
-    size_x, size_y, size_z = part_ref.shape[1] - 2, part_ref.shape[2], part_ref.shape[3]
+    size_x, size_y, size_z = whole_ref.shape[1] - 4, whole_ref.shape[2], whole_ref.shape[3]
     boxes = size_x // BOX
     count = near.shape[2]
     position = lax.broadcasted_iota(jnp.int32, (count, size_z), 0)
@@ -709,9 +749,8 @@
             stacked(before_ref.at[field], slice(box * size_z, (box + 1) * size_z), parts)
     for field in range(2):
         spectral.append(spectral_ref[field] + dot(lines_ref[...], before_ref[field]))
-    solve(spectral, inverse_ref, (c1, c2, c3), after_ref, part_ref, part_rows_ref)
-    pack_x(flags, part_ref, part_rows_ref, even_ref, odd_ref)
-    pack_lines(flags, part_ref, part_rows_ref, even_lines, odd_lines)
+    solve(spectral, inverse_ref, (c2, c3), after_ref)
+    pack_x(flags, after_ref, edges_ref, even_ref, odd_ref)
 
 
 def first_sums_kernel(load_ref, whole_ref, image_ref, deltas_ref, changes_ref, precond_ref, out_ref, sums_ref):
@@ -753,7 +792,7 @@
 
 
 def second_image_kernel(
-    mesh, whole_ref, image_ref, first_lines, second_lines, first_ends, second_ends,
+    mesh, whole_ref, image_ref, first_ref, second_ref,
     half_lines, mass_lines, face_lines, old_image_ref, old_sums_ref, own_sums_ref,
     deltas_ref, changes_ref, sums_ref, came_ref,
 ):
@@ -762,8 +801,10 @@
     own = slice(2, size_x + 2)
     rows = slice(ROW0, ROW0 + size_x)
     total_c = total_d = jnp.zeros((size_x, size_z), F32)
-    for field in range(2):
-        unpack_lines(flags, (first_lines, second_lines), (first_ends, second_ends), came_ref.at[field], field)
+    lines_refs = [ref.at[:, pl.ds(0, 2 * size_x)] for ref in (first_ref, second_ref)]
+    ends_refs = [ref.at[:, pl.ds(2 * size_x, 8)] for ref in (first_ref, second_ref)]
+    for field in range(2):
+        unpack_lines(flags, lines_refs, ends_refs, came_ref.at[field], field)
     for side, row, beside in ((0, 0, 1), (1, size_y - 1, size_y - 2)):
         outer, delta = [[came_ref[field, side, line] for field in range(2)] for line in range(2)]
         at_edge, at_next = line_changes(delta, outer, half_lines, mass_lines, face_lines, side)
@@ -854,8 +895,10 @@
     boxes = size_x // BOX
     count = size_x + 8
     sds = lambda *shape: jax.ShapeDtypeStruct(shape, F32)
-    forward, back, line_forward, line_back, ends_forward, lines_forward = [jnp.asarray(c) for c in constants(size_z)]
-    consts = (back, line_forward, line_back)
+    forward, back, line_forward, line_back, ends_forward, lines_forward, edges_back = [
+        jnp.asarray(c) for c in constants(size_z)
+    ]
+    consts = (line_forward, line_back)
     modes, lanes = forward.shape[0], size_z // BOX * SPAN
     assert size_z == 128
     packed = call(
@@ -886,29 +929,21 @@
     y_halo = swap(mesh, "gy", *packed)
     laws = [conductance, capacity, coupling]
     padded_shape = sds(2, size_x + 4, size_y + 16, size_z)
-    half, mass, face = call(
+    half, mass, face, table = call(
         mesh,
         coefficient_kernel,
         laws,
         [zones, *x_halo],
-        [padded_shape, sds(3, size_x + 2, size_y, size_z), sds(2, 2, size_x + 2, size_y, size_z)],
+        [padded_shape, sds(3, size_x + 2, size_y, size_z), sds(2, 2, size_x + 2, size_y, size_z)]
+        + [sds(5, coupling.shape[0], size_z)],
         flops=20_000_000,
-    )
-    half, half_lines, mass_lines, face_lines = call(
-        mesh,
-        coefficient_lines_kernel,
-        laws,
-        [half, mass, face, *y_halo],
-        [padded_shape, sds(2, 8, count, size_z), sds(3, 4, count, size_z), sds(2, 2, 4, count, size_z)],
-        [pltpu.VMEM((4, count, size_z), F32)],
-        flops=2_000_000,
-        aliases={3: 0},
     )
     parts = [sds(2, size_x + 2, size_y, size_z), sds(2, 2, count, size_z)]
     packed_x = [[sds(2, depth, size_y + 8, size_z)] * 2 for depth in (3, 2)]
     wholes = [sds(2, size_x + 4, size_y, size_z), sds(2, 2, count, size_z)]
-    packed_lines = [[sds(2, depth * size_x, size_z)] * 2 for depth in (3, 2)]
-    packed_ends = [[sds(2, depth * 8, size_z)] * 2 for depth in (3, 2)]
+    packed_lines = [sds(2, 3 * size_x, size_z)] * 2
+    packed_ends = [sds(2, 3 * 8, size_z)] * 2
+    packed_y = [sds(2, 2 * size_x + 8, size_z)] * 2
     rows = SPAN * size_y + 48
     wide = boxes * size_z
     spectrum = sds(2, modes, wide)
@@ -918,19 +953,31 @@
     own = sds(2, size_x, size_y, size_z)
 
     (spectral,) = call(None, own_transform_kernel, [], [load, forward], [spectrum], [halo, stack(3 * rows)], 700_000_000)
-    part, part_rows, *packed = call(
+    stacked_cells = jax.ShapeDtypeStruct((2, 3 * rows, wide), BF16)
+    after, *packed = call(
         mesh,
         first_solve_kernel,
         [],
-        [spectral, mass, *x_halo, *y_halo, inverse, *consts, ends_forward],
-        parts + packed_x[0] + packed_lines[0],
-        [pltpu.VMEM((2, 2, count, size_z), F32), stack(ends_forward.shape[1]), stack(3 * rows)],
+        [spectral, mass, *x_halo, *y_halo, inverse, *consts, ends_forward, edges_back],
+        [stacked_cells] + packed_x[0],
+        [pltpu.VMEM((2, 2, count, size_z), F32), stack(ends_forward.shape[1])],
         2_000_000_000,
     )
-    lines = swap(mesh, "gy", *packed[2:])
-    received = swap(mesh, "gx", *packed[:2])
-    whole, whole_rows, *packed = call(mesh, merge_x_kernel, [], [part, part_rows, *received], wholes + packed_ends[0])
+    received = swap(mesh, "gx", *packed)
+    part, part_rows, *packed = call(mesh, solved_kernel, [], [after, back], parts + packed_lines, (), 700_000_000)
+    lines = swap(mesh, "gy", *packed)
+    whole, whole_rows, *packed = call(mesh, merge_x_kernel, [], [part, part_rows, *received], wholes + packed_ends)
     ends = swap(mesh, "gy", *packed)
+    half, half_lines, mass_lines, face_lines = call(
+        mesh,
+        coefficient_lines_kernel,
+        [],
+        [half, mass, face, table, *y_halo, whole_rows],
+        [padded_shape, sds(2, 8, count, size_z), sds(3, 4, count, size_z), sds(2, 2, 4, count, size_z)],
+        [pltpu.VMEM((4, count, size_z), F32)],
+        flops=2_000_000,
+        aliases={0: 0},
+    )
     own_image, spectral = call(
         mesh,
         own_image_kernel,
@@ -940,27 +987,27 @@
         [padded, stack(3 * rows)],
         700_000_000,
     )
-    deltas, changes, part, part_rows, *packed = call(
+    deltas, changes, after, *packed = call(
         mesh,
         second_solve_kernel,
         [],
-        [whole, whole_rows, *lines, *ends, half_lines, mass_lines, face_lines, spectral, inverse, *consts, lines_forward],
-        [sds(2, 2, count, size_z), sds(2, 6, count, size_z)] + parts + packed_x[1] + packed_lines[1],
+        [whole, whole_rows, *lines, *ends, half_lines, mass_lines, face_lines, spectral, inverse, *consts]
+        + [lines_forward, edges_back],
+        [sds(2, 2, count, size_z), sds(2, 6, count, size_z), stacked_cells] + packed_x[1],
         [
             pltpu.VMEM((2, 2, 3, count, size_z), F32),
             pltpu.VMEM((2, 2, count, size_z), F32),
             stack(lines_forward.shape[1]),
-            stack(3 * rows),
         ],
         2_000_000_000,
     )
-    lines = swap(mesh, "gy", *packed[2:])
-    received = swap(mesh, "gx", *packed[:2])
+    received = swap(mesh, "gx", *packed)
+    part, part_rows = call(mesh, solved_kernel, [], [after, back], parts, (), 700_000_000)
     precond, image, sums = call(
         None, first_sums_kernel, [], [load, whole, own_image, deltas, changes], [own, own, sds(8, size_z)], flops=1_000_000
     )
-    whole, whole_rows, *packed = call(mesh, merge_x_kernel, [], [part, part_rows, *received], wholes + packed_ends[1])
-    ends = swap(mesh, "gy", *packed)
+    whole, whole_rows, *packed = call(mesh, merge_x_kernel, [], [part, part_rows, *received], wholes + packed_y)
+    received = swap(mesh, "gy", *packed)
     last_image, own_sums = call(
         mesh,
         own_second_image_kernel,
@@ -975,7 +1022,7 @@
         mesh,
         second_image_kernel,
         [],
-        [whole, last_image, *lines, *ends, half_lines, mass_lines, face_lines, image, sums, own_sums],
+        [whole, last_image, *received, half_lines, mass_lines, face_lines, image, sums, own_sums],
         [sds(2, 2, size_x, size_z), sds(2, 4, size_x, size_z), sds(devices, size_z)],
         [pltpu.VMEM((2, 2, 2, count, size_z), F32)],
         1_000_000,

time: 52.3 us -> 51.5 us (0.985)
  waiting for transfers between devices: 0.89 us -> 5.41 us
  starting transfers between devices: 19.4 us -> 16 us
  blocking collectives: 13.9 us -> 12.1 us
    ppermute x8 -> x7, starting transfers between devices: 14.7 us -> 11.5 us  [swap(): first = lax.ppermute(even_part, AXES, swap_pairs(mesh, axis, False))]
    ppermute x8 -> x7, waiting for transfers between devices: 0.02 us -> 2.91 us  [swap(): second = lax.ppermute(odd_part, AXES, swap_pairs(mesh, axis, True))]
    all_to_all x1, blocking collectives: 13.9 us -> 12.1 us  [shards(): sums = lax.all_to_all(sums, AXES, 0, 0, tiled=True)]
    ppermute x8 -> x7, waiting for transfers between devices: 0.87 us -> 2.5 us  [swap(): first = lax.ppermute(even_part, AXES, swap_pairs(mesh, axis, False))]
    ppermute x8 -> x7, starting transfers between devices: 4.71 us -> 4.44 us  [swap(): second = lax.ppermute(odd_part, AXES, swap_pairs(mesh, axis, True))]
    pallas_call x16 -> x18, Pallas kernels: 14.8 us -> 14.7 us  [call(): pl.pallas_call(kernel if mesh is None else functools.partial(kernel, mesh...]
    unnamed x26 -> x28, local copies, waits for them, and re-layouts: 2.05 us -> 2.06 us
  transfers between devices with their start and end apart: 16 -> 14, of which waited for: 2 -> 3; matrix products, arithmetic and copies ran while one was open for 0% -> 0% of each run, Pallas kernels for 14% -> 15%
where the time goes in v8:
time: 51.5 us; the launch traced here: 51.2 us
  starting transfers between devices  16 us (31%)
  Pallas kernels  14.7 us (29%)
  blocking collectives  12.1 us (23%)
  waiting for transfers between devices  5.41 us (11%)
  local copies, waits for them, and re-layouts  2.06 us (4%)
  between operations  0.93 us (2%)
    pallas_call x18, Pallas kernels, call(): pl.pallas_call(kernel if mesh is None else functools.partial(kernel, mesh...  14.7 us
    all_to_all x1, blocking collectives, shards(): sums = lax.all_to_all(sums, AXES, 0, 0, tiled=True)  12.1 us
    ppermute x7, starting transfers between devices, swap(): first = lax.ppermute(even_part, AXES, swap_pairs(mesh, axis, False))  11.5 us
    ppermute x7, starting transfers between devices, swap(): second = lax.ppermute(odd_part, AXES, swap_pairs(mesh, axis, True))  4.44 us
    ppermute x7, waiting for transfers between devices, swap(): second = lax.ppermute(odd_part, AXES, swap_pairs(mesh, axis, True))  2.91 us
    ppermute x7, waiting for transfers between devices, swap(): first = lax.ppermute(even_part, AXES, swap_pairs(mesh, axis, False))  2.5 us
    unnamed x28, local copies, waits for them, and re-layouts  2.06 us
  transfers between devices with their start and end apart: 14, of which 3 were waited for; matrix products, arithmetic and copies ran while one was open for 0% of the time, Pallas kernels for 15%

profile of v8, /device:TPU:0, one launch (start us, length us, event | category | flops | bytes accessed | tf_op | source)
XLA Modules:
  0.0 51.2 jit_solution(12296625111805880685)
XLA Ops:
  0.7 1.5 %shard_map.132 = (f32[4,16,128]{2,1,0:T(8,128)}, f32[4,16,128]{2,1,0:T(8,128)}) custom-call(f32[2,32,16,128]{3,2,1,0:T(8,128)} %load_ref.9, s32[32,16,128]{2,1,0:T(8,128)} %zones_ref.7), custom_call_target="tpu_custom_call" | custom-call | bytes 851968 | tf_op jit(solution)/shard_map/pallas_call | solution.py:880
  2.1 0.5 %collective-permute-start = (f32[4,16,128]{2,1,0:T(8,128)}, f32[4,16,128]{2,1,0:T(8,128)S(1)}, u32[]{:S(2)}, u32[]{:S(2)}) collective-permute-start(f32[4,16,128]{2,1,0:T(8,128)} %get-tuple-element.46), channel_id=1, source_target_pairs={{0,8},{1,9},{2,10},{3,11},{4,12},{5,13},{6,14},{7,15},{8,0},{9,1},... | collective-permute-start | bytes 98312 | tf_op jit(solution)/shard_map/ppermute | solution.py:118
  2.7 2.6 %collective-permute-start.1 = (f32[4,16,128]{2,1,0:T(8,128)}, f32[4,16,128]{2,1,0:T(8,128)S(1)}, u32[]{:S(2)}, u32[]{:S(2)}) collective-permute-start(f32[4,16,128]{2,1,0:T(8,128)} %get-tuple-element.47), channel_id=1, source_target_pairs={{0,24},{1,25},{2,26},{3,27},{4,28},{5,29},{6,30},{7,31},{8,16},{9,... | collective-permute-start | bytes 98312 | tf_op jit(solution)/shard_map/ppermute | solution.py:119
  5.3 1.0 %copy-done = f32[2,32,16,128]{3,2,1,0:T(8,128)S(1)} copy-done((f32[2,32,16,128]{3,2,1,0:T(8,128)S(1)}, f32[2,32,16,128]{3,2,1,0:T(8,128)}, u32[]{:S(2)}) %copy-start) | copy-done | bytes 524312
  6.3 0.9 %copy-done.2 = s32[32,16,128]{2,1,0:T(8,128)S(1)} copy-done((s32[32,16,128]{2,1,0:T(8,128)S(1)}, s32[32,16,128]{2,1,0:T(8,128)}, u32[]{:S(2)}) %copy-start.2) | copy-done | bytes 262168
  7.3 0.2 shard_map.135
  7.5 1.6 %collective-permute-start.2 = (f32[144,128]{1,0:T(8,128)S(1)}, f32[144,128]{1,0:T(8,128)S(1)}, u32[]{:S(2)}, u32[]{:S(2)}) collective-permute-start(f32[144,128]{1,0:T(8,128)S(1)} %get-tuple-element.49), channel_id=1, source_target_pairs={{0,1},{1,0},{2,3},{3,2},{4,5},{5,4},{6,7},{7,6},{8,9},{9,8},{10,11... | collective-permute-start | bytes 221192 | tf_op jit(solution)/shard_map/ppermute | solution.py:122
  9.0 0.1 collective-permute-start.3
  9.2 1.6 %shard_map.136.inverse_ref = f32[4,336,144]{2,1,0:T(8,128)S(1)} custom-call(f32[2,8]{1,0:T(2,128)S(1)} %copy-done.5, f32[2,8]{1,0:T(2,128)S(1)} %copy-done.6, s32[32,16,128]{2,1,0:T(8,128)S(1)} %copy-done.3), custom_call_target="tpu_custom_call" | custom-call | flops 40000000 | bytes 1036288 | tf_op jit(solution)/shard_map/pallas_call | solution.py:880
  10.9 0.6 %shard_map.131.spectral_ref = f32[2,336,256]{2,1,0:T(8,128)S(1)} custom-call(f32[2,32,16,128]{3,2,1,0:T(8,128)S(1)} %copy-done.1, bf16[336,1008]{1,0:T(8,128)(2,1)S(1)} %copy-done.4), custom_call_target="tpu_custom_call" | custom-call | flops 700000000 | bytes 1889792 | tf_op jit(solution)/shard_map/pallas_call | solution.py:880
  11.5 1.2 %shard_map.133 = (f32[2,36,32,128]{3,2,1,0:T(8,128)S(1)}, f32[3,34,16,128]{3,2,1,0:T(8,128)S(1)}, f32[2,2,34,16,128]{4,3,2,1,0:T(8,128)S(1)}, f32[5,8,128]{2,1,0:T(8,128)S(1)}) custom-call(f32[2,8]{1,0:T(2,128)S(1)} %copy-done.5, f32[2,8]{1,0:T(2,128)S(1)} %copy-done.6, f32[8]{0:T(128)S(1)} %copy-done.7, s32[32,16,128]{2,1,0:T(8,128)S(1)} %copy-done.3, ...), custom_call_target="tpu_custom_call" | custom-call | flops 20000000 | bytes 3477504 | tf_op jit(solution)/shard_map/pallas_call | solution.py:880
  12.8 1.6 %shard_map.137 = (bf16[2,1008,256]{2,1,0:T(8,128)(2,1)S(1)}, f32[2,3,24,128]{3,2,1,0:T(8,128)S(1)}, f32[2,3,24,128]{3,2,1,0:T(8,128)S(1)}) custom-call(f32[2,336,256]{2,1,0:T(8,128)S(1)} %shard_map.131.spectral_ref, f32[3,34,16,128]{3,2,1,0:T(8,128)S(1)} %get-tuple-element.48.mass_ref, f32[4,16,128]{2,1,0:T(8,128)S(1)} %collective-permute-done.first_x.first_ref, ...), custom_call_target="tpu_custom_call" | custom-call | flops 2000000000 | bytes 4326400 | tf_op jit(solution)/shard_map/pallas_call | solution.py:880
  14.4 0.4 collective-permute-start.4
  14.8 1.2 %collective-permute-start.5 = (f32[2,3,24,128]{3,2,1,0:T(8,128)S(1)}, f32[2,3,24,128]{3,2,1,0:T(8,128)S(1)}, u32[]{:S(2)}, u32[]{:S(2)}) collective-permute-start(f32[2,3,24,128]{3,2,1,0:T(8,128)S(1)} %get-tuple-element.55), channel_id=1, source_target_pairs={{0,24},{1,25},{2,26},{3,27},{4,28},{5,29},{6,30},{7,31},{8,16},{9,... | collective-permute-start | bytes 221192 | tf_op jit(solution)/shard_map/ppermute | solution.py:119
  16.1 0.6 %shard_map.138 = (f32[2,34,16,128]{3,2,1,0:T(8,128)S(1)}, f32[2,2,40,128]{3,2,1,0:T(8,128)S(1)}, f32[2,96,128]{2,1,0:T(8,128)S(1)}, f32[2,96,128]{2,1,0:T(8,128)S(1)}) custom-call(bf16[2,1008,256]{2,1,0:T(8,128)(2,1)S(1)} %get-tuple-element.51.after_ref, bf16[336,1008]{1,0:T(8,128)(2,1)S(1)} %copy-done.8), custom_call_target="tpu_custom_call" | custom-call | flops 700000000 | bytes 2545152 | tf_op jit(solution)/shard_map/pallas_call | solution.py:880
  16.7 3.0 %collective-permute-start.6 = (f32[2,96,128]{2,1,0:T(8,128)S(1)}, f32[2,96,128]{2,1,0:T(8,128)S(1)}, u32[]{:S(2)}, u32[]{:S(2)}) collective-permute-start(f32[2,96,128]{2,1,0:T(8,128)S(1)} %get-tuple-element.58), channel_id=1, source_target_pairs={{0,1},{1,0},{2,3},{3,2},{4,5},{5,4},{6,7},{7,6},{8,9},{9,8},{10,11... | collective-permute-start | bytes 294920 | tf_op jit(solution)/shard_map/ppermute | solution.py:122
  19.7 3.1 %collective-permute-start.8 = (f32[2,24,128]{2,1,0:T(8,128)S(1)}, f32[2,24,128]{2,1,0:T(8,128)S(1)}, u32[]{:S(2)}, u32[]{:S(2)}) collective-permute-start(f32[2,24,128]{2,1,0:T(8,128)S(1)} %get-tuple-element.60), channel_id=1, source_target_pairs={{0,1},{1,0},{2,3},{3,2},{4,5},{5,4},{6,7},{7,6},{8,9},{9,8},{10,11... | collective-permute-start | bytes 73736 | tf_op jit(solution)/shard_map/ppermute | solution.py:122
  22.8 0.7 %shard_map.140 = (f32[2,36,32,128]{3,2,1,0:T(8,128)S(1)}, f32[2,8,40,128]{3,2,1,0:T(8,128)S(1)}, f32[3,4,40,128]{3,2,1,0:T(8,128)S(1)}, f32[2,2,4,40,128]{4,3,2,1,0:T(8,128)S(1)}) custom-call(f32[2,36,32,128]{3,2,1,0:T(8,128)S(1)} %get-tuple-element.62.old_half_ref, ...), custom_call_target="tpu_custom_call", output_to_operand_aliasing={{0}: (0, {})} | custom-call | flops 2000000 | bytes 5459968 | tf_op jit(solution)/shard_map/pallas_call | solution.py:880
  23.5 1.4 %shard_map.141 = (f32[2,34,16,128]{3,2,1,0:T(8,128)S(1)}, f32[2,336,256]{2,1,0:T(8,128)S(1)}) custom-call(f32[2,36,16,128]{3,2,1,0:T(8,128)S(1)} %get-tuple-element.56.whole_ref, f32[2,2,40,128]{3,2,1,0:T(8,128)S(1)} %get-tuple-element.57.after_ref.whole_rows_ref, f32[2,36,32,128]{3,2,1,0:T(8,128)S(1)} %get-tuple-element.68.half_ref, ...), custom_call_target="tpu_custom_call" | custom-call | flops 700000000 | bytes 5723648 | tf_op jit(solution)/shard_map/pallas_call | solution.py:880
  24.9 1.9 %shard_map.142 = (f32[2,2,40,128]{3,2,1,0:T(8,128)S(1)}, f32[2,6,40,128]{3,2,1,0:T(8,128)S(1)}, bf16[2,1008,256]{2,1,0:T(8,128)(2,1)S(1)}, f32[2,2,24,128]{3,2,1,0:T(8,128)S(1)}, f32[2,2,24,128]{3,2,1,0:T(8,128)S(1)}) custom-call(f32[2,36,16,128]{3,2,1,0:T(8,128)S(1)} %get-tuple-element.56.whole_ref, ...), custom_call_target="tpu_custom_call" | custom-call | flops 2000000000 | bytes 5504000 | tf_op jit(solution)/shard_map/pallas_call | solution.py:880
  26.8 0.6 %collective-permute-start.10 = (f32[2,2,24,128]{3,2,1,0:T(8,128)S(1)}, f32[2,2,24,128]{3,2,1,0:T(8,128)S(1)}, u32[]{:S(2)}, u32[]{:S(2)}) collective-permute-start(f32[2,2,24,128]{3,2,1,0:T(8,128)S(1)} %get-tuple-element.73), channel_id=1, source_target_pairs={{0,8},{1,9},{2,10},{3,11},{4,12},{5,13},{6,14},{7,15},{8,0},{9,1},... | collective-permute-start | bytes 147464 | tf_op jit(solution)/shard_map/ppermute | solution.py:118
  27.4 0.2 collective-permute-start.11
  27.7 0.5 %shard_map.143 = (f32[2,34,16,128]{3,2,1,0:T(8,128)S(1)}, f32[2,2,40,128]{3,2,1,0:T(8,128)S(1)}) custom-call(bf16[2,1008,256]{2,1,0:T(8,128)(2,1)S(1)} %get-tuple-element.70.after_ref, bf16[336,1008]{1,0:T(8,128)(2,1)S(1)} %copy-done.8), custom_call_target="tpu_custom_call" | custom-call | flops 700000000 | bytes 2348544 | tf_op jit(solution)/shard_map/pallas_call | solution.py:880
  28.3 2.9 %collective-permute-done.11.second_ref = f32[2,2,24,128]{3,2,1,0:T(8,128)S(1)} collective-permute-done((f32[2,2,24,128]{3,2,1,0:T(8,128)S(1)}, f32[2,2,24,128]{3,2,1,0:T(8,128)S(1)}, u32[]{:S(2)}, u32[]{:S(2)}) %collective-permute-start.11) | collective-permute-done | bytes 49184 | tf_op jit(solution)/shard_map/ppermute | solution.py:119
  31.3 2.4 %collective-permute-start.12 = (f32[2,72,128]{2,1,0:T(8,128)S(1)}, f32[2,72,128]{2,1,0:T(8,128)S(1)}, u32[]{:S(2)}, u32[]{:S(2)}) collective-permute-start(f32[2,72,128]{2,1,0:T(8,128)S(1)} %get-tuple-element.82), channel_id=1, source_target_pairs={{0,1},{1,0},{2,3},{3,2},{4,5},{5,4},{6,7},{7,6},{8,9},{9,8},{10,11... | collective-permute-start | bytes 221192 | tf_op jit(solution)/shard_map/ppermute | solution.py:122
  33.7 0.2 collective-permute-start.13
  33.9 0.4 shard_map.145
  34.3 0.8 %shard_map.146 = (f32[2,32,16,128]{3,2,1,0:T(8,128)S(1)}, f32[8,128]{1,0:T(8,128)S(1)}) custom-call(f32[2,36,16,128]{3,2,1,0:T(8,128)S(1)} %get-tuple-element.75.whole_ref.w_ref, f32[2,2,40,128]{3,2,1,0:T(8,128)S(1)} %get-tuple-element.76.whole_rows_ref, f32[2,36,32,128]{3,2,1,0:T(8,128)S(1)} %get-tuple-element.68.half_ref, ...), custom_call_target="tpu_custom_call" | custom-call | flops 10000000 | bytes 4853760 | tf_op jit(solution)/shard_map/pallas_call | solution.py:880
  35.1 2.3 %collective-permute-done.12.first_ref = f32[2,72,128]{2,1,0:T(8,128)S(1)} collective-permute-done((f32[2,72,128]{2,1,0:T(8,128)S(1)}, f32[2,72,128]{2,1,0:T(8,128)S(1)}, u32[]{:S(2)}, u32[]{:S(2)}) %collective-permute-start.12) | collective-permute-done | bytes 73760 | tf_op jit(solution)/shard_map/ppermute | solution.py:122
  37.5 0.4 shard_map.147
  37.9 12.1 %all_to_all.11 = f32[32,1,128]{2,1,0:T(1,128)S(1)} all-to-all(f32[32,1,128]{2,1,0:T(1,128)S(1)} %bitcast.5), channel_id=1, replica_groups=mesh['gx'=4,'gy'=8] {'gx','gy'}, dimensions={0} | all-to-all | bytes 32768 | tf_op jit(solution)/shard_map/all_to_all | solution.py:1030
  50.0 1.2 %shard_map.148 = (f32[2,32,16,128]{3,2,1,0:T(8,128)}, f32[2,32,16,128]{3,2,1,0:T(8,128)}) custom-call(f32[32,128]{1,0:T(8,128)S(1)} %bitcast.4, f32[2,32,16,128]{3,2,1,0:T(8,128)S(1)} %copy-done.1, f32[2,32,16,128]{3,2,1,0:T(8,128)S(1)} %get-tuple-element.87.z_ref, f32[2,32,16,128]{3,2,1,0:T(8,128)S(1)} %get-tuple-element.80.old_image_ref.q_ref, ...), custom_call_target="tpu_custom_call" | custom-call | bytes 3948544 | tf_op jit(solution)/shard_map/pallas_call | solution.py:880
  (43 shorter events, 0.5 us)
Async XLA Ops:
  0.6 8.6 %copy-start.3 = (s32[32,16,128]{2,1,0:T(8,128)S(1)}, s32[32,16,128]{2,1,0:T(8,128)}, u32[]{:S(2)}) copy-start(s32[32,16,128]{2,1,0:T(8,128)} %zones_ref.7) | copy-start | bytes 786436
  0.6 8.6 %copy-start.6 = (f32[2,8]{1,0:T(2,128)S(1)}, f32[2,8]{1,0:T(2,128)}, u32[]{:S(2)}) copy-start(f32[2,8]{1,0:T(2,128)} %capacity_ref.3) | copy-start | bytes 196
  0.7 8.5 %copy-start.5 = (f32[2,8]{1,0:T(2,128)S(1)}, f32[2,8]{1,0:T(2,128)}, u32[]{:S(2)}) copy-start(f32[2,8]{1,0:T(2,128)} %conductance_ref.3) | copy-start | bytes 196
  2.1 5.2 %collective-permute-start = (f32[4,16,128]{2,1,0:T(8,128)}, f32[4,16,128]{2,1,0:T(8,128)S(1)}, u32[]{:S(2)}, u32[]{:S(2)}) collective-permute-start(f32[4,16,128]{2,1,0:T(8,128)} %get-tuple-element.46), channel_id=1, source_target_pairs={{0,8},{1,9},{2,10},{3,11},{4,12},{5,13},{6,14},{7,15},{8,0},{9,1},... | collective-permute-start | bytes 98312 | tf_op jit(solution)/shard_map/ppermute | solution.py:118
  2.7 4.7 %collective-permute-start.1 = (f32[4,16,128]{2,1,0:T(8,128)}, f32[4,16,128]{2,1,0:T(8,128)S(1)}, u32[]{:S(2)}, u32[]{:S(2)}) collective-permute-start(f32[4,16,128]{2,1,0:T(8,128)} %get-tuple-element.47), channel_id=1, source_target_pairs={{0,24},{1,25},{2,26},{3,27},{4,28},{5,29},{6,30},{7,31},{8,16},{9,... | collective-permute-start | bytes 98312 | tf_op jit(solution)/shard_map/ppermute | solution.py:119
  5.3 1.0 %copy-start = (f32[2,32,16,128]{3,2,1,0:T(8,128)S(1)}, f32[2,32,16,128]{3,2,1,0:T(8,128)}, u32[]{:S(2)}) copy-start(f32[2,32,16,128]{3,2,1,0:T(8,128)} %load_ref.9) | copy-start | bytes 1572868
  6.3 0.9 %copy-start.2 = (s32[32,16,128]{2,1,0:T(8,128)S(1)}, s32[32,16,128]{2,1,0:T(8,128)}, u32[]{:S(2)}) copy-start(s32[32,16,128]{2,1,0:T(8,128)} %zones_ref.7) | copy-start | bytes 786436
  7.3 3.5 %copy-start.1 = (f32[2,32,16,128]{3,2,1,0:T(8,128)S(1)}, f32[2,32,16,128]{3,2,1,0:T(8,128)}, u32[]{:S(2)}) copy-start(f32[2,32,16,128]{3,2,1,0:T(8,128)} %load_ref.9) | copy-start | bytes 1572868
  7.3 3.5 %copy-start.4 = (bf16[336,1008]{1,0:T(8,128)(2,1)S(1)}, bf16[336,1008]{1,0:T(8,128)(2,1)}, u32[]{:S(2)}) copy-start(bf16[336,1008]{1,0:T(8,128)(2,1)} %constant.14.clone.forward_ref) | copy-start | bytes 2032132
  7.5 5.3 %collective-permute-start.2 = (f32[144,128]{1,0:T(8,128)S(1)}, f32[144,128]{1,0:T(8,128)S(1)}, u32[]{:S(2)}, u32[]{:S(2)}) collective-permute-start(f32[144,128]{1,0:T(8,128)S(1)} %get-tuple-element.49), channel_id=1, source_target_pairs={{0,1},{1,0},{2,3},{3,2},{4,5},{5,4},{6,7},{7,6},{8,9},{9,8},{10,11... | collective-permute-start | bytes 221192 | tf_op jit(solution)/shard_map/ppermute | solution.py:122
  9.0 3.7 %collective-permute-start.3 = (f32[144,128]{1,0:T(8,128)S(1)}, f32[144,128]{1,0:T(8,128)S(1)}, u32[]{:S(2)}, u32[]{:S(2)}) collective-permute-start(f32[144,128]{1,0:T(8,128)S(1)} %get-tuple-element.50), channel_id=1, source_target_pairs={{0,8},{1,2},{2,1},{3,4},{4,3},{5,6},{6,5},{7,15},{8,0},{9,10},{10,... | collective-permute-start | bytes 221192 | tf_op jit(solution)/shard_map/ppermute | solution.py:121
  10.8 0.7 %copy-start.7 = (f32[8]{0:T(128)S(1)}, f32[8]{0:T(128)}, u32[]{:S(2)}) copy-start(f32[8]{0:T(128)} %coupling_ref.1) | copy-start | bytes 100
  10.8 2.0 %copy-start.10 = (bf16[144,1008]{1,0:T(8,128)(2,1)S(1)}, bf16[144,1008]{1,0:T(8,128)(2,1)}, u32[]{:S(2)}) copy-start(bf16[144,1008]{1,0:T(8,128)(2,1)} %constant.20.clone.edges_ref) | copy-start | bytes 870916
  10.8 2.0 %copy-start.11 = (bf16[384,144]{1,0:T(8,128)(2,1)S(1)}, bf16[384,144]{1,0:T(8,128)(2,1)}, u32[]{:S(2)}) copy-start(bf16[384,144]{1,0:T(8,128)(2,1)} %constant.16.clone.c2) | copy-start | bytes 331780
  10.9 2.0 %copy-start.12 = (bf16[336,240]{1,0:T(8,128)(2,1)S(1)}, bf16[336,240]{1,0:T(8,128)(2,1)}, u32[]{:S(2)}) copy-start(bf16[336,240]{1,0:T(8,128)(2,1)} %constant.18.clone.ends_ref) | copy-start | bytes 483844
  10.9 2.0 %copy-start.13 = (bf16[144,256]{1,0:T(8,128)(2,1)S(1)}, bf16[144,256]{1,0:T(8,128)(2,1)}, u32[]{:S(2)}) copy-start(bf16[144,256]{1,0:T(8,128)(2,1)} %constant.17.clone.c3) | copy-start | bytes 221188
  12.8 3.3 %copy-start.8 = (bf16[336,1008]{1,0:T(8,128)(2,1)S(1)}, bf16[336,1008]{1,0:T(8,128)(2,1)}, u32[]{:S(2)}) copy-start(bf16[336,1008]{1,0:T(8,128)(2,1)} %constant.15.clone.back_ref) | copy-start | bytes 2032132
  14.4 5.2 %collective-permute-start.4 = (f32[2,3,24,128]{3,2,1,0:T(8,128)S(1)}, f32[2,3,24,128]{3,2,1,0:T(8,128)S(1)}, u32[]{:S(2)}, u32[]{:S(2)}) collective-permute-start(f32[2,3,24,128]{3,2,1,0:T(8,128)S(1)} %get-tuple-element.54), channel_id=1, source_target_pairs={{0,8},{1,9},{2,10},{3,11},{4,12},{5,13},{6,14},{7,15},{8,0},{9,1},... | collective-permute-start | bytes 221192 | tf_op jit(solution)/shard_map/ppermute | solution.py:118
  14.8 4.8 %collective-permute-start.5 = (f32[2,3,24,128]{3,2,1,0:T(8,128)S(1)}, f32[2,3,24,128]{3,2,1,0:T(8,128)S(1)}, u32[]{:S(2)}, u32[]{:S(2)}) collective-permute-start(f32[2,3,24,128]{3,2,1,0:T(8,128)S(1)} %get-tuple-element.55), channel_id=1, source_target_pairs={{0,24},{1,25},{2,26},{3,27},{4,28},{5,29},{6,30},{7,31},{8,16},{9,... | collective-permute-start | bytes 221192 | tf_op jit(solution)/shard_map/ppermute | solution.py:119
  16.7 8.2 %collective-permute-start.6 = (f32[2,96,128]{2,1,0:T(8,128)S(1)}, f32[2,96,128]{2,1,0:T(8,128)S(1)}, u32[]{:S(2)}, u32[]{:S(2)}) collective-permute-start(f32[2,96,128]{2,1,0:T(8,128)S(1)} %get-tuple-element.58), channel_id=1, source_target_pairs={{0,1},{1,0},{2,3},{3,2},{4,5},{5,4},{6,7},{7,6},{8,9},{9,8},{10,11... | collective-permute-start | bytes 294920 | tf_op jit(solution)/shard_map/ppermute | solution.py:122
  19.6 5.3 %collective-permute-start.7 = (f32[2,96,128]{2,1,0:T(8,128)S(1)}, f32[2,96,128]{2,1,0:T(8,128)S(1)}, u32[]{:S(2)}, u32[]{:S(2)}) collective-permute-start(f32[2,96,128]{2,1,0:T(8,128)S(1)} %get-tuple-element.59), channel_id=1, source_target_pairs={{0,8},{1,2},{2,1},{3,4},{4,3},{5,6},{6,5},{7,15},{8,0},{9,10},{10,... | collective-permute-start | bytes 294920 | tf_op jit(solution)/shard_map/ppermute | solution.py:121
  19.7 5.2 %collective-permute-start.8 = (f32[2,24,128]{2,1,0:T(8,128)S(1)}, f32[2,24,128]{2,1,0:T(8,128)S(1)}, u32[]{:S(2)}, u32[]{:S(2)}) collective-permute-start(f32[2,24,128]{2,1,0:T(8,128)S(1)} %get-tuple-element.60), channel_id=1, source_target_pairs={{0,1},{1,0},{2,3},{3,2},{4,5},{5,4},{6,7},{7,6},{8,9},{9,8},{10,11... | collective-permute-start | bytes 73736 | tf_op jit(solution)/shard_map/ppermute | solution.py:122
  22.8 2.1 %collective-permute-start.9 = (f32[2,24,128]{2,1,0:T(8,128)S(1)}, f32[2,24,128]{2,1,0:T(8,128)S(1)}, u32[]{:S(2)}, u32[]{:S(2)}) collective-permute-start(f32[2,24,128]{2,1,0:T(8,128)S(1)} %get-tuple-element.61), channel_id=1, source_target_pairs={{0,8},{1,2},{2,1},{3,4},{4,3},{5,6},{6,5},{7,15},{8,0},{9,10},{10,... | collective-permute-start | bytes 73736 | tf_op jit(solution)/shard_map/ppermute | solution.py:121
  23.5 1.4 %copy-start.9 = (bf16[336,432]{1,0:T(8,128)(2,1)S(1)}, bf16[336,432]{1,0:T(8,128)(2,1)}, u32[]{:S(2)}) copy-start(bf16[336,432]{1,0:T(8,128)(2,1)} %constant.19.clone.lines_ref) | copy-start | bytes 870916
  26.8 1.5 %collective-permute-start.10 = (f32[2,2,24,128]{3,2,1,0:T(8,128)S(1)}, f32[2,2,24,128]{3,2,1,0:T(8,128)S(1)}, u32[]{:S(2)}, u32[]{:S(2)}) collective-permute-start(f32[2,2,24,128]{3,2,1,0:T(8,128)S(1)} %get-tuple-element.73), channel_id=1, source_target_pairs={{0,8},{1,9},{2,10},{3,11},{4,12},{5,13},{6,14},{7,15},{8,0},{9,1},... | collective-permute-start | bytes 147464 | tf_op jit(solution)/shard_map/ppermute | solution.py:118
  27.4 3.8 %collective-permute-start.11 = (f32[2,2,24,128]{3,2,1,0:T(8,128)S(1)}, f32[2,2,24,128]{3,2,1,0:T(8,128)S(1)}, u32[]{:S(2)}, u32[]{:S(2)}) collective-permute-start(f32[2,2,24,128]{3,2,1,0:T(8,128)S(1)} %get-tuple-element.74), channel_id=1, source_target_pairs={{0,24},{1,25},{2,26},{3,27},{4,28},{5,29},{6,30},{7,31},{8,16},{9,... | collective-permute-start | bytes 147464 | tf_op jit(solution)/shard_map/ppermute | solution.py:119
  31.3 6.2 %collective-permute-start.12 = (f32[2,72,128]{2,1,0:T(8,128)S(1)}, f32[2,72,128]{2,1,0:T(8,128)S(1)}, u32[]{:S(2)}, u32[]{:S(2)}) collective-permute-start(f32[2,72,128]{2,1,0:T(8,128)S(1)} %get-tuple-element.82), channel_id=1, source_target_pairs={{0,1},{1,0},{2,3},{3,2},{4,5},{5,4},{6,7},{7,6},{8,9},{9,8},{10,11... | collective-permute-start | bytes 221192 | tf_op jit(solution)/shard_map/ppermute | solution.py:122
  33.7 3.8 %collective-permute-start.13 = (f32[2,72,128]{2,1,0:T(8,128)S(1)}, f32[2,72,128]{2,1,0:T(8,128)S(1)}, u32[]{:S(2)}, u32[]{:S(2)}) collective-permute-start(f32[2,72,128]{2,1,0:T(8,128)S(1)} %get-tuple-element.83), channel_id=1, source_target_pairs={{0,8},{1,2},{2,1},{3,4},{4,3},{5,6},{6,5},{7,15},{8,0},{9,10},{10,... | collective-permute-start | bytes 221192 | tf_op jit(solution)/shard_map/ppermute | solution.py:121

commit v9 on v8

--- a/solution.py
+++ b/solution.py
@@ -226,28 +226,28 @@
         pack_lines(standing(mesh), out_ref, out_rows_ref, *lines_refs)
 
 
+def x_depth(message_ref):
+    return message_ref.shape[1] // SPAN
+
+
 def pack_x(flags, after_ref, edges_ref, even_ref, odd_ref):
-    depth, size_z = even_ref.shape[1], even_ref.shape[3]
-    size_y = BOX
-    after = len(EDGE_LAYERS) * size_y
+    depth, size_z = x_depth(even_ref), even_ref.shape[2]
+    layers = depth * BOX
+    after = len(EDGE_LAYERS) * BOX
     for field in range(2):
         result = dot(edges_ref[...], after_ref[field])
         low, high = result[:, :size_z], result[:, result.shape[1] - size_z :]
-        for layer in range(depth):
-            far = len(EDGE_LAYERS) - depth + layer
-            pairs = [(slice(0, size_y), low[layer * size_y : (layer + 1) * size_y], high[far * size_y : (far + 1) * size_y])]
-            for side in range(2):
-                near_row = after + 24 * side + ROW0 - 1 + layer
-                far_row = after + 24 * side + ROW0 - 1 + SPAN - depth + layer
-                pairs.append(
-                    (slice(size_y + side, size_y + side + 1), low[near_row : near_row + 1], high[far_row : far_row + 1])
-                )
-            for place, to_low, to_high in pairs:
-                even_ref[field, layer, place] = chosen(flags, EVEN_X, to_high, to_low)
-                odd_ref[field, layer, place] = chosen(flags, EVEN_X, to_low, to_high)
-            blank = jnp.zeros((even_ref.shape[2] - size_y - 2, size_z), F32)
-            even_ref[field, layer, size_y + 2 :] = blank
-            odd_ref[field, layer, size_y + 2 :] = blank
+        pairs = [(0, low[:layers], high[after - layers : after])]
+        for side in range(2):
+            near = after + 24 * side + ROW0 - 1
+            far = near + SPAN - depth
+            pairs.append((layers + depth * side, low[near : near + depth], high[far : far + depth]))
+        blank = jnp.zeros((even_ref.shape[1] - SPAN * depth, size_z), F32)
+        pairs.append((SPAN * depth, blank, blank))
+        for start, to_low, to_high in pairs:
+            place = slice(start, start + to_low.shape[0])
+            even_ref[field, place] = chosen(flags, EVEN_X, to_high, to_low)
+            odd_ref[field, place] = chosen(flags, EVEN_X, to_low, to_high)
 
 
 def line_pairs(whole_ref, whole_rows_ref, field, layers, rows, depth):
@@ -555,35 +555,41 @@
     flags = standing(mesh)
     size_x = part_ref.shape[1] - 2
     size_y, size_z = part_ref.shape[2:]
-    depth = first_ref.shape[1]
+    depth = x_depth(first_ref)
     end = ROW0 + size_x
     for field in range(2):
         low = keep(flags, LOW_X, chosen(flags, EVEN_X, second_ref[field], first_ref[field]))
         high = keep(flags, HIGH_X, chosen(flags, EVEN_X, first_ref[field], second_ref[field]))
-        whole_ref[field, 1] = keep(flags, LOW_X, part_ref[field, 0]) + low[depth - 2, :size_y]
-        whole_ref[field, 2] = part_ref[field, 1] + low[depth - 1, :size_y]
+        low_layers, high_layers = [
+            [came[layer * size_y : (layer + 1) * size_y] for layer in range(depth)] for came in (low, high)
+        ]
+        whole_ref[field, 1] = keep(flags, LOW_X, part_ref[field, 0]) + low_layers[depth - 2]
+        whole_ref[field, 2] = part_ref[field, 1] + low_layers[depth - 1]
         whole_ref[field, 3 : size_x + 1] = part_ref[field, 2:size_x]
-        whole_ref[field, size_x + 1] = part_ref[field, size_x] + high[0, :size_y]
-        whole_ref[field, size_x + 2] = keep(flags, HIGH_X, part_ref[field, size_x + 1]) + high[1, :size_y]
-        whole_ref[field, 0] = low[0, :size_y] if depth == 3 else jnp.zeros((size_y, size_z), F32)
-        whole_ref[field, size_x + 3] = high[2, :size_y] if depth == 3 else jnp.zeros((size_y, size_z), F32)
+        whole_ref[field, size_x + 1] = part_ref[field, size_x] + high_layers[0]
+        whole_ref[field, size_x + 2] = keep(flags, HIGH_X, part_ref[field, size_x + 1]) + high_layers[1]
+        whole_ref[field, 0] = low_layers[0] if depth == 3 else jnp.zeros((size_y, size_z), F32)
+        whole_ref[field, size_x + 3] = high_layers[2] if depth == 3 else jnp.zeros((size_y, size_z), F32)
         for side in range(2):
-            row = slice(size_y + side, size_y + side + 1)
+            start = depth * (size_y + side)
+            low_row, high_row = [
+                [came[start + layer : start + layer + 1] for layer in range(depth)] for came in (low, high)
+            ]
             edge = ROW0 - 1
             whole_rows_ref[field, side] = part_rows_ref[field, side]
             whole_rows_ref[field, side, edge : edge + 1] = (
-                keep(flags, LOW_X, part_rows_ref[field, side, edge : edge + 1]) + low[depth - 2, row]
+                keep(flags, LOW_X, part_rows_ref[field, side, edge : edge + 1]) + low_row[depth - 2]
             )
             whole_rows_ref[field, side, edge + 1 : edge + 2] = (
-                part_rows_ref[field, side, edge + 1 : edge + 2] + low[depth - 1, row]
+                part_rows_ref[field, side, edge + 1 : edge + 2] + low_row[depth - 1]
             )
-            whole_rows_ref[field, side, end - 1 : end] = part_rows_ref[field, side, end - 1 : end] + high[0, row]
+            whole_rows_ref[field, side, end - 1 : end] = part_rows_ref[field, side, end - 1 : end] + high_row[0]
             whole_rows_ref[field, side, end : end + 1] = (
-                keep(flags, HIGH_X, part_rows_ref[field, side, end : end + 1]) + high[1, row]
+                keep(flags, HIGH_X, part_rows_ref[field, side, end : end + 1]) + high_row[1]
             )
             if depth == 3:
-                whole_rows_ref[field, side, edge - 1 : edge] = low[0, row]
-                whole_rows_ref[field, side, end + 1 : end + 2] = high[2, row]
+                whole_rows_ref[field, side, edge - 1 : edge] = low_row[0]
+                whole_rows_ref[field, side, end + 1 : end + 2] = high_row[2]
 
         base = 2 * size_x if depth == 2 else 0
         for ref in (even_ref, odd_ref):
@@ -650,6 +656,10 @@
     return values, (first, second)
 
 
+def merge_x_after_kernel(mesh, part_ref, part_rows_ref, first_ref, second_ref, sums_ref, *outs):
+    merge_x_kernel(mesh, part_ref, part_rows_ref, first_ref, second_ref, *outs)
+
+
 def fill(flags, whole_ref, whole_rows_ref, value_ref):
     size_x, size_y = whole_ref.shape[1] - 4, whole_ref.shape[2]
     spread = slice(ROW0 - 2, ROW0 + size_x + 2)
@@ -884,7 +894,7 @@
         out_specs=tuple([HBM if outs_in_hbm else VMEM] * len(outs)),
         scratch_shapes=list(scratch),
         input_output_aliases=dict(aliases),
-        compiler_params=pltpu.CompilerParams(vmem_limit_bytes=limit * 1024 * 1024),
+        compiler_params=pltpu.CompilerParams(vmem_limit_bytes=int(limit * 1024 * 1024)),
         cost_estimate=pl.CostEstimate(flops=flops, bytes_accessed=moved, transcendentals=0),
     )(*scalars, *arrays)
 
@@ -913,7 +923,7 @@
             pltpu.SemaphoreType.DMA((4,)),
         ],
         in_hbm=True,
-        limit=56,
+        limit=53.75,
     )
     (token,) = call(None, fetched_kernel, [], [load, zones], [sds(8, size_z)])
     x_halo = swap(mesh, "gx", *packed)
@@ -939,7 +949,7 @@
         flops=20_000_000,
     )
     parts = [sds(2, size_x + 2, size_y, size_z), sds(2, 2, count, size_z)]
-    packed_x = [[sds(2, depth, size_y + 8, size_z)] * 2 for depth in (3, 2)]
+    packed_x = [[sds(2, round_up(depth * SPAN, 8), size_z)] * 2 for depth in (3, 2)]
     wholes = [sds(2, size_x + 4, size_y, size_z), sds(2, 2, count, size_z)]
     packed_lines = [sds(2, 3 * size_x, size_z)] * 2
     packed_ends = [sds(2, 3 * 8, size_z)] * 2
@@ -1006,7 +1016,9 @@
     precond, image, sums = call(
         None, first_sums_kernel, [], [load, whole, own_image, deltas, changes], [own, own, sds(8, size_z)], flops=1_000_000
     )
-    whole, whole_rows, *packed = call(mesh, merge_x_kernel, [], [part, part_rows, *received], wholes + packed_y)
+    whole, whole_rows, *packed = call(
+        mesh, merge_x_after_kernel, [], [part, part_rows, *received, sums], wholes + packed_y
+    )
     received = swap(mesh, "gy", *packed)
     last_image, own_sums = call(
         mesh,

time: 51.5 us -> 50.2 us (0.975)
    ppermute x7, waiting for transfers between devices: 2.91 us -> 2.24 us  [swap(): second = lax.ppermute(odd_part, AXES, swap_pairs(mesh, axis, True))]
    pallas_call x18, Pallas kernels: 14.7 us -> 14.2 us  [call(): pl.pallas_call(kernel if mesh is None else functools.partial(kernel, mesh...]
  transfers between devices with their start and end apart: 14 -> 14, of which waited for: 3 -> 2; matrix products, arithmetic and copies ran while one was open for 0% -> 0% of each run, Pallas kernels for 15% -> 16%
where the time goes in v9:
time: 50.2 us; the launch traced here: 49.9 us
  starting transfers between devices  16.1 us (32%)
  Pallas kernels  14.2 us (28%)
  blocking collectives  11.7 us (23%)
  waiting for transfers between devices  4.99 us (10%)
  local copies, waits for them, and re-layouts  2.06 us (4%)
  between operations  0.96 us (2%)
    pallas_call x18, Pallas kernels, call(): pl.pallas_call(kernel if mesh is None else functools.partial(kernel, mesh...  14.2 us
    ppermute x7, starting transfers between devices, swap(): first = lax.ppermute(even_part, AXES, swap_pairs(mesh, axis, False))  11.8 us
    all_to_all x1, blocking collectives, shards(): sums = lax.all_to_all(sums, AXES, 0, 0, tiled=True)  11.7 us
    ppermute x7, starting transfers between devices, swap(): second = lax.ppermute(odd_part, AXES, swap_pairs(mesh, axis, True))  4.3 us
    ppermute x7, waiting for transfers between devices, swap(): first = lax.ppermute(even_part, AXES, swap_pairs(mesh, axis, False))  2.75 us
    ppermute x7, waiting for transfers between devices, swap(): second = lax.ppermute(odd_part, AXES, swap_pairs(mesh, axis, True))  2.24 us
    unnamed x28, local copies, waits for them, and re-layouts  2.06 us
  transfers between devices with their start and end apart: 14, of which 2 were waited for; matrix products, arithmetic and copies ran while one was open for 0% of the time, Pallas kernels for 16%

profile of v9, /device:TPU:0, one launch (start us, length us, event | category | flops | bytes accessed | tf_op | source)
XLA Modules:
  0.0 49.9 jit_solution(9598217623826550155)
XLA Ops:
  0.7 0.8 %shard_map.132 = (f32[4,16,128]{2,1,0:T(8,128)S(1)}, f32[4,16,128]{2,1,0:T(8,128)S(1)}) custom-call(f32[2,32,16,128]{3,2,1,0:T(8,128)} %load_ref.9, s32[32,16,128]{2,1,0:T(8,128)} %zones_ref.7), custom_call_target="tpu_custom_call" | custom-call | bytes 851968 | tf_op jit(solution)/shard_map/pallas_call | solution.py:890
  1.5 0.5 %collective-permute-start = (f32[4,16,128]{2,1,0:T(8,128)S(1)}, f32[4,16,128]{2,1,0:T(8,128)S(1)}, u32[]{:S(2)}, u32[]{:S(2)}) collective-permute-start(f32[4,16,128]{2,1,0:T(8,128)S(1)} %get-tuple-element.46), channel_id=1, source_target_pairs={{0,8},{1,9},{2,10},{3,11},{4,12},{5,13},{6,14},{7,15},{8,0},{9,1},... | collective-permute-start | bytes 98312 | tf_op jit(solution)/shard_map/ppermute | solution.py:118
  2.0 2.6 %collective-permute-start.1 = (f32[4,16,128]{2,1,0:T(8,128)S(1)}, f32[4,16,128]{2,1,0:T(8,128)S(1)}, u32[]{:S(2)}, u32[]{:S(2)}) collective-permute-start(f32[4,16,128]{2,1,0:T(8,128)S(1)} %get-tuple-element.47), channel_id=1, source_target_pairs={{0,24},{1,25},{2,26},{3,27},{4,28},{5,29},{6,30},{7,31},{8,16},{9,... | collective-permute-start | bytes 98312 | tf_op jit(solution)/shard_map/ppermute | solution.py:119
  4.7 1.0 %copy-done = f32[2,32,16,128]{3,2,1,0:T(8,128)S(1)} copy-done((f32[2,32,16,128]{3,2,1,0:T(8,128)S(1)}, f32[2,32,16,128]{3,2,1,0:T(8,128)}, u32[]{:S(2)}) %copy-start) | copy-done | bytes 524312
  5.7 0.9 %copy-done.2 = s32[32,16,128]{2,1,0:T(8,128)S(1)} copy-done((s32[32,16,128]{2,1,0:T(8,128)S(1)}, s32[32,16,128]{2,1,0:T(8,128)}, u32[]{:S(2)}) %copy-start.2) | copy-done | bytes 262168
  6.7 0.2 shard_map.135
  6.9 1.6 %collective-permute-start.2 = (f32[144,128]{1,0:T(8,128)S(1)}, f32[144,128]{1,0:T(8,128)S(1)}, u32[]{:S(2)}, u32[]{:S(2)}) collective-permute-start(f32[144,128]{1,0:T(8,128)S(1)} %get-tuple-element.49), channel_id=1, source_target_pairs={{0,1},{1,0},{2,3},{3,2},{4,5},{5,4},{6,7},{7,6},{8,9},{9,8},{10,11... | collective-permute-start | bytes 221192 | tf_op jit(solution)/shard_map/ppermute | solution.py:122
  8.4 1.6 %shard_map.136.inverse_ref = f32[4,336,144]{2,1,0:T(8,128)S(1)} custom-call(f32[2,8]{1,0:T(2,128)S(1)} %copy-done.5, f32[2,8]{1,0:T(2,128)S(1)} %copy-done.6, s32[32,16,128]{2,1,0:T(8,128)S(1)} %copy-done.3), custom_call_target="tpu_custom_call" | custom-call | flops 40000000 | bytes 1036288 | tf_op jit(solution)/shard_map/pallas_call | solution.py:890
  10.1 0.6 %shard_map.131.spectral_ref = f32[2,336,256]{2,1,0:T(8,128)S(1)} custom-call(f32[2,32,16,128]{3,2,1,0:T(8,128)S(1)} %copy-done.1, bf16[336,1008]{1,0:T(8,128)(2,1)S(1)} %copy-done.4), custom_call_target="tpu_custom_call" | custom-call | flops 700000000 | bytes 1889792 | tf_op jit(solution)/shard_map/pallas_call | solution.py:890
  10.8 1.2 %shard_map.133 = (f32[2,36,32,128]{3,2,1,0:T(8,128)S(1)}, f32[3,34,16,128]{3,2,1,0:T(8,128)S(1)}, f32[2,2,34,16,128]{4,3,2,1,0:T(8,128)S(1)}, f32[5,8,128]{2,1,0:T(8,128)S(1)}) custom-call(f32[2,8]{1,0:T(2,128)S(1)} %copy-done.5, f32[2,8]{1,0:T(2,128)S(1)} %copy-done.6, f32[8]{0:T(128)S(1)} %copy-done.7, s32[32,16,128]{2,1,0:T(8,128)S(1)} %copy-done.3, ...), custom_call_target="tpu_custom_call" | custom-call | flops 20000000 | bytes 3477504 | tf_op jit(solution)/shard_map/pallas_call | solution.py:890
  12.1 1.6 %shard_map.137 = (bf16[2,1008,256]{2,1,0:T(8,128)(2,1)S(1)}, f32[2,56,128]{2,1,0:T(8,128)S(1)}, f32[2,56,128]{2,1,0:T(8,128)S(1)}) custom-call(f32[2,336,256]{2,1,0:T(8,128)S(1)} %shard_map.131.spectral_ref, f32[3,34,16,128]{3,2,1,0:T(8,128)S(1)} %get-tuple-element.48.mass_ref, f32[4,16,128]{2,1,0:T(8,128)S(1)} %collective-permute-done.first_x.first_ref, ...), custom_call_target="tpu_custom_call" | custom-call | flops 2000000000 | bytes 4293632 | tf_op jit(solution)/shard_map/pallas_call | solution.py:890
  13.7 0.6 %collective-permute-start.4 = (f32[2,56,128]{2,1,0:T(8,128)S(1)}, f32[2,56,128]{2,1,0:T(8,128)S(1)}, u32[]{:S(2)}, u32[]{:S(2)}) collective-permute-start(f32[2,56,128]{2,1,0:T(8,128)S(1)} %get-tuple-element.54), channel_id=1, source_target_pairs={{0,8},{1,9},{2,10},{3,11},{4,12},{5,13},{6,14},{7,15},{8,0},{9,1},... | collective-permute-start | bytes 172040 | tf_op jit(solution)/shard_map/ppermute | solution.py:118
  14.2 1.0 %collective-permute-start.5 = (f32[2,56,128]{2,1,0:T(8,128)S(1)}, f32[2,56,128]{2,1,0:T(8,128)S(1)}, u32[]{:S(2)}, u32[]{:S(2)}) collective-permute-start(f32[2,56,128]{2,1,0:T(8,128)S(1)} %get-tuple-element.55), channel_id=1, source_target_pairs={{0,24},{1,25},{2,26},{3,27},{4,28},{5,29},{6,30},{7,31},{8,16},{9,... | collective-permute-start | bytes 172040 | tf_op jit(solution)/shard_map/ppermute | solution.py:119
  15.3 0.6 %shard_map.138 = (f32[2,34,16,128]{3,2,1,0:T(8,128)S(1)}, f32[2,2,40,128]{3,2,1,0:T(8,128)S(1)}, f32[2,96,128]{2,1,0:T(8,128)S(1)}, f32[2,96,128]{2,1,0:T(8,128)S(1)}) custom-call(bf16[2,1008,256]{2,1,0:T(8,128)(2,1)S(1)} %get-tuple-element.51.after_ref, bf16[336,1008]{1,0:T(8,128)(2,1)S(1)} %copy-done.8), custom_call_target="tpu_custom_call" | custom-call | flops 700000000 | bytes 2545152 | tf_op jit(solution)/shard_map/pallas_call | solution.py:890
  15.8 3.0 %collective-permute-start.6 = (f32[2,96,128]{2,1,0:T(8,128)S(1)}, f32[2,96,128]{2,1,0:T(8,128)S(1)}, u32[]{:S(2)}, u32[]{:S(2)}) collective-permute-start(f32[2,96,128]{2,1,0:T(8,128)S(1)} %get-tuple-element.58), channel_id=1, source_target_pairs={{0,1},{1,0},{2,3},{3,2},{4,5},{5,4},{6,7},{7,6},{8,9},{9,8},{10,11... | collective-permute-start | bytes 294920 | tf_op jit(solution)/shard_map/ppermute | solution.py:122
  18.9 3.1 %collective-permute-start.8 = (f32[2,24,128]{2,1,0:T(8,128)S(1)}, f32[2,24,128]{2,1,0:T(8,128)S(1)}, u32[]{:S(2)}, u32[]{:S(2)}) collective-permute-start(f32[2,24,128]{2,1,0:T(8,128)S(1)} %get-tuple-element.60), channel_id=1, source_target_pairs={{0,1},{1,0},{2,3},{3,2},{4,5},{5,4},{6,7},{7,6},{8,9},{9,8},{10,11... | collective-permute-start | bytes 73736 | tf_op jit(solution)/shard_map/ppermute | solution.py:122
  22.0 0.7 %shard_map.140 = (f32[2,36,32,128]{3,2,1,0:T(8,128)S(1)}, f32[2,8,40,128]{3,2,1,0:T(8,128)S(1)}, f32[3,4,40,128]{3,2,1,0:T(8,128)S(1)}, f32[2,2,4,40,128]{4,3,2,1,0:T(8,128)S(1)}) custom-call(f32[2,36,32,128]{3,2,1,0:T(8,128)S(1)} %get-tuple-element.62.old_half_ref, ...), custom_call_target="tpu_custom_call", output_to_operand_aliasing={{0}: (0, {})} | custom-call | flops 2000000 | bytes 5459968 | tf_op jit(solution)/shard_map/pallas_call | solution.py:890
  22.7 1.4 %shard_map.141 = (f32[2,34,16,128]{3,2,1,0:T(8,128)S(1)}, f32[2,336,256]{2,1,0:T(8,128)S(1)}) custom-call(f32[2,36,16,128]{3,2,1,0:T(8,128)S(1)} %get-tuple-element.56.whole_ref, f32[2,2,40,128]{3,2,1,0:T(8,128)S(1)} %get-tuple-element.57.after_ref.whole_rows_ref, f32[2,36,32,128]{3,2,1,0:T(8,128)S(1)} %get-tuple-element.68.half_ref, ...), custom_call_target="tpu_custom_call" | custom-call | flops 700000000 | bytes 5723648 | tf_op jit(solution)/shard_map/pallas_call | solution.py:890
  24.1 1.9 %shard_map.142 = (f32[2,2,40,128]{3,2,1,0:T(8,128)S(1)}, f32[2,6,40,128]{3,2,1,0:T(8,128)S(1)}, bf16[2,1008,256]{2,1,0:T(8,128)(2,1)S(1)}, f32[2,40,128]{2,1,0:T(8,128)S(1)}, f32[2,40,128]{2,1,0:T(8,128)S(1)}) custom-call(f32[2,36,16,128]{3,2,1,0:T(8,128)S(1)} %get-tuple-element.56.whole_ref, ...), custom_call_target="tpu_custom_call" | custom-call | flops 2000000000 | bytes 5487616 | tf_op jit(solution)/shard_map/pallas_call | solution.py:890
  26.1 0.6 %collective-permute-start.10 = (f32[2,40,128]{2,1,0:T(8,128)S(1)}, f32[2,40,128]{2,1,0:T(8,128)S(1)}, u32[]{:S(2)}, u32[]{:S(2)}) collective-permute-start(f32[2,40,128]{2,1,0:T(8,128)S(1)} %get-tuple-element.73), channel_id=1, source_target_pairs={{0,8},{1,9},{2,10},{3,11},{4,12},{5,13},{6,14},{7,15},{8,0},{9,1},... | collective-permute-start | bytes 122888 | tf_op jit(solution)/shard_map/ppermute | solution.py:118
  26.6 0.4 collective-permute-start.11
  27.1 0.4 shard_map.144
  27.5 0.5 %shard_map.143 = (f32[2,34,16,128]{3,2,1,0:T(8,128)S(1)}, f32[2,2,40,128]{3,2,1,0:T(8,128)S(1)}) custom-call(bf16[2,1008,256]{2,1,0:T(8,128)(2,1)S(1)} %get-tuple-element.70.after_ref, bf16[336,1008]{1,0:T(8,128)(2,1)S(1)} %copy-done.8), custom_call_target="tpu_custom_call" | custom-call | flops 700000000 | bytes 2348544 | tf_op jit(solution)/shard_map/pallas_call | solution.py:890
  28.0 2.2 %collective-permute-done.11.second_ref = f32[2,40,128]{2,1,0:T(8,128)S(1)} collective-permute-done((f32[2,40,128]{2,1,0:T(8,128)S(1)}, f32[2,40,128]{2,1,0:T(8,128)S(1)}, u32[]{:S(2)}, u32[]{:S(2)}) %collective-permute-start.11) | collective-permute-done | bytes 40992 | tf_op jit(solution)/shard_map/ppermute | solution.py:119
  30.2 0.1 shard_map.145
  30.4 2.5 %collective-permute-start.12 = (f32[2,72,128]{2,1,0:T(8,128)S(1)}, f32[2,72,128]{2,1,0:T(8,128)S(1)}, u32[]{:S(2)}, u32[]{:S(2)}) collective-permute-start(f32[2,72,128]{2,1,0:T(8,128)S(1)} %get-tuple-element.83), channel_id=1, source_target_pairs={{0,1},{1,0},{2,3},{3,2},{4,5},{5,4},{6,7},{7,6},{8,9},{9,8},{10,11... | collective-permute-start | bytes 221192 | tf_op jit(solution)/shard_map/ppermute | solution.py:122
  32.9 0.2 collective-permute-start.13
  33.0 0.8 %shard_map.146 = (f32[2,32,16,128]{3,2,1,0:T(8,128)S(1)}, f32[8,128]{1,0:T(8,128)S(1)}) custom-call(f32[2,36,16,128]{3,2,1,0:T(8,128)S(1)} %get-tuple-element.79.whole_ref.w_ref, f32[2,2,40,128]{3,2,1,0:T(8,128)S(1)} %get-tuple-element.80.whole_rows_ref, f32[2,36,32,128]{3,2,1,0:T(8,128)S(1)} %get-tuple-element.68.half_ref, ...), custom_call_target="tpu_custom_call" | custom-call | flops 10000000 | bytes 4853760 | tf_op jit(solution)/shard_map/pallas_call | solution.py:890
  33.9 2.7 %collective-permute-done.12.first_ref = f32[2,72,128]{2,1,0:T(8,128)S(1)} collective-permute-done((f32[2,72,128]{2,1,0:T(8,128)S(1)}, f32[2,72,128]{2,1,0:T(8,128)S(1)}, u32[]{:S(2)}, u32[]{:S(2)}) %collective-permute-start.12) | collective-permute-done | bytes 73760 | tf_op jit(solution)/shard_map/ppermute | solution.py:122
  36.6 0.4 shard_map.147
  37.0 11.7 %all_to_all.11 = f32[32,1,128]{2,1,0:T(1,128)S(1)} all-to-all(f32[32,1,128]{2,1,0:T(1,128)S(1)} %bitcast.5), channel_id=1, replica_groups=mesh['gx'=4,'gy'=8] {'gx','gy'}, dimensions={0} | all-to-all | bytes 32768 | tf_op jit(solution)/shard_map/all_to_all | solution.py:1042
  48.7 1.2 %shard_map.148 = (f32[2,32,16,128]{3,2,1,0:T(8,128)}, f32[2,32,16,128]{3,2,1,0:T(8,128)}) custom-call(f32[32,128]{1,0:T(8,128)S(1)} %bitcast.4, f32[2,32,16,128]{3,2,1,0:T(8,128)S(1)} %copy-done.1, f32[2,32,16,128]{3,2,1,0:T(8,128)S(1)} %get-tuple-element.87.z_ref, f32[2,32,16,128]{3,2,1,0:T(8,128)S(1)} %get-tuple-element.81.old_image_ref.q_ref, ...), custom_call_target="tpu_custom_call" | custom-call | bytes 3948544 | tf_op jit(solution)/shard_map/pallas_call | solution.py:890
  (43 shorter events, 0.2 us)
Async XLA Ops:
  0.6 7.8 %copy-start.3 = (s32[32,16,128]{2,1,0:T(8,128)S(1)}, s32[32,16,128]{2,1,0:T(8,128)}, u32[]{:S(2)}) copy-start(s32[32,16,128]{2,1,0:T(8,128)} %zones_ref.7) | copy-start | bytes 786436
  0.6 7.8 %copy-start.6 = (f32[2,8]{1,0:T(2,128)S(1)}, f32[2,8]{1,0:T(2,128)}, u32[]{:S(2)}) copy-start(f32[2,8]{1,0:T(2,128)} %capacity_ref.3) | copy-start | bytes 196
  0.7 7.8 %copy-start.5 = (f32[2,8]{1,0:T(2,128)S(1)}, f32[2,8]{1,0:T(2,128)}, u32[]{:S(2)}) copy-start(f32[2,8]{1,0:T(2,128)} %conductance_ref.3) | copy-start | bytes 196
  1.5 5.2 %collective-permute-start = (f32[4,16,128]{2,1,0:T(8,128)S(1)}, f32[4,16,128]{2,1,0:T(8,128)S(1)}, u32[]{:S(2)}, u32[]{:S(2)}) collective-permute-start(f32[4,16,128]{2,1,0:T(8,128)S(1)} %get-tuple-element.46), channel_id=1, source_target_pairs={{0,8},{1,9},{2,10},{3,11},{4,12},{5,13},{6,14},{7,15},{8,0},{9,1},... | collective-permute-start | bytes 98312 | tf_op jit(solution)/shard_map/ppermute | solution.py:118
  2.0 4.7 %collective-permute-start.1 = (f32[4,16,128]{2,1,0:T(8,128)S(1)}, f32[4,16,128]{2,1,0:T(8,128)S(1)}, u32[]{:S(2)}, u32[]{:S(2)}) collective-permute-start(f32[4,16,128]{2,1,0:T(8,128)S(1)} %get-tuple-element.47), channel_id=1, source_target_pairs={{0,24},{1,25},{2,26},{3,27},{4,28},{5,29},{6,30},{7,31},{8,16},{9,... | collective-permute-start | bytes 98312 | tf_op jit(solution)/shard_map/ppermute | solution.py:119
  4.7 1.0 %copy-start = (f32[2,32,16,128]{3,2,1,0:T(8,128)S(1)}, f32[2,32,16,128]{3,2,1,0:T(8,128)}, u32[]{:S(2)}) copy-start(f32[2,32,16,128]{3,2,1,0:T(8,128)} %load_ref.9) | copy-start | bytes 1572868
  5.7 0.9 %copy-start.2 = (s32[32,16,128]{2,1,0:T(8,128)S(1)}, s32[32,16,128]{2,1,0:T(8,128)}, u32[]{:S(2)}) copy-start(s32[32,16,128]{2,1,0:T(8,128)} %zones_ref.7) | copy-start | bytes 786436
  6.7 3.4 %copy-start.1 = (f32[2,32,16,128]{3,2,1,0:T(8,128)S(1)}, f32[2,32,16,128]{3,2,1,0:T(8,128)}, u32[]{:S(2)}) copy-start(f32[2,32,16,128]{3,2,1,0:T(8,128)} %load_ref.9) | copy-start | bytes 1572868
  6.7 3.4 %copy-start.4 = (bf16[336,1008]{1,0:T(8,128)(2,1)S(1)}, bf16[336,1008]{1,0:T(8,128)(2,1)}, u32[]{:S(2)}) copy-start(bf16[336,1008]{1,0:T(8,128)(2,1)} %constant.14.clone.forward_ref) | copy-start | bytes 2032132
  6.9 5.1 %collective-permute-start.2 = (f32[144,128]{1,0:T(8,128)S(1)}, f32[144,128]{1,0:T(8,128)S(1)}, u32[]{:S(2)}, u32[]{:S(2)}) collective-permute-start(f32[144,128]{1,0:T(8,128)S(1)} %get-tuple-element.49), channel_id=1, source_target_pairs={{0,1},{1,0},{2,3},{3,2},{4,5},{5,4},{6,7},{7,6},{8,9},{9,8},{10,11... | collective-permute-start | bytes 221192 | tf_op jit(solution)/shard_map/ppermute | solution.py:122
  8.4 3.6 %collective-permute-start.3 = (f32[144,128]{1,0:T(8,128)S(1)}, f32[144,128]{1,0:T(8,128)S(1)}, u32[]{:S(2)}, u32[]{:S(2)}) collective-permute-start(f32[144,128]{1,0:T(8,128)S(1)} %get-tuple-element.50), channel_id=1, source_target_pairs={{0,8},{1,2},{2,1},{3,4},{4,3},{5,6},{6,5},{7,15},{8,0},{9,10},{10,... | collective-permute-start | bytes 221192 | tf_op jit(solution)/shard_map/ppermute | solution.py:121
  10.1 0.7 %copy-start.7 = (f32[8]{0:T(128)S(1)}, f32[8]{0:T(128)}, u32[]{:S(2)}) copy-start(f32[8]{0:T(128)} %coupling_ref.1) | copy-start | bytes 100
  10.1 2.0 %copy-start.10 = (bf16[144,1008]{1,0:T(8,128)(2,1)S(1)}, bf16[144,1008]{1,0:T(8,128)(2,1)}, u32[]{:S(2)}) copy-start(bf16[144,1008]{1,0:T(8,128)(2,1)} %constant.20.clone.edges_ref) | copy-start | bytes 870916
  10.1 2.0 %copy-start.11 = (bf16[384,144]{1,0:T(8,128)(2,1)S(1)}, bf16[384,144]{1,0:T(8,128)(2,1)}, u32[]{:S(2)}) copy-start(bf16[384,144]{1,0:T(8,128)(2,1)} %constant.16.clone.c2) | copy-start | bytes 331780
  10.1 2.0 %copy-start.12 = (bf16[336,240]{1,0:T(8,128)(2,1)S(1)}, bf16[336,240]{1,0:T(8,128)(2,1)}, u32[]{:S(2)}) copy-start(bf16[336,240]{1,0:T(8,128)(2,1)} %constant.18.clone.ends_ref) | copy-start | bytes 483844
  10.1 2.0 %copy-start.13 = (bf16[144,256]{1,0:T(8,128)(2,1)S(1)}, bf16[144,256]{1,0:T(8,128)(2,1)}, u32[]{:S(2)}) copy-start(bf16[144,256]{1,0:T(8,128)(2,1)} %constant.17.clone.c3) | copy-start | bytes 221188
  12.1 3.2 %copy-start.8 = (bf16[336,1008]{1,0:T(8,128)(2,1)S(1)}, bf16[336,1008]{1,0:T(8,128)(2,1)}, u32[]{:S(2)}) copy-start(bf16[336,1008]{1,0:T(8,128)(2,1)} %constant.15.clone.back_ref) | copy-start | bytes 2032132
  13.7 5.1 %collective-permute-start.4 = (f32[2,56,128]{2,1,0:T(8,128)S(1)}, f32[2,56,128]{2,1,0:T(8,128)S(1)}, u32[]{:S(2)}, u32[]{:S(2)}) collective-permute-start(f32[2,56,128]{2,1,0:T(8,128)S(1)} %get-tuple-element.54), channel_id=1, source_target_pairs={{0,8},{1,9},{2,10},{3,11},{4,12},{5,13},{6,14},{7,15},{8,0},{9,1},... | collective-permute-start | bytes 172040 | tf_op jit(solution)/shard_map/ppermute | solution.py:118
  14.2 4.6 %collective-permute-start.5 = (f32[2,56,128]{2,1,0:T(8,128)S(1)}, f32[2,56,128]{2,1,0:T(8,128)S(1)}, u32[]{:S(2)}, u32[]{:S(2)}) collective-permute-start(f32[2,56,128]{2,1,0:T(8,128)S(1)} %get-tuple-element.55), channel_id=1, source_target_pairs={{0,24},{1,25},{2,26},{3,27},{4,28},{5,29},{6,30},{7,31},{8,16},{9,... | collective-permute-start | bytes 172040 | tf_op jit(solution)/shard_map/ppermute | solution.py:119
  15.8 8.3 %collective-permute-start.6 = (f32[2,96,128]{2,1,0:T(8,128)S(1)}, f32[2,96,128]{2,1,0:T(8,128)S(1)}, u32[]{:S(2)}, u32[]{:S(2)}) collective-permute-start(f32[2,96,128]{2,1,0:T(8,128)S(1)} %get-tuple-element.58), channel_id=1, source_target_pairs={{0,1},{1,0},{2,3},{3,2},{4,5},{5,4},{6,7},{7,6},{8,9},{9,8},{10,11... | collective-permute-start | bytes 294920 | tf_op jit(solution)/shard_map/ppermute | solution.py:122
  18.8 5.3 %collective-permute-start.7 = (f32[2,96,128]{2,1,0:T(8,128)S(1)}, f32[2,96,128]{2,1,0:T(8,128)S(1)}, u32[]{:S(2)}, u32[]{:S(2)}) collective-permute-start(f32[2,96,128]{2,1,0:T(8,128)S(1)} %get-tuple-element.59), channel_id=1, source_target_pairs={{0,8},{1,2},{2,1},{3,4},{4,3},{5,6},{6,5},{7,15},{8,0},{9,10},{10,... | collective-permute-start | bytes 294920 | tf_op jit(solution)/shard_map/ppermute | solution.py:121
  18.9 5.2 %collective-permute-start.8 = (f32[2,24,128]{2,1,0:T(8,128)S(1)}, f32[2,24,128]{2,1,0:T(8,128)S(1)}, u32[]{:S(2)}, u32[]{:S(2)}) collective-permute-start(f32[2,24,128]{2,1,0:T(8,128)S(1)} %get-tuple-element.60), channel_id=1, source_target_pairs={{0,1},{1,0},{2,3},{3,2},{4,5},{5,4},{6,7},{7,6},{8,9},{9,8},{10,11... | collective-permute-start | bytes 73736 | tf_op jit(solution)/shard_map/ppermute | solution.py:122
  22.0 2.1 %collective-permute-start.9 = (f32[2,24,128]{2,1,0:T(8,128)S(1)}, f32[2,24,128]{2,1,0:T(8,128)S(1)}, u32[]{:S(2)}, u32[]{:S(2)}) collective-permute-start(f32[2,24,128]{2,1,0:T(8,128)S(1)} %get-tuple-element.61), channel_id=1, source_target_pairs={{0,8},{1,2},{2,1},{3,4},{4,3},{5,6},{6,5},{7,15},{8,0},{9,10},{10,... | collective-permute-start | bytes 73736 | tf_op jit(solution)/shard_map/ppermute | solution.py:121
  22.7 1.4 %copy-start.9 = (bf16[336,432]{1,0:T(8,128)(2,1)S(1)}, bf16[336,432]{1,0:T(8,128)(2,1)}, u32[]{:S(2)}) copy-start(bf16[336,432]{1,0:T(8,128)(2,1)} %constant.19.clone.lines_ref) | copy-start | bytes 870916
  26.1 1.9 %collective-permute-start.10 = (f32[2,40,128]{2,1,0:T(8,128)S(1)}, f32[2,40,128]{2,1,0:T(8,128)S(1)}, u32[]{:S(2)}, u32[]{:S(2)}) collective-permute-start(f32[2,40,128]{2,1,0:T(8,128)S(1)} %get-tuple-element.73), channel_id=1, source_target_pairs={{0,8},{1,9},{2,10},{3,11},{4,12},{5,13},{6,14},{7,15},{8,0},{9,1},... | collective-permute-start | bytes 122888 | tf_op jit(solution)/shard_map/ppermute | solution.py:118
  26.6 3.6 %collective-permute-start.11 = (f32[2,40,128]{2,1,0:T(8,128)S(1)}, f32[2,40,128]{2,1,0:T(8,128)S(1)}, u32[]{:S(2)}, u32[]{:S(2)}) collective-permute-start(f32[2,40,128]{2,1,0:T(8,128)S(1)} %get-tuple-element.74), channel_id=1, source_target_pairs={{0,24},{1,25},{2,26},{3,27},{4,28},{5,29},{6,30},{7,31},{8,16},{9,... | collective-permute-start | bytes 122888 | tf_op jit(solution)/shard_map/ppermute | solution.py:119
  30.4 6.2 %collective-permute-start.12 = (f32[2,72,128]{2,1,0:T(8,128)S(1)}, f32[2,72,128]{2,1,0:T(8,128)S(1)}, u32[]{:S(2)}, u32[]{:S(2)}) collective-permute-start(f32[2,72,128]{2,1,0:T(8,128)S(1)} %get-tuple-element.83), channel_id=1, source_target_pairs={{0,1},{1,0},{2,3},{3,2},{4,5},{5,4},{6,7},{7,6},{8,9},{9,8},{10,11... | collective-permute-start | bytes 221192 | tf_op jit(solution)/shard_map/ppermute | solution.py:122
  32.9 3.8 %collective-permute-start.13 = (f32[2,72,128]{2,1,0:T(8,128)S(1)}, f32[2,72,128]{2,1,0:T(8,128)S(1)}, u32[]{:S(2)}, u32[]{:S(2)}) collective-permute-start(f32[2,72,128]{2,1,0:T(8,128)S(1)} %get-tuple-element.84), channel_id=1, source_target_pairs={{0,8},{1,2},{2,1},{3,4},{4,3},{5,6},{6,5},{7,15},{8,0},{9,10},{10,... | collective-permute-start | bytes 221192 | tf_op jit(solution)/shard_map/ppermute | solution.py:121

commit v10 on v9

--- a/solution.py
+++ b/solution.py
@@ -301,13 +301,14 @@
     boxes = size_x // BOX
     lines = []
     for table_ref, which in ((capacity_ref, 0), (capacity_ref, 1), (conductance_ref, 0), (conductance_ref, 1)):
+        entries = entries_of(table_ref, which, size_z)
         for box in range(boxes):
             total = jnp.zeros((size_y, size_z), F32)
             for x in range(box * BOX, (box + 1) * BOX):
                 zone = zones_ref[x]
-                value = jnp.full((size_y, size_z), table_ref[which, 0], F32)
-                for label in range(1, table_ref.shape[1]):
-                    value = jnp.where(zone == label, table_ref[which, label], value)
+                value = jnp.broadcast_to(entries[0], zone.shape)
+                for label in range(1, len(entries)):
+                    value = jnp.where(zone == label, entries[label], value)
                 total = total + value
             lines.append(jnp.sum(total, axis=0, keepdims=True))
     sums = jnp.concatenate(lines, axis=0)
@@ -396,12 +397,17 @@
             put_end(6 + 4 * line + depth, from_high[2 + depth], line, far)
 
 
+def entries_of(ref, row, size_z):
+    return [
+        jnp.broadcast_to(ref[row : row + 1, label : label + 1], (1, size_z)) for label in range(ref.shape[1])
+    ]
+
+
 def tables(conductance_ref, capacity_ref, coupling_ref, size_z):
-    labels = range(coupling_ref.shape[0])
-    halves_of = [[0.5 * conductance_ref[field, label] for label in labels] for field in range(2)]
-    masses = [[capacity_ref[field, label] for label in labels] for field in range(2)]
-    products = [jnp.full((8, size_z), capacity_ref[0, label] * capacity_ref[1, label], F32) for label in labels]
-    masses.append([coupling_ref[label] * jnp.sqrt(products[label])[0:1] for label in labels])
+    halves_of = [[0.5 * entry for entry in entries_of(conductance_ref, field, size_z)] for field in range(2)]
+    masses = [entries_of(capacity_ref, field, size_z) for field in range(2)]
+    shares = entries_of(coupling_ref, 0, size_z)
+    masses.append([share * jnp.sqrt(one * two) for share, one, two in zip(shares, *masses)])
     return halves_of, masses
 
 
@@ -880,7 +886,6 @@
         copy.wait()
 
 
-SMEM = pl.BlockSpec(memory_space=pltpu.SMEM)
 VMEM = pl.BlockSpec(memory_space=pltpu.VMEM)
 HBM = pl.BlockSpec(memory_space=pltpu.HBM)
 
@@ -890,7 +895,7 @@
     return pl.pallas_call(
         kernel if mesh is None else functools.partial(kernel, mesh),
         out_shape=tuple(outs),
-        in_specs=[SMEM] * len(scalars) + [HBM if in_hbm else VMEM] * len(arrays),
+        in_specs=[VMEM] * len(scalars) + [HBM if in_hbm else VMEM] * len(arrays),
         out_specs=tuple([HBM if outs_in_hbm else VMEM] * len(outs)),
         scratch_shapes=list(scratch),
         input_output_aliases=dict(aliases),
@@ -937,7 +942,7 @@
     )
     packed = call(mesh, edge_lines_kernel, [], [load, zones, token, *x_halo], [sds(4 * size_x + 16, size_z)] * 2)
     y_halo = swap(mesh, "gy", *packed)
-    laws = [conductance, capacity, coupling]
+    laws = [conductance, capacity, coupling[None]]
     padded_shape = sds(2, size_x + 4, size_y + 16, size_z)
     half, mass, face, table = call(
         mesh,

time: 50.2 us -> 50.2 us (level)
  Pallas kernels: 14.2 us -> 13.3 us
    pallas_call x18, Pallas kernels: 14.2 us -> 13.3 us  [call(): pl.pallas_call(kernel if mesh is None else functools.partial(kernel, mesh...]
    ppermute x7, starting transfers between devices: 4.3 us -> 4.87 us  [swap(): second = lax.ppermute(odd_part, AXES, swap_pairs(mesh, axis, True))]
    ppermute x7, starting transfers between devices: 11.8 us -> 11.2 us  [swap(): first = lax.ppermute(even_part, AXES, swap_pairs(mesh, axis, False))]
  transfers between devices with their start and end apart: 14 -> 14, of which waited for: 2 -> 3; matrix products, arithmetic and copies ran while one was open for 0% -> 0% of each run, Pallas kernels for 16% -> 14%
where the time goes in v10:
time: 50.2 us; the launch traced here: 49.9 us
  starting transfers between devices  16.1 us (32%)
  Pallas kernels  13.3 us (26%)
  blocking collectives  12.1 us (24%)
  waiting for transfers between devices  5.35 us (11%)
  local copies, waits for them, and re-layouts  2.06 us (4%)
  between operations  0.93 us (2%)
    pallas_call x18, Pallas kernels, call(): pl.pallas_call(kernel if mesh is None else functools.partial(kernel, mesh...  13.3 us
    all_to_all x1, blocking collectives, shards(): sums = lax.all_to_all(sums, AXES, 0, 0, tiled=True)  12.1 us
    ppermute x7, starting transfers between devices, swap(): first = lax.ppermute(even_part, AXES, swap_pairs(mesh, axis, False))  11.2 us
    ppermute x7, starting transfers between devices, swap(): second = lax.ppermute(odd_part, AXES, swap_pairs(mesh, axis, True))  4.87 us
    ppermute x7, waiting for transfers between devices, swap(): first = lax.ppermute(even_part, AXES, swap_pairs(mesh, axis, False))  2.86 us
    ppermute x7, waiting for transfers between devices, swap(): second = lax.ppermute(odd_part, AXES, swap_pairs(mesh, axis, True))  2.49 us
    unnamed x28, local copies, waits for them, and re-layouts  2.06 us
  transfers between devices with their start and end apart: 14, of which 3 were waited for; matrix products, arithmetic and copies ran while one was open for 0% of the time, Pallas kernels for 14%

profile of v10, /device:TPU:0, one launch (start us, length us, event | category | flops | bytes accessed | tf_op | source)
XLA Modules:
  0.0 49.9 jit_solution(12195106887112327493)
XLA Ops:
  0.7 0.8 %shard_map.132 = (f32[4,16,128]{2,1,0:T(8,128)S(1)}, f32[4,16,128]{2,1,0:T(8,128)S(1)}) custom-call(f32[2,32,16,128]{3,2,1,0:T(8,128)} %load_ref.9, s32[32,16,128]{2,1,0:T(8,128)} %zones_ref.7), custom_call_target="tpu_custom_call" | custom-call | bytes 851968 | tf_op jit(solution)/shard_map/pallas_call | solution.py:895
  1.5 0.5 %collective-permute-start = (f32[4,16,128]{2,1,0:T(8,128)S(1)}, f32[4,16,128]{2,1,0:T(8,128)S(1)}, u32[]{:S(2)}, u32[]{:S(2)}) collective-permute-start(f32[4,16,128]{2,1,0:T(8,128)S(1)} %get-tuple-element.46), channel_id=1, source_target_pairs={{0,8},{1,9},{2,10},{3,11},{4,12},{5,13},{6,14},{7,15},{8,0},{9,1},... | collective-permute-start | bytes 98312 | tf_op jit(solution)/shard_map/ppermute | solution.py:118
  2.0 2.6 %collective-permute-start.1 = (f32[4,16,128]{2,1,0:T(8,128)S(1)}, f32[4,16,128]{2,1,0:T(8,128)S(1)}, u32[]{:S(2)}, u32[]{:S(2)}) collective-permute-start(f32[4,16,128]{2,1,0:T(8,128)S(1)} %get-tuple-element.47), channel_id=1, source_target_pairs={{0,24},{1,25},{2,26},{3,27},{4,28},{5,29},{6,30},{7,31},{8,16},{9,... | collective-permute-start | bytes 98312 | tf_op jit(solution)/shard_map/ppermute | solution.py:119
  4.7 1.0 %copy-done = f32[2,32,16,128]{3,2,1,0:T(8,128)S(1)} copy-done((f32[2,32,16,128]{3,2,1,0:T(8,128)S(1)}, f32[2,32,16,128]{3,2,1,0:T(8,128)}, u32[]{:S(2)}) %copy-start) | copy-done | bytes 524312
  5.7 0.9 %copy-done.2 = s32[32,16,128]{2,1,0:T(8,128)S(1)} copy-done((s32[32,16,128]{2,1,0:T(8,128)S(1)}, s32[32,16,128]{2,1,0:T(8,128)}, u32[]{:S(2)}) %copy-start.2) | copy-done | bytes 262168
  6.7 0.2 shard_map.135
  6.9 1.6 %collective-permute-start.2 = (f32[144,128]{1,0:T(8,128)S(1)}, f32[144,128]{1,0:T(8,128)S(1)}, u32[]{:S(2)}, u32[]{:S(2)}) collective-permute-start(f32[144,128]{1,0:T(8,128)S(1)} %get-tuple-element.49), channel_id=1, source_target_pairs={{0,1},{1,0},{2,3},{3,2},{4,5},{5,4},{6,7},{7,6},{8,9},{9,8},{10,11... | collective-permute-start | bytes 221192 | tf_op jit(solution)/shard_map/ppermute | solution.py:122
  8.4 1.1 %shard_map.136.inverse_ref = f32[4,336,144]{2,1,0:T(8,128)S(1)} custom-call(f32[2,8]{1,0:T(2,128)S(1)} %copy-done.5, f32[2,8]{1,0:T(2,128)S(1)} %copy-done.6, s32[32,16,128]{2,1,0:T(8,128)S(1)} %copy-done.3), custom_call_target="tpu_custom_call" | custom-call | flops 40000000 | bytes 1036288 | tf_op jit(solution)/shard_map/pallas_call | solution.py:895
  9.6 0.6 %shard_map.131.spectral_ref = f32[2,336,256]{2,1,0:T(8,128)S(1)} custom-call(f32[2,32,16,128]{3,2,1,0:T(8,128)S(1)} %copy-done.1, bf16[336,1008]{1,0:T(8,128)(2,1)S(1)} %copy-done.4), custom_call_target="tpu_custom_call" | custom-call | flops 700000000 | bytes 1889792 | tf_op jit(solution)/shard_map/pallas_call | solution.py:895
  10.3 0.9 %shard_map.133 = (f32[2,36,32,128]{3,2,1,0:T(8,128)S(1)}, f32[3,34,16,128]{3,2,1,0:T(8,128)S(1)}, f32[2,2,34,16,128]{4,3,2,1,0:T(8,128)S(1)}, f32[5,8,128]{2,1,0:T(8,128)S(1)}) custom-call(f32[2,8]{1,0:T(2,128)S(1)} %copy-done.5, f32[2,8]{1,0:T(2,128)S(1)} %copy-done.6, f32[1,8]{1,0:T(1,128)S(1)} %bitcast.7, s32[32,16,128]{2,1,0:T(8,128)S(1)} %copy-done.3, ...), custom_call_target="tpu_custom_call" | custom-call | flops 20000000 | bytes 3477504 | tf_op jit(solution)/shard_map/pallas_call | solution.py:895
  11.3 1.6 %shard_map.137 = (bf16[2,1008,256]{2,1,0:T(8,128)(2,1)S(1)}, f32[2,56,128]{2,1,0:T(8,128)S(1)}, f32[2,56,128]{2,1,0:T(8,128)S(1)}) custom-call(f32[2,336,256]{2,1,0:T(8,128)S(1)} %shard_map.131.spectral_ref, f32[3,34,16,128]{3,2,1,0:T(8,128)S(1)} %get-tuple-element.48.mass_ref, f32[4,16,128]{2,1,0:T(8,128)S(1)} %collective-permute-done.first_x.first_ref, ...), custom_call_target="tpu_custom_call" | custom-call | flops 2000000000 | bytes 4293632 | tf_op jit(solution)/shard_map/pallas_call | solution.py:895
  12.9 0.5 collective-permute-start.4
  13.4 1.9 %collective-permute-start.5 = (f32[2,56,128]{2,1,0:T(8,128)S(1)}, f32[2,56,128]{2,1,0:T(8,128)S(1)}, u32[]{:S(2)}, u32[]{:S(2)}) collective-permute-start(f32[2,56,128]{2,1,0:T(8,128)S(1)} %get-tuple-element.55), channel_id=1, source_target_pairs={{0,24},{1,25},{2,26},{3,27},{4,28},{5,29},{6,30},{7,31},{8,16},{9,... | collective-permute-start | bytes 172040 | tf_op jit(solution)/shard_map/ppermute | solution.py:119
  15.3 0.6 %shard_map.138 = (f32[2,34,16,128]{3,2,1,0:T(8,128)S(1)}, f32[2,2,40,128]{3,2,1,0:T(8,128)S(1)}, f32[2,96,128]{2,1,0:T(8,128)S(1)}, f32[2,96,128]{2,1,0:T(8,128)S(1)}) custom-call(bf16[2,1008,256]{2,1,0:T(8,128)(2,1)S(1)} %get-tuple-element.51.after_ref, bf16[336,1008]{1,0:T(8,128)(2,1)S(1)} %copy-done.8), custom_call_target="tpu_custom_call" | custom-call | flops 700000000 | bytes 2545152 | tf_op jit(solution)/shard_map/pallas_call | solution.py:895
  15.8 2.5 %collective-permute-start.6 = (f32[2,96,128]{2,1,0:T(8,128)S(1)}, f32[2,96,128]{2,1,0:T(8,128)S(1)}, u32[]{:S(2)}, u32[]{:S(2)}) collective-permute-start(f32[2,96,128]{2,1,0:T(8,128)S(1)} %get-tuple-element.58), channel_id=1, source_target_pairs={{0,1},{1,0},{2,3},{3,2},{4,5},{5,4},{6,7},{7,6},{8,9},{9,8},{10,11... | collective-permute-start | bytes 294920 | tf_op jit(solution)/shard_map/ppermute | solution.py:122
  18.5 3.1 %collective-permute-start.8 = (f32[2,24,128]{2,1,0:T(8,128)S(1)}, f32[2,24,128]{2,1,0:T(8,128)S(1)}, u32[]{:S(2)}, u32[]{:S(2)}) collective-permute-start(f32[2,24,128]{2,1,0:T(8,128)S(1)} %get-tuple-element.60), channel_id=1, source_target_pairs={{0,1},{1,0},{2,3},{3,2},{4,5},{5,4},{6,7},{7,6},{8,9},{9,8},{10,11... | collective-permute-start | bytes 73736 | tf_op jit(solution)/shard_map/ppermute | solution.py:122
  21.6 0.7 %shard_map.140 = (f32[2,36,32,128]{3,2,1,0:T(8,128)S(1)}, f32[2,8,40,128]{3,2,1,0:T(8,128)S(1)}, f32[3,4,40,128]{3,2,1,0:T(8,128)S(1)}, f32[2,2,4,40,128]{4,3,2,1,0:T(8,128)S(1)}) custom-call(f32[2,36,32,128]{3,2,1,0:T(8,128)S(1)} %get-tuple-element.62.old_half_ref, ...), custom_call_target="tpu_custom_call", output_to_operand_aliasing={{0}: (0, {})} | custom-call | flops 2000000 | bytes 5459968 | tf_op jit(solution)/shard_map/pallas_call | solution.py:895
  22.3 1.4 %shard_map.141 = (f32[2,34,16,128]{3,2,1,0:T(8,128)S(1)}, f32[2,336,256]{2,1,0:T(8,128)S(1)}) custom-call(f32[2,36,16,128]{3,2,1,0:T(8,128)S(1)} %get-tuple-element.56.whole_ref, f32[2,2,40,128]{3,2,1,0:T(8,128)S(1)} %get-tuple-element.57.after_ref.whole_rows_ref, f32[2,36,32,128]{3,2,1,0:T(8,128)S(1)} %get-tuple-element.68.half_ref, ...), custom_call_target="tpu_custom_call" | custom-call | flops 700000000 | bytes 5723648 | tf_op jit(solution)/shard_map/pallas_call | solution.py:895
  23.7 1.9 %shard_map.142 = (f32[2,2,40,128]{3,2,1,0:T(8,128)S(1)}, f32[2,6,40,128]{3,2,1,0:T(8,128)S(1)}, bf16[2,1008,256]{2,1,0:T(8,128)(2,1)S(1)}, f32[2,40,128]{2,1,0:T(8,128)S(1)}, f32[2,40,128]{2,1,0:T(8,128)S(1)}) custom-call(f32[2,36,16,128]{3,2,1,0:T(8,128)S(1)} %get-tuple-element.56.whole_ref, ...), custom_call_target="tpu_custom_call" | custom-call | flops 2000000000 | bytes 5487616 | tf_op jit(solution)/shard_map/pallas_call | solution.py:895
  25.6 0.6 %collective-permute-start.10 = (f32[2,40,128]{2,1,0:T(8,128)S(1)}, f32[2,40,128]{2,1,0:T(8,128)S(1)}, u32[]{:S(2)}, u32[]{:S(2)}) collective-permute-start(f32[2,40,128]{2,1,0:T(8,128)S(1)} %get-tuple-element.73), channel_id=1, source_target_pairs={{0,8},{1,9},{2,10},{3,11},{4,12},{5,13},{6,14},{7,15},{8,0},{9,1},... | collective-permute-start | bytes 122888 | tf_op jit(solution)/shard_map/ppermute | solution.py:118
  26.2 0.2 collective-permute-start.11
  26.4 0.4 shard_map.144
  26.8 0.5 %shard_map.143 = (f32[2,34,16,128]{3,2,1,0:T(8,128)S(1)}, f32[2,2,40,128]{3,2,1,0:T(8,128)S(1)}) custom-call(bf16[2,1008,256]{2,1,0:T(8,128)(2,1)S(1)} %get-tuple-element.70.after_ref, bf16[336,1008]{1,0:T(8,128)(2,1)S(1)} %copy-done.8), custom_call_target="tpu_custom_call" | custom-call | flops 700000000 | bytes 2348544 | tf_op jit(solution)/shard_map/pallas_call | solution.py:895
  27.3 2.5 %collective-permute-done.11.second_ref = f32[2,40,128]{2,1,0:T(8,128)S(1)} collective-permute-done((f32[2,40,128]{2,1,0:T(8,128)S(1)}, f32[2,40,128]{2,1,0:T(8,128)S(1)}, u32[]{:S(2)}, u32[]{:S(2)}) %collective-permute-start.11) | collective-permute-done | bytes 40992 | tf_op jit(solution)/shard_map/ppermute | solution.py:119
  29.8 0.1 shard_map.145
  29.9 2.5 %collective-permute-start.12 = (f32[2,72,128]{2,1,0:T(8,128)S(1)}, f32[2,72,128]{2,1,0:T(8,128)S(1)}, u32[]{:S(2)}, u32[]{:S(2)}) collective-permute-start(f32[2,72,128]{2,1,0:T(8,128)S(1)} %get-tuple-element.83), channel_id=1, source_target_pairs={{0,1},{1,0},{2,3},{3,2},{4,5},{5,4},{6,7},{7,6},{8,9},{9,8},{10,11... | collective-permute-start | bytes 221192 | tf_op jit(solution)/shard_map/ppermute | solution.py:122
  32.4 0.2 collective-permute-start.13
  32.6 0.8 %shard_map.146 = (f32[2,32,16,128]{3,2,1,0:T(8,128)S(1)}, f32[8,128]{1,0:T(8,128)S(1)}) custom-call(f32[2,36,16,128]{3,2,1,0:T(8,128)S(1)} %get-tuple-element.79.whole_ref.w_ref, f32[2,2,40,128]{3,2,1,0:T(8,128)S(1)} %get-tuple-element.80.whole_rows_ref, f32[2,36,32,128]{3,2,1,0:T(8,128)S(1)} %get-tuple-element.68.half_ref, ...), custom_call_target="tpu_custom_call" | custom-call | flops 10000000 | bytes 4853760 | tf_op jit(solution)/shard_map/pallas_call | solution.py:895
  33.4 2.7 %collective-permute-done.12.first_ref = f32[2,72,128]{2,1,0:T(8,128)S(1)} collective-permute-done((f32[2,72,128]{2,1,0:T(8,128)S(1)}, f32[2,72,128]{2,1,0:T(8,128)S(1)}, u32[]{:S(2)}, u32[]{:S(2)}) %collective-permute-start.12) | collective-permute-done | bytes 73760 | tf_op jit(solution)/shard_map/ppermute | solution.py:122
  36.2 0.4 shard_map.147
  36.6 12.1 %all_to_all.11 = f32[32,1,128]{2,1,0:T(1,128)S(1)} all-to-all(f32[32,1,128]{2,1,0:T(1,128)S(1)} %bitcast.6), channel_id=1, replica_groups=mesh['gx'=4,'gy'=8] {'gx','gy'}, dimensions={0} | all-to-all | bytes 32768 | tf_op jit(solution)/shard_map/all_to_all | solution.py:1047
  48.7 1.2 %shard_map.148 = (f32[2,32,16,128]{3,2,1,0:T(8,128)}, f32[2,32,16,128]{3,2,1,0:T(8,128)}) custom-call(f32[32,128]{1,0:T(8,128)S(1)} %bitcast.5, f32[2,32,16,128]{3,2,1,0:T(8,128)S(1)} %copy-done.1, f32[2,32,16,128]{3,2,1,0:T(8,128)S(1)} %get-tuple-element.87.z_ref, f32[2,32,16,128]{3,2,1,0:T(8,128)S(1)} %get-tuple-element.81.old_image_ref.q_ref, ...), custom_call_target="tpu_custom_call" | custom-call | bytes 3948544 | tf_op jit(solution)/shard_map/pallas_call | solution.py:895
  (43 shorter events, 0.3 us)
Async XLA Ops:
  0.6 7.8 %copy-start.3 = (s32[32,16,128]{2,1,0:T(8,128)S(1)}, s32[32,16,128]{2,1,0:T(8,128)}, u32[]{:S(2)}) copy-start(s32[32,16,128]{2,1,0:T(8,128)} %zones_ref.7) | copy-start | bytes 786436
  0.6 7.8 %copy-start.6 = (f32[2,8]{1,0:T(2,128)S(1)}, f32[2,8]{1,0:T(2,128)}, u32[]{:S(2)}) copy-start(f32[2,8]{1,0:T(2,128)} %capacity_ref.3) | copy-start | bytes 196
  0.7 7.8 %copy-start.5 = (f32[2,8]{1,0:T(2,128)S(1)}, f32[2,8]{1,0:T(2,128)}, u32[]{:S(2)}) copy-start(f32[2,8]{1,0:T(2,128)} %conductance_ref.3) | copy-start | bytes 196
  1.5 5.2 %collective-permute-start = (f32[4,16,128]{2,1,0:T(8,128)S(1)}, f32[4,16,128]{2,1,0:T(8,128)S(1)}, u32[]{:S(2)}, u32[]{:S(2)}) collective-permute-start(f32[4,16,128]{2,1,0:T(8,128)S(1)} %get-tuple-element.46), channel_id=1, source_target_pairs={{0,8},{1,9},{2,10},{3,11},{4,12},{5,13},{6,14},{7,15},{8,0},{9,1},... | collective-permute-start | bytes 98312 | tf_op jit(solution)/shard_map/ppermute | solution.py:118
  2.0 4.7 %collective-permute-start.1 = (f32[4,16,128]{2,1,0:T(8,128)S(1)}, f32[4,16,128]{2,1,0:T(8,128)S(1)}, u32[]{:S(2)}, u32[]{:S(2)}) collective-permute-start(f32[4,16,128]{2,1,0:T(8,128)S(1)} %get-tuple-element.47), channel_id=1, source_target_pairs={{0,24},{1,25},{2,26},{3,27},{4,28},{5,29},{6,30},{7,31},{8,16},{9,... | collective-permute-start | bytes 98312 | tf_op jit(solution)/shard_map/ppermute | solution.py:119
  4.7 1.0 %copy-start = (f32[2,32,16,128]{3,2,1,0:T(8,128)S(1)}, f32[2,32,16,128]{3,2,1,0:T(8,128)}, u32[]{:S(2)}) copy-start(f32[2,32,16,128]{3,2,1,0:T(8,128)} %load_ref.9) | copy-start | bytes 1572868
  5.7 0.9 %copy-start.2 = (s32[32,16,128]{2,1,0:T(8,128)S(1)}, s32[32,16,128]{2,1,0:T(8,128)}, u32[]{:S(2)}) copy-start(s32[32,16,128]{2,1,0:T(8,128)} %zones_ref.7) | copy-start | bytes 786436
  6.7 2.9 %copy-start.1 = (f32[2,32,16,128]{3,2,1,0:T(8,128)S(1)}, f32[2,32,16,128]{3,2,1,0:T(8,128)}, u32[]{:S(2)}) copy-start(f32[2,32,16,128]{3,2,1,0:T(8,128)} %load_ref.9) | copy-start | bytes 1572868
  6.7 2.9 %copy-start.4 = (bf16[336,1008]{1,0:T(8,128)(2,1)S(1)}, bf16[336,1008]{1,0:T(8,128)(2,1)}, u32[]{:S(2)}) copy-start(bf16[336,1008]{1,0:T(8,128)(2,1)} %constant.14.clone.forward_ref) | copy-start | bytes 2032132
  6.9 4.4 %collective-permute-start.2 = (f32[144,128]{1,0:T(8,128)S(1)}, f32[144,128]{1,0:T(8,128)S(1)}, u32[]{:S(2)}, u32[]{:S(2)}) collective-permute-start(f32[144,128]{1,0:T(8,128)S(1)} %get-tuple-element.49), channel_id=1, source_target_pairs={{0,1},{1,0},{2,3},{3,2},{4,5},{5,4},{6,7},{7,6},{8,9},{9,8},{10,11... | collective-permute-start | bytes 221192 | tf_op jit(solution)/shard_map/ppermute | solution.py:122
  8.4 2.9 %collective-permute-start.3 = (f32[144,128]{1,0:T(8,128)S(1)}, f32[144,128]{1,0:T(8,128)S(1)}, u32[]{:S(2)}, u32[]{:S(2)}) collective-permute-start(f32[144,128]{1,0:T(8,128)S(1)} %get-tuple-element.50), channel_id=1, source_target_pairs={{0,8},{1,2},{2,1},{3,4},{4,3},{5,6},{6,5},{7,15},{8,0},{9,10},{10,... | collective-permute-start | bytes 221192 | tf_op jit(solution)/shard_map/ppermute | solution.py:121
  9.6 0.7 %copy-start.7 = (f32[8]{0:T(128)S(1)}, f32[8]{0:T(128)}, u32[]{:S(2)}) copy-start(f32[8]{0:T(128)} %param.16) | copy-start | bytes 100
  9.6 1.7 %copy-start.10 = (bf16[144,1008]{1,0:T(8,128)(2,1)S(1)}, bf16[144,1008]{1,0:T(8,128)(2,1)}, u32[]{:S(2)}) copy-start(bf16[144,1008]{1,0:T(8,128)(2,1)} %constant.20.clone.edges_ref) | copy-start | bytes 870916
  9.6 1.7 %copy-start.11 = (bf16[384,144]{1,0:T(8,128)(2,1)S(1)}, bf16[384,144]{1,0:T(8,128)(2,1)}, u32[]{:S(2)}) copy-start(bf16[384,144]{1,0:T(8,128)(2,1)} %constant.16.clone.c2) | copy-start | bytes 331780
  9.6 1.7 %copy-start.12 = (bf16[336,240]{1,0:T(8,128)(2,1)S(1)}, bf16[336,240]{1,0:T(8,128)(2,1)}, u32[]{:S(2)}) copy-start(bf16[336,240]{1,0:T(8,128)(2,1)} %constant.18.clone.ends_ref) | copy-start | bytes 483844
  9.6 1.7 %copy-start.13 = (bf16[144,256]{1,0:T(8,128)(2,1)S(1)}, bf16[144,256]{1,0:T(8,128)(2,1)}, u32[]{:S(2)}) copy-start(bf16[144,256]{1,0:T(8,128)(2,1)} %constant.17.clone.c3) | copy-start | bytes 221188
  11.3 3.9 %copy-start.8 = (bf16[336,1008]{1,0:T(8,128)(2,1)S(1)}, bf16[336,1008]{1,0:T(8,128)(2,1)}, u32[]{:S(2)}) copy-start(bf16[336,1008]{1,0:T(8,128)(2,1)} %constant.15.clone.back_ref) | copy-start | bytes 2032132
  12.9 5.4 %collective-permute-start.4 = (f32[2,56,128]{2,1,0:T(8,128)S(1)}, f32[2,56,128]{2,1,0:T(8,128)S(1)}, u32[]{:S(2)}, u32[]{:S(2)}) collective-permute-start(f32[2,56,128]{2,1,0:T(8,128)S(1)} %get-tuple-element.54), channel_id=1, source_target_pairs={{0,8},{1,9},{2,10},{3,11},{4,12},{5,13},{6,14},{7,15},{8,0},{9,1},... | collective-permute-start | bytes 172040 | tf_op jit(solution)/shard_map/ppermute | solution.py:118
  13.4 5.0 %collective-permute-start.5 = (f32[2,56,128]{2,1,0:T(8,128)S(1)}, f32[2,56,128]{2,1,0:T(8,128)S(1)}, u32[]{:S(2)}, u32[]{:S(2)}) collective-permute-start(f32[2,56,128]{2,1,0:T(8,128)S(1)} %get-tuple-element.55), channel_id=1, source_target_pairs={{0,24},{1,25},{2,26},{3,27},{4,28},{5,29},{6,30},{7,31},{8,16},{9,... | collective-permute-start | bytes 172040 | tf_op jit(solution)/shard_map/ppermute | solution.py:119
  15.8 7.8 %collective-permute-start.6 = (f32[2,96,128]{2,1,0:T(8,128)S(1)}, f32[2,96,128]{2,1,0:T(8,128)S(1)}, u32[]{:S(2)}, u32[]{:S(2)}) collective-permute-start(f32[2,96,128]{2,1,0:T(8,128)S(1)} %get-tuple-element.58), channel_id=1, source_target_pairs={{0,1},{1,0},{2,3},{3,2},{4,5},{5,4},{6,7},{7,6},{8,9},{9,8},{10,11... | collective-permute-start | bytes 294920 | tf_op jit(solution)/shard_map/ppermute | solution.py:122
  18.4 5.3 %collective-permute-start.7 = (f32[2,96,128]{2,1,0:T(8,128)S(1)}, f32[2,96,128]{2,1,0:T(8,128)S(1)}, u32[]{:S(2)}, u32[]{:S(2)}) collective-permute-start(f32[2,96,128]{2,1,0:T(8,128)S(1)} %get-tuple-element.59), channel_id=1, source_target_pairs={{0,8},{1,2},{2,1},{3,4},{4,3},{5,6},{6,5},{7,15},{8,0},{9,10},{10,... | collective-permute-start | bytes 294920 | tf_op jit(solution)/shard_map/ppermute | solution.py:121
  18.5 5.2 %collective-permute-start.8 = (f32[2,24,128]{2,1,0:T(8,128)S(1)}, f32[2,24,128]{2,1,0:T(8,128)S(1)}, u32[]{:S(2)}, u32[]{:S(2)}) collective-permute-start(f32[2,24,128]{2,1,0:T(8,128)S(1)} %get-tuple-element.60), channel_id=1, source_target_pairs={{0,1},{1,0},{2,3},{3,2},{4,5},{5,4},{6,7},{7,6},{8,9},{9,8},{10,11... | collective-permute-start | bytes 73736 | tf_op jit(solution)/shard_map/ppermute | solution.py:122
  21.6 2.1 %collective-permute-start.9 = (f32[2,24,128]{2,1,0:T(8,128)S(1)}, f32[2,24,128]{2,1,0:T(8,128)S(1)}, u32[]{:S(2)}, u32[]{:S(2)}) collective-permute-start(f32[2,24,128]{2,1,0:T(8,128)S(1)} %get-tuple-element.61), channel_id=1, source_target_pairs={{0,8},{1,2},{2,1},{3,4},{4,3},{5,6},{6,5},{7,15},{8,0},{9,10},{10,... | collective-permute-start | bytes 73736 | tf_op jit(solution)/shard_map/ppermute | solution.py:121
  22.3 1.4 %copy-start.9 = (bf16[336,432]{1,0:T(8,128)(2,1)S(1)}, bf16[336,432]{1,0:T(8,128)(2,1)}, u32[]{:S(2)}) copy-start(bf16[336,432]{1,0:T(8,128)(2,1)} %constant.19.clone.lines_ref) | copy-start | bytes 870916
  25.6 1.7 %collective-permute-start.10 = (f32[2,40,128]{2,1,0:T(8,128)S(1)}, f32[2,40,128]{2,1,0:T(8,128)S(1)}, u32[]{:S(2)}, u32[]{:S(2)}) collective-permute-start(f32[2,40,128]{2,1,0:T(8,128)S(1)} %get-tuple-element.73), channel_id=1, source_target_pairs={{0,8},{1,9},{2,10},{3,11},{4,12},{5,13},{6,14},{7,15},{8,0},{9,1},... | collective-permute-start | bytes 122888 | tf_op jit(solution)/shard_map/ppermute | solution.py:118
  26.2 3.6 %collective-permute-start.11 = (f32[2,40,128]{2,1,0:T(8,128)S(1)}, f32[2,40,128]{2,1,0:T(8,128)S(1)}, u32[]{:S(2)}, u32[]{:S(2)}) collective-permute-start(f32[2,40,128]{2,1,0:T(8,128)S(1)} %get-tuple-element.74), channel_id=1, source_target_pairs={{0,24},{1,25},{2,26},{3,27},{4,28},{5,29},{6,30},{7,31},{8,16},{9,... | collective-permute-start | bytes 122888 | tf_op jit(solution)/shard_map/ppermute | solution.py:119
  29.9 6.2 %collective-permute-start.12 = (f32[2,72,128]{2,1,0:T(8,128)S(1)}, f32[2,72,128]{2,1,0:T(8,128)S(1)}, u32[]{:S(2)}, u32[]{:S(2)}) collective-permute-start(f32[2,72,128]{2,1,0:T(8,128)S(1)} %get-tuple-element.83), channel_id=1, source_target_pairs={{0,1},{1,0},{2,3},{3,2},{4,5},{5,4},{6,7},{7,6},{8,9},{9,8},{10,11... | collective-permute-start | bytes 221192 | tf_op jit(solution)/shard_map/ppermute | solution.py:122
  32.4 3.8 %collective-permute-start.13 = (f32[2,72,128]{2,1,0:T(8,128)S(1)}, f32[2,72,128]{2,1,0:T(8,128)S(1)}, u32[]{:S(2)}, u32[]{:S(2)}) collective-permute-start(f32[2,72,128]{2,1,0:T(8,128)S(1)} %get-tuple-element.84), channel_id=1, source_target_pairs={{0,8},{1,2},{2,1},{3,4},{4,3},{5,6},{6,5},{7,15},{8,0},{9,10},{10,... | collective-permute-start | bytes 221192 | tf_op jit(solution)/shard_map/ppermute | solution.py:121

commit v11 on v9

--- a/solution.py
+++ b/solution.py
@@ -847,10 +847,9 @@
     lane = lax.broadcasted_iota(jnp.int32, line.shape, 1)
     rz, zq, qw, ws = [jnp.sum(jnp.where(lane == place, line, 0.0), axis=1, keepdims=True) for place in range(4)]
     alpha = rz / zq
-    rz_next = rz - alpha * (2.0 * zq) + alpha * alpha * qw
-    grown = 1.0 + rz_next / rz
-    curvature = grown * grown * zq - 2.0 * grown * alpha * qw + alpha * alpha * ws
-    alpha_next = rz_next / curvature
+    ratio = qw / zq
+    grown = alpha * ratio
+    alpha_next = (qw - zq * (zq / rz)) / (ws - qw * ratio)
     along = alpha + alpha_next * grown
     against = alpha_next * alpha
     copies = []

time: 50.2 us -> 50.2 us (level)
  no operation moved by 1% of the time
where the time goes in v11:
time: 50.2 us; the launch traced here: 49.9 us
  starting transfers between devices  16.1 us (32%)
  Pallas kernels  14.2 us (28%)
  blocking collectives  11.7 us (23%)
  waiting for transfers between devices  4.99 us (10%)
  local copies, waits for them, and re-layouts  2.06 us (4%)
  between operations  0.96 us (2%)
    pallas_call x18, Pallas kernels, call(): pl.pallas_call(kernel if mesh is None else functools.partial(kernel, mesh...  14.2 us
    ppermute x7, starting transfers between devices, swap(): first = lax.ppermute(even_part, AXES, swap_pairs(mesh, axis, False))  11.8 us
    all_to_all x1, blocking collectives, shards(): sums = lax.all_to_all(sums, AXES, 0, 0, tiled=True)  11.7 us
    ppermute x7, starting transfers between devices, swap(): second = lax.ppermute(odd_part, AXES, swap_pairs(mesh, axis, True))  4.3 us
    ppermute x7, waiting for transfers between devices, swap(): first = lax.ppermute(even_part, AXES, swap_pairs(mesh, axis, False))  2.75 us
    ppermute x7, waiting for transfers between devices, swap(): second = lax.ppermute(odd_part, AXES, swap_pairs(mesh, axis, True))  2.24 us
    unnamed x28, local copies, waits for them, and re-layouts  2.06 us
  transfers between devices with their start and end apart: 14, of which 2 were waited for; matrix products, arithmetic and copies ran while one was open for 0% of the time, Pallas kernels for 16%

profile of v11, /device:TPU:0, one launch (start us, length us, event | category | flops | bytes accessed | tf_op | source)
XLA Modules:
  0.0 49.9 jit_solution(5346773562659370662)
XLA Ops:
  0.7 0.8 %shard_map.132 = (f32[4,16,128]{2,1,0:T(8,128)S(1)}, f32[4,16,128]{2,1,0:T(8,128)S(1)}) custom-call(f32[2,32,16,128]{3,2,1,0:T(8,128)} %load_ref.9, s32[32,16,128]{2,1,0:T(8,128)} %zones_ref.7), custom_call_target="tpu_custom_call" | custom-call | bytes 851968 | tf_op jit(solution)/shard_map/pallas_call | solution.py:889
  1.5 0.5 %collective-permute-start = (f32[4,16,128]{2,1,0:T(8,128)S(1)}, f32[4,16,128]{2,1,0:T(8,128)S(1)}, u32[]{:S(2)}, u32[]{:S(2)}) collective-permute-start(f32[4,16,128]{2,1,0:T(8,128)S(1)} %get-tuple-element.46), channel_id=1, source_target_pairs={{0,8},{1,9},{2,10},{3,11},{4,12},{5,13},{6,14},{7,15},{8,0},{9,1},... | collective-permute-start | bytes 98312 | tf_op jit(solution)/shard_map/ppermute | solution.py:118
  2.0 2.6 %collective-permute-start.1 = (f32[4,16,128]{2,1,0:T(8,128)S(1)}, f32[4,16,128]{2,1,0:T(8,128)S(1)}, u32[]{:S(2)}, u32[]{:S(2)}) collective-permute-start(f32[4,16,128]{2,1,0:T(8,128)S(1)} %get-tuple-element.47), channel_id=1, source_target_pairs={{0,24},{1,25},{2,26},{3,27},{4,28},{5,29},{6,30},{7,31},{8,16},{9,... | collective-permute-start | bytes 98312 | tf_op jit(solution)/shard_map/ppermute | solution.py:119
  4.7 1.0 %copy-done = f32[2,32,16,128]{3,2,1,0:T(8,128)S(1)} copy-done((f32[2,32,16,128]{3,2,1,0:T(8,128)S(1)}, f32[2,32,16,128]{3,2,1,0:T(8,128)}, u32[]{:S(2)}) %copy-start) | copy-done | bytes 524312
  5.7 0.9 %copy-done.2 = s32[32,16,128]{2,1,0:T(8,128)S(1)} copy-done((s32[32,16,128]{2,1,0:T(8,128)S(1)}, s32[32,16,128]{2,1,0:T(8,128)}, u32[]{:S(2)}) %copy-start.2) | copy-done | bytes 262168
  6.7 0.2 shard_map.135
  6.9 1.6 %collective-permute-start.2 = (f32[144,128]{1,0:T(8,128)S(1)}, f32[144,128]{1,0:T(8,128)S(1)}, u32[]{:S(2)}, u32[]{:S(2)}) collective-permute-start(f32[144,128]{1,0:T(8,128)S(1)} %get-tuple-element.49), channel_id=1, source_target_pairs={{0,1},{1,0},{2,3},{3,2},{4,5},{5,4},{6,7},{7,6},{8,9},{9,8},{10,11... | collective-permute-start | bytes 221192 | tf_op jit(solution)/shard_map/ppermute | solution.py:122
  8.4 1.6 %shard_map.136.inverse_ref = f32[4,336,144]{2,1,0:T(8,128)S(1)} custom-call(f32[2,8]{1,0:T(2,128)S(1)} %copy-done.5, f32[2,8]{1,0:T(2,128)S(1)} %copy-done.6, s32[32,16,128]{2,1,0:T(8,128)S(1)} %copy-done.3), custom_call_target="tpu_custom_call" | custom-call | flops 40000000 | bytes 1036288 | tf_op jit(solution)/shard_map/pallas_call | solution.py:889
  10.1 0.6 %shard_map.131.spectral_ref = f32[2,336,256]{2,1,0:T(8,128)S(1)} custom-call(f32[2,32,16,128]{3,2,1,0:T(8,128)S(1)} %copy-done.1, bf16[336,1008]{1,0:T(8,128)(2,1)S(1)} %copy-done.4), custom_call_target="tpu_custom_call" | custom-call | flops 700000000 | bytes 1889792 | tf_op jit(solution)/shard_map/pallas_call | solution.py:889
  10.8 1.2 %shard_map.133 = (f32[2,36,32,128]{3,2,1,0:T(8,128)S(1)}, f32[3,34,16,128]{3,2,1,0:T(8,128)S(1)}, f32[2,2,34,16,128]{4,3,2,1,0:T(8,128)S(1)}, f32[5,8,128]{2,1,0:T(8,128)S(1)}) custom-call(f32[2,8]{1,0:T(2,128)S(1)} %copy-done.5, f32[2,8]{1,0:T(2,128)S(1)} %copy-done.6, f32[8]{0:T(128)S(1)} %copy-done.7, s32[32,16,128]{2,1,0:T(8,128)S(1)} %copy-done.3, ...), custom_call_target="tpu_custom_call" | custom-call | flops 20000000 | bytes 3477504 | tf_op jit(solution)/shard_map/pallas_call | solution.py:889
  12.1 1.6 %shard_map.137 = (bf16[2,1008,256]{2,1,0:T(8,128)(2,1)S(1)}, f32[2,56,128]{2,1,0:T(8,128)S(1)}, f32[2,56,128]{2,1,0:T(8,128)S(1)}) custom-call(f32[2,336,256]{2,1,0:T(8,128)S(1)} %shard_map.131.spectral_ref, f32[3,34,16,128]{3,2,1,0:T(8,128)S(1)} %get-tuple-element.48.mass_ref, f32[4,16,128]{2,1,0:T(8,128)S(1)} %collective-permute-done.first_x.first_ref, ...), custom_call_target="tpu_custom_call" | custom-call | flops 2000000000 | bytes 4293632 | tf_op jit(solution)/shard_map/pallas_call | solution.py:889
  13.7 0.6 %collective-permute-start.4 = (f32[2,56,128]{2,1,0:T(8,128)S(1)}, f32[2,56,128]{2,1,0:T(8,128)S(1)}, u32[]{:S(2)}, u32[]{:S(2)}) collective-permute-start(f32[2,56,128]{2,1,0:T(8,128)S(1)} %get-tuple-element.54), channel_id=1, source_target_pairs={{0,8},{1,9},{2,10},{3,11},{4,12},{5,13},{6,14},{7,15},{8,0},{9,1},... | collective-permute-start | bytes 172040 | tf_op jit(solution)/shard_map/ppermute | solution.py:118
  14.2 1.0 %collective-permute-start.5 = (f32[2,56,128]{2,1,0:T(8,128)S(1)}, f32[2,56,128]{2,1,0:T(8,128)S(1)}, u32[]{:S(2)}, u32[]{:S(2)}) collective-permute-start(f32[2,56,128]{2,1,0:T(8,128)S(1)} %get-tuple-element.55), channel_id=1, source_target_pairs={{0,24},{1,25},{2,26},{3,27},{4,28},{5,29},{6,30},{7,31},{8,16},{9,... | collective-permute-start | bytes 172040 | tf_op jit(solution)/shard_map/ppermute | solution.py:119
  15.3 0.6 %shard_map.138 = (f32[2,34,16,128]{3,2,1,0:T(8,128)S(1)}, f32[2,2,40,128]{3,2,1,0:T(8,128)S(1)}, f32[2,96,128]{2,1,0:T(8,128)S(1)}, f32[2,96,128]{2,1,0:T(8,128)S(1)}) custom-call(bf16[2,1008,256]{2,1,0:T(8,128)(2,1)S(1)} %get-tuple-element.51.after_ref, bf16[336,1008]{1,0:T(8,128)(2,1)S(1)} %copy-done.8), custom_call_target="tpu_custom_call" | custom-call | flops 700000000 | bytes 2545152 | tf_op jit(solution)/shard_map/pallas_call | solution.py:889
  15.8 3.0 %collective-permute-start.6 = (f32[2,96,128]{2,1,0:T(8,128)S(1)}, f32[2,96,128]{2,1,0:T(8,128)S(1)}, u32[]{:S(2)}, u32[]{:S(2)}) collective-permute-start(f32[2,96,128]{2,1,0:T(8,128)S(1)} %get-tuple-element.58), channel_id=1, source_target_pairs={{0,1},{1,0},{2,3},{3,2},{4,5},{5,4},{6,7},{7,6},{8,9},{9,8},{10,11... | collective-permute-start | bytes 294920 | tf_op jit(solution)/shard_map/ppermute | solution.py:122
  18.9 3.1 %collective-permute-start.8 = (f32[2,24,128]{2,1,0:T(8,128)S(1)}, f32[2,24,128]{2,1,0:T(8,128)S(1)}, u32[]{:S(2)}, u32[]{:S(2)}) collective-permute-start(f32[2,24,128]{2,1,0:T(8,128)S(1)} %get-tuple-element.60), channel_id=1, source_target_pairs={{0,1},{1,0},{2,3},{3,2},{4,5},{5,4},{6,7},{7,6},{8,9},{9,8},{10,11... | collective-permute-start | bytes 73736 | tf_op jit(solution)/shard_map/ppermute | solution.py:122
  22.0 0.7 %shard_map.140 = (f32[2,36,32,128]{3,2,1,0:T(8,128)S(1)}, f32[2,8,40,128]{3,2,1,0:T(8,128)S(1)}, f32[3,4,40,128]{3,2,1,0:T(8,128)S(1)}, f32[2,2,4,40,128]{4,3,2,1,0:T(8,128)S(1)}) custom-call(f32[2,36,32,128]{3,2,1,0:T(8,128)S(1)} %get-tuple-element.62.old_half_ref, ...), custom_call_target="tpu_custom_call", output_to_operand_aliasing={{0}: (0, {})} | custom-call | flops 2000000 | bytes 5459968 | tf_op jit(solution)/shard_map/pallas_call | solution.py:889
  22.7 1.4 %shard_map.141 = (f32[2,34,16,128]{3,2,1,0:T(8,128)S(1)}, f32[2,336,256]{2,1,0:T(8,128)S(1)}) custom-call(f32[2,36,16,128]{3,2,1,0:T(8,128)S(1)} %get-tuple-element.56.whole_ref, f32[2,2,40,128]{3,2,1,0:T(8,128)S(1)} %get-tuple-element.57.after_ref.whole_rows_ref, f32[2,36,32,128]{3,2,1,0:T(8,128)S(1)} %get-tuple-element.68.half_ref, ...), custom_call_target="tpu_custom_call" | custom-call | flops 700000000 | bytes 5723648 | tf_op jit(solution)/shard_map/pallas_call | solution.py:889
  24.1 1.9 %shard_map.142 = (f32[2,2,40,128]{3,2,1,0:T(8,128)S(1)}, f32[2,6,40,128]{3,2,1,0:T(8,128)S(1)}, bf16[2,1008,256]{2,1,0:T(8,128)(2,1)S(1)}, f32[2,40,128]{2,1,0:T(8,128)S(1)}, f32[2,40,128]{2,1,0:T(8,128)S(1)}) custom-call(f32[2,36,16,128]{3,2,1,0:T(8,128)S(1)} %get-tuple-element.56.whole_ref, ...), custom_call_target="tpu_custom_call" | custom-call | flops 2000000000 | bytes 5487616 | tf_op jit(solution)/shard_map/pallas_call | solution.py:889
  26.1 0.6 %collective-permute-start.10 = (f32[2,40,128]{2,1,0:T(8,128)S(1)}, f32[2,40,128]{2,1,0:T(8,128)S(1)}, u32[]{:S(2)}, u32[]{:S(2)}) collective-permute-start(f32[2,40,128]{2,1,0:T(8,128)S(1)} %get-tuple-element.73), channel_id=1, source_target_pairs={{0,8},{1,9},{2,10},{3,11},{4,12},{5,13},{6,14},{7,15},{8,0},{9,1},... | collective-permute-start | bytes 122888 | tf_op jit(solution)/shard_map/ppermute | solution.py:118
  26.6 0.4 collective-permute-start.11
  27.1 0.4 shard_map.144
  27.5 0.5 %shard_map.143 = (f32[2,34,16,128]{3,2,1,0:T(8,128)S(1)}, f32[2,2,40,128]{3,2,1,0:T(8,128)S(1)}) custom-call(bf16[2,1008,256]{2,1,0:T(8,128)(2,1)S(1)} %get-tuple-element.70.after_ref, bf16[336,1008]{1,0:T(8,128)(2,1)S(1)} %copy-done.8), custom_call_target="tpu_custom_call" | custom-call | flops 700000000 | bytes 2348544 | tf_op jit(solution)/shard_map/pallas_call | solution.py:889
  28.0 2.2 %collective-permute-done.11.second_ref = f32[2,40,128]{2,1,0:T(8,128)S(1)} collective-permute-done((f32[2,40,128]{2,1,0:T(8,128)S(1)}, f32[2,40,128]{2,1,0:T(8,128)S(1)}, u32[]{:S(2)}, u32[]{:S(2)}) %collective-permute-start.11) | collective-permute-done | bytes 40992 | tf_op jit(solution)/shard_map/ppermute | solution.py:119
  30.2 0.1 shard_map.145
  30.4 2.5 %collective-permute-start.12 = (f32[2,72,128]{2,1,0:T(8,128)S(1)}, f32[2,72,128]{2,1,0:T(8,128)S(1)}, u32[]{:S(2)}, u32[]{:S(2)}) collective-permute-start(f32[2,72,128]{2,1,0:T(8,128)S(1)} %get-tuple-element.83), channel_id=1, source_target_pairs={{0,1},{1,0},{2,3},{3,2},{4,5},{5,4},{6,7},{7,6},{8,9},{9,8},{10,11... | collective-permute-start | bytes 221192 | tf_op jit(solution)/shard_map/ppermute | solution.py:122
  32.9 0.2 collective-permute-start.13
  33.0 0.8 %shard_map.146 = (f32[2,32,16,128]{3,2,1,0:T(8,128)S(1)}, f32[8,128]{1,0:T(8,128)S(1)}) custom-call(f32[2,36,16,128]{3,2,1,0:T(8,128)S(1)} %get-tuple-element.79.whole_ref.w_ref, f32[2,2,40,128]{3,2,1,0:T(8,128)S(1)} %get-tuple-element.80.whole_rows_ref, f32[2,36,32,128]{3,2,1,0:T(8,128)S(1)} %get-tuple-element.68.half_ref, ...), custom_call_target="tpu_custom_call" | custom-call | flops 10000000 | bytes 4853760 | tf_op jit(solution)/shard_map/pallas_call | solution.py:889
  33.9 2.7 %collective-permute-done.12.first_ref = f32[2,72,128]{2,1,0:T(8,128)S(1)} collective-permute-done((f32[2,72,128]{2,1,0:T(8,128)S(1)}, f32[2,72,128]{2,1,0:T(8,128)S(1)}, u32[]{:S(2)}, u32[]{:S(2)}) %collective-permute-start.12) | collective-permute-done | bytes 73760 | tf_op jit(solution)/shard_map/ppermute | solution.py:122
  36.6 0.4 shard_map.147
  37.0 11.7 %all_to_all.11 = f32[32,1,128]{2,1,0:T(1,128)S(1)} all-to-all(f32[32,1,128]{2,1,0:T(1,128)S(1)} %bitcast.5), channel_id=1, replica_groups=mesh['gx'=4,'gy'=8] {'gx','gy'}, dimensions={0} | all-to-all | bytes 32768 | tf_op jit(solution)/shard_map/all_to_all | solution.py:1041
  48.7 1.2 %shard_map.148 = (f32[2,32,16,128]{3,2,1,0:T(8,128)}, f32[2,32,16,128]{3,2,1,0:T(8,128)}) custom-call(f32[32,128]{1,0:T(8,128)S(1)} %bitcast.4, f32[2,32,16,128]{3,2,1,0:T(8,128)S(1)} %copy-done.1, f32[2,32,16,128]{3,2,1,0:T(8,128)S(1)} %get-tuple-element.87.z_ref, f32[2,32,16,128]{3,2,1,0:T(8,128)S(1)} %get-tuple-element.81.old_image_ref.q_ref, ...), custom_call_target="tpu_custom_call" | custom-call | bytes 3948544 | tf_op jit(solution)/shard_map/pallas_call | solution.py:889
  (43 shorter events, 0.2 us)
Async XLA Ops:
  0.6 7.8 %copy-start.3 = (s32[32,16,128]{2,1,0:T(8,128)S(1)}, s32[32,16,128]{2,1,0:T(8,128)}, u32[]{:S(2)}) copy-start(s32[32,16,128]{2,1,0:T(8,128)} %zones_ref.7) | copy-start | bytes 786436
  0.6 7.8 %copy-start.6 = (f32[2,8]{1,0:T(2,128)S(1)}, f32[2,8]{1,0:T(2,128)}, u32[]{:S(2)}) copy-start(f32[2,8]{1,0:T(2,128)} %capacity_ref.3) | copy-start | bytes 196
  0.7 7.8 %copy-start.5 = (f32[2,8]{1,0:T(2,128)S(1)}, f32[2,8]{1,0:T(2,128)}, u32[]{:S(2)}) copy-start(f32[2,8]{1,0:T(2,128)} %conductance_ref.3) | copy-start | bytes 196
  1.5 5.2 %collective-permute-start = (f32[4,16,128]{2,1,0:T(8,128)S(1)}, f32[4,16,128]{2,1,0:T(8,128)S(1)}, u32[]{:S(2)}, u32[]{:S(2)}) collective-permute-start(f32[4,16,128]{2,1,0:T(8,128)S(1)} %get-tuple-element.46), channel_id=1, source_target_pairs={{0,8},{1,9},{2,10},{3,11},{4,12},{5,13},{6,14},{7,15},{8,0},{9,1},... | collective-permute-start | bytes 98312 | tf_op jit(solution)/shard_map/ppermute | solution.py:118
  2.0 4.7 %collective-permute-start.1 = (f32[4,16,128]{2,1,0:T(8,128)S(1)}, f32[4,16,128]{2,1,0:T(8,128)S(1)}, u32[]{:S(2)}, u32[]{:S(2)}) collective-permute-start(f32[4,16,128]{2,1,0:T(8,128)S(1)} %get-tuple-element.47), channel_id=1, source_target_pairs={{0,24},{1,25},{2,26},{3,27},{4,28},{5,29},{6,30},{7,31},{8,16},{9,... | collective-permute-start | bytes 98312 | tf_op jit(solution)/shard_map/ppermute | solution.py:119
  4.7 1.0 %copy-start = (f32[2,32,16,128]{3,2,1,0:T(8,128)S(1)}, f32[2,32,16,128]{3,2,1,0:T(8,128)}, u32[]{:S(2)}) copy-start(f32[2,32,16,128]{3,2,1,0:T(8,128)} %load_ref.9) | copy-start | bytes 1572868
  5.7 0.9 %copy-start.2 = (s32[32,16,128]{2,1,0:T(8,128)S(1)}, s32[32,16,128]{2,1,0:T(8,128)}, u32[]{:S(2)}) copy-start(s32[32,16,128]{2,1,0:T(8,128)} %zones_ref.7) | copy-start | bytes 786436
  6.7 3.4 %copy-start.1 = (f32[2,32,16,128]{3,2,1,0:T(8,128)S(1)}, f32[2,32,16,128]{3,2,1,0:T(8,128)}, u32[]{:S(2)}) copy-start(f32[2,32,16,128]{3,2,1,0:T(8,128)} %load_ref.9) | copy-start | bytes 1572868
  6.7 3.4 %copy-start.4 = (bf16[336,1008]{1,0:T(8,128)(2,1)S(1)}, bf16[336,1008]{1,0:T(8,128)(2,1)}, u32[]{:S(2)}) copy-start(bf16[336,1008]{1,0:T(8,128)(2,1)} %constant.14.clone.forward_ref) | copy-start | bytes 2032132
  6.9 5.1 %collective-permute-start.2 = (f32[144,128]{1,0:T(8,128)S(1)}, f32[144,128]{1,0:T(8,128)S(1)}, u32[]{:S(2)}, u32[]{:S(2)}) collective-permute-start(f32[144,128]{1,0:T(8,128)S(1)} %get-tuple-element.49), channel_id=1, source_target_pairs={{0,1},{1,0},{2,3},{3,2},{4,5},{5,4},{6,7},{7,6},{8,9},{9,8},{10,11... | collective-permute-start | bytes 221192 | tf_op jit(solution)/shard_map/ppermute | solution.py:122
  8.4 3.6 %collective-permute-start.3 = (f32[144,128]{1,0:T(8,128)S(1)}, f32[144,128]{1,0:T(8,128)S(1)}, u32[]{:S(2)}, u32[]{:S(2)}) collective-permute-start(f32[144,128]{1,0:T(8,128)S(1)} %get-tuple-element.50), channel_id=1, source_target_pairs={{0,8},{1,2},{2,1},{3,4},{4,3},{5,6},{6,5},{7,15},{8,0},{9,10},{10,... | collective-permute-start | bytes 221192 | tf_op jit(solution)/shard_map/ppermute | solution.py:121
  10.1 0.7 %copy-start.7 = (f32[8]{0:T(128)S(1)}, f32[8]{0:T(128)}, u32[]{:S(2)}) copy-start(f32[8]{0:T(128)} %coupling_ref.1) | copy-start | bytes 100
  10.1 2.0 %copy-start.10 = (bf16[144,1008]{1,0:T(8,128)(2,1)S(1)}, bf16[144,1008]{1,0:T(8,128)(2,1)}, u32[]{:S(2)}) copy-start(bf16[144,1008]{1,0:T(8,128)(2,1)} %constant.20.clone.edges_ref) | copy-start | bytes 870916
  10.1 2.0 %copy-start.11 = (bf16[384,144]{1,0:T(8,128)(2,1)S(1)}, bf16[384,144]{1,0:T(8,128)(2,1)}, u32[]{:S(2)}) copy-start(bf16[384,144]{1,0:T(8,128)(2,1)} %constant.16.clone.c2) | copy-start | bytes 331780
  10.1 2.0 %copy-start.12 = (bf16[336,240]{1,0:T(8,128)(2,1)S(1)}, bf16[336,240]{1,0:T(8,128)(2,1)}, u32[]{:S(2)}) copy-start(bf16[336,240]{1,0:T(8,128)(2,1)} %constant.18.clone.ends_ref) | copy-start | bytes 483844
  10.1 2.0 %copy-start.13 = (bf16[144,256]{1,0:T(8,128)(2,1)S(1)}, bf16[144,256]{1,0:T(8,128)(2,1)}, u32[]{:S(2)}) copy-start(bf16[144,256]{1,0:T(8,128)(2,1)} %constant.17.clone.c3) | copy-start | bytes 221188
  12.1 3.2 %copy-start.8 = (bf16[336,1008]{1,0:T(8,128)(2,1)S(1)}, bf16[336,1008]{1,0:T(8,128)(2,1)}, u32[]{:S(2)}) copy-start(bf16[336,1008]{1,0:T(8,128)(2,1)} %constant.15.clone.back_ref) | copy-start | bytes 2032132
  13.7 5.1 %collective-permute-start.4 = (f32[2,56,128]{2,1,0:T(8,128)S(1)}, f32[2,56,128]{2,1,0:T(8,128)S(1)}, u32[]{:S(2)}, u32[]{:S(2)}) collective-permute-start(f32[2,56,128]{2,1,0:T(8,128)S(1)} %get-tuple-element.54), channel_id=1, source_target_pairs={{0,8},{1,9},{2,10},{3,11},{4,12},{5,13},{6,14},{7,15},{8,0},{9,1},... | collective-permute-start | bytes 172040 | tf_op jit(solution)/shard_map/ppermute | solution.py:118
  14.2 4.6 %collective-permute-start.5 = (f32[2,56,128]{2,1,0:T(8,128)S(1)}, f32[2,56,128]{2,1,0:T(8,128)S(1)}, u32[]{:S(2)}, u32[]{:S(2)}) collective-permute-start(f32[2,56,128]{2,1,0:T(8,128)S(1)} %get-tuple-element.55), channel_id=1, source_target_pairs={{0,24},{1,25},{2,26},{3,27},{4,28},{5,29},{6,30},{7,31},{8,16},{9,... | collective-permute-start | bytes 172040 | tf_op jit(solution)/shard_map/ppermute | solution.py:119
  15.8 8.3 %collective-permute-start.6 = (f32[2,96,128]{2,1,0:T(8,128)S(1)}, f32[2,96,128]{2,1,0:T(8,128)S(1)}, u32[]{:S(2)}, u32[]{:S(2)}) collective-permute-start(f32[2,96,128]{2,1,0:T(8,128)S(1)} %get-tuple-element.58), channel_id=1, source_target_pairs={{0,1},{1,0},{2,3},{3,2},{4,5},{5,4},{6,7},{7,6},{8,9},{9,8},{10,11... | collective-permute-start | bytes 294920 | tf_op jit(solution)/shard_map/ppermute | solution.py:122
  18.8 5.3 %collective-permute-start.7 = (f32[2,96,128]{2,1,0:T(8,128)S(1)}, f32[2,96,128]{2,1,0:T(8,128)S(1)}, u32[]{:S(2)}, u32[]{:S(2)}) collective-permute-start(f32[2,96,128]{2,1,0:T(8,128)S(1)} %get-tuple-element.59), channel_id=1, source_target_pairs={{0,8},{1,2},{2,1},{3,4},{4,3},{5,6},{6,5},{7,15},{8,0},{9,10},{10,... | collective-permute-start | bytes 294920 | tf_op jit(solution)/shard_map/ppermute | solution.py:121
  18.9 5.2 %collective-permute-start.8 = (f32[2,24,128]{2,1,0:T(8,128)S(1)}, f32[2,24,128]{2,1,0:T(8,128)S(1)}, u32[]{:S(2)}, u32[]{:S(2)}) collective-permute-start(f32[2,24,128]{2,1,0:T(8,128)S(1)} %get-tuple-element.60), channel_id=1, source_target_pairs={{0,1},{1,0},{2,3},{3,2},{4,5},{5,4},{6,7},{7,6},{8,9},{9,8},{10,11... | collective-permute-start | bytes 73736 | tf_op jit(solution)/shard_map/ppermute | solution.py:122
  22.0 2.1 %collective-permute-start.9 = (f32[2,24,128]{2,1,0:T(8,128)S(1)}, f32[2,24,128]{2,1,0:T(8,128)S(1)}, u32[]{:S(2)}, u32[]{:S(2)}) collective-permute-start(f32[2,24,128]{2,1,0:T(8,128)S(1)} %get-tuple-element.61), channel_id=1, source_target_pairs={{0,8},{1,2},{2,1},{3,4},{4,3},{5,6},{6,5},{7,15},{8,0},{9,10},{10,... | collective-permute-start | bytes 73736 | tf_op jit(solution)/shard_map/ppermute | solution.py:121
  22.7 1.4 %copy-start.9 = (bf16[336,432]{1,0:T(8,128)(2,1)S(1)}, bf16[336,432]{1,0:T(8,128)(2,1)}, u32[]{:S(2)}) copy-start(bf16[336,432]{1,0:T(8,128)(2,1)} %constant.19.clone.lines_ref) | copy-start | bytes 870916
  26.1 1.9 %collective-permute-start.10 = (f32[2,40,128]{2,1,0:T(8,128)S(1)}, f32[2,40,128]{2,1,0:T(8,128)S(1)}, u32[]{:S(2)}, u32[]{:S(2)}) collective-permute-start(f32[2,40,128]{2,1,0:T(8,128)S(1)} %get-tuple-element.73), channel_id=1, source_target_pairs={{0,8},{1,9},{2,10},{3,11},{4,12},{5,13},{6,14},{7,15},{8,0},{9,1},... | collective-permute-start | bytes 122888 | tf_op jit(solution)/shard_map/ppermute | solution.py:118
  26.6 3.6 %collective-permute-start.11 = (f32[2,40,128]{2,1,0:T(8,128)S(1)}, f32[2,40,128]{2,1,0:T(8,128)S(1)}, u32[]{:S(2)}, u32[]{:S(2)}) collective-permute-start(f32[2,40,128]{2,1,0:T(8,128)S(1)} %get-tuple-element.74), channel_id=1, source_target_pairs={{0,24},{1,25},{2,26},{3,27},{4,28},{5,29},{6,30},{7,31},{8,16},{9,... | collective-permute-start | bytes 122888 | tf_op jit(solution)/shard_map/ppermute | solution.py:119
  30.4 6.2 %collective-permute-start.12 = (f32[2,72,128]{2,1,0:T(8,128)S(1)}, f32[2,72,128]{2,1,0:T(8,128)S(1)}, u32[]{:S(2)}, u32[]{:S(2)}) collective-permute-start(f32[2,72,128]{2,1,0:T(8,128)S(1)} %get-tuple-element.83), channel_id=1, source_target_pairs={{0,1},{1,0},{2,3},{3,2},{4,5},{5,4},{6,7},{7,6},{8,9},{9,8},{10,11... | collective-permute-start | bytes 221192 | tf_op jit(solution)/shard_map/ppermute | solution.py:122
  32.9 3.8 %collective-permute-start.13 = (f32[2,72,128]{2,1,0:T(8,128)S(1)}, f32[2,72,128]{2,1,0:T(8,128)S(1)}, u32[]{:S(2)}, u32[]{:S(2)}) collective-permute-start(f32[2,72,128]{2,1,0:T(8,128)S(1)} %get-tuple-element.84), channel_id=1, source_target_pairs={{0,8},{1,2},{2,1},{3,4},{4,3},{5,6},{6,5},{7,15},{8,0},{9,10},{10,... | collective-permute-start | bytes 221192 | tf_op jit(solution)/shard_map/ppermute | solution.py:121
